TPU v7x, 32 devices: a whole 2x2x4 slice. The times are simulated.
32 devices in a mesh: node: 4 (over x, core), head: 8 (over z, y).
Axes of the slice: x: 2, y: 2, z: 4, core: 2. Of those that a mesh axis runs over, the one named last changes fastest.
Arguments:
- node_feats: bfloat16 [1024, 4096], P('node', 'head'), may hold values from -6 to 6
- w_qk: bfloat16 [4096, 4096], P('node', 'head'), may hold values from -0.09375 to 0.09375
- w_val: bfloat16 [4096, 4096], P('node', 'head'), may hold values from -0.09375 to 0.09375
- w_out: bfloat16 [4096, 4096], P('head', 'node'), may hold values from -0.75 to 0.75
- edge_types: int32 [8, 8], P('node'), may hold values from 0 to 236
- rel_bias: float32 [237, 32], P(None, 'head'), may hold values from -8 to 300
Outputs:
- mixed: bfloat16 [1024, 4096], P('node', 'head')
All inputs are finite; a program needn't handle non-finite values.
Results may differ from a plain program's by a relative error of at most 0.018.
Values may be sent and summed in bfloat16 or wider, within the bound.
No kernel may reach another device: no remote copies, remote signals or barrier semaphores. Data moves between devices by JAX's collectives and lax.ppermute only.
A program may use at most 64 MiB of HBM per device.

v0:
```python
import jax
import jax.numpy as jnp
from jax import lax
from jax.sharding import PartitionSpec as P

DH = 128
TILE = 128


NEG_BIG = -1e30


def from_behind(value, axis, by):
    peers = lax.axis_size(axis)
    return lax.ppermute(value, axis, [(i, (i + by) % peers) for i in range(peers)])


def pair_scores(queries, key_rows):
    inv_root = 1.0 / DH**0.5
    return (
        jnp.einsum("qhd,khd->hqk", queries, key_rows, preferred_element_type=jnp.float32) * inv_root
    )


def update(carried, scaled, bias_cols, value_rows, self_mask):
    head_count, query_count, key_count = scaled.shape
    tiles = bias_cols.shape[1]
    biased = (
        scaled.reshape(head_count, tiles, query_count // tiles, key_count)
        + bias_cols[:, :, None, :]
    )
    biased = biased.reshape(head_count, query_count, key_count)
    if self_mask is not None:
        biased = jnp.where(self_mask[None], NEG_BIG, biased)
    top_old, total_old, accum_old = carried
    top_new = jnp.maximum(top_old, jnp.max(biased, axis=2))
    expd = jnp.exp(biased - top_new[:, :, None])
    if self_mask is not None:
        expd = jnp.where(self_mask[None], 0.0, expd)
    factor = jnp.exp(top_old - top_new)
    total_new = total_old * factor + jnp.sum(expd, axis=2)
    product = jnp.einsum(
        "hqk,khd->hqd", expd.astype(jnp.bfloat16), value_rows, preferred_element_type=jnp.float32
    )
    return (top_new, total_new, accum_old * factor[:, :, None] + product)


def on_device(node_feats, w_qk, w_val, w_out, edge_types, rel_bias):
    row_count = node_feats.shape[0]
    col_width = w_qk.shape[1]
    head_count = rel_bias.shape[1]
    tile_rows = edge_types.shape[0]
    full_qk, full_val = (
        lax.all_gather(w_qk, "node", axis=0, tiled=True),
        lax.all_gather(w_val, "node", axis=0, tiled=True),
    )
    shard_piece = lax.all_gather(node_feats, "head", axis=1, tiled=True)
    proj_qk = jnp.dot(shard_piece, full_qk, preferred_element_type=jnp.float32)
    proj_val = jnp.dot(shard_piece, full_val, preferred_element_type=jnp.float32)
    qk_local = proj_qk.astype(jnp.bfloat16)
    val_local = proj_val.astype(jnp.bfloat16)
    queries = qk_local.reshape(row_count, head_count, DH)
    values = val_local.reshape(row_count, head_count, DH)
    relation_ids = jnp.arange(rel_bias.shape[0], dtype=jnp.int32)
    one_hot = (edge_types[:, :, None] == relation_ids[None, None, :]).astype(jnp.float32)
    tile_bias = jnp.einsum("abr,rh->hab", one_hot, rel_bias, precision=lax.Precision.HIGHEST)
    expanded = jnp.repeat(tile_bias, TILE, axis=2)
    my_block = lax.axis_index("node")
    first_row = my_block * row_count
    row_ids = first_row + jnp.arange(row_count, dtype=jnp.int32)
    initial = (
        jnp.full((head_count, row_count), NEG_BIG, jnp.float32),
        jnp.zeros((head_count, row_count), jnp.float32),
        jnp.zeros((head_count, row_count, DH), jnp.float32),
    )
    node_count = lax.axis_size("node")
    rounds = node_count // 2
    own_cols = lax.dynamic_slice_in_dim(expanded, first_row, row_count, 2)
    own_mask = row_ids[:, None] == row_ids[None, :]
    own_state = update(initial, pair_scores(queries, queries), own_cols, values, own_mask)

    def one_round(round_no, carried):
        mine, moving_block, moving_state = carried
        key_flat, value_flat = from_behind((moving_block[0], moving_block[1]), "node", 1)
        bias_moved, top_moved, total_moved, accum_moved = (
            from_behind(moving_state[0].astype(jnp.bfloat16), "node", 1).astype(jnp.float32),
            from_behind(moving_state[1].astype(jnp.bfloat16), "node", 1).astype(jnp.float32),
            from_behind(moving_state[2].astype(jnp.bfloat16), "node", 1).astype(jnp.float32),
            from_behind(moving_state[3].astype(jnp.bfloat16), "node", 1).astype(jnp.float32),
        )
        partner = (my_block - round_no) % node_count
        key_rows = key_flat.reshape(row_count, head_count, DH)
        value_rows = value_flat.reshape(row_count, head_count, DH)
        raw_scores = pair_scores(queries, key_rows)
        mine_cols = lax.dynamic_slice_in_dim(expanded, partner * row_count, row_count, 2)
        mine = update(mine, raw_scores, mine_cols, value_rows, None)
        back_tiles = lax.dynamic_slice_in_dim(bias_moved, my_block * tile_rows, tile_rows, 2)
        back_cols = jnp.repeat(back_tiles, TILE, axis=2)
        passed = update(
            (top_moved, total_moved, accum_moved),
            jnp.transpose(raw_scores, (0, 2, 1)),
            back_cols,
            values,
            None,
        )
        keep_flag = 2 * round_no != node_count
        kept = jax.tree.map(
            lambda fresh, stale: jnp.where(keep_flag, fresh, stale),
            passed,
            (top_moved, total_moved, accum_moved),
        )
        return (mine, (key_flat, value_flat), (bias_moved, kept[0], kept[1], kept[2]))

    start_state = (tile_bias, initial[0], initial[1], initial[2])
    own_state, _, final_moving = lax.fori_loop(
        1, rounds + 1, one_round, (own_state, (qk_local, val_local), start_state)
    )
    top_home, total_home, accum_home = (
        from_behind(final_moving[1].astype(jnp.bfloat16), "node", -rounds).astype(jnp.float32),
        from_behind(final_moving[2].astype(jnp.bfloat16), "node", -rounds).astype(jnp.float32),
        from_behind(final_moving[3].astype(jnp.bfloat16), "node", -rounds).astype(jnp.float32),
    )
    top_fin = jnp.maximum(own_state[0], top_home)
    factor_own = jnp.exp(own_state[0] - top_fin)
    factor_home = jnp.exp(top_home - top_fin)
    total_fin = own_state[1] * factor_own + total_home * factor_home
    accum_fin = own_state[2] * factor_own[:, :, None] + accum_home * factor_home[:, :, None]
    attn_heads = (accum_fin / total_fin[:, :, None]).astype(jnp.bfloat16)
    attn = jnp.transpose(attn_heads, (1, 0, 2)).reshape(row_count, col_width)
    terms = jnp.dot(
        attn, lax.all_gather(w_out, "node", axis=1, tiled=True), preferred_element_type=jnp.float32
    )
    return lax.psum_scatter(terms.astype(jnp.bfloat16), "head", scatter_dimension=1, tiled=True)


def solution(mesh):
    in_specs = (
        P("node", "head"),
        P("node", "head"),
        P("node", "head"),
        P("head", "node"),
        P("node", None),
        P(None, "head"),
    )
    out_specs = P("node", "head")
    return jax.shard_map(
        on_device, mesh=mesh, in_specs=in_specs, out_specs=out_specs, check_vma=False
    )
```

profile of v0, /device:TPU:0, one launch (start us, length us, event | category | flops | bytes accessed | tf_op | source)
XLA Modules:
  0.0 274.9 jit_solution(7688410776885783441)
XLA Ops:
  6.5 0.7 all-gather.5.cloned.1.call-update
  7.3 0.7 all-gather.9.cloned.1.call-update
  8.1 0.7 all-gather.7.cloned.1.call-update
  8.8 0.5 all-gather.11.cloned.1.call-update
  9.4 0.9 convolution_bitcast_fusion
  10.3 0.2 copy.28
  10.6 0.2 copy.23
  10.8 1.2 add.190
  12.0 0.8 add.191
  12.9 0.1 broadcast_compare_fusion
  13.0 50.2 %all-gather.5.cloned.1.call-done = bf16[256,4096]{1,0:T(8,128)(2,1)} async-done(((bf16[256,512]{1,0:T(8,128)(2,1)}), bf16[256,4096]{1,0:T(8,128)(2,1)}) %all-gather.5.cloned.1.call-update) | async-done | bytes 2097168 | tf_op jit(solution)/shard_map/all_gather | solution.py:57
  63.2 34.3 %all-gather.9.cloned.1.call-done = bf16[4096,512]{1,0:T(8,128)(2,1)} async-done(((bf16[1024,512]{1,0:T(8,128)(2,1)}), bf16[4096,512]{1,0:T(8,128)(2,1)}) %all-gather.9.cloned.1.call-update) | async-done | bytes 4194320 | tf_op jit(solution)/shard_map/all_gather | solution.py:55
  97.5 4.1 %convolution_convert_fusion.1 = bf16[256,512]{1,0:T(8,128)(2,1)S(1)} fusion(bf16[256,4096]{1,0:T(8,128)(2,1)} %all-gather.5.cloned.1.call-done, bf16[4096,512]{1,0:T(8,128)(2,1)} %all-gather.9.cloned.1.call-done), kind=kOutput, calls=%fused_computation.36 | convolution fusion | flops 1073872896 | bytes 6553600 | tf_op jit(solution)/shard_map/dot_general | solution.py:59
  101.5 0.9 copy.27
  102.5 31.1 %all-gather.7.cloned.1.call-done = bf16[4096,512]{1,0:T(8,128)(2,1)} async-done(((bf16[1024,512]{1,0:T(8,128)(2,1)}), bf16[4096,512]{1,0:T(8,128)(2,1)}) %all-gather.7.cloned.1.call-update) | async-done | bytes 4194320 | tf_op jit(solution)/shard_map/all_gather | solution.py:54
  133.5 4.1 %convolution_convert_fusion.2 = bf16[256,512]{1,0:T(8,128)(2,1)S(1)} fusion(bf16[256,4096]{1,0:T(8,128)(2,1)} %all-gather.5.cloned.1.call-done, bf16[4096,512]{1,0:T(8,128)(2,1)} %all-gather.7.cloned.1.call-done), kind=kOutput, calls=%fused_computation.37 | convolution fusion | flops 1073872896 | bytes 6553600 | tf_op jit(solution)/shard_map/dot_general | solution.py:58
  137.6 0.8 copy.26
  138.5 0.4 fusion.31
  138.8 0.2 fusion.17
  139.0 0.7 copy_bitcast_fusion.1
  139.8 0.5 convolution_add_fusion.1
  140.3 45.8 %while.32 = (s32[]{:T(128)}, f32[4,256]{1,0:T(4,128)S(1)}, f32[4,256]{1,0:T(4,128)S(1)}, f32[4,256,128]{2,1,0:T(8,128)S(1)}, bf16[256,512]{0,1:T(8,128)(2,1)}, /...) while((s32[]{:T(128)}, f32[4,256]{1,0:T(4,128)S(1)}, ...), condition=%wide.region_7.8_spmd.clone, body=%wide.region_2.7_spmd.clone.sunk | while | flops 206190736 | bytes 20111428 | solution.py:115
  140.3 0.3 collective-permute-start
  140.6 0.2 collective-permute-start.2
  140.8 0.2 collective-permute-start.4
  141.0 1.6 collective-permute-start.3
  142.6 0.8 select_convert_fusion.8
  143.4 0.2 collective-permute-start.5
  143.6 4.7 %collective-permute-done.2 = bf16[4,2,8]{1,2,0:T(8,128)(2,1)S(1)} collective-permute-done((bf16[4,2,8]{1,2,0:T(8,128)(2,1)S(1)}, bf16[4,2,8]{1,2,0:T(8,128)(2,1)S(1)}, u32[]{:S(2)}, u32[]{:S(2)}) %collective-permute-start.2) | collective-permute-done | bytes 160 | tf_op jit(solution)/shard_map/while/body/eval_jaxpr/ppermute | solution.py:15
  148.4 1.2 add.279
  149.6 0.8 add.280
  150.5 1.4 fusion.63
  151.8 0.4 fusion.64
  152.3 0.2 fusion.65
  152.4 0.2 fusion.66
  152.7 0.7 copy.69
  153.4 11.9 %collective-permute-done.1 = bf16[256,512]{0,1:T(8,128)(2,1)S(1)} collective-permute-done((bf16[256,512]{0,1:T(8,128)(2,1)}, bf16[256,512]{0,1:T(8,128)(2,1)S(1)}, u32[]{:S(2)}, u32[]{:S(2)}) %collective-permute-start.1) | collective-permute-done | bytes 262176 | tf_op jit(solution)/shard_map/while/body/eval_jaxpr/ppermute | solution.py:15
  165.3 0.7 copy.70
  166.1 0.4 convolution_add_fusion.3
  166.5 1.4 convert_select_fusion.6
  168.0 0.4 collective-permute-start.2
  168.5 1.7 collective-permute-start.3
  170.3 0.8 select_convert_fusion.8
  171.1 6.4 %collective-permute-done.2 = bf16[4,2,8]{1,2,0:T(8,128)(2,1)S(1)} collective-permute-done((bf16[4,2,8]{1,2,0:T(8,128)(2,1)S(1)}, bf16[4,2,8]{1,2,0:T(8,128)(2,1)S(1)}, u32[]{:S(2)}, u32[]{:S(2)}) %collective-permute-start.2) | collective-permute-done | bytes 160 | tf_op jit(solution)/shard_map/while/body/eval_jaxpr/ppermute | solution.py:15
  177.5 1.2 add.279
  178.7 0.8 add.280
  179.6 1.4 fusion.63
  181.0 0.4 fusion.64
  181.4 0.2 fusion.65
  181.6 0.2 fusion.66
  181.8 0.7 copy.69
  182.5 1.0 collective-permute-done.1
  183.5 0.7 copy.70
  184.2 0.4 convolution_add_fusion.3
  184.7 1.4 convert_select_fusion.6
  186.1 0.1 copy.32
  186.2 0.4 collective-permute-start.7
  186.6 1.7 collective-permute-start.6
  188.3 0.3 collective-permute-start.8
  188.6 0.2 copy.31
  188.8 5.2 %collective-permute-done.6 = bf16[4,256]{1,0:T(4,128)(2,1)S(1)} collective-permute-done((bf16[4,256]{1,0:T(4,128)(2,1)S(1)}, bf16[4,256]{1,0:T(4,128)(2,1)S(1)}, u32[]{:S(2)}, u32[]{:S(2)}) %collective-permute-start.6) | collective-permute-done | bytes 2080 | tf_op jit(solution)/shard_map/ppermute | solution.py:15
  194.1 0.1 divide_convert_fusion
  194.2 4.8 %convolution_convert_fusion = bf16[256,4096]{1,0:T(8,128)(2,1)} fusion(bf16[256,512]{0,1:T(8,128)(2,1)S(1)} %bitcast.96, bf16[512,4096]{1,0:T(8,128)(2,1)} %all-gather.11.cloned.1.call-done), kind=kOutput, calls=%fused_computation.31 | convolution fusion | flops 1074790400 | bytes 6553600 | tf_op jit(solution)/shard_map/dot_general | solution.py:130
  199.0 69.3 %reduce-scatter.2.cloned.1.call-done = bf16[256,512]{1,0:T(8,128)(2,1)} async-done(((bf16[256,4096]{1,0:T(8,128)(2,1)}), bf16[256,512]{1,0:T(8,128)(2,1)}) %reduce-scatter.2.cloned.1.call-update) | async-done | bytes 262160 | tf_op jit(solution)/shard_map/reduce_scatter | solution.py:133
  (60 shorter events, 0.9 us)
Async XLA Ops:
  6.5 2.8 %copy-start = (f32[237,4]{0,1:T(4,128)S(1)}, f32[237,4]{0,1:T(4,128)}, u32[]{:S(2)}) copy-start(f32[237,4]{0,1:T(4,128)} %param.13) | copy-start | bytes 11380
  6.5 56.7 %all-gather.5.cloned.1.call-start = ((), (), s32[]{:S(2)}) async-start(), calls=%async_computation.1 | async-start | bytes 2359296 | tf_op jit(solution)/shard_map/all_gather | solution.py:57
  7.3 90.2 %all-gather.9.cloned.1.call-start = ((), (), s32[]{:S(2)}) async-start(), calls=%async_computation.3 | async-start | bytes 5242880 | tf_op jit(solution)/shard_map/all_gather | solution.py:55
  8.0 125.5 %all-gather.7.cloned.1.call-start = ((), (), s32[]{:S(2)}) async-start(), calls=%async_computation.2 | async-start | bytes 5242880 | tf_op jit(solution)/shard_map/all_gather | solution.py:54
  8.7 185.5 %all-gather.11.cloned.1.call-start = ((), (), s32[]{:S(2)}) async-start(), calls=%async_computation.4 | async-start | bytes 5242880 | tf_op jit(solution)/shard_map/all_gather | solution.py:131
  9.3 259.1 %reduce-scatter.2.cloned.1.call-start = ((), (), s32[]{:S(2)}) async-start(), calls=%async_computation.5 | async-start | bytes 2359296 | tf_op jit(solution)/shard_map/reduce_scatter | solution.py:133
  140.3 10.2 %collective-permute-start = (bf16[256,512]{0,1:T(8,128)(2,1)}, bf16[256,512]{0,1:T(8,128)(2,1)S(1)}, u32[]{:S(2)}, u32[]{:S(2)}) collective-permute-start(bf16[256,512]{0,1:T(8,128)(2,1)} %get-tuple-element.615), channel_id=1, source_target_pairs={{0,8},{8,16},{16,24},{24,0},{1,9},{9,17},{17,25},{25,1},{2,10},{10... | collective-permute-start | bytes 786440 | tf_op jit(solution)/shard_map/while/body/eval_jaxpr/ppermute | solution.py:15
  140.6 7.7 %collective-permute-start.2 = (bf16[4,2,8]{1,2,0:T(8,128)(2,1)S(1)}, bf16[4,2,8]{1,2,0:T(8,128)(2,1)S(1)}, u32[]{:S(2)}, u32[]{:S(2)}) collective-permute-start(bf16[4,2,8]{1,2,0:T(8,128)(2,1)S(1)} %convert_element_type.213), channel_id=1, source_target_pairs={{0,8},{8,16},{16,24},{24,0},{1,9},{9,17},{17,25},{25,1},{2,10},{10... | collective-permute-start | bytes 392 | tf_op jit(solution)/shard_map/while/body/eval_jaxpr/ppermute | solution.py:15
  140.8 11.7 %collective-permute-start.4 = (bf16[4,256]{1,0:T(4,128)(2,1)S(1)}, bf16[4,256]{1,0:T(4,128)(2,1)S(1)}, u32[]{:S(2)}, u32[]{:S(2)}) collective-permute-start(bf16[4,256]{1,0:T(4,128)(2,1)S(1)} %select_convert_fusion.7), channel_id=1, source_target_pairs={{0,8},{8,16},{16,24},{24,0},{1,9},{9,17},{17,25},{25,1},{2,10},{10... | collective-permute-start | bytes 6152 | tf_op jit(solution)/shard_map/while/body/eval_jaxpr/ppermute | solution.py:15
  141.0 25.0 %collective-permute-start.3 = (bf16[4,256]{1,0:T(4,128)(2,1)S(1)}, bf16[4,256]{1,0:T(4,128)(2,1)S(1)}, u32[]{:S(2)}, u32[]{:S(2)}) collective-permute-start(bf16[4,256]{1,0:T(4,128)(2,1)S(1)} %select_convert_fusion.6), channel_id=1, source_target_pairs={{0,8},{8,16},{16,24},{24,0},{1,9},{9,17},{17,25},{25,1},{2,10},{10... | collective-permute-start | bytes 6152 | tf_op jit(solution)/shard_map/while/body/eval_jaxpr/ppermute | solution.py:15
  143.4 23.2 %collective-permute-start.5 = (bf16[4,256,128]{2,1,0:T(8,128)(2,1)}, bf16[4,256,128]{2,1,0:T(8,128)(2,1)}, u32[]{:S(2)}, u32[]{:S(2)}) collective-permute-start(bf16[4,256,128]{2,1,0:T(8,128)(2,1)} %select_convert_fusion.8), channel_id=1, source_target_pairs={{0,8},{8,16},{16,24},{24,0},{1,9},{9,17},{17,25},{25,1},{2,10},{10... | collective-permute-start | bytes 786440 | tf_op jit(solution)/shard_map/while/body/eval_jaxpr/ppermute | solution.py:15
  148.3 17.0 %collective-permute-start.1 = (bf16[256,512]{0,1:T(8,128)(2,1)}, bf16[256,512]{0,1:T(8,128)(2,1)S(1)}, u32[]{:S(2)}, u32[]{:S(2)}) collective-permute-start(bf16[256,512]{0,1:T(8,128)(2,1)} %get-tuple-element.616), channel_id=1, source_target_pairs={{0,8},{8,16},{16,24},{24,0},{1,9},{9,17},{17,25},{25,1},{2,10},{10... | collective-permute-start | bytes 786440 | tf_op jit(solution)/shard_map/while/body/eval_jaxpr/ppermute | solution.py:15
  167.9 11.7 %collective-permute-start = (bf16[256,512]{0,1:T(8,128)(2,1)}, bf16[256,512]{0,1:T(8,128)(2,1)S(1)}, u32[]{:S(2)}, u32[]{:S(2)}) collective-permute-start(bf16[256,512]{0,1:T(8,128)(2,1)} %get-tuple-element.615), channel_id=1, source_target_pairs={{0,8},{8,16},{16,24},{24,0},{1,9},{9,17},{17,25},{25,1},{2,10},{10... | collective-permute-start | bytes 786440 | tf_op jit(solution)/shard_map/while/body/eval_jaxpr/ppermute | solution.py:15
  168.0 9.4 %collective-permute-start.2 = (bf16[4,2,8]{1,2,0:T(8,128)(2,1)S(1)}, bf16[4,2,8]{1,2,0:T(8,128)(2,1)S(1)}, u32[]{:S(2)}, u32[]{:S(2)}) collective-permute-start(bf16[4,2,8]{1,2,0:T(8,128)(2,1)S(1)} %convert_element_type.213), channel_id=1, source_target_pairs={{0,8},{8,16},{16,24},{24,0},{1,9},{9,17},{17,25},{25,1},{2,10},{10... | collective-permute-start | bytes 392 | tf_op jit(solution)/shard_map/while/body/eval_jaxpr/ppermute | solution.py:15
  168.4 13.1 %collective-permute-start.4 = (bf16[4,256]{1,0:T(4,128)(2,1)S(1)}, bf16[4,256]{1,0:T(4,128)(2,1)S(1)}, u32[]{:S(2)}, u32[]{:S(2)}) collective-permute-start(bf16[4,256]{1,0:T(4,128)(2,1)S(1)} %select_convert_fusion.7), channel_id=1, source_target_pairs={{0,8},{8,16},{16,24},{24,0},{1,9},{9,17},{17,25},{25,1},{2,10},{10... | collective-permute-start | bytes 6152 | tf_op jit(solution)/shard_map/while/body/eval_jaxpr/ppermute | solution.py:15
  168.5 15.7 %collective-permute-start.3 = (bf16[4,256]{1,0:T(4,128)(2,1)S(1)}, bf16[4,256]{1,0:T(4,128)(2,1)S(1)}, u32[]{:S(2)}, u32[]{:S(2)}) collective-permute-start(bf16[4,256]{1,0:T(4,128)(2,1)S(1)} %select_convert_fusion.6), channel_id=1, source_target_pairs={{0,8},{8,16},{16,24},{24,0},{1,9},{9,17},{17,25},{25,1},{2,10},{10... | collective-permute-start | bytes 6152 | tf_op jit(solution)/shard_map/while/body/eval_jaxpr/ppermute | solution.py:15
  171.0 13.6 %collective-permute-start.5 = (bf16[4,256,128]{2,1,0:T(8,128)(2,1)}, bf16[4,256,128]{2,1,0:T(8,128)(2,1)}, u32[]{:S(2)}, u32[]{:S(2)}) collective-permute-start(bf16[4,256,128]{2,1,0:T(8,128)(2,1)} %select_convert_fusion.8), channel_id=1, source_target_pairs={{0,8},{8,16},{16,24},{24,0},{1,9},{9,17},{17,25},{25,1},{2,10},{10... | collective-permute-start | bytes 786440 | tf_op jit(solution)/shard_map/while/body/eval_jaxpr/ppermute | solution.py:15
  177.4 6.0 %collective-permute-start.1 = (bf16[256,512]{0,1:T(8,128)(2,1)}, bf16[256,512]{0,1:T(8,128)(2,1)S(1)}, u32[]{:S(2)}, u32[]{:S(2)}) collective-permute-start(bf16[256,512]{0,1:T(8,128)(2,1)} %get-tuple-element.616), channel_id=1, source_target_pairs={{0,8},{8,16},{16,24},{24,0},{1,9},{9,17},{17,25},{25,1},{2,10},{10... | collective-permute-start | bytes 786440 | tf_op jit(solution)/shard_map/while/body/eval_jaxpr/ppermute | solution.py:15
  186.2 7.8 %collective-permute-start.7 = (bf16[4,256,128]{1,2,0:T(8,128)(2,1)S(1)}, bf16[4,256,128]{1,2,0:T(8,128)(2,1)S(1)}, u32[]{:S(2)}, u32[]{:S(2)}) collective-permute-start(bf16[4,256,128]{1,2,0:T(8,128)(2,1)S(1)} %copy.32), channel_id=1, source_target_pairs={{0,16},{8,24},{16,0},{24,8},{1,17},{9,25},{17,1},{25,9},{2,18},{10... | collective-permute-start | bytes 786440 | tf_op jit(solution)/shard_map/ppermute | solution.py:15
  186.6 7.4 %collective-permute-start.6 = (bf16[4,256]{1,0:T(4,128)(2,1)S(1)}, bf16[4,256]{1,0:T(4,128)(2,1)S(1)}, u32[]{:S(2)}, u32[]{:S(2)}) collective-permute-start(bf16[4,256]{1,0:T(4,128)(2,1)S(1)} %get-tuple-element.352), channel_id=1, source_target_pairs={{0,16},{8,24},{16,0},{24,8},{1,17},{9,25},{17,1},{25,9},{2,18},{10... | collective-permute-start | bytes 6152 | tf_op jit(solution)/shard_map/ppermute | solution.py:15
  188.3 5.7 %collective-permute-start.8 = (bf16[4,256]{1,0:T(4,128)(2,1)S(1)}, bf16[4,256]{1,0:T(4,128)(2,1)S(1)}, u32[]{:S(2)}, u32[]{:S(2)}) collective-permute-start(bf16[4,256]{1,0:T(4,128)(2,1)S(1)} %get-tuple-element.355), channel_id=1, source_target_pairs={{0,16},{8,24},{16,0},{24,8},{1,17},{9,25},{17,1},{25,9},{2,18},{10... | collective-permute-start | bytes 6152 | tf_op jit(solution)/shard_map/ppermute | solution.py:15
Sparse Core Ops, SparseCore 0:
  9.4 53.7 all-gather.4
  64.8 32.6 all-gather.8
  99.0 34.4 all-gather.6
  135.0 42.8 all-gather.10
  199.1 69.1 reduce-scatter.1
where the time goes:
time: 275 us
  waiting for transfers between devices  217 us (79%)
  matrix products  21 us (8%)
  between operations  13.3 us (5%)
  local copies, waits for them, and re-layouts  12.5 us (5%)
  starting transfers between devices  7.49 us (3%)
  other arithmetic  3.61 us (1%)
    reduce_scatter x1, waiting for transfers between devices, on_device(): lax.psum_scatter(terms.astype(jnp.bfloat16), 'head', scatter_dimension=1,...  69.3 us
    all_gather x1, waiting for transfers between devices, on_device(): shard_piece = lax.all_gather(node_feats, 'head', axis=1, tiled=True)  50.2 us
    all_gather x1, waiting for transfers between devices, on_device(): lax.all_gather(w_val, 'node', axis=0, tiled=True)  34.3 us
    all_gather x1, waiting for transfers between devices, on_device(): lax.all_gather(w_qk, 'node', axis=0, tiled=True)  31.1 us
    ppermute x15, waiting for transfers between devices, from_behind(): lax.ppermute(value, axis, [(i, (i + by) % peers) for i in range(peers)])  29.2 us
    ppermute x15, starting transfers between devices, from_behind(): lax.ppermute(value, axis, [(i, (i + by) % peers) for i in range(peers)])  7.34 us
    add x6, local copies, waits for them, and re-layouts, update(): scaled.reshape(head_count, tiles, query_count // tiles, key_count)  6.22 us
  transfers between devices with their start and end apart: 20, of which 9 were waited for; matrix products, arithmetic and copies ran while one was open for 12% of the time, Pallas kernels for 0%

commit v1 on v0

--- a/solution.py
+++ b/solution.py
@@ -1,6 +1,10 @@
+import functools
+
 import jax
 import jax.numpy as jnp
 from jax import lax
+from jax.experimental import pallas as pl
+from jax.experimental.pallas import tpu as pltpu
 from jax.sharding import PartitionSpec as P
 
 DH = 128
@@ -8,6 +12,227 @@
 
 
 NEG_BIG = -1e30
+
+
+def swap(value, axis, mask):
+    peers = lax.axis_size(axis)
+    return lax.ppermute(value, axis, [(i, i ^ mask) for i in range(peers)])
+
+
+def after(value, *others):
+    return lax.optimization_barrier((value, *others))[0]
+
+
+def vmem_spec():
+    return pl.BlockSpec(memory_space=pltpu.VMEM)
+
+
+def smem_spec():
+    return pl.BlockSpec(memory_space=pltpu.SMEM)
+
+
+def any_spec():
+    return pl.BlockSpec(memory_space=pl.ANY)
+
+
+def project_kernel(place_ref, *refs):
+    pieces, weights, outs = refs[:8], refs[8:12], refs[12:16]
+    feats, held, total, heads, piece_sem, weight_sem = refs[16:]
+    node, head = place_ref[0], place_ref[1]
+    copies = []
+    for i in range(8):
+        copy = pltpu.make_async_copy(pieces[i], feats.at[head ^ i], piece_sem.at[i])
+        copy.start()
+        copies.append(copy)
+    weight_copies = []
+    for i in range(4):
+        copy = pltpu.make_async_copy(weights[i], held.at[i], weight_sem.at[i])
+        copy.start()
+        weight_copies.append(copy)
+    for copy in copies:
+        copy.wait()
+    depth = feats.shape[2]
+    for i in range(4):
+        weight_copies[i].wait()
+        for part in range(2):
+            term = jnp.dot(
+                feats[2 * (node ^ i) + part],
+                held[i, part * depth : (part + 1) * depth, :],
+                preferred_element_type=jnp.float32,
+            )
+            if i == 0 and part == 0:
+                total[...] = term
+            else:
+                total[...] += term
+    for i in range(4):
+        heads[i] = total[:, i * DH : (i + 1) * DH].astype(jnp.bfloat16)
+    for i in range(4):
+        outs[i][...] = heads[node ^ i]
+
+
+def project(place, pieces, weights):
+    rows, depth = pieces[0].shape
+    cols = weights[0].shape[1]
+    flops = 2 * rows * 8 * depth * cols
+    moved = 2 * (8 * rows * depth + 8 * depth * cols + rows * cols)
+    return pl.pallas_call(
+        project_kernel,
+        out_shape=[jax.ShapeDtypeStruct((rows, DH), jnp.bfloat16)] * 4,
+        in_specs=[smem_spec()] + [any_spec()] * 12,
+        out_specs=[vmem_spec()] * 4,
+        scratch_shapes=[
+            pltpu.VMEM((8, rows, depth), jnp.bfloat16),
+            pltpu.VMEM((4, 2 * depth, cols), jnp.bfloat16),
+            pltpu.VMEM((rows, cols), jnp.float32),
+            pltpu.VMEM((4, rows, DH), jnp.bfloat16),
+            pltpu.SemaphoreType.DMA((8,)),
+            pltpu.SemaphoreType.DMA((4,)),
+        ],
+        compiler_params=pltpu.CompilerParams(vmem_limit_bytes=20 * 2**20),
+        cost_estimate=pl.CostEstimate(flops=flops, bytes_accessed=moved, transcendentals=0),
+        name="project",
+    )(place, *pieces, *weights)
+
+
+def attend_kernel(place_ref, edge_ref, bias_ref, *refs):
+    queries, values, outs = refs[:4], refs[4:8], refs[8:12]
+    node = place_ref[0]
+    inv_root = 1.0 / DH**0.5
+    rows = queries[0].shape[0]
+    tiles = rows // TILE
+    for i in range(4):
+        for ti in range(tiles):
+            mine = queries[i][ti * TILE : (ti + 1) * TILE, :]
+            row_tile = tiles * (node ^ i) + ti
+            scores = []
+            for j in range(4):
+                raw = lax.dot_general(
+                    mine, queries[j][...], (((1,), (1,)), ((), ())),
+                    preferred_element_type=jnp.float32,
+                )
+                for tj in range(tiles):
+                    relation = edge_ref[row_tile, tiles * (node ^ j) + tj]
+                    part = raw[:, tj * TILE : (tj + 1) * TILE] * inv_root + bias_ref[relation]
+                    if i == j and ti == tj:
+                        row_ids = lax.broadcasted_iota(jnp.int32, (TILE, TILE), 0)
+                        col_ids = lax.broadcasted_iota(jnp.int32, (TILE, TILE), 1)
+                        part = jnp.where(row_ids == col_ids, NEG_BIG, part)
+                    scores.append(part)
+            top = functools.reduce(jnp.maximum, scores)
+            top = jnp.max(top, axis=1, keepdims=True)
+            expd = [jnp.exp(part - top) for part in scores]
+            total = jnp.sum(functools.reduce(jnp.add, expd), axis=1, keepdims=True)
+            mixed = None
+            for j in range(4):
+                block = jnp.concatenate(
+                    [part.astype(jnp.bfloat16) for part in expd[tiles * j : tiles * (j + 1)]], axis=1
+                )
+                term = jnp.dot(block, values[j][...], preferred_element_type=jnp.float32)
+                mixed = term if mixed is None else mixed + term
+            outs[i][ti * TILE : (ti + 1) * TILE, :] = (mixed / total).astype(jnp.bfloat16)
+
+
+def attend(place, edges, bias, queries, values):
+    rows = queries[0].shape[0]
+    nodes = 4 * rows
+    return pl.pallas_call(
+        attend_kernel,
+        out_shape=[jax.ShapeDtypeStruct((rows, DH), jnp.bfloat16)] * 4,
+        in_specs=[smem_spec()] * 3 + [vmem_spec()] * 8,
+        out_specs=[vmem_spec()] * 4,
+        compiler_params=pltpu.CompilerParams(vmem_limit_bytes=16 * 2**20),
+        cost_estimate=pl.CostEstimate(
+            flops=4 * nodes * nodes * DH, bytes_accessed=6 * nodes * DH, transcendentals=nodes * nodes
+        ),
+        name="attend",
+    )(place, edges, bias, *queries, *values)
+
+
+def emit_kernel(place_ref, *refs):
+    parts, weights, outs = refs[:4], refs[4:8], refs[8:16]
+    held, heads, weight_sem = refs[16:]
+    node, head = place_ref[0], place_ref[1]
+    far, near = head // 2, head % 2
+    copies = []
+    for i in range(4):
+        copy = pltpu.make_async_copy(weights[i], held.at[node ^ i], weight_sem.at[i])
+        copy.start()
+        copies.append(copy)
+    for i in range(4):
+        heads[node ^ i] = parts[i][...]
+    attn = jnp.concatenate([heads[i] for i in range(4)], axis=1)
+    for copy in copies:
+        copy.wait()
+    width = outs[0].shape[1]
+    for i in (3, 2, 1, 0):
+        for side in range(2):
+            start = pl.multiple_of((near ^ side) * width, width)
+            term = jnp.dot(
+                attn, held[far ^ i, :, pl.ds(start, width)], preferred_element_type=jnp.float32
+            )
+            outs[4 * side + i][...] = term.astype(jnp.bfloat16)
+
+
+def emit(place, parts, weights):
+    rows = parts[0].shape[0]
+    depth, cols = weights[0].shape
+    flops = 2 * rows * depth * 4 * cols
+    moved = 2 * (rows * depth + 4 * depth * cols + 4 * rows * cols)
+    return pl.pallas_call(
+        emit_kernel,
+        out_shape=[jax.ShapeDtypeStruct((rows, cols // 2), jnp.bfloat16)] * 8,
+        in_specs=[smem_spec()] + [vmem_spec()] * 4 + [any_spec()] * 4,
+        out_specs=[vmem_spec()] * 8,
+        scratch_shapes=[
+            pltpu.VMEM((4, depth, cols), jnp.bfloat16),
+            pltpu.VMEM((4, rows, DH), jnp.bfloat16),
+            pltpu.SemaphoreType.DMA((4,)),
+        ],
+        compiler_params=pltpu.CompilerParams(vmem_limit_bytes=20 * 2**20),
+        cost_estimate=pl.CostEstimate(flops=flops, bytes_accessed=moved, transcendentals=0),
+        name="emit",
+    )(place, *parts, *weights)
+
+
+def gather_pairs(value):
+    across = swap(value, "node", 2)
+    beside = swap(value, "node", 1)
+    return [value, beside, across, swap(across, "node", 1)]
+
+
+def exchange_heads(pieces):
+    return [pieces[0]] + [swap(pieces[i], "node", i) for i in range(1, 4)]
+
+
+def one_head_each(node_feats, w_qk, w_val, w_out, edge_types, rel_bias):
+    node, head = lax.axis_index("node"), lax.axis_index("head")
+    place = jnp.stack([node, head]).astype(jnp.int32)
+    edges = lax.all_gather(edge_types, "node", axis=0, tiled=True)
+    bias = lax.dynamic_index_in_dim(rel_bias, node, 1, keepdims=False)
+
+    far = {i: swap(node_feats, "head", 2 * i) for i in (3, 2, 1)}
+    far[0] = node_feats
+    full_qk = gather_pairs(w_qk)
+    pieces = [None] * 8
+    for i in (0, 1, 2, 3):
+        pieces[2 * i] = far[i]
+        pieces[2 * i + 1] = swap(far[i], "head", 1)
+    full_val = gather_pairs(after(w_val, full_qk[2]))
+    full_out = gather_pairs(after(w_out, full_val[2]))
+
+    queries = exchange_heads(project(place, pieces, full_qk))
+    values = exchange_heads(project(place, pieces, full_val))
+    attn = exchange_heads(attend(place, edges, bias, queries, values))
+    terms = emit(place, attn, full_out)
+    sums = [None] * 4
+    for i in (3, 2, 1, 0):
+        near = swap(terms[4 + i], "head", 1)
+        sums[i] = terms[i].astype(jnp.float32) + near.astype(jnp.float32)
+    total = sums[0]
+    for i in (3, 2, 1):
+        moved = swap(sums[i].astype(jnp.bfloat16), "head", 2 * i)
+        total = total + moved.astype(jnp.float32)
+    return total.astype(jnp.bfloat16)
 
 
 def from_behind(value, axis, by):
@@ -132,7 +357,6 @@
     )
     return lax.psum_scatter(terms.astype(jnp.bfloat16), "head", scatter_dimension=1, tiled=True)
 
-
 def solution(mesh):
     in_specs = (
         P("node", "head"),
@@ -143,6 +367,20 @@
         P(None, "head"),
     )
     out_specs = P("node", "head")
-    return jax.shard_map(
-        on_device, mesh=mesh, in_specs=in_specs, out_specs=out_specs, check_vma=False
-    )
+
+    def whole(node_feats, w_qk, w_val, w_out, edge_types, rel_bias):
+        node_count, head_count = mesh.shape["node"], mesh.shape["head"]
+        column_heads = rel_bias.shape[1] // head_count
+        fits = (
+            node_count == 4
+            and head_count == 2 * node_count
+            and column_heads == node_count
+            and node_feats.shape[0] % (node_count * TILE) == 0
+        )
+        body = one_head_each if fits else on_device
+        mapped = jax.shard_map(
+            body, mesh=mesh, in_specs=in_specs, out_specs=out_specs, check_vma=False
+        )
+        return mapped(node_feats, w_qk, w_val, w_out, edge_types, rel_bias)
+
+    return whole

time: 275 us -> 165 us (0.60)
  waiting for transfers between devices: 217 us -> 97 us
  starting transfers between devices: 7.49 us -> 32.9 us
  matrix products: 21 us -> 0 us
  between operations: 13.3 us -> 0.12 us
  Pallas kernels: 0 us -> 11.9 us
  blocking collectives: 0 us -> 5.06 us
    all_gather x4 -> x0, waiting for transfers between devices: 116 us -> none  [the longest x1 50.2 us: on_device(): shard_piece = lax.all_gather(node_feats, 'head', axis=1, tiled=True)]
    reduce_scatter x1 -> x0, waiting for transfers between devices: 69.3 us -> none  [on_device(): lax.psum_scatter(terms.astype(jnp.bfloat16), 'head', scatter_dimension=1,...]
    ppermute x15 -> x32, waiting for transfers between devices: 29.2 us -> 97 us  [swap(): return lax.ppermute(value, axis, [(i, i ^ mask) for i in range(peers)])]
    ppermute x15 -> x32, starting transfers between devices: 7.34 us -> 32.9 us  [swap(): return lax.ppermute(value, axis, [(i, i ^ mask) for i in range(peers)])]
    dot_general x12 -> x0, matrix products: 21 us -> none  [the longest x1 4.79 us: on_device(): jnp.dot(attn, lax.all_gather(w_out, 'node', axis=1, tiled=True), preferre...]
    unnamed x5 -> x40, local copies, waits for them, and re-layouts: 1.87 us -> 15 us
    pallas_call x0 -> x4, Pallas kernels: none -> 11.9 us  [the longest x2 6.15 us: project(): pl.pallas_call(project_kernel, out_shape=[jax.ShapeDtypeStruct((rows, DH)...]
    add x6 -> x0, local copies, waits for them, and re-layouts: 6.22 us -> none  [update(): scaled.reshape(head_count, tiles, query_count // tiles, key_count)]
  transfers between devices with their start and end apart: 20 -> 32, of which waited for: 9 -> 14; matrix products, arithmetic and copies ran while one was open for 12% -> 0% of each run, Pallas kernels for 0% -> 6%
where the time goes in v1:
time: 165 us; the launch traced here: 163 us
  waiting for transfers between devices  97 us (59%)
  starting transfers between devices  32.9 us (20%)
  local copies, waits for them, and re-layouts  15 us (9%)
  Pallas kernels  11.9 us (7%)
  blocking collectives  5.06 us (3%)
    ppermute x32, waiting for transfers between devices, swap(): return lax.ppermute(value, axis, [(i, i ^ mask) for i in range(peers)])  97 us
    ppermute x32, starting transfers between devices, swap(): return lax.ppermute(value, axis, [(i, i ^ mask) for i in range(peers)])  32.9 us
    unnamed x40, local copies, waits for them, and re-layouts  15 us
    pallas_call x2, Pallas kernels, project(): pl.pallas_call(project_kernel, out_shape=[jax.ShapeDtypeStruct((rows, DH)...  6.15 us
    all_gather x1, blocking collectives, one_head_each(): edges = lax.all_gather(edge_types, 'node', axis=0, tiled=True)  5.06 us
    pallas_call x1, Pallas kernels, attend(): pl.pallas_call(attend_kernel, out_shape=[jax.ShapeDtypeStruct((rows, DH),...  3.53 us
  transfers between devices with their start and end apart: 32, of which 14 were waited for; matrix products, arithmetic and copies ran while one was open for 0% of the time, Pallas kernels for 6%

profile of v1, /device:TPU:0, one launch (start us, length us, event | category | flops | bytes accessed | tf_op | source)
XLA Modules:
  0.0 163.1 jit_solution(18414317657957848553)
XLA Ops:
  0.0 2.9 %collective-permute-start.8 = (bf16[1024,512]{1,0:T(8,128)(2,1)}, bf16[1024,512]{1,0:T(8,128)(2,1)}, u32[]{:S(2)}, u32[]{:S(2)}) collective-permute-start(bf16[1024,512]{1,0:T(8,128)(2,1)} %refs_8_.1), channel_id=1, source_target_pairs={{0,16},{8,24},{16,0},{24,8},{1,17},{9,25},{17,1},{25,9},{2,18},{10... | collective-permute-start | bytes 3145736 | tf_op jit(solution)/shard_map/ppermute | solution.py:19
  2.9 23.5 %collective-permute-done.8.refs_10_ = bf16[1024,512]{1,0:T(8,128)(2,1)} collective-permute-done((bf16[1024,512]{1,0:T(8,128)(2,1)}, bf16[1024,512]{1,0:T(8,128)(2,1)}, u32[]{:S(2)}, u32[]{:S(2)}) %collective-permute-start.8) | collective-permute-done | bytes 1048608 | tf_op jit(solution)/shard_map/ppermute | solution.py:19
  26.4 1.7 %collective-permute-start.14 = (bf16[1024,512]{1,0:T(8,128)(2,1)}, bf16[1024,512]{1,0:T(8,128)(2,1)}, u32[]{:S(2)}, u32[]{:S(2)}) collective-permute-start(bf16[1024,512]{1,0:T(8,128)(2,1)} %refs_8_.2), channel_id=1, source_target_pairs={{0,16},{8,24},{16,0},{24,8},{1,17},{9,25},{17,1},{25,9},{2,18},{10... | collective-permute-start | bytes 3145736 | tf_op jit(solution)/shard_map/ppermute | solution.py:19
  28.2 1.5 collective-permute-start
  29.7 21.4 %collective-permute-done.14.refs_10_ = bf16[1024,512]{1,0:T(8,128)(2,1)} collective-permute-done((bf16[1024,512]{1,0:T(8,128)(2,1)}, bf16[1024,512]{1,0:T(8,128)(2,1)}, u32[]{:S(2)}, u32[]{:S(2)}) %collective-permute-start.14) | collective-permute-done | bytes 1048608 | tf_op jit(solution)/shard_map/ppermute | solution.py:19
  51.1 1.4 collective-permute-start.23
  52.5 1.6 collective-permute-start.1
  54.1 2.6 %collective-permute-start.3 = (bf16[256,512]{1,0:T(8,128)(2,1)}, bf16[256,512]{1,0:T(8,128)(2,1)S(1)}, u32[]{:S(2)}, u32[]{:S(2)}) collective-permute-start(bf16[256,512]{1,0:T(8,128)(2,1)} %refs_0_.3), channel_id=1, source_target_pairs={{0,4},{1,5},{2,6},{3,7},{4,0},{5,1},{6,2},{7,3},{8,12},{9,13},{10,... | collective-permute-start | bytes 786440 | tf_op jit(solution)/shard_map/ppermute | solution.py:19
  56.7 0.2 collective-permute-start.5
  56.9 5.5 %collective-permute-done.1.refs_2_ = bf16[256,512]{1,0:T(8,128)(2,1)S(1)} collective-permute-done((bf16[256,512]{1,0:T(8,128)(2,1)}, bf16[256,512]{1,0:T(8,128)(2,1)S(1)}, u32[]{:S(2)}, u32[]{:S(2)}) %collective-permute-start.1) | collective-permute-done | bytes 262176 | tf_op jit(solution)/shard_map/ppermute | solution.py:19
  62.4 1.5 collective-permute-start.2
  63.9 0.7 copy-done.7
  64.6 10.4 %collective-permute-done.3.refs_4_ = bf16[256,512]{1,0:T(8,128)(2,1)S(1)} collective-permute-done((bf16[256,512]{1,0:T(8,128)(2,1)}, bf16[256,512]{1,0:T(8,128)(2,1)S(1)}, u32[]{:S(2)}, u32[]{:S(2)}) %collective-permute-start.3) | collective-permute-done | bytes 262176 | tf_op jit(solution)/shard_map/ppermute | solution.py:19
  75.0 1.5 collective-permute-start.4
  76.5 0.7 copy-done.9
  77.2 0.5 collective-permute-start.6
  77.7 0.7 copy-done.11
  78.4 0.7 copy-done.13
  79.1 2.2 %collective-permute-done.4.refs_5_ = bf16[256,512]{1,0:T(8,128)(2,1)S(1)} collective-permute-done((bf16[256,512]{1,0:T(8,128)(2,1)S(1)}, bf16[256,512]{1,0:T(8,128)(2,1)S(1)}, u32[]{:S(2)}, u32[]{:S(2)}) %collective-permute-start.4) | collective-permute-done | bytes 262176 | tf_op jit(solution)/shard_map/ppermute | solution.py:19
  81.4 0.7 copy-done.15
  82.1 2.1 %collective-permute-done.6.refs_7_ = bf16[256,512]{1,0:T(8,128)(2,1)S(1)} collective-permute-done((bf16[256,512]{1,0:T(8,128)(2,1)S(1)}, bf16[256,512]{1,0:T(8,128)(2,1)S(1)}, u32[]{:S(2)}, u32[]{:S(2)}) %collective-permute-start.6) | collective-permute-done | bytes 262176 | tf_op jit(solution)/shard_map/ppermute | solution.py:19
  84.2 0.7 copy-done.17
  84.9 1.0 copy-done.4
  85.9 0.5 collective-permute-start.22
  86.4 0.7 copy-done.19
  87.1 5.1 %all-gather = s32[4,2,8]{2,1,0:T(2,128)S(1)} all-gather(s32[1,2,8]{2,1,0:T(2,128)S(1)} %bitcast.7), channel_id=1, replica_groups=mesh['node'=4,'head'=8] {'node'}, dimensions={0}, use_global_device_ids=true | all-gather | bytes 320 | tf_op jit(solution)/shard_map/all_gather | solution.py:210
  92.2 1.2 copy-done.1
  93.5 1.2 copy-done.5
  94.7 0.9 copy-done.6
  95.6 0.9 copy-done.8
  96.6 0.9 copy-done.10
  97.5 0.9 copy-done.12
  98.5 0.9 copy-done.14
  99.4 0.9 copy-done.16
  100.4 0.9 copy-done.18
  101.3 2.9 %project.2 = (bf16[256,128]{1,0:T(8,128)(2,1)S(1)}, bf16[256,128]{1,0:T(8,128)(2,1)S(1)}, bf16[256,128]{1,0:T(8,128)(2,1)S(1)}, bf16[256,128]{1,0:T(8,128)(2,1)S(1)}) custom-call(s32[2]{0:T(128)S(1)} %pad_add_fusion.place_ref, bf16[256,512]{1,0:T(8,128)(2,1)S(1)} %copy-done.6, bf16[256,512]{1,0:T(8,128)(2,1)S(1)} %collective-permute-done.refs_1_, ...), custom_call_target="tpu_custom_call" | custom-call | flops 1073741824 | bytes 6553600 | tf_op jit(solution)/shard_map/project/pallas_call | solution.py:78
  104.3 0.4 collective-permute-start.10
  104.7 0.5 collective-permute-start.11
  105.2 1.0 collective-permute-start.12
  106.2 3.2 %project.3 = (bf16[256,128]{1,0:T(8,128)(2,1)S(1)}, bf16[256,128]{1,0:T(8,128)(2,1)S(1)}, bf16[256,128]{1,0:T(8,128)(2,1)S(1)}, bf16[256,128]{1,0:T(8,128)(2,1)S(1)}) custom-call(s32[2]{0:T(128)S(1)} %pad_add_fusion.place_ref, bf16[256,512]{1,0:T(8,128)(2,1)S(1)} %copy-done.6, bf16[256,512]{1,0:T(8,128)(2,1)S(1)} %collective-permute-done.refs_1_, ...), custom_call_target="tpu_custom_call" | custom-call | flops 1073741824 | bytes 6553600 | tf_op jit(solution)/shard_map/project/pallas_call | solution.py:78
  109.5 0.7 collective-permute-start.16
  110.1 0.5 collective-permute-start.17
  110.7 0.9 collective-permute-start.18
  111.6 3.5 %collective-permute-done.17.refs_6_ = bf16[256,128]{1,0:T(8,128)(2,1)S(1)} collective-permute-done((bf16[256,128]{1,0:T(8,128)(2,1)S(1)}, bf16[256,128]{1,0:T(8,128)(2,1)S(1)}, u32[]{:S(2)}, u32[]{:S(2)}) %collective-permute-start.17) | collective-permute-done | bytes 65568 | tf_op jit(solution)/shard_map/ppermute | solution.py:19
  115.1 3.5 %attend.1 = (bf16[256,128]{1,0:T(8,128)(2,1)S(1)}, bf16[256,128]{1,0:T(8,128)(2,1)S(1)}, bf16[256,128]{1,0:T(8,128)(2,1)S(1)}, bf16[256,128]{1,0:T(8,128)(2,1)S(1)}) custom-call(s32[2]{0:T(128)S(1)} %pad_add_fusion.place_ref, s32[8,8]{1,0:T(8,128)S(1)} %bitcast.5, f32[237]{0:T(256)S(1)} %bitcast.6, bf16[256,128]{1,0:T(8,128)(2,1)S(1)} %get-tuple-element.27.refs_0_, ...), custom_call_target="tpu_custom_call" | custom-call | flops 536870912 | bytes 786432 | tf_op jit(solution)/shard_map/attend/pallas_call | solution.py:138
  118.6 0.6 collective-permute-start.19
  119.2 1.1 collective-permute-start.20
  120.2 0.4 collective-permute-start.21
  120.6 3.1 %collective-permute-done.20.refs_2_ = bf16[256,128]{1,0:T(8,128)(2,1)S(1)} collective-permute-done((bf16[256,128]{1,0:T(8,128)(2,1)S(1)}, bf16[256,128]{1,0:T(8,128)(2,1)S(1)}, u32[]{:S(2)}, u32[]{:S(2)}) %collective-permute-start.20) | collective-permute-done | bytes 65568 | tf_op jit(solution)/shard_map/ppermute | solution.py:19
  123.8 0.8 collective-permute-done.21.refs_3_
  124.6 2.2 %emit.1 = (bf16[256,512]{1,0:T(8,128)(2,1)S(1)}, bf16[256,512]{1,0:T(8,128)(2,1)S(1)}, bf16[256,512]{1,0:T(8,128)(2,1)S(1)}, bf16[256,512]{1,0:T(8,128)(2,1)S(1)...) custom-call(s32[2]{0:T(128)S(1)} %pad_add_fusion.place_ref, ...), custom_call_target="tpu_custom_call" | custom-call | flops 1073741824 | bytes 6553600 | tf_op jit(solution)/shard_map/emit/pallas_call | solution.py:181
  126.7 1.6 collective-permute-start.30
  128.3 0.5 collective-permute-start.28
  128.8 1.5 collective-permute-start.26
  130.4 0.5 collective-permute-start.25
  130.9 5.1 %collective-permute-done.30 = bf16[256,512]{1,0:T(8,128)(2,1)S(1)} collective-permute-done((bf16[256,512]{1,0:T(8,128)(2,1)S(1)}, bf16[256,512]{1,0:T(8,128)(2,1)S(1)}, u32[]{:S(2)}, u32[]{:S(2)}) %collective-permute-start.30) | collective-permute-done | bytes 262176 | tf_op jit(solution)/shard_map/ppermute | solution.py:19
  136.0 2.1 %collective-permute-start.31 = (bf16[256,512]{1,0:T(8,128)(2,1)S(1)}, bf16[256,512]{1,0:T(8,128)(2,1)S(1)}, u32[]{:S(2)}, u32[]{:S(2)}) collective-permute-start(bf16[256,512]{1,0:T(8,128)(2,1)S(1)} %add_convert_fusion.1), channel_id=1, source_target_pairs={{0,2},{1,3},{2,0},{3,1},{4,6},{5,7},{6,4},{7,5},{8,10},{9,11},{10,... | collective-permute-start | bytes 786440 | tf_op jit(solution)/shard_map/ppermute | solution.py:19
  138.1 3.5 %collective-permute-done.28 = bf16[256,512]{1,0:T(8,128)(2,1)S(1)} collective-permute-done((bf16[256,512]{1,0:T(8,128)(2,1)S(1)}, bf16[256,512]{1,0:T(8,128)(2,1)S(1)}, u32[]{:S(2)}, u32[]{:S(2)}) %collective-permute-start.28) | collective-permute-done | bytes 262176 | tf_op jit(solution)/shard_map/ppermute | solution.py:19
  141.7 2.5 %collective-permute-start.29 = (bf16[256,512]{1,0:T(8,128)(2,1)S(1)}, bf16[256,512]{1,0:T(8,128)(2,1)S(1)}, u32[]{:S(2)}, u32[]{:S(2)}) collective-permute-start(bf16[256,512]{1,0:T(8,128)(2,1)S(1)} %add_convert_fusion.2), channel_id=1, source_target_pairs={{0,4},{1,5},{2,6},{3,7},{4,0},{5,1},{6,2},{7,3},{8,12},{9,13},{10,... | collective-permute-start | bytes 786440 | tf_op jit(solution)/shard_map/ppermute | solution.py:19
  144.2 3.0 %collective-permute-done.26 = bf16[256,512]{1,0:T(8,128)(2,1)S(1)} collective-permute-done((bf16[256,512]{1,0:T(8,128)(2,1)S(1)}, bf16[256,512]{1,0:T(8,128)(2,1)S(1)}, u32[]{:S(2)}, u32[]{:S(2)}) %collective-permute-start.26) | collective-permute-done | bytes 262176 | tf_op jit(solution)/shard_map/ppermute | solution.py:19
  147.3 2.0 %collective-permute-start.27 = (bf16[256,512]{1,0:T(8,128)(2,1)S(1)}, bf16[256,512]{1,0:T(8,128)(2,1)S(1)}, u32[]{:S(2)}, u32[]{:S(2)}) collective-permute-start(bf16[256,512]{1,0:T(8,128)(2,1)S(1)} %add_convert_fusion.3), channel_id=1, source_target_pairs={{0,6},{1,7},{2,4},{3,5},{4,2},{5,3},{6,0},{7,1},{8,14},{9,15},{10,... | collective-permute-start | bytes 786440 | tf_op jit(solution)/shard_map/ppermute | solution.py:19
  149.3 2.7 %collective-permute-done.25 = bf16[256,512]{1,0:T(8,128)(2,1)S(1)} collective-permute-done((bf16[256,512]{1,0:T(8,128)(2,1)S(1)}, bf16[256,512]{1,0:T(8,128)(2,1)S(1)}, u32[]{:S(2)}, u32[]{:S(2)}) %collective-permute-start.25) | collective-permute-done | bytes 262176 | tf_op jit(solution)/shard_map/ppermute | solution.py:19
  152.0 10.2 %collective-permute-done.29 = bf16[256,512]{1,0:T(8,128)(2,1)S(1)} collective-permute-done((bf16[256,512]{1,0:T(8,128)(2,1)S(1)}, bf16[256,512]{1,0:T(8,128)(2,1)S(1)}, u32[]{:S(2)}, u32[]{:S(2)}) %collective-permute-start.29) | collective-permute-done | bytes 262176 | tf_op jit(solution)/shard_map/ppermute | solution.py:19
  162.2 0.9 add_convert_fusion
  (51 shorter events, 0.4 us)
Async XLA Ops:
  0.0 111.6 %copy-start = (f32[237,4]{0,1:T(4,128)S(1)}, f32[237,4]{0,1:T(4,128)}, u32[]{:S(2)}) copy-start(f32[237,4]{0,1:T(4,128)} %param.11) | copy-start | bytes 11380
  0.0 26.4 %collective-permute-start.8 = (bf16[1024,512]{1,0:T(8,128)(2,1)}, bf16[1024,512]{1,0:T(8,128)(2,1)}, u32[]{:S(2)}, u32[]{:S(2)}) collective-permute-start(bf16[1024,512]{1,0:T(8,128)(2,1)} %refs_8_.1), channel_id=1, source_target_pairs={{0,16},{8,24},{16,0},{24,8},{1,17},{9,25},{17,1},{25,9},{2,18},{10... | collective-permute-start | bytes 3145736 | tf_op jit(solution)/shard_map/ppermute | solution.py:19
  26.4 24.7 %collective-permute-start.14 = (bf16[1024,512]{1,0:T(8,128)(2,1)}, bf16[1024,512]{1,0:T(8,128)(2,1)}, u32[]{:S(2)}, u32[]{:S(2)}) collective-permute-start(bf16[1024,512]{1,0:T(8,128)(2,1)} %refs_8_.2), channel_id=1, source_target_pairs={{0,16},{8,24},{16,0},{24,8},{1,17},{9,25},{17,1},{25,9},{2,18},{10... | collective-permute-start | bytes 3145736 | tf_op jit(solution)/shard_map/ppermute | solution.py:19
  28.2 28.5 %collective-permute-start = (bf16[256,512]{1,0:T(8,128)(2,1)}, bf16[256,512]{1,0:T(8,128)(2,1)S(1)}, u32[]{:S(2)}, u32[]{:S(2)}) collective-permute-start(bf16[256,512]{1,0:T(8,128)(2,1)} %refs_0_.3), channel_id=1, source_target_pairs={{0,1},{1,0},{2,3},{3,2},{4,5},{5,4},{6,7},{7,6},{8,9},{9,8},{10,11... | collective-permute-start | bytes 786440 | tf_op jit(solution)/shard_map/ppermute | solution.py:19
  29.7 55.2 %collective-permute-start.7 = (bf16[1024,512]{1,0:T(8,128)(2,1)}, bf16[1024,512]{1,0:T(8,128)(2,1)S(1)}, u32[]{:S(2)}, u32[]{:S(2)}) collective-permute-start(bf16[1024,512]{1,0:T(8,128)(2,1)} %refs_8_.1), channel_id=1, source_target_pairs={{0,8},{8,0},{16,24},{24,16},{1,9},{9,1},{17,25},{25,17},{2,10},{10... | collective-permute-start | bytes 3145736 | tf_op jit(solution)/shard_map/ppermute | solution.py:19
  51.1 35.3 %collective-permute-start.23 = (bf16[512,1024]{1,0:T(8,128)(2,1)}, bf16[512,1024]{1,0:T(8,128)(2,1)S(1)}, u32[]{:S(2)}, u32[]{:S(2)}) collective-permute-start(bf16[512,1024]{1,0:T(8,128)(2,1)} %refs_4_), channel_id=1, source_target_pairs={{0,16},{8,24},{16,0},{24,8},{1,17},{9,25},{17,1},{25,9},{2,18},{10... | collective-permute-start | bytes 3145736 | tf_op jit(solution)/shard_map/ppermute | solution.py:19
  52.5 9.9 %collective-permute-start.1 = (bf16[256,512]{1,0:T(8,128)(2,1)}, bf16[256,512]{1,0:T(8,128)(2,1)S(1)}, u32[]{:S(2)}, u32[]{:S(2)}) collective-permute-start(bf16[256,512]{1,0:T(8,128)(2,1)} %refs_0_.3), channel_id=1, source_target_pairs={{0,2},{1,3},{2,0},{3,1},{4,6},{5,7},{6,4},{7,5},{8,10},{9,11},{10,... | collective-permute-start | bytes 786440 | tf_op jit(solution)/shard_map/ppermute | solution.py:19
  54.1 20.9 %collective-permute-start.3 = (bf16[256,512]{1,0:T(8,128)(2,1)}, bf16[256,512]{1,0:T(8,128)(2,1)S(1)}, u32[]{:S(2)}, u32[]{:S(2)}) collective-permute-start(bf16[256,512]{1,0:T(8,128)(2,1)} %refs_0_.3), channel_id=1, source_target_pairs={{0,4},{1,5},{2,6},{3,7},{4,0},{5,1},{6,2},{7,3},{8,12},{9,13},{10,... | collective-permute-start | bytes 786440 | tf_op jit(solution)/shard_map/ppermute | solution.py:19
  56.7 20.5 %collective-permute-start.5 = (bf16[256,512]{1,0:T(8,128)(2,1)}, bf16[256,512]{1,0:T(8,128)(2,1)S(1)}, u32[]{:S(2)}, u32[]{:S(2)}) collective-permute-start(bf16[256,512]{1,0:T(8,128)(2,1)} %refs_0_.3), channel_id=1, source_target_pairs={{0,6},{1,7},{2,4},{3,5},{4,2},{5,3},{6,0},{7,1},{8,14},{9,15},{10,... | collective-permute-start | bytes 786440 | tf_op jit(solution)/shard_map/ppermute | solution.py:19
  62.4 16.0 %collective-permute-start.2 = (bf16[256,512]{1,0:T(8,128)(2,1)S(1)}, bf16[256,512]{1,0:T(8,128)(2,1)S(1)}, u32[]{:S(2)}, u32[]{:S(2)}) collective-permute-start(bf16[256,512]{1,0:T(8,128)(2,1)S(1)} %collective-permute-done.1.refs_2_), channel_id=1, source_target_pairs={{0,1},{1,0},{2,3},{3,2},{4,5},{5,4},{6,7},{7,6},{8,9},{9,8},{10,11... | collective-permute-start | bytes 786440 | tf_op jit(solution)/shard_map/ppermute | solution.py:19
  63.9 0.7 copy-start.7
  75.0 6.4 %collective-permute-start.4 = (bf16[256,512]{1,0:T(8,128)(2,1)S(1)}, bf16[256,512]{1,0:T(8,128)(2,1)S(1)}, u32[]{:S(2)}, u32[]{:S(2)}) collective-permute-start(bf16[256,512]{1,0:T(8,128)(2,1)S(1)} %collective-permute-done.3.refs_4_), channel_id=1, source_target_pairs={{0,1},{1,0},{2,3},{3,2},{4,5},{5,4},{6,7},{7,6},{8,9},{9,8},{10,11... | collective-permute-start | bytes 786440 | tf_op jit(solution)/shard_map/ppermute | solution.py:19
  76.5 0.7 copy-start.9
  77.2 7.0 %collective-permute-start.6 = (bf16[256,512]{1,0:T(8,128)(2,1)S(1)}, bf16[256,512]{1,0:T(8,128)(2,1)S(1)}, u32[]{:S(2)}, u32[]{:S(2)}) collective-permute-start(bf16[256,512]{1,0:T(8,128)(2,1)S(1)} %collective-permute-done.5.refs_6_), channel_id=1, source_target_pairs={{0,1},{1,0},{2,3},{3,2},{4,5},{5,4},{6,7},{7,6},{8,9},{9,8},{10,11... | collective-permute-start | bytes 786440 | tf_op jit(solution)/shard_map/ppermute | solution.py:19
  77.7 0.7 copy-start.11
  78.4 0.7 copy-start.13
  79.1 13.1 %collective-permute-start.9 = (bf16[1024,512]{1,0:T(8,128)(2,1)}, bf16[1024,512]{1,0:T(8,128)(2,1)}, u32[]{:S(2)}, u32[]{:S(2)}) collective-permute-start(bf16[1024,512]{1,0:T(8,128)(2,1)} %collective-permute-done.8.refs_10_), channel_id=1, source_target_pairs={{0,8},{8,0},{16,24},{24,16},{1,9},{9,1},{17,25},{25,17},{2,10},{10... | collective-permute-start | bytes 3145736 | tf_op jit(solution)/shard_map/ppermute | solution.py:19
  81.4 0.7 copy-start.15
  82.1 22.6 %collective-permute-start.13 = (bf16[1024,512]{1,0:T(8,128)(2,1)}, bf16[1024,512]{1,0:T(8,128)(2,1)}, u32[]{:S(2)}, u32[]{:S(2)}) collective-permute-start(bf16[1024,512]{1,0:T(8,128)(2,1)} %refs_8_.2), channel_id=1, source_target_pairs={{0,8},{8,0},{16,24},{24,16},{1,9},{9,1},{17,25},{25,17},{2,10},{10... | collective-permute-start | bytes 3145736 | tf_op jit(solution)/shard_map/ppermute | solution.py:19
  84.2 0.7 copy-start.17
  84.9 20.3 %collective-permute-start.15 = (bf16[1024,512]{1,0:T(8,128)(2,1)}, bf16[1024,512]{1,0:T(8,128)(2,1)}, u32[]{:S(2)}, u32[]{:S(2)}) collective-permute-start(bf16[1024,512]{1,0:T(8,128)(2,1)} %collective-permute-done.14.refs_10_), channel_id=1, source_target_pairs={{0,8},{8,0},{16,24},{24,16},{1,9},{9,1},{17,25},{25,17},{2,10},{10... | collective-permute-start | bytes 3145736 | tf_op jit(solution)/shard_map/ppermute | solution.py:19
  84.9 1.0 copy-start.4
  85.9 34.7 %collective-permute-start.22 = (bf16[512,1024]{1,0:T(8,128)(2,1)}, bf16[512,1024]{1,0:T(8,128)(2,1)S(1)}, u32[]{:S(2)}, u32[]{:S(2)}) collective-permute-start(bf16[512,1024]{1,0:T(8,128)(2,1)} %refs_4_), channel_id=1, source_target_pairs={{0,8},{8,0},{16,24},{24,16},{1,9},{9,1},{17,25},{25,17},{2,10},{10... | collective-permute-start | bytes 3145736 | tf_op jit(solution)/shard_map/ppermute | solution.py:19
  86.4 38.1 %collective-permute-start.24 = (bf16[512,1024]{1,0:T(8,128)(2,1)S(1)}, bf16[512,1024]{1,0:T(8,128)(2,1)S(1)}, u32[]{:S(2)}, u32[]{:S(2)}) collective-permute-start(bf16[512,1024]{1,0:T(8,128)(2,1)S(1)} %collective-permute-done.23.refs_6_), channel_id=1, source_target_pairs={{0,8},{8,0},{16,24},{24,16},{1,9},{9,1},{17,25},{25,17},{2,10},{10... | collective-permute-start | bytes 3145736 | tf_op jit(solution)/shard_map/ppermute | solution.py:19
  86.4 0.7 copy-start.19
  92.2 1.2 copy-start.1
  93.5 1.2 copy-start.5
  94.7 0.9 copy-start.6
  95.6 0.9 copy-start.8
  96.6 0.9 copy-start.10
  97.5 0.9 copy-start.12
  98.5 0.9 copy-start.14
  99.4 0.9 copy-start.16
  100.4 0.9 copy-start.18
  101.3 4.9 %copy-start.2 = (bf16[1024,512]{1,0:T(8,128)(2,1)S(1)}, bf16[1024,512]{1,0:T(8,128)(2,1)}, u32[]{:S(2)}) copy-start(bf16[1024,512]{1,0:T(8,128)(2,1)} %refs_8_.2) | copy-start | bytes 3145732
  104.3 5.2 %collective-permute-start.10 = (bf16[256,128]{1,0:T(8,128)(2,1)S(1)}, bf16[256,128]{1,0:T(8,128)(2,1)S(1)}, u32[]{:S(2)}, u32[]{:S(2)}) collective-permute-start(bf16[256,128]{1,0:T(8,128)(2,1)S(1)} %get-tuple-element.28), channel_id=1, source_target_pairs={{0,8},{8,0},{16,24},{24,16},{1,9},{9,1},{17,25},{25,17},{2,10},{10... | collective-permute-start | bytes 196616 | tf_op jit(solution)/shard_map/ppermute | solution.py:19
  104.7 5.4 %collective-permute-start.11 = (bf16[256,128]{1,0:T(8,128)(2,1)S(1)}, bf16[256,128]{1,0:T(8,128)(2,1)S(1)}, u32[]{:S(2)}, u32[]{:S(2)}) collective-permute-start(bf16[256,128]{1,0:T(8,128)(2,1)S(1)} %get-tuple-element.29), channel_id=1, source_target_pairs={{0,16},{8,24},{16,0},{24,8},{1,17},{9,25},{17,1},{25,9},{2,18},{10... | collective-permute-start | bytes 196616 | tf_op jit(solution)/shard_map/ppermute | solution.py:19
  105.2 5.5 %collective-permute-start.12 = (bf16[256,128]{1,0:T(8,128)(2,1)S(1)}, bf16[256,128]{1,0:T(8,128)(2,1)S(1)}, u32[]{:S(2)}, u32[]{:S(2)}) collective-permute-start(bf16[256,128]{1,0:T(8,128)(2,1)S(1)} %get-tuple-element.30), channel_id=1, source_target_pairs={{0,24},{8,16},{16,8},{24,0},{1,25},{9,17},{17,9},{25,1},{2,26},{10... | collective-permute-start | bytes 196616 | tf_op jit(solution)/shard_map/ppermute | solution.py:19
  109.4 15.1 %copy-start.3 = (bf16[512,1024]{1,0:T(8,128)(2,1)S(1)}, bf16[512,1024]{1,0:T(8,128)(2,1)}, u32[]{:S(2)}) copy-start(bf16[512,1024]{1,0:T(8,128)(2,1)} %refs_4_) | copy-start | bytes 3145732
  109.5 2.1 %collective-permute-start.16 = (bf16[256,128]{1,0:T(8,128)(2,1)S(1)}, bf16[256,128]{1,0:T(8,128)(2,1)S(1)}, u32[]{:S(2)}, u32[]{:S(2)}) collective-permute-start(bf16[256,128]{1,0:T(8,128)(2,1)S(1)} %get-tuple-element.33), channel_id=1, source_target_pairs={{0,8},{8,0},{16,24},{24,16},{1,9},{9,1},{17,25},{25,17},{2,10},{10... | collective-permute-start | bytes 196616 | tf_op jit(solution)/shard_map/ppermute | solution.py:19
  110.1 4.9 %collective-permute-start.17 = (bf16[256,128]{1,0:T(8,128)(2,1)S(1)}, bf16[256,128]{1,0:T(8,128)(2,1)S(1)}, u32[]{:S(2)}, u32[]{:S(2)}) collective-permute-start(bf16[256,128]{1,0:T(8,128)(2,1)S(1)} %get-tuple-element.34), channel_id=1, source_target_pairs={{0,16},{8,24},{16,0},{24,8},{1,17},{9,25},{17,1},{25,9},{2,18},{10... | collective-permute-start | bytes 196616 | tf_op jit(solution)/shard_map/ppermute | solution.py:19
  110.7 4.4 %collective-permute-start.18 = (bf16[256,128]{1,0:T(8,128)(2,1)S(1)}, bf16[256,128]{1,0:T(8,128)(2,1)S(1)}, u32[]{:S(2)}, u32[]{:S(2)}) collective-permute-start(bf16[256,128]{1,0:T(8,128)(2,1)S(1)} %get-tuple-element.35), channel_id=1, source_target_pairs={{0,24},{8,16},{16,8},{24,0},{1,25},{9,17},{17,9},{25,1},{2,26},{10... | collective-permute-start | bytes 196616 | tf_op jit(solution)/shard_map/ppermute | solution.py:19
  118.6 2.0 %collective-permute-start.19 = (bf16[256,128]{1,0:T(8,128)(2,1)S(1)}, bf16[256,128]{1,0:T(8,128)(2,1)S(1)}, u32[]{:S(2)}, u32[]{:S(2)}) collective-permute-start(bf16[256,128]{1,0:T(8,128)(2,1)S(1)} %get-tuple-element.37), channel_id=1, source_target_pairs={{0,8},{8,0},{16,24},{24,16},{1,9},{9,1},{17,25},{25,17},{2,10},{10... | collective-permute-start | bytes 196616 | tf_op jit(solution)/shard_map/ppermute | solution.py:19
  119.2 4.6 %collective-permute-start.20 = (bf16[256,128]{1,0:T(8,128)(2,1)S(1)}, bf16[256,128]{1,0:T(8,128)(2,1)S(1)}, u32[]{:S(2)}, u32[]{:S(2)}) collective-permute-start(bf16[256,128]{1,0:T(8,128)(2,1)S(1)} %get-tuple-element.38), channel_id=1, source_target_pairs={{0,16},{8,24},{16,0},{24,8},{1,17},{9,25},{17,1},{25,9},{2,18},{10... | collective-permute-start | bytes 196616 | tf_op jit(solution)/shard_map/ppermute | solution.py:19
  120.2 4.3 %collective-permute-start.21 = (bf16[256,128]{1,0:T(8,128)(2,1)S(1)}, bf16[256,128]{1,0:T(8,128)(2,1)S(1)}, u32[]{:S(2)}, u32[]{:S(2)}) collective-permute-start(bf16[256,128]{1,0:T(8,128)(2,1)S(1)} %get-tuple-element.39), channel_id=1, source_target_pairs={{0,24},{8,16},{16,8},{24,0},{1,25},{9,17},{17,9},{25,1},{2,26},{10... | collective-permute-start | bytes 196616 | tf_op jit(solution)/shard_map/ppermute | solution.py:19
  126.7 9.2 %collective-permute-start.30 = (bf16[256,512]{1,0:T(8,128)(2,1)S(1)}, bf16[256,512]{1,0:T(8,128)(2,1)S(1)}, u32[]{:S(2)}, u32[]{:S(2)}) collective-permute-start(bf16[256,512]{1,0:T(8,128)(2,1)S(1)} %get-tuple-element.48), channel_id=1, source_target_pairs={{0,1},{1,0},{2,3},{3,2},{4,5},{5,4},{6,7},{7,6},{8,9},{9,8},{10,11... | collective-permute-start | bytes 786440 | tf_op jit(solution)/shard_map/ppermute | solution.py:19
  128.3 13.3 %collective-permute-start.28 = (bf16[256,512]{1,0:T(8,128)(2,1)S(1)}, bf16[256,512]{1,0:T(8,128)(2,1)S(1)}, u32[]{:S(2)}, u32[]{:S(2)}) collective-permute-start(bf16[256,512]{1,0:T(8,128)(2,1)S(1)} %get-tuple-element.46), channel_id=1, source_target_pairs={{0,1},{1,0},{2,3},{3,2},{4,5},{5,4},{6,7},{7,6},{8,9},{9,8},{10,11... | collective-permute-start | bytes 786440 | tf_op jit(solution)/shard_map/ppermute | solution.py:19
  128.8 18.4 %collective-permute-start.26 = (bf16[256,512]{1,0:T(8,128)(2,1)S(1)}, bf16[256,512]{1,0:T(8,128)(2,1)S(1)}, u32[]{:S(2)}, u32[]{:S(2)}) collective-permute-start(bf16[256,512]{1,0:T(8,128)(2,1)S(1)} %get-tuple-element.44), channel_id=1, source_target_pairs={{0,1},{1,0},{2,3},{3,2},{4,5},{5,4},{6,7},{7,6},{8,9},{9,8},{10,11... | collective-permute-start | bytes 786440 | tf_op jit(solution)/shard_map/ppermute | solution.py:19
  130.4 21.6 %collective-permute-start.25 = (bf16[256,512]{1,0:T(8,128)(2,1)S(1)}, bf16[256,512]{1,0:T(8,128)(2,1)S(1)}, u32[]{:S(2)}, u32[]{:S(2)}) collective-permute-start(bf16[256,512]{1,0:T(8,128)(2,1)S(1)} %get-tuple-element.42), channel_id=1, source_target_pairs={{0,1},{1,0},{2,3},{3,2},{4,5},{5,4},{6,7},{7,6},{8,9},{9,8},{10,11... | collective-permute-start | bytes 786440 | tf_op jit(solution)/shard_map/ppermute | solution.py:19
  136.0 16.0 %collective-permute-start.31 = (bf16[256,512]{1,0:T(8,128)(2,1)S(1)}, bf16[256,512]{1,0:T(8,128)(2,1)S(1)}, u32[]{:S(2)}, u32[]{:S(2)}) collective-permute-start(bf16[256,512]{1,0:T(8,128)(2,1)S(1)} %add_convert_fusion.1), channel_id=1, source_target_pairs={{0,2},{1,3},{2,0},{3,1},{4,6},{5,7},{6,4},{7,5},{8,10},{9,11},{10,... | collective-permute-start | bytes 786440 | tf_op jit(solution)/shard_map/ppermute | solution.py:19
  141.7 20.5 %collective-permute-start.29 = (bf16[256,512]{1,0:T(8,128)(2,1)S(1)}, bf16[256,512]{1,0:T(8,128)(2,1)S(1)}, u32[]{:S(2)}, u32[]{:S(2)}) collective-permute-start(bf16[256,512]{1,0:T(8,128)(2,1)S(1)} %add_convert_fusion.2), channel_id=1, source_target_pairs={{0,4},{1,5},{2,6},{3,7},{4,0},{5,1},{6,2},{7,3},{8,12},{9,13},{10,... | collective-permute-start | bytes 786440 | tf_op jit(solution)/shard_map/ppermute | solution.py:19
  147.3 14.9 %collective-permute-start.27 = (bf16[256,512]{1,0:T(8,128)(2,1)S(1)}, bf16[256,512]{1,0:T(8,128)(2,1)S(1)}, u32[]{:S(2)}, u32[]{:S(2)}) collective-permute-start(bf16[256,512]{1,0:T(8,128)(2,1)S(1)} %add_convert_fusion.3), channel_id=1, source_target_pairs={{0,6},{1,7},{2,4},{3,5},{4,2},{5,3},{6,0},{7,1},{8,14},{9,15},{10,... | collective-permute-start | bytes 786440 | tf_op jit(solution)/shard_map/ppermute | solution.py:19

commit v2 on v1

--- a/solution.py
+++ b/solution.py
@@ -31,8 +31,8 @@
     return pl.BlockSpec(memory_space=pltpu.SMEM)
 
 
-def any_spec():
-    return pl.BlockSpec(memory_space=pl.ANY)
+def hbm_spec():
+    return pl.BlockSpec(memory_space=pltpu.HBM)
 
 
 def project_kernel(place_ref, *refs):
@@ -78,7 +78,7 @@
     return pl.pallas_call(
         project_kernel,
         out_shape=[jax.ShapeDtypeStruct((rows, DH), jnp.bfloat16)] * 4,
-        in_specs=[smem_spec()] + [any_spec()] * 12,
+        in_specs=[smem_spec()] + [hbm_spec()] * 12,
         out_specs=[vmem_spec()] * 4,
         scratch_shapes=[
             pltpu.VMEM((8, rows, depth), jnp.bfloat16),
@@ -181,7 +181,7 @@
     return pl.pallas_call(
         emit_kernel,
         out_shape=[jax.ShapeDtypeStruct((rows, cols // 2), jnp.bfloat16)] * 8,
-        in_specs=[smem_spec()] + [vmem_spec()] * 4 + [any_spec()] * 4,
+        in_specs=[smem_spec()] + [vmem_spec()] * 4 + [hbm_spec()] * 4,
         out_specs=[vmem_spec()] * 8,
         scratch_shapes=[
             pltpu.VMEM((4, depth, cols), jnp.bfloat16),
@@ -194,12 +194,6 @@
     )(place, *parts, *weights)
 
 
-def gather_pairs(value):
-    across = swap(value, "node", 2)
-    beside = swap(value, "node", 1)
-    return [value, beside, across, swap(across, "node", 1)]
-
-
 def exchange_heads(pieces):
     return [pieces[0]] + [swap(pieces[i], "node", i) for i in range(1, 4)]
 
@@ -212,16 +206,22 @@
 
     far = {i: swap(node_feats, "head", 2 * i) for i in (3, 2, 1)}
     far[0] = node_feats
-    full_qk = gather_pairs(w_qk)
-    pieces = [None] * 8
-    for i in (0, 1, 2, 3):
-        pieces[2 * i] = far[i]
-        pieces[2 * i + 1] = swap(far[i], "head", 1)
-    full_val = gather_pairs(after(w_val, full_qk[2]))
-    full_out = gather_pairs(after(w_out, full_val[2]))
+    beside = swap(node_feats, "head", 1)
+    qk_across, qk_beside = swap(w_qk, "node", 2), swap(w_qk, "node", 1)
+    w_val = after(w_val, qk_across, qk_beside, far[1], far[2], far[3], beside, edges)
+    val_across, val_beside = swap(w_val, "node", 2), swap(w_val, "node", 1)
+    qk_sent = after(qk_across, far[1], far[2], far[3], beside)
+    full_qk = [w_qk, qk_beside, qk_across, swap(qk_sent, "node", 1)]
+    pieces = [node_feats, beside]
+    for i in (1, 2, 3):
+        pieces += [far[i], swap(after(far[i], beside), "head", 1)]
 
     queries = exchange_heads(project(place, pieces, full_qk))
+    w_out = after(w_out, val_across, val_beside, *queries)
+    out_across, out_beside = swap(w_out, "node", 2), swap(w_out, "node", 1)
+    full_val = [w_val, val_beside, val_across, swap(val_across, "node", 1)]
     values = exchange_heads(project(place, pieces, full_val))
+    full_out = [w_out, out_beside, out_across, swap(out_across, "node", 1)]
     attn = exchange_heads(attend(place, edges, bias, queries, values))
     terms = emit(place, attn, full_out)
     sums = [None] * 4

time: 165 us -> 177 us (1.073)
  local copies, waits for them, and re-layouts: 15 us -> 28.3 us
  waiting for transfers between devices: 97 us -> 93.9 us
  starting transfers between devices: 32.9 us -> 34.8 us
    unnamed x40 -> x76, local copies, waits for them, and re-layouts: 15 us -> 28.3 us
    ppermute x32, waiting for transfers between devices: 97 us -> 93.9 us  [swap(): return lax.ppermute(value, axis, [(i, i ^ mask) for i in range(peers)])]
    ppermute x32, starting transfers between devices: 32.9 us -> 34.8 us  [swap(): return lax.ppermute(value, axis, [(i, i ^ mask) for i in range(peers)])]
  transfers between devices with their start and end apart: 32 -> 32, of which waited for: 14 -> 17; matrix products, arithmetic and copies ran while one was open for 0% -> 0% of each run, Pallas kernels for 6% -> 5%
where the time goes in v2:
time: 177 us; the launch traced here: 176 us
  waiting for transfers between devices  93.9 us (53%)
  starting transfers between devices  34.8 us (20%)
  local copies, waits for them, and re-layouts  28.3 us (16%)
  Pallas kernels  12.8 us (7%)
  blocking collectives  5.06 us (3%)
    ppermute x32, waiting for transfers between devices, swap(): return lax.ppermute(value, axis, [(i, i ^ mask) for i in range(peers)])  93.9 us
    ppermute x32, starting transfers between devices, swap(): return lax.ppermute(value, axis, [(i, i ^ mask) for i in range(peers)])  34.8 us
    unnamed x76, local copies, waits for them, and re-layouts  28.3 us
    pallas_call x2, Pallas kernels, project(): pl.pallas_call(project_kernel, out_shape=[jax.ShapeDtypeStruct((rows, DH)...  5.74 us
    all_gather x1, blocking collectives, one_head_each(): edges = lax.all_gather(edge_types, 'node', axis=0, tiled=True)  5.06 us
    pallas_call x1, Pallas kernels, attend(): pl.pallas_call(attend_kernel, out_shape=[jax.ShapeDtypeStruct((rows, DH),...  3.56 us
  transfers between devices with their start and end apart: 32, of which 17 were waited for; matrix products, arithmetic and copies ran while one was open for 0% of the time, Pallas kernels for 5%

profile of v2, /device:TPU:0, one launch (start us, length us, event | category | flops | bytes accessed | tf_op | source)
XLA Modules:
  0.0 176.2 jit_solution(14338576493769866699)
XLA Ops:
  0.0 2.9 %collective-permute-start.8 = (bf16[1024,512]{1,0:T(8,128)(2,1)}, bf16[1024,512]{1,0:T(8,128)(2,1)S(1)}, u32[]{:S(2)}, u32[]{:S(2)}) collective-permute-start(bf16[1024,512]{1,0:T(8,128)(2,1)} %refs_8_.1), channel_id=1, source_target_pairs={{0,16},{8,24},{16,0},{24,8},{1,17},{9,25},{17,1},{25,9},{2,18},{10... | collective-permute-start | bytes 3145736 | tf_op jit(solution)/shard_map/ppermute | solution.py:19
  2.9 3.6 %collective-permute-start.5 = (bf16[256,512]{1,0:T(8,128)(2,1)}, bf16[256,512]{1,0:T(8,128)(2,1)S(1)}, u32[]{:S(2)}, u32[]{:S(2)}) collective-permute-start(bf16[256,512]{1,0:T(8,128)(2,1)} %refs_0_.3), channel_id=1, source_target_pairs={{0,6},{1,7},{2,4},{3,5},{4,2},{5,3},{6,0},{7,1},{8,14},{9,15},{10,... | collective-permute-start | bytes 786440 | tf_op jit(solution)/shard_map/ppermute | solution.py:19
  6.6 0.8 collective-permute-start.1
  7.3 6.9 %collective-permute-done.5.refs_6_ = bf16[256,512]{1,0:T(8,128)(2,1)S(1)} collective-permute-done((bf16[256,512]{1,0:T(8,128)(2,1)}, bf16[256,512]{1,0:T(8,128)(2,1)S(1)}, u32[]{:S(2)}, u32[]{:S(2)}) %collective-permute-start.5) | collective-permute-done | bytes 262176 | tf_op jit(solution)/shard_map/ppermute | solution.py:19
  14.2 1.5 collective-permute-start
  15.7 14.0 %collective-permute-done.3.refs_4_ = bf16[256,512]{1,0:T(8,128)(2,1)S(1)} collective-permute-done((bf16[256,512]{1,0:T(8,128)(2,1)}, bf16[256,512]{1,0:T(8,128)(2,1)S(1)}, u32[]{:S(2)}, u32[]{:S(2)}) %collective-permute-start.3) | collective-permute-done | bytes 262176 | tf_op jit(solution)/shard_map/ppermute | solution.py:19
  29.8 0.7 copy-done.21
  30.5 1.0 copy-done.4
  31.4 5.1 %all-gather = s32[4,2,8]{2,1,0:T(2,128)S(1)} all-gather(s32[1,2,8]{2,1,0:T(2,128)S(1)} %bitcast.7), channel_id=1, replica_groups=mesh['node'=4,'head'=8] {'node'}, dimensions={0}, use_global_device_ids=true | all-gather | bytes 320 | tf_op jit(solution)/shard_map/all_gather | solution.py:204
  36.5 1.0 copy-done.6
  38.1 1.5 collective-permute-start.2
  39.6 0.7 copy-done.18
  40.8 0.7 copy-done.15
  41.5 5.7 %collective-permute-done.2.refs_3_ = bf16[256,512]{1,0:T(8,128)(2,1)S(1)} collective-permute-done((bf16[256,512]{1,0:T(8,128)(2,1)S(1)}, bf16[256,512]{1,0:T(8,128)(2,1)S(1)}, u32[]{:S(2)}, u32[]{:S(2)}) %collective-permute-start.2) | collective-permute-done | bytes 262176 | tf_op jit(solution)/shard_map/ppermute | solution.py:19
  47.2 0.7 copy-done.24
  47.9 1.5 collective-permute-start.6
  50.2 2.6 %collective-permute-done.4.refs_5_ = bf16[256,512]{1,0:T(8,128)(2,1)S(1)} collective-permute-done((bf16[256,512]{1,0:T(8,128)(2,1)S(1)}, bf16[256,512]{1,0:T(8,128)(2,1)S(1)}, u32[]{:S(2)}, u32[]{:S(2)}) %collective-permute-start.4) | collective-permute-done | bytes 262176 | tf_op jit(solution)/shard_map/ppermute | solution.py:19
  52.8 0.7 copy-done.27
  53.5 4.5 %collective-permute-done.6.refs_7_ = bf16[256,512]{1,0:T(8,128)(2,1)S(1)} collective-permute-done((bf16[256,512]{1,0:T(8,128)(2,1)S(1)}, bf16[256,512]{1,0:T(8,128)(2,1)S(1)}, u32[]{:S(2)}, u32[]{:S(2)}) %collective-permute-start.6) | collective-permute-done | bytes 262176 | tf_op jit(solution)/shard_map/ppermute | solution.py:19
  58.7 1.0 copy-done.8
  59.7 1.2 copy-done.1
  60.9 1.2 copy-done.5
  62.1 1.2 copy-done.7
  63.4 1.2 copy-done.9
  64.6 0.9 copy-done.10
  65.5 0.9 copy-done.13
  66.5 0.9 copy-done.16
  67.4 0.9 copy-done.19
  68.4 0.9 copy-done.22
  69.3 0.9 copy-done.25
  70.3 0.9 copy-done.28
  71.2 0.9 copy-done.31
  72.2 2.5 %project.2 = (bf16[256,128]{1,0:T(8,128)(2,1)S(1)}, bf16[256,128]{1,0:T(8,128)(2,1)S(1)}, bf16[256,128]{1,0:T(8,128)(2,1)S(1)}, bf16[256,128]{1,0:T(8,128)(2,1)S(1)}) custom-call(s32[2]{0:T(128)S(1)} %pad_add_fusion.place_ref, bf16[256,512]{1,0:T(8,128)(2,1)S(1)} %copy-done.10, bf16[256,512]{1,0:T(8,128)(2,1)S(1)} %copy-done.22, ...), custom_call_target="tpu_custom_call" | custom-call | flops 1073741824 | bytes 6553600 | tf_op jit(solution)/shard_map/project/pallas_call | solution.py:78
  74.8 1.6 collective-permute-start.11
  76.7 2.6 %collective-permute-done.11.refs_2_ = bf16[256,128]{1,0:T(8,128)(2,1)S(1)} collective-permute-done((bf16[256,128]{1,0:T(8,128)(2,1)S(1)}, bf16[256,128]{1,0:T(8,128)(2,1)S(1)}, u32[]{:S(2)}, u32[]{:S(2)}) %collective-permute-start.11) | collective-permute-done | bytes 65568 | tf_op jit(solution)/shard_map/ppermute | solution.py:19
  81.0 1.5 collective-permute-start.23
  83.0 23.3 %collective-permute-done.23.refs_6_ = bf16[512,1024]{1,0:T(8,128)(2,1)S(1)} collective-permute-done((bf16[512,1024]{1,0:T(8,128)(2,1)S(1)}, bf16[512,1024]{1,0:T(8,128)(2,1)S(1)}, u32[]{:S(2)}, u32[]{:S(2)}) %collective-permute-start.23) | collective-permute-done | bytes 1048608 | tf_op jit(solution)/shard_map/ppermute | solution.py:19
  106.3 0.9 copy-done.14
  107.2 0.9 copy-done.17
  108.2 0.9 copy-done.20
  109.1 0.9 copy-done.23
  110.1 0.9 copy-done.26
  111.0 0.9 copy-done.29
  112.0 0.9 copy-done.32
  112.9 3.2 %project.3 = (bf16[256,128]{1,0:T(8,128)(2,1)S(1)}, bf16[256,128]{1,0:T(8,128)(2,1)S(1)}, bf16[256,128]{1,0:T(8,128)(2,1)S(1)}, bf16[256,128]{1,0:T(8,128)(2,1)S(1)}) custom-call(s32[2]{0:T(128)S(1)} %pad_add_fusion.place_ref, bf16[256,512]{1,0:T(8,128)(2,1)S(1)} %copy-done.11, bf16[256,512]{1,0:T(8,128)(2,1)S(1)} %copy-done.23, ...), custom_call_target="tpu_custom_call" | custom-call | flops 1073741824 | bytes 6553600 | tf_op jit(solution)/shard_map/project/pallas_call | solution.py:78
  116.7 1.5 collective-permute-start.17
  118.2 2.8 %collective-permute-done.17.refs_6_ = bf16[256,128]{1,0:T(8,128)(2,1)S(1)} collective-permute-done((bf16[256,128]{1,0:T(8,128)(2,1)S(1)}, bf16[256,128]{1,0:T(8,128)(2,1)S(1)}, u32[]{:S(2)}, u32[]{:S(2)}) %collective-permute-start.17) | collective-permute-done | bytes 65568 | tf_op jit(solution)/shard_map/ppermute | solution.py:19
  121.0 1.6 collective-permute-done.18.refs_7_
  122.6 3.6 %attend.1 = (bf16[256,128]{1,0:T(8,128)(2,1)S(1)}, bf16[256,128]{1,0:T(8,128)(2,1)S(1)}, bf16[256,128]{1,0:T(8,128)(2,1)S(1)}, bf16[256,128]{1,0:T(8,128)(2,1)S(1)}) custom-call(s32[2]{0:T(128)S(1)} %pad_add_fusion.place_ref, s32[8,8]{1,0:T(8,128)S(1)} %bitcast.5, f32[237]{0:T(256)S(1)} %bitcast.6, bf16[256,128]{1,0:T(8,128)(2,1)S(1)} %get-tuple-element.35.refs_0_, ...), custom_call_target="tpu_custom_call" | custom-call | flops 536870912 | bytes 786432 | tf_op jit(solution)/shard_map/attend/pallas_call | solution.py:138
  126.3 1.0 collective-permute-start.20
  127.3 0.8 collective-permute-start.21
  128.1 3.0 %collective-permute-done.20.refs_2_ = bf16[256,128]{1,0:T(8,128)(2,1)S(1)} collective-permute-done((bf16[256,128]{1,0:T(8,128)(2,1)S(1)}, bf16[256,128]{1,0:T(8,128)(2,1)S(1)}, u32[]{:S(2)}, u32[]{:S(2)}) %collective-permute-start.20) | collective-permute-done | bytes 65568 | tf_op jit(solution)/shard_map/ppermute | solution.py:19
  131.7 3.5 %emit.1 = (bf16[256,512]{1,0:T(8,128)(2,1)S(1)}, bf16[256,512]{1,0:T(8,128)(2,1)S(1)}, bf16[256,512]{1,0:T(8,128)(2,1)S(1)}, bf16[256,512]{1,0:T(8,128)(2,1)S(1)...) custom-call(s32[2]{0:T(128)S(1)} %pad_add_fusion.place_ref, ...), custom_call_target="tpu_custom_call" | custom-call | flops 1073741824 | bytes 6553600 | tf_op jit(solution)/shard_map/emit/pallas_call | solution.py:181
  135.2 1.6 collective-permute-start.26
  137.3 1.5 collective-permute-start.25
  139.3 5.1 %collective-permute-done.26 = bf16[256,512]{1,0:T(8,128)(2,1)S(1)} collective-permute-done((bf16[256,512]{1,0:T(8,128)(2,1)S(1)}, bf16[256,512]{1,0:T(8,128)(2,1)S(1)}, u32[]{:S(2)}, u32[]{:S(2)}) %collective-permute-start.26) | collective-permute-done | bytes 262176 | tf_op jit(solution)/shard_map/ppermute | solution.py:19
  144.5 2.5 %collective-permute-start.27 = (bf16[256,512]{1,0:T(8,128)(2,1)S(1)}, bf16[256,512]{1,0:T(8,128)(2,1)S(1)}, u32[]{:S(2)}, u32[]{:S(2)}) collective-permute-start(bf16[256,512]{1,0:T(8,128)(2,1)S(1)} %add_convert_fusion.3), channel_id=1, source_target_pairs={{0,6},{1,7},{2,4},{3,5},{4,2},{5,3},{6,0},{7,1},{8,14},{9,15},{10,... | collective-permute-start | bytes 786440 | tf_op jit(solution)/shard_map/ppermute | solution.py:19
  147.0 3.0 %collective-permute-done.28 = bf16[256,512]{1,0:T(8,128)(2,1)S(1)} collective-permute-done((bf16[256,512]{1,0:T(8,128)(2,1)S(1)}, bf16[256,512]{1,0:T(8,128)(2,1)S(1)}, u32[]{:S(2)}, u32[]{:S(2)}) %collective-permute-start.28) | collective-permute-done | bytes 262176 | tf_op jit(solution)/shard_map/ppermute | solution.py:19
  150.1 4.2 %collective-permute-start.29 = (bf16[256,512]{1,0:T(8,128)(2,1)S(1)}, bf16[256,512]{1,0:T(8,128)(2,1)S(1)}, u32[]{:S(2)}, u32[]{:S(2)}) collective-permute-start(bf16[256,512]{1,0:T(8,128)(2,1)S(1)} %add_convert_fusion.2), channel_id=1, source_target_pairs={{0,4},{1,5},{2,6},{3,7},{4,0},{5,1},{6,2},{7,3},{8,12},{9,13},{10,... | collective-permute-start | bytes 786440 | tf_op jit(solution)/shard_map/ppermute | solution.py:19
  154.2 6.3 %collective-permute-done.30 = bf16[256,512]{1,0:T(8,128)(2,1)S(1)} collective-permute-done((bf16[256,512]{1,0:T(8,128)(2,1)S(1)}, bf16[256,512]{1,0:T(8,128)(2,1)S(1)}, u32[]{:S(2)}, u32[]{:S(2)}) %collective-permute-start.30) | collective-permute-done | bytes 262176 | tf_op jit(solution)/shard_map/ppermute | solution.py:19
  160.6 3.2 %collective-permute-start.31 = (bf16[256,512]{1,0:T(8,128)(2,1)S(1)}, bf16[256,512]{1,0:T(8,128)(2,1)S(1)}, u32[]{:S(2)}, u32[]{:S(2)}) collective-permute-start(bf16[256,512]{1,0:T(8,128)(2,1)S(1)} %add_convert_fusion.1), channel_id=1, source_target_pairs={{0,2},{1,3},{2,0},{3,1},{4,6},{5,7},{6,4},{7,5},{8,10},{9,11},{10,... | collective-permute-start | bytes 786440 | tf_op jit(solution)/shard_map/ppermute | solution.py:19
  163.8 6.4 %collective-permute-done.29 = bf16[256,512]{1,0:T(8,128)(2,1)S(1)} collective-permute-done((bf16[256,512]{1,0:T(8,128)(2,1)S(1)}, bf16[256,512]{1,0:T(8,128)(2,1)S(1)}, u32[]{:S(2)}, u32[]{:S(2)}) %collective-permute-start.29) | collective-permute-done | bytes 262176 | tf_op jit(solution)/shard_map/ppermute | solution.py:19
  170.2 5.1 %collective-permute-done.31 = bf16[256,512]{1,0:T(8,128)(2,1)S(1)} collective-permute-done((bf16[256,512]{1,0:T(8,128)(2,1)S(1)}, bf16[256,512]{1,0:T(8,128)(2,1)S(1)}, u32[]{:S(2)}, u32[]{:S(2)}) %collective-permute-start.31) | collective-permute-done | bytes 262176 | tf_op jit(solution)/shard_map/ppermute | solution.py:19
  175.3 0.9 add_convert_fusion
  (87 shorter events, 7.8 us)
Async XLA Ops:
  0.0 118.2 %copy-start = (f32[237,4]{0,1:T(4,128)S(1)}, f32[237,4]{0,1:T(4,128)}, u32[]{:S(2)}) copy-start(f32[237,4]{0,1:T(4,128)} %param.11) | copy-start | bytes 11380
  0.0 31.4 %copy-start.37 = (s32[2,8]{1,0:T(2,128)S(1)}, s32[2,8]{1,0:T(2,128)}, u32[]{:S(2)}) copy-start(s32[2,8]{1,0:T(2,128)} %param.10) | copy-start | bytes 196
  0.0 30.5 %collective-permute-start.8 = (bf16[1024,512]{1,0:T(8,128)(2,1)}, bf16[1024,512]{1,0:T(8,128)(2,1)S(1)}, u32[]{:S(2)}, u32[]{:S(2)}) collective-permute-start(bf16[1024,512]{1,0:T(8,128)(2,1)} %refs_8_.1), channel_id=1, source_target_pairs={{0,16},{8,24},{16,0},{24,8},{1,17},{9,25},{17,1},{25,9},{2,18},{10... | collective-permute-start | bytes 3145736 | tf_op jit(solution)/shard_map/ppermute | solution.py:19
  2.9 33.5 %collective-permute-start.7 = (bf16[1024,512]{1,0:T(8,128)(2,1)}, bf16[1024,512]{1,0:T(8,128)(2,1)S(1)}, u32[]{:S(2)}, u32[]{:S(2)}) collective-permute-start(bf16[1024,512]{1,0:T(8,128)(2,1)} %refs_8_.1), channel_id=1, source_target_pairs={{0,8},{8,0},{16,24},{24,16},{1,9},{9,1},{17,25},{25,17},{2,10},{10... | collective-permute-start | bytes 3145736 | tf_op jit(solution)/shard_map/ppermute | solution.py:19
  2.9 11.2 %collective-permute-start.5 = (bf16[256,512]{1,0:T(8,128)(2,1)}, bf16[256,512]{1,0:T(8,128)(2,1)S(1)}, u32[]{:S(2)}, u32[]{:S(2)}) collective-permute-start(bf16[256,512]{1,0:T(8,128)(2,1)} %refs_0_.3), channel_id=1, source_target_pairs={{0,6},{1,7},{2,4},{3,5},{4,2},{5,3},{6,0},{7,1},{8,14},{9,15},{10,... | collective-permute-start | bytes 786440 | tf_op jit(solution)/shard_map/ppermute | solution.py:19
  6.5 23.2 %collective-permute-start.3 = (bf16[256,512]{1,0:T(8,128)(2,1)}, bf16[256,512]{1,0:T(8,128)(2,1)S(1)}, u32[]{:S(2)}, u32[]{:S(2)}) collective-permute-start(bf16[256,512]{1,0:T(8,128)(2,1)} %refs_0_.3), channel_id=1, source_target_pairs={{0,4},{1,5},{2,6},{3,7},{4,0},{5,1},{6,2},{7,3},{8,12},{9,13},{10,... | collective-permute-start | bytes 786440 | tf_op jit(solution)/shard_map/ppermute | solution.py:19
  6.6 23.2 %collective-permute-start.1 = (bf16[256,512]{1,0:T(8,128)(2,1)}, bf16[256,512]{1,0:T(8,128)(2,1)S(1)}, u32[]{:S(2)}, u32[]{:S(2)}) collective-permute-start(bf16[256,512]{1,0:T(8,128)(2,1)} %refs_0_.3), channel_id=1, source_target_pairs={{0,2},{1,3},{2,0},{3,1},{4,6},{5,7},{6,4},{7,5},{8,10},{9,11},{10,... | collective-permute-start | bytes 786440 | tf_op jit(solution)/shard_map/ppermute | solution.py:19
  14.2 15.6 %collective-permute-start = (bf16[256,512]{1,0:T(8,128)(2,1)}, bf16[256,512]{1,0:T(8,128)(2,1)S(1)}, u32[]{:S(2)}, u32[]{:S(2)}) collective-permute-start(bf16[256,512]{1,0:T(8,128)(2,1)} %refs_0_.3), channel_id=1, source_target_pairs={{0,1},{1,0},{2,3},{3,2},{4,5},{5,4},{6,7},{7,6},{8,9},{9,8},{10,11... | collective-permute-start | bytes 786440 | tf_op jit(solution)/shard_map/ppermute | solution.py:19
  30.5 28.2 %collective-permute-start.9 = (bf16[1024,512]{1,0:T(8,128)(2,1)S(1)}, bf16[1024,512]{1,0:T(8,128)(2,1)S(1)}, u32[]{:S(2)}, u32[]{:S(2)}) collective-permute-start(bf16[1024,512]{1,0:T(8,128)(2,1)S(1)} %collective-permute-done.8.refs_10_), channel_id=1, source_target_pairs={{0,8},{8,0},{16,24},{24,16},{1,9},{9,1},{17,25},{25,17},{2,10},{10... | collective-permute-start | bytes 3145736 | tf_op jit(solution)/shard_map/ppermute | solution.py:19
  30.5 1.0 copy-start.4
  36.5 1.0 copy-start.6
  37.5 39.2 %collective-permute-start.14 = (bf16[1024,512]{1,0:T(8,128)(2,1)}, bf16[1024,512]{1,0:T(8,128)(2,1)}, u32[]{:S(2)}, u32[]{:S(2)}) collective-permute-start(bf16[1024,512]{1,0:T(8,128)(2,1)} %refs_8_.2), channel_id=1, source_target_pairs={{0,16},{8,24},{16,0},{24,8},{1,17},{9,25},{17,1},{25,9},{2,18},{10... | collective-permute-start | bytes 3145736 | tf_op jit(solution)/shard_map/ppermute | solution.py:19
  38.0 38.7 %collective-permute-start.13 = (bf16[1024,512]{1,0:T(8,128)(2,1)}, bf16[1024,512]{1,0:T(8,128)(2,1)}, u32[]{:S(2)}, u32[]{:S(2)}) collective-permute-start(bf16[1024,512]{1,0:T(8,128)(2,1)} %refs_8_.2), channel_id=1, source_target_pairs={{0,8},{8,0},{16,24},{24,16},{1,9},{9,1},{17,25},{25,17},{2,10},{10... | collective-permute-start | bytes 3145736 | tf_op jit(solution)/shard_map/ppermute | solution.py:19
  38.1 9.1 %collective-permute-start.2 = (bf16[256,512]{1,0:T(8,128)(2,1)S(1)}, bf16[256,512]{1,0:T(8,128)(2,1)S(1)}, u32[]{:S(2)}, u32[]{:S(2)}) collective-permute-start(bf16[256,512]{1,0:T(8,128)(2,1)S(1)} %collective-permute-done.1.refs_2_), channel_id=1, source_target_pairs={{0,1},{1,0},{2,3},{3,2},{4,5},{5,4},{6,7},{7,6},{8,9},{9,8},{10,11... | collective-permute-start | bytes 786440 | tf_op jit(solution)/shard_map/ppermute | solution.py:19
  40.3 12.5 %collective-permute-start.4 = (bf16[256,512]{1,0:T(8,128)(2,1)S(1)}, bf16[256,512]{1,0:T(8,128)(2,1)S(1)}, u32[]{:S(2)}, u32[]{:S(2)}) collective-permute-start(bf16[256,512]{1,0:T(8,128)(2,1)S(1)} %collective-permute-done.3.refs_4_), channel_id=1, source_target_pairs={{0,1},{1,0},{2,3},{3,2},{4,5},{5,4},{6,7},{7,6},{8,9},{9,8},{10,11... | collective-permute-start | bytes 786440 | tf_op jit(solution)/shard_map/ppermute | solution.py:19
  40.8 0.7 copy-start.15
  47.2 0.7 copy-start.24
  47.9 10.1 %collective-permute-start.6 = (bf16[256,512]{1,0:T(8,128)(2,1)S(1)}, bf16[256,512]{1,0:T(8,128)(2,1)S(1)}, u32[]{:S(2)}, u32[]{:S(2)}) collective-permute-start(bf16[256,512]{1,0:T(8,128)(2,1)S(1)} %collective-permute-done.5.refs_6_), channel_id=1, source_target_pairs={{0,1},{1,0},{2,3},{3,2},{4,5},{5,4},{6,7},{7,6},{8,9},{9,8},{10,11... | collective-permute-start | bytes 786440 | tf_op jit(solution)/shard_map/ppermute | solution.py:19
  52.8 0.7 copy-start.27
  58.7 1.0 copy-start.8
  59.7 1.2 copy-start.1
  60.9 1.2 copy-start.5
  62.1 1.2 copy-start.7
  63.3 1.2 copy-start.9
  64.6 0.9 copy-start.10
  65.5 0.9 copy-start.13
  66.5 0.9 copy-start.16
  67.4 0.9 copy-start.19
  68.4 0.9 copy-start.22
  69.3 0.9 copy-start.25
  70.3 0.9 copy-start.28
  71.2 0.9 copy-start.31
  72.2 8.9 %copy-start.3 = (bf16[512,1024]{1,0:T(8,128)(2,1)S(1)}, bf16[512,1024]{1,0:T(8,128)(2,1)}, u32[]{:S(2)}) copy-start(bf16[512,1024]{1,0:T(8,128)(2,1)} %refs_4_) | copy-start | bytes 3145732
  72.2 34.1 %copy-start.2 = (bf16[1024,512]{1,0:T(8,128)(2,1)S(1)}, bf16[1024,512]{1,0:T(8,128)(2,1)}, u32[]{:S(2)}) copy-start(bf16[1024,512]{1,0:T(8,128)(2,1)} %refs_8_.2) | copy-start | bytes 3145732
  72.2 34.1 %copy-start.11 = (bf16[256,512]{1,0:T(8,128)(2,1)S(1)}, bf16[256,512]{1,0:T(8,128)(2,1)}, u32[]{:S(2)}) copy-start(bf16[256,512]{1,0:T(8,128)(2,1)} %refs_0_.3) | copy-start | bytes 786436
  74.7 2.0 %collective-permute-start.10 = (bf16[256,128]{1,0:T(8,128)(2,1)S(1)}, bf16[256,128]{1,0:T(8,128)(2,1)S(1)}, u32[]{:S(2)}, u32[]{:S(2)}) collective-permute-start(bf16[256,128]{1,0:T(8,128)(2,1)S(1)} %get-tuple-element.36), channel_id=1, source_target_pairs={{0,8},{8,0},{16,24},{24,16},{1,9},{9,1},{17,25},{25,17},{2,10},{10... | collective-permute-start | bytes 196616 | tf_op jit(solution)/shard_map/ppermute | solution.py:19
  74.8 4.5 %collective-permute-start.11 = (bf16[256,128]{1,0:T(8,128)(2,1)S(1)}, bf16[256,128]{1,0:T(8,128)(2,1)S(1)}, u32[]{:S(2)}, u32[]{:S(2)}) collective-permute-start(bf16[256,128]{1,0:T(8,128)(2,1)S(1)} %get-tuple-element.37), channel_id=1, source_target_pairs={{0,16},{8,24},{16,0},{24,8},{1,17},{9,25},{17,1},{25,9},{2,18},{10... | collective-permute-start | bytes 196616 | tf_op jit(solution)/shard_map/ppermute | solution.py:19
  76.4 4.0 %collective-permute-start.12 = (bf16[256,128]{1,0:T(8,128)(2,1)S(1)}, bf16[256,128]{1,0:T(8,128)(2,1)S(1)}, u32[]{:S(2)}, u32[]{:S(2)}) collective-permute-start(bf16[256,128]{1,0:T(8,128)(2,1)S(1)} %get-tuple-element.38), channel_id=1, source_target_pairs={{0,24},{8,16},{16,8},{24,0},{1,25},{9,17},{17,9},{25,1},{2,26},{10... | collective-permute-start | bytes 196616 | tf_op jit(solution)/shard_map/ppermute | solution.py:19
  81.0 25.2 %collective-permute-start.23 = (bf16[512,1024]{1,0:T(8,128)(2,1)S(1)}, bf16[512,1024]{1,0:T(8,128)(2,1)S(1)}, u32[]{:S(2)}, u32[]{:S(2)}) collective-permute-start(bf16[512,1024]{1,0:T(8,128)(2,1)S(1)} %copy-done.3), channel_id=1, source_target_pairs={{0,16},{8,24},{16,0},{24,8},{1,17},{9,25},{17,1},{25,9},{2,18},{10... | collective-permute-start | bytes 3145736 | tf_op jit(solution)/shard_map/ppermute | solution.py:19
  82.5 23.8 %collective-permute-start.15 = (bf16[1024,512]{1,0:T(8,128)(2,1)}, bf16[1024,512]{1,0:T(8,128)(2,1)}, u32[]{:S(2)}, u32[]{:S(2)}) collective-permute-start(bf16[1024,512]{1,0:T(8,128)(2,1)} %collective-permute-done.14.refs_10_), channel_id=1, source_target_pairs={{0,8},{8,0},{16,24},{24,16},{1,9},{9,1},{17,25},{25,17},{2,10},{10... | collective-permute-start | bytes 3145736 | tf_op jit(solution)/shard_map/ppermute | solution.py:19
  82.5 45.6 %collective-permute-start.22 = (bf16[512,1024]{1,0:T(8,128)(2,1)S(1)}, bf16[512,1024]{1,0:T(8,128)(2,1)}, u32[]{:S(2)}, u32[]{:S(2)}) collective-permute-start(bf16[512,1024]{1,0:T(8,128)(2,1)S(1)} %copy-done.3), channel_id=1, source_target_pairs={{0,8},{8,0},{16,24},{24,16},{1,9},{9,1},{17,25},{25,17},{2,10},{10... | collective-permute-start | bytes 3145736 | tf_op jit(solution)/shard_map/ppermute | solution.py:19
  106.3 25.4 %collective-permute-start.24 = (bf16[512,1024]{1,0:T(8,128)(2,1)S(1)}, bf16[512,1024]{1,0:T(8,128)(2,1)}, u32[]{:S(2)}, u32[]{:S(2)}) collective-permute-start(bf16[512,1024]{1,0:T(8,128)(2,1)S(1)} %collective-permute-done.23.refs_6_), channel_id=1, source_target_pairs={{0,8},{8,0},{16,24},{24,16},{1,9},{9,1},{17,25},{25,17},{2,10},{10... | collective-permute-start | bytes 3145736 | tf_op jit(solution)/shard_map/ppermute | solution.py:19
  106.3 1.0 copy-start.14
  107.2 0.9 copy-start.17
  108.2 0.9 copy-start.20
  109.1 0.9 copy-start.23
  110.1 0.9 copy-start.26
  111.0 0.9 copy-start.29
  112.0 0.9 copy-start.32
  112.9 9.6 %copy-start.34 = (bf16[256,128]{1,0:T(8,128)(2,1)S(1)}, bf16[256,128]{1,0:T(8,128)(2,1)}, u32[]{:S(2)}) copy-start(bf16[256,128]{1,0:T(8,128)(2,1)} %copy-done.33) | copy-start | bytes 196612
  112.9 9.6 %copy-start.36 = (bf16[256,128]{1,0:T(8,128)(2,1)S(1)}, bf16[256,128]{1,0:T(8,128)(2,1)}, u32[]{:S(2)}) copy-start(bf16[256,128]{1,0:T(8,128)(2,1)} %copy-done.35) | copy-start | bytes 196612
  116.2 2.1 %collective-permute-start.16 = (bf16[256,128]{1,0:T(8,128)(2,1)S(1)}, bf16[256,128]{1,0:T(8,128)(2,1)S(1)}, u32[]{:S(2)}, u32[]{:S(2)}) collective-permute-start(bf16[256,128]{1,0:T(8,128)(2,1)S(1)} %get-tuple-element.41), channel_id=1, source_target_pairs={{0,8},{8,0},{16,24},{24,16},{1,9},{9,1},{17,25},{25,17},{2,10},{10... | collective-permute-start | bytes 196616 | tf_op jit(solution)/shard_map/ppermute | solution.py:19
  116.7 4.3 %collective-permute-start.17 = (bf16[256,128]{1,0:T(8,128)(2,1)S(1)}, bf16[256,128]{1,0:T(8,128)(2,1)S(1)}, u32[]{:S(2)}, u32[]{:S(2)}) collective-permute-start(bf16[256,128]{1,0:T(8,128)(2,1)S(1)} %get-tuple-element.42), channel_id=1, source_target_pairs={{0,16},{8,24},{16,0},{24,8},{1,17},{9,25},{17,1},{25,9},{2,18},{10... | collective-permute-start | bytes 196616 | tf_op jit(solution)/shard_map/ppermute | solution.py:19
  118.2 4.4 %collective-permute-start.18 = (bf16[256,128]{1,0:T(8,128)(2,1)S(1)}, bf16[256,128]{1,0:T(8,128)(2,1)S(1)}, u32[]{:S(2)}, u32[]{:S(2)}) collective-permute-start(bf16[256,128]{1,0:T(8,128)(2,1)S(1)} %get-tuple-element.43), channel_id=1, source_target_pairs={{0,24},{8,16},{16,8},{24,0},{1,25},{9,17},{17,9},{25,1},{2,26},{10... | collective-permute-start | bytes 196616 | tf_op jit(solution)/shard_map/ppermute | solution.py:19
  126.1 1.9 %collective-permute-start.19 = (bf16[256,128]{1,0:T(8,128)(2,1)S(1)}, bf16[256,128]{1,0:T(8,128)(2,1)S(1)}, u32[]{:S(2)}, u32[]{:S(2)}) collective-permute-start(bf16[256,128]{1,0:T(8,128)(2,1)S(1)} %get-tuple-element.45), channel_id=1, source_target_pairs={{0,8},{8,0},{16,24},{24,16},{1,9},{9,1},{17,25},{25,17},{2,10},{10... | collective-permute-start | bytes 196616 | tf_op jit(solution)/shard_map/ppermute | solution.py:19
  126.3 4.8 %collective-permute-start.20 = (bf16[256,128]{1,0:T(8,128)(2,1)S(1)}, bf16[256,128]{1,0:T(8,128)(2,1)S(1)}, u32[]{:S(2)}, u32[]{:S(2)}) collective-permute-start(bf16[256,128]{1,0:T(8,128)(2,1)S(1)} %get-tuple-element.46), channel_id=1, source_target_pairs={{0,16},{8,24},{16,0},{24,8},{1,17},{9,25},{17,1},{25,9},{2,18},{10... | collective-permute-start | bytes 196616 | tf_op jit(solution)/shard_map/ppermute | solution.py:19
  127.3 4.4 %collective-permute-start.21 = (bf16[256,128]{1,0:T(8,128)(2,1)S(1)}, bf16[256,128]{1,0:T(8,128)(2,1)S(1)}, u32[]{:S(2)}, u32[]{:S(2)}) collective-permute-start(bf16[256,128]{1,0:T(8,128)(2,1)S(1)} %get-tuple-element.47), channel_id=1, source_target_pairs={{0,24},{8,16},{16,8},{24,0},{1,25},{9,17},{17,9},{25,1},{2,26},{10... | collective-permute-start | bytes 196616 | tf_op jit(solution)/shard_map/ppermute | solution.py:19
  135.2 9.2 %collective-permute-start.26 = (bf16[256,512]{1,0:T(8,128)(2,1)S(1)}, bf16[256,512]{1,0:T(8,128)(2,1)S(1)}, u32[]{:S(2)}, u32[]{:S(2)}) collective-permute-start(bf16[256,512]{1,0:T(8,128)(2,1)S(1)} %get-tuple-element.52), channel_id=1, source_target_pairs={{0,1},{1,0},{2,3},{3,2},{4,5},{5,4},{6,7},{7,6},{8,9},{9,8},{10,11... | collective-permute-start | bytes 786440 | tf_op jit(solution)/shard_map/ppermute | solution.py:19
  136.8 13.2 %collective-permute-start.28 = (bf16[256,512]{1,0:T(8,128)(2,1)S(1)}, bf16[256,512]{1,0:T(8,128)(2,1)S(1)}, u32[]{:S(2)}, u32[]{:S(2)}) collective-permute-start(bf16[256,512]{1,0:T(8,128)(2,1)S(1)} %get-tuple-element.54), channel_id=1, source_target_pairs={{0,1},{1,0},{2,3},{3,2},{4,5},{5,4},{6,7},{7,6},{8,9},{9,8},{10,11... | collective-permute-start | bytes 786440 | tf_op jit(solution)/shard_map/ppermute | solution.py:19
  137.3 26.5 %collective-permute-start.25 = (bf16[256,512]{1,0:T(8,128)(2,1)S(1)}, bf16[256,512]{1,0:T(8,128)(2,1)S(1)}, u32[]{:S(2)}, u32[]{:S(2)}) collective-permute-start(bf16[256,512]{1,0:T(8,128)(2,1)S(1)} %get-tuple-element.50), channel_id=1, source_target_pairs={{0,1},{1,0},{2,3},{3,2},{4,5},{5,4},{6,7},{7,6},{8,9},{9,8},{10,11... | collective-permute-start | bytes 786440 | tf_op jit(solution)/shard_map/ppermute | solution.py:19
  138.8 21.7 %collective-permute-start.30 = (bf16[256,512]{1,0:T(8,128)(2,1)S(1)}, bf16[256,512]{1,0:T(8,128)(2,1)S(1)}, u32[]{:S(2)}, u32[]{:S(2)}) collective-permute-start(bf16[256,512]{1,0:T(8,128)(2,1)S(1)} %get-tuple-element.56), channel_id=1, source_target_pairs={{0,1},{1,0},{2,3},{3,2},{4,5},{5,4},{6,7},{7,6},{8,9},{9,8},{10,11... | collective-permute-start | bytes 786440 | tf_op jit(solution)/shard_map/ppermute | solution.py:19
  144.5 19.3 %collective-permute-start.27 = (bf16[256,512]{1,0:T(8,128)(2,1)S(1)}, bf16[256,512]{1,0:T(8,128)(2,1)S(1)}, u32[]{:S(2)}, u32[]{:S(2)}) collective-permute-start(bf16[256,512]{1,0:T(8,128)(2,1)S(1)} %add_convert_fusion.3), channel_id=1, source_target_pairs={{0,6},{1,7},{2,4},{3,5},{4,2},{5,3},{6,0},{7,1},{8,14},{9,15},{10,... | collective-permute-start | bytes 786440 | tf_op jit(solution)/shard_map/ppermute | solution.py:19
  150.1 20.1 %collective-permute-start.29 = (bf16[256,512]{1,0:T(8,128)(2,1)S(1)}, bf16[256,512]{1,0:T(8,128)(2,1)S(1)}, u32[]{:S(2)}, u32[]{:S(2)}) collective-permute-start(bf16[256,512]{1,0:T(8,128)(2,1)S(1)} %add_convert_fusion.2), channel_id=1, source_target_pairs={{0,4},{1,5},{2,6},{3,7},{4,0},{5,1},{6,2},{7,3},{8,12},{9,13},{10,... | collective-permute-start | bytes 786440 | tf_op jit(solution)/shard_map/ppermute | solution.py:19
  160.6 14.7 %collective-permute-start.31 = (bf16[256,512]{1,0:T(8,128)(2,1)S(1)}, bf16[256,512]{1,0:T(8,128)(2,1)S(1)}, u32[]{:S(2)}, u32[]{:S(2)}) collective-permute-start(bf16[256,512]{1,0:T(8,128)(2,1)S(1)} %add_convert_fusion.1), channel_id=1, source_target_pairs={{0,2},{1,3},{2,0},{3,1},{4,6},{5,7},{6,4},{7,5},{8,10},{9,11},{10,... | collective-permute-start | bytes 786440 | tf_op jit(solution)/shard_map/ppermute | solution.py:19
  (6 other events, 4.0 us)

commit v3 on v2

--- a/solution.py
+++ b/solution.py
@@ -31,33 +31,23 @@
     return pl.BlockSpec(memory_space=pltpu.SMEM)
 
 
-def hbm_spec():
-    return pl.BlockSpec(memory_space=pltpu.HBM)
-
-
-def project_kernel(place_ref, *refs):
+def project_kernel(*refs):
     pieces, weights, outs = refs[:8], refs[8:12], refs[12:16]
-    feats, held, total, heads, piece_sem, weight_sem = refs[16:]
-    node, head = place_ref[0], place_ref[1]
+    feats, total, heads, piece_sem = refs[16:]
+    node, head = lax.axis_index("node"), lax.axis_index("head")
     copies = []
     for i in range(8):
         copy = pltpu.make_async_copy(pieces[i], feats.at[head ^ i], piece_sem.at[i])
         copy.start()
         copies.append(copy)
-    weight_copies = []
-    for i in range(4):
-        copy = pltpu.make_async_copy(weights[i], held.at[i], weight_sem.at[i])
-        copy.start()
-        weight_copies.append(copy)
     for copy in copies:
         copy.wait()
     depth = feats.shape[2]
     for i in range(4):
-        weight_copies[i].wait()
         for part in range(2):
             term = jnp.dot(
                 feats[2 * (node ^ i) + part],
-                held[i, part * depth : (part + 1) * depth, :],
+                weights[i][part * depth : (part + 1) * depth, :],
                 preferred_element_type=jnp.float32,
             )
             if i == 0 and part == 0:
@@ -70,7 +60,7 @@
         outs[i][...] = heads[node ^ i]
 
 
-def project(place, pieces, weights):
+def project(pieces, weights):
     rows, depth = pieces[0].shape
     cols = weights[0].shape[1]
     flops = 2 * rows * 8 * depth * cols
@@ -78,32 +68,29 @@
     return pl.pallas_call(
         project_kernel,
         out_shape=[jax.ShapeDtypeStruct((rows, DH), jnp.bfloat16)] * 4,
-        in_specs=[smem_spec()] + [hbm_spec()] * 12,
+        in_specs=[vmem_spec()] * 12,
         out_specs=[vmem_spec()] * 4,
         scratch_shapes=[
             pltpu.VMEM((8, rows, depth), jnp.bfloat16),
-            pltpu.VMEM((4, 2 * depth, cols), jnp.bfloat16),
             pltpu.VMEM((rows, cols), jnp.float32),
             pltpu.VMEM((4, rows, DH), jnp.bfloat16),
             pltpu.SemaphoreType.DMA((8,)),
-            pltpu.SemaphoreType.DMA((4,)),
         ],
-        compiler_params=pltpu.CompilerParams(vmem_limit_bytes=20 * 2**20),
+        compiler_params=pltpu.CompilerParams(vmem_limit_bytes=24 * 2**20),
         cost_estimate=pl.CostEstimate(flops=flops, bytes_accessed=moved, transcendentals=0),
         name="project",
-    )(place, *pieces, *weights)
-
-
-def attend_kernel(place_ref, edge_ref, bias_ref, *refs):
-    queries, values, outs = refs[:4], refs[4:8], refs[8:12]
-    node = place_ref[0]
+    )(*pieces, *weights)
+
+
+def attend_kernel(bias_ref, *refs):
+    edges, queries, values, outs = refs[:4], refs[4:8], refs[8:12], refs[12:16]
+    node = lax.axis_index("node")
     inv_root = 1.0 / DH**0.5
     rows = queries[0].shape[0]
     tiles = rows // TILE
     for i in range(4):
         for ti in range(tiles):
             mine = queries[i][ti * TILE : (ti + 1) * TILE, :]
-            row_tile = tiles * (node ^ i) + ti
             scores = []
             for j in range(4):
                 raw = lax.dot_general(
@@ -111,8 +98,8 @@
                     preferred_element_type=jnp.float32,
                 )
                 for tj in range(tiles):
-                    relation = edge_ref[row_tile, tiles * (node ^ j) + tj]
-                    part = raw[:, tj * TILE : (tj + 1) * TILE] * inv_root + bias_ref[relation]
+                    relation = edges[i][ti, tiles * (node ^ j) + tj]
+                    part = raw[:, tj * TILE : (tj + 1) * TILE] * inv_root + bias_ref[node, relation]
                     if i == j and ti == tj:
                         row_ids = lax.broadcasted_iota(jnp.int32, (TILE, TILE), 0)
                         col_ids = lax.broadcasted_iota(jnp.int32, (TILE, TILE), 1)
@@ -132,48 +119,44 @@
             outs[i][ti * TILE : (ti + 1) * TILE, :] = (mixed / total).astype(jnp.bfloat16)
 
 
-def attend(place, edges, bias, queries, values):
+def attend(bias, edges, queries, values):
     rows = queries[0].shape[0]
     nodes = 4 * rows
     return pl.pallas_call(
         attend_kernel,
         out_shape=[jax.ShapeDtypeStruct((rows, DH), jnp.bfloat16)] * 4,
-        in_specs=[smem_spec()] * 3 + [vmem_spec()] * 8,
+        in_specs=[smem_spec()] * 5 + [vmem_spec()] * 8,
         out_specs=[vmem_spec()] * 4,
         compiler_params=pltpu.CompilerParams(vmem_limit_bytes=16 * 2**20),
         cost_estimate=pl.CostEstimate(
             flops=4 * nodes * nodes * DH, bytes_accessed=6 * nodes * DH, transcendentals=nodes * nodes
         ),
         name="attend",
-    )(place, edges, bias, *queries, *values)
-
-
-def emit_kernel(place_ref, *refs):
+    )(bias, *edges, *queries, *values)
+
+
+def emit_kernel(*refs):
     parts, weights, outs = refs[:4], refs[4:8], refs[8:16]
-    held, heads, weight_sem = refs[16:]
-    node, head = place_ref[0], place_ref[1]
+    heads, terms = refs[16:]
+    node, head = lax.axis_index("node"), lax.axis_index("head")
     far, near = head // 2, head % 2
-    copies = []
-    for i in range(4):
-        copy = pltpu.make_async_copy(weights[i], held.at[node ^ i], weight_sem.at[i])
-        copy.start()
-        copies.append(copy)
     for i in range(4):
         heads[node ^ i] = parts[i][...]
     attn = jnp.concatenate([heads[i] for i in range(4)], axis=1)
-    for copy in copies:
-        copy.wait()
     width = outs[0].shape[1]
-    for i in (3, 2, 1, 0):
+    for i in range(4):
+        plane = node ^ i ^ far
         for side in range(2):
             start = pl.multiple_of((near ^ side) * width, width)
             term = jnp.dot(
-                attn, held[far ^ i, :, pl.ds(start, width)], preferred_element_type=jnp.float32
+                attn, weights[i][:, pl.ds(start, width)], preferred_element_type=jnp.float32
             )
-            outs[4 * side + i][...] = term.astype(jnp.bfloat16)
-
-
-def emit(place, parts, weights):
+            terms[4 * side + plane] = term.astype(jnp.bfloat16)
+    for i in range(8):
+        outs[i][...] = terms[i]
+
+
+def emit(parts, weights):
     rows = parts[0].shape[0]
     depth, cols = weights[0].shape
     flops = 2 * rows * depth * 4 * cols
@@ -181,56 +164,55 @@
     return pl.pallas_call(
         emit_kernel,
         out_shape=[jax.ShapeDtypeStruct((rows, cols // 2), jnp.bfloat16)] * 8,
-        in_specs=[smem_spec()] + [vmem_spec()] * 4 + [hbm_spec()] * 4,
+        in_specs=[vmem_spec()] * 8,
         out_specs=[vmem_spec()] * 8,
         scratch_shapes=[
-            pltpu.VMEM((4, depth, cols), jnp.bfloat16),
             pltpu.VMEM((4, rows, DH), jnp.bfloat16),
-            pltpu.SemaphoreType.DMA((4,)),
+            pltpu.VMEM((8, rows, cols // 2), jnp.bfloat16),
         ],
-        compiler_params=pltpu.CompilerParams(vmem_limit_bytes=20 * 2**20),
+        compiler_params=pltpu.CompilerParams(vmem_limit_bytes=24 * 2**20),
         cost_estimate=pl.CostEstimate(flops=flops, bytes_accessed=moved, transcendentals=0),
         name="emit",
-    )(place, *parts, *weights)
-
-
-def exchange_heads(pieces):
+    )(*parts, *weights)
+
+
+def exchange(pieces):
     return [pieces[0]] + [swap(pieces[i], "node", i) for i in range(1, 4)]
 
 
 def one_head_each(node_feats, w_qk, w_val, w_out, edge_types, rel_bias):
-    node, head = lax.axis_index("node"), lax.axis_index("head")
-    place = jnp.stack([node, head]).astype(jnp.int32)
-    edges = lax.all_gather(edge_types, "node", axis=0, tiled=True)
-    bias = lax.dynamic_index_in_dim(rel_bias, node, 1, keepdims=False)
-
+    edges = exchange([edge_types] * 4)
     far = {i: swap(node_feats, "head", 2 * i) for i in (3, 2, 1)}
     far[0] = node_feats
-    beside = swap(node_feats, "head", 1)
+    near = {0: swap(after(node_feats, *edges), "head", 1)}
+    for i in (3, 1, 2):
+        near[i] = swap(far[i], "head", 1)
     qk_across, qk_beside = swap(w_qk, "node", 2), swap(w_qk, "node", 1)
-    w_val = after(w_val, qk_across, qk_beside, far[1], far[2], far[3], beside, edges)
+    gate = (far[1], far[2], far[3], near[0], near[1], near[3], qk_beside)
+    qk_across, *gate = lax.optimization_barrier((qk_across, *gate))
+    w_val = after(w_val, qk_across)
     val_across, val_beside = swap(w_val, "node", 2), swap(w_val, "node", 1)
-    qk_sent = after(qk_across, far[1], far[2], far[3], beside)
-    full_qk = [w_qk, qk_beside, qk_across, swap(qk_sent, "node", 1)]
-    pieces = [node_feats, beside]
-    for i in (1, 2, 3):
-        pieces += [far[i], swap(after(far[i], beside), "head", 1)]
-
-    queries = exchange_heads(project(place, pieces, full_qk))
-    w_out = after(w_out, val_across, val_beside, *queries)
+    full_qk = [w_qk, qk_beside, qk_across, swap(qk_across, "node", 1)]
+    pieces = [side[i] for i in range(4) for side in (far, near)]
+
+    queries = exchange(project(pieces, full_qk))
+    val_across = after(val_across, *queries)
+    w_out = after(w_out, val_across, val_beside)
     out_across, out_beside = swap(w_out, "node", 2), swap(w_out, "node", 1)
     full_val = [w_val, val_beside, val_across, swap(val_across, "node", 1)]
-    values = exchange_heads(project(place, pieces, full_val))
+    values = exchange(project(pieces, full_val))
+    attn = attend(rel_bias.T, edges, queries, values)
+    out_across = after(out_across, *attn)
+    attn = exchange(attn)
     full_out = [w_out, out_beside, out_across, swap(out_across, "node", 1)]
-    attn = exchange_heads(attend(place, edges, bias, queries, values))
-    terms = emit(place, attn, full_out)
-    sums = [None] * 4
-    for i in (3, 2, 1, 0):
-        near = swap(terms[4 + i], "head", 1)
-        sums[i] = terms[i].astype(jnp.float32) + near.astype(jnp.float32)
-    total = sums[0]
+    terms = emit(attn, full_out)
+    other = {3: swap(terms[7], "head", 1), 2: swap(terms[6], "head", 1)}
+    other[1] = swap(after(terms[5], other[3]), "head", 1)
+    other[0] = swap(after(terms[4], other[2]), "head", 1)
+    total = terms[0].astype(jnp.float32) + other[0].astype(jnp.float32)
     for i in (3, 2, 1):
-        moved = swap(sums[i].astype(jnp.bfloat16), "head", 2 * i)
+        pair = terms[i].astype(jnp.float32) + other[i].astype(jnp.float32)
+        moved = swap(pair.astype(jnp.bfloat16), "head", 2 * i)
         total = total + moved.astype(jnp.float32)
     return total.astype(jnp.bfloat16)
 

time: 177 us -> 169 us (0.955)
  local copies, waits for them, and re-layouts: 28.3 us -> 2.86 us
  waiting for transfers between devices: 93.9 us -> 118 us
  blocking collectives: 5.06 us -> 0 us
  Pallas kernels: 12.8 us -> 8.06 us
    unnamed x76 -> x12, local copies, waits for them, and re-layouts: 28.3 us -> 2.86 us
    ppermute x32 -> x35, waiting for transfers between devices: 93.9 us -> 118 us  [swap(): return lax.ppermute(value, axis, [(i, i ^ mask) for i in range(peers)])]
    all_gather x1 -> x0, blocking collectives: 5.06 us -> none  [one_head_each(): edges = lax.all_gather(edge_types, 'node', axis=0, tiled=True)]
    pallas_call x2, Pallas kernels: 5.74 us -> 3.04 us  [project(): pl.pallas_call(project_kernel, out_shape=[jax.ShapeDtypeStruct((rows, DH)...]
    pallas_call x1, Pallas kernels: 3.48 us -> 1.41 us  [emit(): pl.pallas_call(emit_kernel, out_shape=[jax.ShapeDtypeStruct((rows, cols /...]
    ppermute x32 -> x35, starting transfers between devices: 34.8 us -> 36.5 us  [swap(): return lax.ppermute(value, axis, [(i, i ^ mask) for i in range(peers)])]
  transfers between devices with their start and end apart: 32 -> 35, of which waited for: 17 -> 17; matrix products, arithmetic and copies ran while one was open for 0% -> 0% of each run, Pallas kernels for 5% -> 4%
where the time goes in v3:
time: 169 us; the launch traced here: 167 us
  waiting for transfers between devices  118 us (70%)
  starting transfers between devices  36.5 us (22%)
  Pallas kernels  8.06 us (5%)
  local copies, waits for them, and re-layouts  2.86 us (2%)
    ppermute x35, waiting for transfers between devices, swap(): return lax.ppermute(value, axis, [(i, i ^ mask) for i in range(peers)])  118 us
    ppermute x35, starting transfers between devices, swap(): return lax.ppermute(value, axis, [(i, i ^ mask) for i in range(peers)])  36.5 us
    pallas_call x1, Pallas kernels, attend(): pl.pallas_call(attend_kernel, out_shape=[jax.ShapeDtypeStruct((rows, DH),...  3.6 us
  transfers between devices with their start and end apart: 35, of which 17 were waited for; matrix products, arithmetic and copies ran while one was open for 0% of the time, Pallas kernels for 4%

profile of v3, /device:TPU:0, one launch (start us, length us, event | category | flops | bytes accessed | tf_op | source)
XLA Modules:
  0.0 166.7 jit_solution(8386894530248521180)
XLA Ops:
  0.0 0.5 collective-permute-start.10
  0.5 2.5 %collective-permute-start.11 = (bf16[1024,512]{1,0:T(8,128)(2,1)}, bf16[1024,512]{1,0:T(8,128)(2,1)S(1)}, u32[]{:S(2)}, u32[]{:S(2)}) collective-permute-start(bf16[1024,512]{1,0:T(8,128)(2,1)} %refs_8_.1), channel_id=1, source_target_pairs={{0,16},{8,24},{16,0},{24,8},{1,17},{9,25},{17,1},{25,9},{2,18},{10... | collective-permute-start | bytes 3145736 | tf_op jit(solution)/shard_map/ppermute | solution.py:19
  3.0 0.2 collective-permute-start
  3.2 0.3 collective-permute-start.1
  3.5 1.8 %collective-permute-start.4 = (bf16[256,512]{1,0:T(8,128)(2,1)}, bf16[256,512]{1,0:T(8,128)(2,1)S(1)}, u32[]{:S(2)}, u32[]{:S(2)}) collective-permute-start(bf16[256,512]{1,0:T(8,128)(2,1)} %refs_0_.4), channel_id=1, source_target_pairs={{0,2},{1,3},{2,0},{3,1},{4,6},{5,7},{6,4},{7,5},{8,10},{9,11},{10,... | collective-permute-start | bytes 786440 | tf_op jit(solution)/shard_map/ppermute | solution.py:19
  5.3 0.9 collective-permute-start.2
  6.2 20.9 %collective-permute-done.1.refs_2_ = s32[2,8]{1,0:T(2,128)S(1)} collective-permute-done((s32[2,8]{1,0:T(2,128)}, s32[2,8]{1,0:T(2,128)S(1)}, u32[]{:S(2)}, u32[]{:S(2)}) %collective-permute-start.1) | collective-permute-done | bytes 96 | tf_op jit(solution)/shard_map/ppermute | solution.py:19
  27.1 2.8 %collective-permute-start.6 = (bf16[256,512]{1,0:T(8,128)(2,1)}, bf16[256,512]{1,0:T(8,128)(2,1)S(1)}, u32[]{:S(2)}, u32[]{:S(2)}) collective-permute-start(bf16[256,512]{1,0:T(8,128)(2,1)} %refs_0_.4), channel_id=1, source_target_pairs={{0,4},{1,5},{2,6},{3,7},{4,0},{5,1},{6,2},{7,3},{8,12},{9,13},{10,... | collective-permute-start | bytes 786440 | tf_op jit(solution)/shard_map/ppermute | solution.py:19
  29.9 1.3 collective-permute-start.8
  31.2 0.0 collective-permute-done.4.refs_2_
  31.3 1.5 collective-permute-start.3
  32.8 15.8 %collective-permute-done.6.refs_4_ = bf16[256,512]{1,0:T(8,128)(2,1)S(1)} collective-permute-done((bf16[256,512]{1,0:T(8,128)(2,1)}, bf16[256,512]{1,0:T(8,128)(2,1)S(1)}, u32[]{:S(2)}, u32[]{:S(2)}) %collective-permute-start.6) | collective-permute-done | bytes 262176 | tf_op jit(solution)/shard_map/ppermute | solution.py:19
  48.6 1.6 collective-permute-start.5
  50.1 0.5 collective-permute-start.9
  50.6 6.8 %collective-permute-done.5.refs_3_ = bf16[256,512]{1,0:T(8,128)(2,1)S(1)} collective-permute-done((bf16[256,512]{1,0:T(8,128)(2,1)S(1)}, bf16[256,512]{1,0:T(8,128)(2,1)S(1)}, u32[]{:S(2)}, u32[]{:S(2)}) %collective-permute-start.5) | collective-permute-done | bytes 262176 | tf_op jit(solution)/shard_map/ppermute | solution.py:19
  57.4 2.8 %collective-permute-done.9.refs_7_ = bf16[256,512]{1,0:T(8,128)(2,1)S(1)} collective-permute-done((bf16[256,512]{1,0:T(8,128)(2,1)S(1)}, bf16[256,512]{1,0:T(8,128)(2,1)S(1)}, u32[]{:S(2)}, u32[]{:S(2)}) %collective-permute-start.9) | collective-permute-done | bytes 262176 | tf_op jit(solution)/shard_map/ppermute | solution.py:19
  60.2 1.6 collective-permute-start.17
  61.8 0.2 collective-permute-start.16
  62.0 1.5 collective-permute-start.7
  63.5 7.0 %collective-permute-done.7.refs_5_ = bf16[256,512]{1,0:T(8,128)(2,1)S(1)} collective-permute-done((bf16[256,512]{1,0:T(8,128)(2,1)S(1)}, bf16[256,512]{1,0:T(8,128)(2,1)S(1)}, u32[]{:S(2)}, u32[]{:S(2)}) %collective-permute-start.7) | collective-permute-done | bytes 262176 | tf_op jit(solution)/shard_map/ppermute | solution.py:19
  70.6 0.9 copy-done.1
  71.5 1.2 copy-done.2
  72.7 1.5 project.2
  74.3 0.1 collective-permute-start.13
  74.3 0.6 collective-permute-start.14
  74.9 1.3 collective-permute-start.15
  76.2 10.3 %collective-permute-done.17.refs_10_ = bf16[1024,512]{1,0:T(8,128)(2,1)S(1)} collective-permute-done((bf16[1024,512]{1,0:T(8,128)(2,1)}, bf16[1024,512]{1,0:T(8,128)(2,1)S(1)}, u32[]{:S(2)}, u32[]{:S(2)}) %collective-permute-start.17) | collective-permute-done | bytes 1048608 | tf_op jit(solution)/shard_map/ppermute | solution.py:19
  86.5 1.4 collective-permute-done.14.refs_6_
  87.9 0.5 collective-permute-done.15.refs_7_
  88.3 0.3 collective-permute-start.18
  88.6 1.5 collective-permute-start.26
  90.2 0.8 collective-permute-done.18.refs_11_
  91.0 1.5 project.3
  92.5 0.0 copy-start.4
  92.5 0.4 collective-permute-start.19
  92.9 1.5 collective-permute-start.20
  94.5 0.0 collective-permute-start.21
  94.5 0.6 collective-permute-start.25
  95.1 21.0 %collective-permute-done.20.refs_10_ = bf16[256,128]{1,0:T(8,128)(2,1)S(1)} collective-permute-done((bf16[256,128]{1,0:T(8,128)(2,1)S(1)}, bf16[256,128]{1,0:T(8,128)(2,1)S(1)}, u32[]{:S(2)}, u32[]{:S(2)}) %collective-permute-start.20) | collective-permute-done | bytes 65568 | tf_op jit(solution)/shard_map/ppermute | solution.py:19
  116.0 0.7 copy-done.5
  116.7 3.6 %attend.1 = (bf16[256,128]{1,0:T(8,128)(2,1)S(1)}, bf16[256,128]{1,0:T(8,128)(2,1)S(1)}, bf16[256,128]{1,0:T(8,128)(2,1)S(1)}, bf16[256,128]{1,0:T(8,128)(2,1)S(1)}) custom-call(f32[4,237]{1,0:T(4,128)S(1)} %bitcast.1, s32[2,8]{1,0:T(2,128)S(1)} %copy-done.5, s32[2,8]{1,0:T(2,128)S(1)} %collective-permute-done.refs_1_, ...), custom_call_target="tpu_custom_call" | custom-call | flops 536870912 | bytes 786432 | tf_op jit(solution)/shard_map/attend/pallas_call | solution.py:125
  120.3 0.6 collective-permute-start.27
  120.9 0.1 collective-permute-start.22
  121.0 1.5 collective-permute-start.23
  122.5 0.3 collective-permute-start.24
  122.8 0.5 collective-permute-done.22.refs_1_
  123.3 2.1 %collective-permute-done.23.refs_2_ = bf16[256,128]{1,0:T(8,128)(2,1)S(1)} collective-permute-done((bf16[256,128]{1,0:T(8,128)(2,1)S(1)}, bf16[256,128]{1,0:T(8,128)(2,1)S(1)}, u32[]{:S(2)}, u32[]{:S(2)}) %collective-permute-start.23) | collective-permute-done | bytes 65568 | tf_op jit(solution)/shard_map/ppermute | solution.py:19
  125.4 1.1 collective-permute-done.24.refs_3_
  126.6 1.4 emit.1
  128.0 1.6 collective-permute-start.30
  129.6 0.5 collective-permute-start.28
  130.1 7.1 %collective-permute-done.30 = bf16[256,512]{1,0:T(8,128)(2,1)S(1)} collective-permute-done((bf16[256,512]{1,0:T(8,128)(2,1)S(1)}, bf16[256,512]{1,0:T(8,128)(2,1)S(1)}, u32[]{:S(2)}, u32[]{:S(2)}) %collective-permute-start.30) | collective-permute-done | bytes 262176 | tf_op jit(solution)/shard_map/ppermute | solution.py:19
  137.2 1.6 collective-permute-start.33
  138.8 4.1 %collective-permute-done.28 = bf16[256,512]{1,0:T(8,128)(2,1)S(1)} collective-permute-done((bf16[256,512]{1,0:T(8,128)(2,1)S(1)}, bf16[256,512]{1,0:T(8,128)(2,1)S(1)}, u32[]{:S(2)}, u32[]{:S(2)}) %collective-permute-start.28) | collective-permute-done | bytes 262176 | tf_op jit(solution)/shard_map/ppermute | solution.py:19
  142.8 0.1 add_convert_fusion.2
  142.9 3.7 %collective-permute-start.32 = (bf16[256,512]{1,0:T(8,128)(2,1)S(1)}, bf16[256,512]{1,0:T(8,128)(2,1)S(1)}, u32[]{:S(2)}, u32[]{:S(2)}) collective-permute-start(bf16[256,512]{1,0:T(8,128)(2,1)S(1)} %add_convert_fusion.2), channel_id=1, source_target_pairs={{0,4},{1,5},{2,6},{3,7},{4,0},{5,1},{6,2},{7,3},{8,12},{9,13},{10,... | collective-permute-start | bytes 786440 | tf_op jit(solution)/shard_map/ppermute | solution.py:19
  146.6 0.1 add_convert_fusion.3
  146.7 1.0 collective-permute-start.31
  147.7 1.6 collective-permute-start.29
  149.2 0.1 add_convert_fusion.1
  149.3 0.7 collective-permute-start.34
  150.0 14.0 %collective-permute-done.32 = bf16[256,512]{1,0:T(8,128)(2,1)S(1)} collective-permute-done((bf16[256,512]{1,0:T(8,128)(2,1)S(1)}, bf16[256,512]{1,0:T(8,128)(2,1)S(1)}, u32[]{:S(2)}, u32[]{:S(2)}) %collective-permute-start.32) | collective-permute-done | bytes 262176 | tf_op jit(solution)/shard_map/ppermute | solution.py:19
  164.0 1.8 %collective-permute-done.34 = bf16[256,512]{1,0:T(8,128)(2,1)S(1)} collective-permute-done((bf16[256,512]{1,0:T(8,128)(2,1)S(1)}, bf16[256,512]{1,0:T(8,128)(2,1)S(1)}, u32[]{:S(2)}, u32[]{:S(2)}) %collective-permute-start.34) | collective-permute-done | bytes 262176 | tf_op jit(solution)/shard_map/ppermute | solution.py:19
  165.8 0.9 add_convert_fusion
  (26 shorter events, 0.1 us)
Async XLA Ops:
  0.0 88.6 %copy-start = (bf16[512,1024]{1,0:T(8,128)(2,1)S(1)}, bf16[512,1024]{1,0:T(8,128)(2,1)}, u32[]{:S(2)}) copy-start(bf16[512,1024]{1,0:T(8,128)(2,1)} %refs_4_) | copy-start | bytes 3145732
  0.0 60.2 %collective-permute-start.10 = (bf16[1024,512]{1,0:T(8,128)(2,1)}, bf16[1024,512]{1,0:T(8,128)(2,1)S(1)}, u32[]{:S(2)}, u32[]{:S(2)}) collective-permute-start(bf16[1024,512]{1,0:T(8,128)(2,1)} %refs_8_.1), channel_id=1, source_target_pairs={{0,8},{8,0},{16,24},{24,16},{1,9},{9,1},{17,25},{25,17},{2,10},{10... | collective-permute-start | bytes 3145736 | tf_op jit(solution)/shard_map/ppermute | solution.py:19
  0.5 59.8 %collective-permute-start.11 = (bf16[1024,512]{1,0:T(8,128)(2,1)}, bf16[1024,512]{1,0:T(8,128)(2,1)S(1)}, u32[]{:S(2)}, u32[]{:S(2)}) collective-permute-start(bf16[1024,512]{1,0:T(8,128)(2,1)} %refs_8_.1), channel_id=1, source_target_pairs={{0,16},{8,24},{16,0},{24,8},{1,17},{9,25},{17,1},{25,9},{2,18},{10... | collective-permute-start | bytes 3145736 | tf_op jit(solution)/shard_map/ppermute | solution.py:19
  3.0 2.3 %collective-permute-start = (s32[2,8]{1,0:T(2,128)}, s32[2,8]{1,0:T(2,128)S(1)}, u32[]{:S(2)}, u32[]{:S(2)}) collective-permute-start(s32[2,8]{1,0:T(2,128)} %refs_0_.5), channel_id=1, source_target_pairs={{0,8},{8,0},{16,24},{24,16},{1,9},{9,1},{17,25},{25,17},{2,10},{10... | collective-permute-start | bytes 200 | tf_op jit(solution)/shard_map/ppermute | solution.py:19
  3.2 23.9 %collective-permute-start.1 = (s32[2,8]{1,0:T(2,128)}, s32[2,8]{1,0:T(2,128)S(1)}, u32[]{:S(2)}, u32[]{:S(2)}) collective-permute-start(s32[2,8]{1,0:T(2,128)} %refs_0_.5), channel_id=1, source_target_pairs={{0,16},{8,24},{16,0},{24,8},{1,17},{9,25},{17,1},{25,9},{2,18},{10... | collective-permute-start | bytes 200 | tf_op jit(solution)/shard_map/ppermute | solution.py:19
  3.5 27.8 %collective-permute-start.4 = (bf16[256,512]{1,0:T(8,128)(2,1)}, bf16[256,512]{1,0:T(8,128)(2,1)S(1)}, u32[]{:S(2)}, u32[]{:S(2)}) collective-permute-start(bf16[256,512]{1,0:T(8,128)(2,1)} %refs_0_.4), channel_id=1, source_target_pairs={{0,2},{1,3},{2,0},{3,1},{4,6},{5,7},{6,4},{7,5},{8,10},{9,11},{10,... | collective-permute-start | bytes 786440 | tf_op jit(solution)/shard_map/ppermute | solution.py:19
  5.3 24.6 %collective-permute-start.2 = (s32[2,8]{1,0:T(2,128)}, s32[2,8]{1,0:T(2,128)S(1)}, u32[]{:S(2)}, u32[]{:S(2)}) collective-permute-start(s32[2,8]{1,0:T(2,128)} %refs_0_.5), channel_id=1, source_target_pairs={{0,24},{8,16},{16,8},{24,0},{1,25},{9,17},{17,9},{25,1},{2,26},{10... | collective-permute-start | bytes 200 | tf_op jit(solution)/shard_map/ppermute | solution.py:19
  27.1 21.5 %collective-permute-start.6 = (bf16[256,512]{1,0:T(8,128)(2,1)}, bf16[256,512]{1,0:T(8,128)(2,1)S(1)}, u32[]{:S(2)}, u32[]{:S(2)}) collective-permute-start(bf16[256,512]{1,0:T(8,128)(2,1)} %refs_0_.4), channel_id=1, source_target_pairs={{0,4},{1,5},{2,6},{3,7},{4,0},{5,1},{6,2},{7,3},{8,12},{9,13},{10,... | collective-permute-start | bytes 786440 | tf_op jit(solution)/shard_map/ppermute | solution.py:19
  29.9 20.3 %collective-permute-start.8 = (bf16[256,512]{1,0:T(8,128)(2,1)}, bf16[256,512]{1,0:T(8,128)(2,1)S(1)}, u32[]{:S(2)}, u32[]{:S(2)}) collective-permute-start(bf16[256,512]{1,0:T(8,128)(2,1)} %refs_0_.4), channel_id=1, source_target_pairs={{0,6},{1,7},{2,4},{3,5},{4,2},{5,3},{6,0},{7,1},{8,14},{9,15},{10,... | collective-permute-start | bytes 786440 | tf_op jit(solution)/shard_map/ppermute | solution.py:19
  31.3 19.4 %collective-permute-start.3 = (bf16[256,512]{1,0:T(8,128)(2,1)}, bf16[256,512]{1,0:T(8,128)(2,1)S(1)}, u32[]{:S(2)}, u32[]{:S(2)}) collective-permute-start(bf16[256,512]{1,0:T(8,128)(2,1)} %refs_0_.4), channel_id=1, source_target_pairs={{0,1},{1,0},{2,3},{3,2},{4,5},{5,4},{6,7},{7,6},{8,9},{9,8},{10,11... | collective-permute-start | bytes 786440 | tf_op jit(solution)/shard_map/ppermute | solution.py:19
  48.6 8.8 %collective-permute-start.5 = (bf16[256,512]{1,0:T(8,128)(2,1)S(1)}, bf16[256,512]{1,0:T(8,128)(2,1)S(1)}, u32[]{:S(2)}, u32[]{:S(2)}) collective-permute-start(bf16[256,512]{1,0:T(8,128)(2,1)S(1)} %collective-permute-done.4.refs_2_), channel_id=1, source_target_pairs={{0,1},{1,0},{2,3},{3,2},{4,5},{5,4},{6,7},{7,6},{8,9},{9,8},{10,11... | collective-permute-start | bytes 786440 | tf_op jit(solution)/shard_map/ppermute | solution.py:19
  50.1 10.1 %collective-permute-start.9 = (bf16[256,512]{1,0:T(8,128)(2,1)S(1)}, bf16[256,512]{1,0:T(8,128)(2,1)S(1)}, u32[]{:S(2)}, u32[]{:S(2)}) collective-permute-start(bf16[256,512]{1,0:T(8,128)(2,1)S(1)} %collective-permute-done.8.refs_6_), channel_id=1, source_target_pairs={{0,1},{1,0},{2,3},{3,2},{4,5},{5,4},{6,7},{7,6},{8,9},{9,8},{10,11... | collective-permute-start | bytes 786440 | tf_op jit(solution)/shard_map/ppermute | solution.py:19
  60.2 10.3 %collective-permute-start.12 = (bf16[1024,512]{1,0:T(8,128)(2,1)S(1)}, bf16[1024,512]{1,0:T(8,128)(2,1)S(1)}, u32[]{:S(2)}, u32[]{:S(2)}) collective-permute-start(bf16[1024,512]{1,0:T(8,128)(2,1)S(1)} %collective-permute-done.11.refs_10_), channel_id=1, source_target_pairs={{0,8},{8,0},{16,24},{24,16},{1,9},{9,1},{17,25},{25,17},{2,10},{10... | collective-permute-start | bytes 3145736 | tf_op jit(solution)/shard_map/ppermute | solution.py:19
  60.2 26.2 %collective-permute-start.17 = (bf16[1024,512]{1,0:T(8,128)(2,1)}, bf16[1024,512]{1,0:T(8,128)(2,1)S(1)}, u32[]{:S(2)}, u32[]{:S(2)}) collective-permute-start(bf16[1024,512]{1,0:T(8,128)(2,1)} %refs_8_.2), channel_id=1, source_target_pairs={{0,16},{8,24},{16,0},{24,8},{1,17},{9,25},{17,1},{25,9},{2,18},{10... | collective-permute-start | bytes 3145736 | tf_op jit(solution)/shard_map/ppermute | solution.py:19
  61.8 26.8 %collective-permute-start.16 = (bf16[1024,512]{1,0:T(8,128)(2,1)}, bf16[1024,512]{1,0:T(8,128)(2,1)S(1)}, u32[]{:S(2)}, u32[]{:S(2)}) collective-permute-start(bf16[1024,512]{1,0:T(8,128)(2,1)} %refs_8_.2), channel_id=1, source_target_pairs={{0,8},{8,0},{16,24},{24,16},{1,9},{9,1},{17,25},{25,17},{2,10},{10... | collective-permute-start | bytes 3145736 | tf_op jit(solution)/shard_map/ppermute | solution.py:19
  62.0 8.6 %collective-permute-start.7 = (bf16[256,512]{1,0:T(8,128)(2,1)S(1)}, bf16[256,512]{1,0:T(8,128)(2,1)S(1)}, u32[]{:S(2)}, u32[]{:S(2)}) collective-permute-start(bf16[256,512]{1,0:T(8,128)(2,1)S(1)} %collective-permute-done.6.refs_4_), channel_id=1, source_target_pairs={{0,1},{1,0},{2,3},{3,2},{4,5},{5,4},{6,7},{7,6},{8,9},{9,8},{10,11... | collective-permute-start | bytes 786440 | tf_op jit(solution)/shard_map/ppermute | solution.py:19
  70.5 1.0 copy-start.1
  71.5 1.2 copy-start.2
  72.7 18.3 %copy-start.3 = (bf16[1024,512]{1,0:T(8,128)(2,1)S(1)}, bf16[1024,512]{1,0:T(8,128)(2,1)}, u32[]{:S(2)}) copy-start(bf16[1024,512]{1,0:T(8,128)(2,1)} %refs_8_.2) | copy-start | bytes 3145732
  74.3 12.2 %collective-permute-start.13 = (bf16[256,128]{1,0:T(8,128)(2,1)S(1)}, bf16[256,128]{1,0:T(8,128)(2,1)S(1)}, u32[]{:S(2)}, u32[]{:S(2)}) collective-permute-start(bf16[256,128]{1,0:T(8,128)(2,1)S(1)} %get-tuple-element.36), channel_id=1, source_target_pairs={{0,8},{8,0},{16,24},{24,16},{1,9},{9,1},{17,25},{25,17},{2,10},{10... | collective-permute-start | bytes 196616 | tf_op jit(solution)/shard_map/ppermute | solution.py:19
  74.3 13.5 %collective-permute-start.14 = (bf16[256,128]{1,0:T(8,128)(2,1)S(1)}, bf16[256,128]{1,0:T(8,128)(2,1)S(1)}, u32[]{:S(2)}, u32[]{:S(2)}) collective-permute-start(bf16[256,128]{1,0:T(8,128)(2,1)S(1)} %get-tuple-element.37), channel_id=1, source_target_pairs={{0,16},{8,24},{16,0},{24,8},{1,17},{9,25},{17,1},{25,9},{2,18},{10... | collective-permute-start | bytes 196616 | tf_op jit(solution)/shard_map/ppermute | solution.py:19
  74.9 13.4 %collective-permute-start.15 = (bf16[256,128]{1,0:T(8,128)(2,1)S(1)}, bf16[256,128]{1,0:T(8,128)(2,1)S(1)}, u32[]{:S(2)}, u32[]{:S(2)}) collective-permute-start(bf16[256,128]{1,0:T(8,128)(2,1)S(1)} %get-tuple-element.38), channel_id=1, source_target_pairs={{0,24},{8,16},{16,8},{24,0},{1,25},{9,17},{17,9},{25,1},{2,26},{10... | collective-permute-start | bytes 196616 | tf_op jit(solution)/shard_map/ppermute | solution.py:19
  88.3 2.7 %collective-permute-start.18 = (bf16[1024,512]{1,0:T(8,128)(2,1)S(1)}, bf16[1024,512]{1,0:T(8,128)(2,1)S(1)}, u32[]{:S(2)}, u32[]{:S(2)}) collective-permute-start(bf16[1024,512]{1,0:T(8,128)(2,1)S(1)} %collective-permute-done.17.refs_10_), channel_id=1, source_target_pairs={{0,8},{8,0},{16,24},{24,16},{1,9},{9,1},{17,25},{25,17},{2,10},{10... | collective-permute-start | bytes 3145736 | tf_op jit(solution)/shard_map/ppermute | solution.py:19
  88.6 31.7 %collective-permute-start.26 = (bf16[512,1024]{1,0:T(8,128)(2,1)S(1)}, bf16[512,1024]{1,0:T(8,128)(2,1)S(1)}, u32[]{:S(2)}, u32[]{:S(2)}) collective-permute-start(bf16[512,1024]{1,0:T(8,128)(2,1)S(1)} %copy-done), channel_id=1, source_target_pairs={{0,16},{8,24},{16,0},{24,8},{1,17},{9,25},{17,1},{25,9},{2,18},{10... | collective-permute-start | bytes 3145736 | tf_op jit(solution)/shard_map/ppermute | solution.py:19
  92.5 23.5 %copy-start.4 = (f32[237,4]{0,1:T(4,128)S(1)}, f32[237,4]{0,1:T(4,128)}, u32[]{:S(2)}) copy-start(f32[237,4]{0,1:T(4,128)} %param.11) | copy-start | bytes 11380
  92.5 2.5 %collective-permute-start.19 = (bf16[256,128]{1,0:T(8,128)(2,1)S(1)}, bf16[256,128]{1,0:T(8,128)(2,1)S(1)}, u32[]{:S(2)}, u32[]{:S(2)}) collective-permute-start(bf16[256,128]{1,0:T(8,128)(2,1)S(1)} %get-tuple-element.42), channel_id=1, source_target_pairs={{0,8},{8,0},{16,24},{24,16},{1,9},{9,1},{17,25},{25,17},{2,10},{10... | collective-permute-start | bytes 196616 | tf_op jit(solution)/shard_map/ppermute | solution.py:19
  92.9 23.1 %collective-permute-start.20 = (bf16[256,128]{1,0:T(8,128)(2,1)S(1)}, bf16[256,128]{1,0:T(8,128)(2,1)S(1)}, u32[]{:S(2)}, u32[]{:S(2)}) collective-permute-start(bf16[256,128]{1,0:T(8,128)(2,1)S(1)} %get-tuple-element.43), channel_id=1, source_target_pairs={{0,16},{8,24},{16,0},{24,8},{1,17},{9,25},{17,1},{25,9},{2,18},{10... | collective-permute-start | bytes 196616 | tf_op jit(solution)/shard_map/ppermute | solution.py:19
  94.5 21.6 %collective-permute-start.21 = (bf16[256,128]{1,0:T(8,128)(2,1)S(1)}, bf16[256,128]{1,0:T(8,128)(2,1)S(1)}, u32[]{:S(2)}, u32[]{:S(2)}) collective-permute-start(bf16[256,128]{1,0:T(8,128)(2,1)S(1)} %get-tuple-element.44), channel_id=1, source_target_pairs={{0,24},{8,16},{16,8},{24,0},{1,25},{9,17},{17,9},{25,1},{2,26},{10... | collective-permute-start | bytes 196616 | tf_op jit(solution)/shard_map/ppermute | solution.py:19
  94.5 28.3 %collective-permute-start.25 = (bf16[512,1024]{1,0:T(8,128)(2,1)S(1)}, bf16[512,1024]{1,0:T(8,128)(2,1)S(1)}, u32[]{:S(2)}, u32[]{:S(2)}) collective-permute-start(bf16[512,1024]{1,0:T(8,128)(2,1)S(1)} %copy-done), channel_id=1, source_target_pairs={{0,8},{8,0},{16,24},{24,16},{1,9},{9,1},{17,25},{25,17},{2,10},{10... | collective-permute-start | bytes 3145736 | tf_op jit(solution)/shard_map/ppermute | solution.py:19
  116.0 0.7 copy-start.5
  120.3 6.3 %collective-permute-start.27 = (bf16[512,1024]{1,0:T(8,128)(2,1)S(1)}, bf16[512,1024]{1,0:T(8,128)(2,1)S(1)}, u32[]{:S(2)}, u32[]{:S(2)}) collective-permute-start(bf16[512,1024]{1,0:T(8,128)(2,1)S(1)} %collective-permute-done.26.refs_6_), channel_id=1, source_target_pairs={{0,8},{8,0},{16,24},{24,16},{1,9},{9,1},{17,25},{25,17},{2,10},{10... | collective-permute-start | bytes 3145736 | tf_op jit(solution)/shard_map/ppermute | solution.py:19
  120.9 2.4 %collective-permute-start.22 = (bf16[256,128]{1,0:T(8,128)(2,1)S(1)}, bf16[256,128]{1,0:T(8,128)(2,1)S(1)}, u32[]{:S(2)}, u32[]{:S(2)}) collective-permute-start(bf16[256,128]{1,0:T(8,128)(2,1)S(1)} %get-tuple-element.46), channel_id=1, source_target_pairs={{0,8},{8,0},{16,24},{24,16},{1,9},{9,1},{17,25},{25,17},{2,10},{10... | collective-permute-start | bytes 196616 | tf_op jit(solution)/shard_map/ppermute | solution.py:19
  121.0 4.4 %collective-permute-start.23 = (bf16[256,128]{1,0:T(8,128)(2,1)S(1)}, bf16[256,128]{1,0:T(8,128)(2,1)S(1)}, u32[]{:S(2)}, u32[]{:S(2)}) collective-permute-start(bf16[256,128]{1,0:T(8,128)(2,1)S(1)} %get-tuple-element.47), channel_id=1, source_target_pairs={{0,16},{8,24},{16,0},{24,8},{1,17},{9,25},{17,1},{25,9},{2,18},{10... | collective-permute-start | bytes 196616 | tf_op jit(solution)/shard_map/ppermute | solution.py:19
  122.5 4.0 %collective-permute-start.24 = (bf16[256,128]{1,0:T(8,128)(2,1)S(1)}, bf16[256,128]{1,0:T(8,128)(2,1)S(1)}, u32[]{:S(2)}, u32[]{:S(2)}) collective-permute-start(bf16[256,128]{1,0:T(8,128)(2,1)S(1)} %get-tuple-element.48), channel_id=1, source_target_pairs={{0,24},{8,16},{16,8},{24,0},{1,25},{9,17},{17,9},{25,1},{2,26},{10... | collective-permute-start | bytes 196616 | tf_op jit(solution)/shard_map/ppermute | solution.py:19
  128.0 9.2 %collective-permute-start.30 = (bf16[256,512]{1,0:T(8,128)(2,1)S(1)}, bf16[256,512]{1,0:T(8,128)(2,1)S(1)}, u32[]{:S(2)}, u32[]{:S(2)}) collective-permute-start(bf16[256,512]{1,0:T(8,128)(2,1)S(1)} %get-tuple-element.56), channel_id=1, source_target_pairs={{0,1},{1,0},{2,3},{3,2},{4,5},{5,4},{6,7},{7,6},{8,9},{9,8},{10,11... | collective-permute-start | bytes 786440 | tf_op jit(solution)/shard_map/ppermute | solution.py:19
  129.6 13.2 %collective-permute-start.28 = (bf16[256,512]{1,0:T(8,128)(2,1)S(1)}, bf16[256,512]{1,0:T(8,128)(2,1)S(1)}, u32[]{:S(2)}, u32[]{:S(2)}) collective-permute-start(bf16[256,512]{1,0:T(8,128)(2,1)S(1)} %get-tuple-element.53), channel_id=1, source_target_pairs={{0,1},{1,0},{2,3},{3,2},{4,5},{5,4},{6,7},{7,6},{8,9},{9,8},{10,11... | collective-permute-start | bytes 786440 | tf_op jit(solution)/shard_map/ppermute | solution.py:19
  137.2 12.0 %collective-permute-start.33 = (bf16[256,512]{1,0:T(8,128)(2,1)S(1)}, bf16[256,512]{1,0:T(8,128)(2,1)S(1)}, u32[]{:S(2)}, u32[]{:S(2)}) collective-permute-start(bf16[256,512]{1,0:T(8,128)(2,1)S(1)} %get-tuple-element.60), channel_id=1, source_target_pairs={{0,1},{1,0},{2,3},{3,2},{4,5},{5,4},{6,7},{7,6},{8,9},{9,8},{10,11... | collective-permute-start | bytes 786440 | tf_op jit(solution)/shard_map/ppermute | solution.py:19
  142.9 21.1 %collective-permute-start.32 = (bf16[256,512]{1,0:T(8,128)(2,1)S(1)}, bf16[256,512]{1,0:T(8,128)(2,1)S(1)}, u32[]{:S(2)}, u32[]{:S(2)}) collective-permute-start(bf16[256,512]{1,0:T(8,128)(2,1)S(1)} %add_convert_fusion.2), channel_id=1, source_target_pairs={{0,4},{1,5},{2,6},{3,7},{4,0},{5,1},{6,2},{7,3},{8,12},{9,13},{10,... | collective-permute-start | bytes 786440 | tf_op jit(solution)/shard_map/ppermute | solution.py:19
  146.7 17.3 %collective-permute-start.31 = (bf16[256,512]{1,0:T(8,128)(2,1)S(1)}, bf16[256,512]{1,0:T(8,128)(2,1)S(1)}, u32[]{:S(2)}, u32[]{:S(2)}) collective-permute-start(bf16[256,512]{1,0:T(8,128)(2,1)S(1)} %add_convert_fusion.3), channel_id=1, source_target_pairs={{0,6},{1,7},{2,4},{3,5},{4,2},{5,3},{6,0},{7,1},{8,14},{9,15},{10,... | collective-permute-start | bytes 786440 | tf_op jit(solution)/shard_map/ppermute | solution.py:19
  147.7 16.3 %collective-permute-start.29 = (bf16[256,512]{1,0:T(8,128)(2,1)S(1)}, bf16[256,512]{1,0:T(8,128)(2,1)S(1)}, u32[]{:S(2)}, u32[]{:S(2)}) collective-permute-start(bf16[256,512]{1,0:T(8,128)(2,1)S(1)} %get-tuple-element.54), channel_id=1, source_target_pairs={{0,1},{1,0},{2,3},{3,2},{4,5},{5,4},{6,7},{7,6},{8,9},{9,8},{10,11... | collective-permute-start | bytes 786440 | tf_op jit(solution)/shard_map/ppermute | solution.py:19
  149.3 16.5 %collective-permute-start.34 = (bf16[256,512]{1,0:T(8,128)(2,1)S(1)}, bf16[256,512]{1,0:T(8,128)(2,1)S(1)}, u32[]{:S(2)}, u32[]{:S(2)}) collective-permute-start(bf16[256,512]{1,0:T(8,128)(2,1)S(1)} %add_convert_fusion.1), channel_id=1, source_target_pairs={{0,2},{1,3},{2,0},{3,1},{4,6},{5,7},{6,4},{7,5},{8,10},{9,11},{10,... | collective-permute-start | bytes 786440 | tf_op jit(solution)/shard_map/ppermute | solution.py:19

commit v4 on v3

--- a/solution.py
+++ b/solution.py
@@ -31,70 +31,141 @@
     return pl.BlockSpec(memory_space=pltpu.SMEM)
 
 
+def in_line(node, head):
+    return node // 2 == head // 4
+
+
+def sort_kernel(close_ref, distant_ref, send_ref, keep_ref):
+    lined = in_line(lax.axis_index("node"), lax.axis_index("head"))
+
+    @pl.when(lined)
+    def _():
+        send_ref[...] = distant_ref[...]
+        keep_ref[...] = close_ref[...]
+
+    @pl.when(jnp.logical_not(lined))
+    def _():
+        send_ref[...] = close_ref[...]
+        keep_ref[...] = distant_ref[...]
+
+
+def sort(close, distant):
+    shape = jax.ShapeDtypeStruct(close.shape, close.dtype)
+    return pl.pallas_call(
+        sort_kernel,
+        out_shape=[shape, shape],
+        in_specs=[vmem_spec()] * 2,
+        out_specs=[vmem_spec()] * 2,
+        compiler_params=pltpu.CompilerParams(vmem_limit_bytes=8 * 2**20),
+        cost_estimate=pl.CostEstimate(flops=0, bytes_accessed=8 * close.size, transcendentals=0),
+        name="sort",
+    )(close, distant)
+
+
 def project_kernel(*refs):
-    pieces, weights, outs = refs[:8], refs[8:12], refs[12:16]
-    feats, total, heads, piece_sem = refs[16:]
+    pieces, weights, keep_ref, send_ref = refs[:8], refs[8:10], refs[10], refs[11]
+    feats, total, piece_sem = refs[12:]
     node, head = lax.axis_index("node"), lax.axis_index("head")
+    side, core = node // 2, node % 2
+    slot = (head // 2) % 2 ^ jnp.where(in_line(node, head), 0, 1)
+    near = head % 2
     copies = []
     for i in range(8):
-        copy = pltpu.make_async_copy(pieces[i], feats.at[head ^ i], piece_sem.at[i])
+        block, plane, other = i // 4, (i // 2) % 2, i % 2
+        place = 4 * block + 2 * (slot ^ plane) + (near ^ other)
+        copy = pltpu.make_async_copy(pieces[i], feats.at[place], piece_sem.at[i])
         copy.start()
         copies.append(copy)
     for copy in copies:
         copy.wait()
-    depth = feats.shape[2]
-    for i in range(4):
-        for part in range(2):
-            term = jnp.dot(
-                feats[2 * (node ^ i) + part],
-                weights[i][part * depth : (part + 1) * depth, :],
-                preferred_element_type=jnp.float32,
-            )
-            if i == 0 and part == 0:
-                total[...] = term
-            else:
-                total[...] += term
-    for i in range(4):
-        heads[i] = total[:, i * DH : (i + 1) * DH].astype(jnp.bfloat16)
-    for i in range(4):
-        outs[i][...] = heads[node ^ i]
+    _, rows, depth = feats.shape
+    width = keep_ref.shape[1]
+    for block in range(2):
+        for i in range(2):
+            for part in range(2):
+                term = jnp.dot(
+                    feats[4 * block + 2 * (core ^ i) + part],
+                    weights[i][part * depth : (part + 1) * depth, :],
+                    preferred_element_type=jnp.float32,
+                )
+                if i == 0 and part == 0:
+                    total[...] = term
+                else:
+                    total[...] += term
+        mine = pl.ds(pl.multiple_of(side * width, width), width)
+        theirs = pl.ds(pl.multiple_of((1 - side) * width, width), width)
+        keep_ref[block * rows : (block + 1) * rows, :] = total[:, mine]
+        send_ref[block * rows : (block + 1) * rows, :] = total[:, theirs].astype(jnp.bfloat16)
 
 
 def project(pieces, weights):
     rows, depth = pieces[0].shape
     cols = weights[0].shape[1]
-    flops = 2 * rows * 8 * depth * cols
-    moved = 2 * (8 * rows * depth + 8 * depth * cols + rows * cols)
+    flops = 2 * 2 * rows * 4 * depth * cols
+    moved = 2 * (8 * rows * depth + 4 * depth * cols + 3 * rows * cols)
     return pl.pallas_call(
         project_kernel,
-        out_shape=[jax.ShapeDtypeStruct((rows, DH), jnp.bfloat16)] * 4,
-        in_specs=[vmem_spec()] * 12,
-        out_specs=[vmem_spec()] * 4,
+        out_shape=[
+            jax.ShapeDtypeStruct((2 * rows, cols // 2), jnp.float32),
+            jax.ShapeDtypeStruct((2 * rows, cols // 2), jnp.bfloat16),
+        ],
+        in_specs=[vmem_spec()] * 10,
+        out_specs=[vmem_spec()] * 2,
         scratch_shapes=[
             pltpu.VMEM((8, rows, depth), jnp.bfloat16),
             pltpu.VMEM((rows, cols), jnp.float32),
-            pltpu.VMEM((4, rows, DH), jnp.bfloat16),
             pltpu.SemaphoreType.DMA((8,)),
         ],
-        compiler_params=pltpu.CompilerParams(vmem_limit_bytes=24 * 2**20),
+        compiler_params=pltpu.CompilerParams(vmem_limit_bytes=20 * 2**20),
         cost_estimate=pl.CostEstimate(flops=flops, bytes_accessed=moved, transcendentals=0),
         name="project",
     )(*pieces, *weights)
 
 
+def combine_kernel(keep_ref, moved_ref, mine_ref, give_ref):
+    core = lax.axis_index("node") % 2
+    rows = keep_ref.shape[0] // 2
+    for out_ref, place in ((mine_ref, core), (give_ref, 1 - core)):
+        cols = pl.ds(pl.multiple_of(place * DH, DH), DH)
+        for block in range(2):
+            here = slice(block * rows, (block + 1) * rows)
+            there = slice((1 - block) * rows, (2 - block) * rows)
+            both = keep_ref[here, cols] + moved_ref[there, cols].astype(jnp.float32)
+            out_ref[here, :] = both.astype(jnp.bfloat16)
+
+
+def combine(keep, moved):
+    shape = jax.ShapeDtypeStruct((keep.shape[0], DH), jnp.bfloat16)
+    return pl.pallas_call(
+        combine_kernel,
+        out_shape=[shape, shape],
+        in_specs=[vmem_spec()] * 2,
+        out_specs=[vmem_spec()] * 2,
+        compiler_params=pltpu.CompilerParams(vmem_limit_bytes=8 * 2**20),
+        cost_estimate=pl.CostEstimate(flops=keep.size, bytes_accessed=8 * keep.size, transcendentals=0),
+        name="combine",
+    )(keep, moved)
+
+
 def attend_kernel(bias_ref, *refs):
-    edges, queries, values, outs = refs[:4], refs[4:8], refs[8:12], refs[12:16]
+    edges, held, outs = refs[:4], refs[4:8], refs[8:12]
     node = lax.axis_index("node")
     inv_root = 1.0 / DH**0.5
-    rows = queries[0].shape[0]
+    rows = outs[0].shape[0]
     tiles = rows // TILE
+
+    def block_of(pair, i):
+        return pair[i % 2], (i // 2) * rows
+
     for i in range(4):
         for ti in range(tiles):
-            mine = queries[i][ti * TILE : (ti + 1) * TILE, :]
+            ref, base = block_of(held[:2], i)
+            mine = ref[base + ti * TILE : base + (ti + 1) * TILE, :]
             scores = []
             for j in range(4):
+                ref, base = block_of(held[:2], j)
                 raw = lax.dot_general(
-                    mine, queries[j][...], (((1,), (1,)), ((), ())),
+                    mine, ref[base : base + rows, :], (((1,), (1,)), ((), ())),
                     preferred_element_type=jnp.float32,
                 )
                 for tj in range(tiles):
@@ -114,18 +185,19 @@
                 block = jnp.concatenate(
                     [part.astype(jnp.bfloat16) for part in expd[tiles * j : tiles * (j + 1)]], axis=1
                 )
-                term = jnp.dot(block, values[j][...], preferred_element_type=jnp.float32)
+                ref, base = block_of(held[2:], j)
+                term = jnp.dot(block, ref[base : base + rows, :], preferred_element_type=jnp.float32)
                 mixed = term if mixed is None else mixed + term
             outs[i][ti * TILE : (ti + 1) * TILE, :] = (mixed / total).astype(jnp.bfloat16)
 
 
 def attend(bias, edges, queries, values):
-    rows = queries[0].shape[0]
+    rows = queries[0].shape[0] // 2
     nodes = 4 * rows
     return pl.pallas_call(
         attend_kernel,
         out_shape=[jax.ShapeDtypeStruct((rows, DH), jnp.bfloat16)] * 4,
-        in_specs=[smem_spec()] * 5 + [vmem_spec()] * 8,
+        in_specs=[smem_spec()] * 5 + [vmem_spec()] * 4,
         out_specs=[vmem_spec()] * 4,
         compiler_params=pltpu.CompilerParams(vmem_limit_bytes=16 * 2**20),
         cost_estimate=pl.CostEstimate(
@@ -135,9 +207,13 @@
     )(bias, *edges, *queries, *values)
 
 
-def emit_kernel(*refs):
-    parts, weights, outs = refs[:4], refs[4:8], refs[8:16]
-    heads, terms = refs[16:]
+def emit_kernel(counts, *refs):
+    parts, refs = refs[:4], refs[4:]
+    weights = []
+    for count in counts:
+        weights.append(refs[:count])
+        refs = refs[count:]
+    outs, heads, terms = refs[:8], refs[8], refs[9]
     node, head = lax.axis_index("node"), lax.axis_index("head")
     far, near = head // 2, head % 2
     for i in range(4):
@@ -148,72 +224,88 @@
         plane = node ^ i ^ far
         for side in range(2):
             start = pl.multiple_of((near ^ side) * width, width)
-            term = jnp.dot(
-                attn, weights[i][:, pl.ds(start, width)], preferred_element_type=jnp.float32
-            )
-            terms[4 * side + plane] = term.astype(jnp.bfloat16)
+            total, first = None, 0
+            for ref in weights[i]:
+                last = first + ref.shape[0]
+                term = jnp.dot(
+                    attn[:, first:last], ref[:, pl.ds(start, width)],
+                    preferred_element_type=jnp.float32,
+                )
+                total, first = term if total is None else total + term, last
+            terms[4 * side + plane] = total.astype(jnp.bfloat16)
     for i in range(8):
         outs[i][...] = terms[i]
 
 
 def emit(parts, weights):
     rows = parts[0].shape[0]
-    depth, cols = weights[0].shape
+    depth, cols = weights[0][0].shape
+    counts = [len(pieces) for pieces in weights]
     flops = 2 * rows * depth * 4 * cols
     moved = 2 * (rows * depth + 4 * depth * cols + 4 * rows * cols)
     return pl.pallas_call(
-        emit_kernel,
+        functools.partial(emit_kernel, counts),
         out_shape=[jax.ShapeDtypeStruct((rows, cols // 2), jnp.bfloat16)] * 8,
-        in_specs=[vmem_spec()] * 8,
+        in_specs=[vmem_spec()] * (4 + sum(counts)),
         out_specs=[vmem_spec()] * 8,
         scratch_shapes=[
             pltpu.VMEM((4, rows, DH), jnp.bfloat16),
             pltpu.VMEM((8, rows, cols // 2), jnp.bfloat16),
         ],
-        compiler_params=pltpu.CompilerParams(vmem_limit_bytes=24 * 2**20),
+        compiler_params=pltpu.CompilerParams(vmem_limit_bytes=20 * 2**20),
         cost_estimate=pl.CostEstimate(flops=flops, bytes_accessed=moved, transcendentals=0),
         name="emit",
-    )(*parts, *weights)
-
-
-def exchange(pieces):
-    return [pieces[0]] + [swap(pieces[i], "node", i) for i in range(1, 4)]
+    )(*parts, *[piece for pieces in weights for piece in pieces])
 
 
 def one_head_each(node_feats, w_qk, w_val, w_out, edge_types, rel_bias):
-    edges = exchange([edge_types] * 4)
+    depth = w_out.shape[0]
+    across = functools.partial(swap, axis="node", mask=2)
+    beside = functools.partial(swap, axis="node", mask=1)
+    along = functools.partial(swap, axis="head", mask=1)
+
+    edges = [edge_types] + [swap(edge_types, "node", i) for i in range(1, 4)]
     far = {i: swap(node_feats, "head", 2 * i) for i in (3, 2, 1)}
-    far[0] = node_feats
-    near = {0: swap(after(node_feats, *edges), "head", 1)}
-    for i in (3, 1, 2):
-        near[i] = swap(far[i], "head", 1)
-    qk_across, qk_beside = swap(w_qk, "node", 2), swap(w_qk, "node", 1)
-    gate = (far[1], far[2], far[3], near[0], near[1], near[3], qk_beside)
-    qk_across, *gate = lax.optimization_barrier((qk_across, *gate))
-    w_val = after(w_val, qk_across)
-    val_across, val_beside = swap(w_val, "node", 2), swap(w_val, "node", 1)
-    full_qk = [w_qk, qk_beside, qk_across, swap(qk_across, "node", 1)]
-    pieces = [side[i] for i in range(4) for side in (far, near)]
-
-    queries = exchange(project(pieces, full_qk))
-    val_across = after(val_across, *queries)
-    w_out = after(w_out, val_across, val_beside)
-    out_across, out_beside = swap(w_out, "node", 2), swap(w_out, "node", 1)
-    full_val = [w_val, val_beside, val_across, swap(val_across, "node", 1)]
-    values = exchange(project(pieces, full_val))
-    attn = attend(rel_bias.T, edges, queries, values)
-    out_across = after(out_across, *attn)
-    attn = exchange(attn)
-    full_out = [w_out, out_beside, out_across, swap(out_across, "node", 1)]
-    terms = emit(attn, full_out)
-    other = {3: swap(terms[7], "head", 1), 2: swap(terms[6], "head", 1)}
-    other[1] = swap(after(terms[5], other[3]), "head", 1)
-    other[0] = swap(after(terms[4], other[2]), "head", 1)
-    total = terms[0].astype(jnp.float32) + other[0].astype(jnp.float32)
+    out_first = across(after(w_out[: depth // 2], *edges))
+    send_0, keep_0 = sort(node_feats, far[3])
+    moved_0, keep_0y = across(send_0), along(keep_0)
+    out_second = across(after(w_out[depth // 2 : 3 * depth // 4], moved_0, out_first))
+    moved_0y = along(moved_0)
+    send_1, keep_1 = sort(*lax.optimization_barrier((far[1], far[2], keep_0y))[:2])
+    moved_1, keep_1y = across(send_1), along(keep_1)
+    moved_1y = along(moved_1)
+    out_third = across(after(w_out[3 * depth // 4 :], moved_1, out_second))
+    qk_beside, val_beside, out_beside = beside(w_qk), beside(w_val), beside(w_out)
+    qk_beside = after(qk_beside, out_first)
+
+    pieces = [keep_0, keep_0y, keep_1, keep_1y, moved_0, moved_0y, moved_1, moved_1y]
+    qk_keep, qk_send = project(pieces, [w_qk, qk_beside])
+    qk_moved = across(after(qk_send, out_third))
+    val_keep, val_send = project(pieces, [w_val, val_beside])
+    val_moved = across(after(val_send, out_third))
+    qk_mine, qk_give = combine(qk_keep, qk_moved)
+    qk_theirs = beside(qk_give)
+    val_mine, val_give = combine(val_keep, val_moved)
+    val_theirs = beside(val_give)
+    attn = attend(rel_bias.T, edges, [qk_mine, qk_theirs], [val_mine, val_theirs])
+    attn = [attn[0]] + [swap(attn[i], "node", i) for i in range(1, 4)]
+
+    out_across = [out_first, out_second, out_third]
+    out_diagonal = [beside(after(piece, qk_moved)) for piece in out_across]
+    terms = emit(attn, [[w_out], [out_beside], out_across, out_diagonal])
+    total, other, pairs = None, {}, {}
+    for i in (3, 2, 1, 0):
+        send = terms[4 + i]
+        if i < 2:
+            send = after(send, pairs[i + 2])
+        other[i] = along(send)
+        pair = terms[i].astype(jnp.float32) + other[i].astype(jnp.float32)
+        if i > 0:
+            pairs[i] = pair.astype(jnp.bfloat16)
+        else:
+            total = pair
     for i in (3, 2, 1):
-        pair = terms[i].astype(jnp.float32) + other[i].astype(jnp.float32)
-        moved = swap(pair.astype(jnp.bfloat16), "head", 2 * i)
-        total = total + moved.astype(jnp.float32)
+        total = total + swap(pairs[i], "head", 2 * i).astype(jnp.float32)
     return total.astype(jnp.bfloat16)
 
 

time: 169 us -> 120 us (0.71); the launches traced: 167 us -> 120 us
  waiting for transfers between devices: 118 us -> 72.5 us
    ppermute x35, waiting for transfers between devices: 118 us -> 72.5 us  [swap(): return lax.ppermute(value, axis, [(i, i ^ mask) for i in range(peers)])]
    unnamed x12, local copies, waits for them, and re-layouts: 2.86 us -> 0.7 us
    pallas_call x3 -> x7, Pallas kernels: 4.45 us -> 4.93 us  [the longest x2 3.05 us: project(): pl.pallas_call(project_kernel, out_shape=[jax.ShapeDtypeStruct((2 * rows,...]
  transfers between devices with their start and end apart: 35 -> 35, of which waited for: 17 -> 20; matrix products, arithmetic and copies ran while one was open for 0% -> 1% of each run, Pallas kernels for 4% -> 6%
where the time goes in v4:
time: 120 us
  waiting for transfers between devices  72.5 us (60%)
  starting transfers between devices  35.4 us (30%)
  Pallas kernels  8.53 us (7%)
  local copies, waits for them, and re-layouts  1.81 us (2%)
    ppermute x35, waiting for transfers between devices, swap(): return lax.ppermute(value, axis, [(i, i ^ mask) for i in range(peers)])  72.5 us
    ppermute x35, starting transfers between devices, swap(): return lax.ppermute(value, axis, [(i, i ^ mask) for i in range(peers)])  35.4 us
    pallas_call x1, Pallas kernels, attend(): pl.pallas_call(attend_kernel, out_shape=[jax.ShapeDtypeStruct((rows, DH),...  3.59 us
    pallas_call x2, Pallas kernels, project(): pl.pallas_call(project_kernel, out_shape=[jax.ShapeDtypeStruct((2 * rows,...  3.05 us
  transfers between devices with their start and end apart: 35, of which 20 were waited for; matrix products, arithmetic and copies ran while one was open for 1% of the time, Pallas kernels for 6%

profile of v4, /device:TPU:0, one launch (start us, length us, event | category | flops | bytes accessed | tf_op | source)
XLA Modules:
  0.0 119.5 jit_solution(18031117902080122600)
XLA Ops:
  0.0 5.0 %collective-permute-start.3 = (bf16[256,512]{1,0:T(8,128)(2,1)}, bf16[256,512]{1,0:T(8,128)(2,1)S(1)}, u32[]{:S(2)}, u32[]{:S(2)}) collective-permute-start(bf16[256,512]{1,0:T(8,128)(2,1)} %close_ref.1), channel_id=1, source_target_pairs={{0,6},{1,7},{2,4},{3,5},{4,2},{5,3},{6,0},{7,1},{8,14},{9,15},{10,... | collective-permute-start | bytes 786440 | tf_op jit(solution)/shard_map/ppermute | solution.py:19
  5.1 0.6 collective-permute-start.6
  5.7 0.2 collective-permute-start
  5.9 2.0 %collective-permute-done.refs_1_ = s32[2,8]{1,0:T(2,128)S(1)} collective-permute-done((s32[2,8]{1,0:T(2,128)}, s32[2,8]{1,0:T(2,128)S(1)}, u32[]{:S(2)}, u32[]{:S(2)}) %collective-permute-start) | collective-permute-done | bytes 96 | tf_op jit(solution)/shard_map/ppermute | solution.py:19
  7.9 1.5 %collective-permute-start.1 = (s32[2,8]{1,0:T(2,128)}, s32[2,8]{1,0:T(2,128)S(1)}, u32[]{:S(2)}, u32[]{:S(2)}) collective-permute-start(s32[2,8]{1,0:T(2,128)} %refs_0_.1), channel_id=1, source_target_pairs={{0,16},{8,24},{16,0},{24,8},{1,17},{9,25},{17,1},{25,9},{2,18},{10... | collective-permute-start | bytes 200 | tf_op jit(solution)/shard_map/ppermute | solution.py:19
  9.4 2.3 %collective-permute-done.1.refs_2_ = s32[2,8]{1,0:T(2,128)S(1)} collective-permute-done((s32[2,8]{1,0:T(2,128)}, s32[2,8]{1,0:T(2,128)S(1)}, u32[]{:S(2)}, u32[]{:S(2)}) %collective-permute-start.1) | collective-permute-done | bytes 96 | tf_op jit(solution)/shard_map/ppermute | solution.py:19
  11.7 0.4 collective-permute-start.2
  12.1 1.1 slice.9
  13.2 0.0 copy-start.1
  13.2 1.7 %collective-permute-done.2.refs_3_ = s32[2,8]{1,0:T(2,128)S(1)} collective-permute-done((s32[2,8]{1,0:T(2,128)}, s32[2,8]{1,0:T(2,128)S(1)}, u32[]{:S(2)}, u32[]{:S(2)}) %collective-permute-start.2) | collective-permute-done | bytes 96 | tf_op jit(solution)/shard_map/ppermute | solution.py:19
  14.9 1.5 %collective-permute-start.13 = (bf16[256,1024]{1,0:T(8,128)(2,1)S(1)}, bf16[256,1024]{1,0:T(8,128)(2,1)S(1)}, u32[]{:S(2)}, u32[]{:S(2)}) collective-permute-start(bf16[256,1024]{1,0:T(8,128)(2,1)S(1)} %slice.9), channel_id=1, source_target_pairs={{0,16},{8,24},{16,0},{24,8},{1,17},{9,25},{17,1},{25,9},{2,18},{10... | collective-permute-start | bytes 1572872 | tf_op jit(solution)/shard_map/ppermute | solution.py:19
  16.5 1.6 %collective-permute-start.4 = (bf16[256,512]{1,0:T(8,128)(2,1)S(1)}, bf16[256,512]{1,0:T(8,128)(2,1)S(1)}, u32[]{:S(2)}, u32[]{:S(2)}) collective-permute-start(bf16[256,512]{1,0:T(8,128)(2,1)S(1)} %get-tuple-element.42.refs_0_), channel_id=1, source_target_pairs={{0,1},{1,0},{2,3},{3,2},{4,5},{5,4},{6,7},{7,6},{8,9},{9,8},{10,11... | collective-permute-start | bytes 786440 | tf_op jit(solution)/shard_map/ppermute | solution.py:19
  18.0 0.4 collective-permute-done.5.close_ref
  18.5 1.4 %collective-permute-start.8 = (bf16[256,512]{1,0:T(8,128)(2,1)S(1)}, bf16[256,512]{1,0:T(8,128)(2,1)S(1)}, u32[]{:S(2)}, u32[]{:S(2)}) collective-permute-start(bf16[256,512]{1,0:T(8,128)(2,1)S(1)} %get-tuple-element.46), channel_id=1, source_target_pairs={{0,16},{8,24},{16,0},{24,8},{1,17},{9,25},{17,1},{25,9},{2,18},{10... | collective-permute-start | bytes 786440 | tf_op jit(solution)/shard_map/ppermute | solution.py:19
  19.9 7.7 %collective-permute-done.6.distant_ref = bf16[256,512]{1,0:T(8,128)(2,1)S(1)} collective-permute-done((bf16[256,512]{1,0:T(8,128)(2,1)}, bf16[256,512]{1,0:T(8,128)(2,1)S(1)}, u32[]{:S(2)}, u32[]{:S(2)}) %collective-permute-start.6) | collective-permute-done | bytes 262176 | tf_op jit(solution)/shard_map/ppermute | solution.py:19
  27.6 1.6 %collective-permute-start.7 = (bf16[256,512]{1,0:T(8,128)(2,1)S(1)}, bf16[256,512]{1,0:T(8,128)(2,1)S(1)}, u32[]{:S(2)}, u32[]{:S(2)}) collective-permute-start(bf16[256,512]{1,0:T(8,128)(2,1)S(1)} %get-tuple-element.45.refs_2_), channel_id=1, source_target_pairs={{0,1},{1,0},{2,3},{3,2},{4,5},{5,4},{6,7},{7,6},{8,9},{9,8},{10,11... | collective-permute-start | bytes 786440 | tf_op jit(solution)/shard_map/ppermute | solution.py:19
  29.2 5.3 %collective-permute-done.8.refs_4_ = bf16[256,512]{1,0:T(8,128)(2,1)S(1)} collective-permute-done((bf16[256,512]{1,0:T(8,128)(2,1)S(1)}, bf16[256,512]{1,0:T(8,128)(2,1)S(1)}, u32[]{:S(2)}, u32[]{:S(2)}) %collective-permute-start.8) | collective-permute-done | bytes 262176 | tf_op jit(solution)/shard_map/ppermute | solution.py:19
  34.5 0.9 collective-permute-start.10
  35.5 1.2 collective-permute-start.14
  36.7 1.5 %collective-permute-start.9 = (bf16[256,512]{1,0:T(8,128)(2,1)S(1)}, bf16[256,512]{1,0:T(8,128)(2,1)S(1)}, u32[]{:S(2)}, u32[]{:S(2)}) collective-permute-start(bf16[256,512]{1,0:T(8,128)(2,1)S(1)} %collective-permute-done.8.refs_4_), channel_id=1, source_target_pairs={{0,1},{1,0},{2,3},{3,2},{4,5},{5,4},{6,7},{7,6},{8,9},{9,8},{10,11... | collective-permute-start | bytes 786440 | tf_op jit(solution)/shard_map/ppermute | solution.py:19
  38.2 5.6 %collective-permute-done.10.refs_6_ = bf16[256,512]{1,0:T(8,128)(2,1)S(1)} collective-permute-done((bf16[256,512]{1,0:T(8,128)(2,1)S(1)}, bf16[256,512]{1,0:T(8,128)(2,1)S(1)}, u32[]{:S(2)}, u32[]{:S(2)}) %collective-permute-start.10) | collective-permute-done | bytes 262176 | tf_op jit(solution)/shard_map/ppermute | solution.py:19
  43.8 1.5 %collective-permute-start.11 = (bf16[256,512]{1,0:T(8,128)(2,1)S(1)}, bf16[256,512]{1,0:T(8,128)(2,1)S(1)}, u32[]{:S(2)}, u32[]{:S(2)}) collective-permute-start(bf16[256,512]{1,0:T(8,128)(2,1)S(1)} %collective-permute-done.10.refs_6_), channel_id=1, source_target_pairs={{0,1},{1,0},{2,3},{3,2},{4,5},{5,4},{6,7},{7,6},{8,9},{9,8},{10,11... | collective-permute-start | bytes 786440 | tf_op jit(solution)/shard_map/ppermute | solution.py:19
  45.3 2.4 %collective-permute-done.14.refs_7_ = bf16[128,1024]{1,0:T(8,128)(2,1)S(1)} collective-permute-done((bf16[128,1024]{1,0:T(8,128)(2,1)S(1)}, bf16[128,1024]{1,0:T(8,128)(2,1)S(1)}, u32[]{:S(2)}, u32[]{:S(2)}) %collective-permute-start.14) | collective-permute-done | bytes 262176 | tf_op jit(solution)/shard_map/ppermute | solution.py:19
  47.7 0.3 collective-permute-start.15
  48.0 2.1 %collective-permute-done.11.refs_7_ = bf16[256,512]{1,0:T(8,128)(2,1)S(1)} collective-permute-done((bf16[256,512]{1,0:T(8,128)(2,1)S(1)}, bf16[256,512]{1,0:T(8,128)(2,1)S(1)}, u32[]{:S(2)}, u32[]{:S(2)}) %collective-permute-start.11) | collective-permute-done | bytes 262176 | tf_op jit(solution)/shard_map/ppermute | solution.py:19
  50.1 1.5 %project.2 = (f32[512,256]{1,0:T(8,128)S(1)}, bf16[512,256]{1,0:T(8,128)(2,1)S(1)}) custom-call(bf16[256,512]{1,0:T(8,128)(2,1)S(1)} %get-tuple-element.42.refs_0_, bf16[256,512]{1,0:T(8,128)(2,1)S(1)} %collective-permute-done.4.refs_1_, bf16[256,512]{1,0:T(8,128)(2,1)S(1)} %get-tuple-element.45.refs_2_, ...), custom_call_target="tpu_custom_call" | custom-call | flops 1073741824 | bytes 4980736 | tf_op jit(solution)/shard_map/project/pallas_call | solution.py:106
  51.7 4.7 %collective-permute-done.15.refs_8_ = bf16[128,1024]{1,0:T(8,128)(2,1)S(1)} collective-permute-done((bf16[128,1024]{1,0:T(8,128)(2,1)S(1)}, bf16[128,1024]{1,0:T(8,128)(2,1)S(1)}, u32[]{:S(2)}, u32[]{:S(2)}) %collective-permute-start.15) | collective-permute-done | bytes 262176 | tf_op jit(solution)/shard_map/ppermute | solution.py:19
  56.4 0.3 collective-permute-start.16
  56.7 1.5 %project.3 = (f32[512,256]{1,0:T(8,128)S(1)}, bf16[512,256]{1,0:T(8,128)(2,1)S(1)}) custom-call(bf16[256,512]{1,0:T(8,128)(2,1)S(1)} %get-tuple-element.42.refs_0_, bf16[256,512]{1,0:T(8,128)(2,1)S(1)} %collective-permute-done.4.refs_1_, bf16[256,512]{1,0:T(8,128)(2,1)S(1)} %get-tuple-element.45.refs_2_, ...), custom_call_target="tpu_custom_call" | custom-call | flops 1073741824 | bytes 4980736 | tf_op jit(solution)/shard_map/project/pallas_call | solution.py:106
  58.2 1.8 %collective-permute-start.19 = (bf16[512,256]{1,0:T(8,128)(2,1)S(1)}, bf16[512,256]{1,0:T(8,128)(2,1)S(1)}, u32[]{:S(2)}, u32[]{:S(2)}) collective-permute-start(bf16[512,256]{1,0:T(8,128)(2,1)S(1)} %get-tuple-element.59), channel_id=1, source_target_pairs={{0,16},{8,24},{16,0},{24,8},{1,17},{9,25},{17,1},{25,9},{2,18},{10... | collective-permute-start | bytes 786440 | tf_op jit(solution)/shard_map/ppermute | solution.py:19
  60.0 5.6 %collective-permute-done.16.moved_ref = bf16[512,256]{1,0:T(8,128)(2,1)S(1)} collective-permute-done((bf16[512,256]{1,0:T(8,128)(2,1)S(1)}, bf16[512,256]{1,0:T(8,128)(2,1)S(1)}, u32[]{:S(2)}, u32[]{:S(2)}) %collective-permute-start.16) | collective-permute-done | bytes 262176 | tf_op jit(solution)/shard_map/ppermute | solution.py:19
  65.6 0.1 combine.2
  65.7 0.6 collective-permute-start.17
  66.3 3.6 %collective-permute-done.19.moved_ref = bf16[512,256]{1,0:T(8,128)(2,1)S(1)} collective-permute-done((bf16[512,256]{1,0:T(8,128)(2,1)S(1)}, bf16[512,256]{1,0:T(8,128)(2,1)S(1)}, u32[]{:S(2)}, u32[]{:S(2)}) %collective-permute-start.19) | collective-permute-done | bytes 262176 | tf_op jit(solution)/shard_map/ppermute | solution.py:19
  69.9 0.1 combine.3
  69.9 0.0 copy-start.4
  70.0 0.1 collective-permute-start.20
  70.0 0.5 collective-permute-start.26
  70.5 0.1 collective-permute-start.27
  70.6 0.8 collective-permute-done.20.refs_7_
  71.4 0.7 copy-done.5
  72.0 3.6 %attend.1 = (bf16[256,128]{1,0:T(8,128)(2,1)S(1)}, bf16[256,128]{1,0:T(8,128)(2,1)S(1)}, bf16[256,128]{1,0:T(8,128)(2,1)S(1)}, bf16[256,128]{1,0:T(8,128)(2,1)S(1)}) custom-call(f32[4,237]{1,0:T(4,128)S(1)} %bitcast.1, s32[2,8]{1,0:T(2,128)S(1)} %copy-done.5, s32[2,8]{1,0:T(2,128)S(1)} %collective-permute-done.refs_1_, ...), custom_call_target="tpu_custom_call" | custom-call | flops 536870912 | bytes 786432 | tf_op jit(solution)/shard_map/attend/pallas_call | solution.py:197
  75.6 0.2 collective-permute-start.21
  75.9 0.3 collective-permute-start.22
  76.2 0.8 collective-permute-done.21.refs_1_
  77.0 0.6 collective-permute-start.23
  77.6 3.0 %collective-permute-done.22.refs_2_ = bf16[256,128]{1,0:T(8,128)(2,1)S(1)} collective-permute-done((bf16[256,128]{1,0:T(8,128)(2,1)S(1)}, bf16[256,128]{1,0:T(8,128)(2,1)S(1)}, u32[]{:S(2)}, u32[]{:S(2)}) %collective-permute-start.22) | collective-permute-done | bytes 65568 | tf_op jit(solution)/shard_map/ppermute | solution.py:19
  80.6 0.7 collective-permute-done.23.refs_3_
  81.3 1.7 %emit.1 = (bf16[256,512]{1,0:T(8,128)(2,1)S(1)}, bf16[256,512]{1,0:T(8,128)(2,1)S(1)}, bf16[256,512]{1,0:T(8,128)(2,1)S(1)}, bf16[256,512]{1,0:T(8,128)(2,1)S(1)...) custom-call(bf16[256,128]{1,0:T(8,128)(2,1)S(1)} %get-tuple-element., ...), custom_call_target="tpu_custom_call" | custom-call | flops 1073741824 | bytes 6553600 | tf_op jit(solution)/shard_map/emit/pallas_call | solution.py:246
  83.0 1.6 %collective-permute-start.30 = (bf16[256,512]{1,0:T(8,128)(2,1)S(1)}, bf16[256,512]{1,0:T(8,128)(2,1)S(1)}, u32[]{:S(2)}, u32[]{:S(2)}) collective-permute-start(bf16[256,512]{1,0:T(8,128)(2,1)S(1)} %get-tuple-element.75), channel_id=1, source_target_pairs={{0,1},{1,0},{2,3},{3,2},{4,5},{5,4},{6,7},{7,6},{8,9},{9,8},{10,11... | collective-permute-start | bytes 786440 | tf_op jit(solution)/shard_map/ppermute | solution.py:19
  84.6 0.5 collective-permute-start.28
  85.1 7.1 %collective-permute-done.30 = bf16[256,512]{1,0:T(8,128)(2,1)S(1)} collective-permute-done((bf16[256,512]{1,0:T(8,128)(2,1)S(1)}, bf16[256,512]{1,0:T(8,128)(2,1)S(1)}, u32[]{:S(2)}, u32[]{:S(2)}) %collective-permute-start.30) | collective-permute-done | bytes 262176 | tf_op jit(solution)/shard_map/ppermute | solution.py:19
  92.2 0.1 add_convert_fusion.2
  92.3 1.6 %collective-permute-start.33 = (bf16[256,512]{1,0:T(8,128)(2,1)S(1)}, bf16[256,512]{1,0:T(8,128)(2,1)S(1)}, u32[]{:S(2)}, u32[]{:S(2)}) collective-permute-start(bf16[256,512]{1,0:T(8,128)(2,1)S(1)} %get-tuple-element.78), channel_id=1, source_target_pairs={{0,1},{1,0},{2,3},{3,2},{4,5},{5,4},{6,7},{7,6},{8,9},{9,8},{10,11... | collective-permute-start | bytes 786440 | tf_op jit(solution)/shard_map/ppermute | solution.py:19
  93.9 2.9 %collective-permute-start.31 = (bf16[256,512]{1,0:T(8,128)(2,1)S(1)}, bf16[256,512]{1,0:T(8,128)(2,1)S(1)}, u32[]{:S(2)}, u32[]{:S(2)}) collective-permute-start(bf16[256,512]{1,0:T(8,128)(2,1)S(1)} %add_convert_fusion.2), channel_id=1, source_target_pairs={{0,6},{1,7},{2,4},{3,5},{4,2},{5,3},{6,0},{7,1},{8,14},{9,15},{10,... | collective-permute-start | bytes 786440 | tf_op jit(solution)/shard_map/ppermute | solution.py:19
  96.8 1.1 collective-permute-done.28
  97.8 0.1 add_convert_fusion.3
  97.9 1.5 %collective-permute-start.32 = (bf16[256,512]{1,0:T(8,128)(2,1)S(1)}, bf16[256,512]{1,0:T(8,128)(2,1)S(1)}, u32[]{:S(2)}, u32[]{:S(2)}) collective-permute-start(bf16[256,512]{1,0:T(8,128)(2,1)S(1)} %add_convert_fusion.3), channel_id=1, source_target_pairs={{0,4},{1,5},{2,6},{3,7},{4,0},{5,1},{6,2},{7,3},{8,12},{9,13},{10,... | collective-permute-start | bytes 786440 | tf_op jit(solution)/shard_map/ppermute | solution.py:19
  99.4 1.5 %collective-permute-start.29 = (bf16[256,512]{1,0:T(8,128)(2,1)S(1)}, bf16[256,512]{1,0:T(8,128)(2,1)S(1)}, u32[]{:S(2)}, u32[]{:S(2)}) collective-permute-start(bf16[256,512]{1,0:T(8,128)(2,1)S(1)} %get-tuple-element.73), channel_id=1, source_target_pairs={{0,1},{1,0},{2,3},{3,2},{4,5},{5,4},{6,7},{7,6},{8,9},{9,8},{10,11... | collective-permute-start | bytes 786440 | tf_op jit(solution)/shard_map/ppermute | solution.py:19
  100.9 2.5 %collective-permute-done.33 = bf16[256,512]{1,0:T(8,128)(2,1)S(1)} collective-permute-done((bf16[256,512]{1,0:T(8,128)(2,1)S(1)}, bf16[256,512]{1,0:T(8,128)(2,1)S(1)}, u32[]{:S(2)}, u32[]{:S(2)}) %collective-permute-start.33) | collective-permute-done | bytes 262176 | tf_op jit(solution)/shard_map/ppermute | solution.py:19
  103.5 0.1 add_convert_fusion.1
  103.5 2.1 %collective-permute-start.34 = (bf16[256,512]{1,0:T(8,128)(2,1)S(1)}, bf16[256,512]{1,0:T(8,128)(2,1)S(1)}, u32[]{:S(2)}, u32[]{:S(2)}) collective-permute-start(bf16[256,512]{1,0:T(8,128)(2,1)S(1)} %add_convert_fusion.1), channel_id=1, source_target_pairs={{0,2},{1,3},{2,0},{3,1},{4,6},{5,7},{6,4},{7,5},{8,10},{9,11},{10,... | collective-permute-start | bytes 786440 | tf_op jit(solution)/shard_map/ppermute | solution.py:19
  105.6 13.0 %collective-permute-done.32 = bf16[256,512]{1,0:T(8,128)(2,1)S(1)} collective-permute-done((bf16[256,512]{1,0:T(8,128)(2,1)S(1)}, bf16[256,512]{1,0:T(8,128)(2,1)S(1)}, u32[]{:S(2)}, u32[]{:S(2)}) %collective-permute-start.32) | collective-permute-done | bytes 262176 | tf_op jit(solution)/shard_map/ppermute | solution.py:19
  118.6 0.9 add_convert_fusion
  (32 shorter events, 0.2 us)
Async XLA Ops:
  0.0 16.4 %copy-start.3 = (bf16[256,512]{1,0:T(8,128)(2,1)S(1)}, bf16[256,512]{1,0:T(8,128)(2,1)}, u32[]{:S(2)}) copy-start(bf16[256,512]{1,0:T(8,128)(2,1)} %close_ref.1) | copy-start | bytes 786436
  0.0 35.4 %copy-start = (bf16[512,1024]{1,0:T(8,128)(2,1)S(1)}, bf16[512,1024]{1,0:T(8,128)(2,1)}, u32[]{:S(2)}) copy-start(bf16[512,1024]{1,0:T(8,128)(2,1)} %refs_4_.1) | copy-start | bytes 3145732
  0.0 16.4 %collective-permute-start.3 = (bf16[256,512]{1,0:T(8,128)(2,1)}, bf16[256,512]{1,0:T(8,128)(2,1)S(1)}, u32[]{:S(2)}, u32[]{:S(2)}) collective-permute-start(bf16[256,512]{1,0:T(8,128)(2,1)} %close_ref.1), channel_id=1, source_target_pairs={{0,6},{1,7},{2,4},{3,5},{4,2},{5,3},{6,0},{7,1},{8,14},{9,15},{10,... | collective-permute-start | bytes 786440 | tf_op jit(solution)/shard_map/ppermute | solution.py:19
  5.1 13.4 %collective-permute-start.5 = (bf16[256,512]{1,0:T(8,128)(2,1)}, bf16[256,512]{1,0:T(8,128)(2,1)S(1)}, u32[]{:S(2)}, u32[]{:S(2)}) collective-permute-start(bf16[256,512]{1,0:T(8,128)(2,1)} %close_ref.1), channel_id=1, source_target_pairs={{0,2},{1,3},{2,0},{3,1},{4,6},{5,7},{6,4},{7,5},{8,10},{9,11},{10,... | collective-permute-start | bytes 786440 | tf_op jit(solution)/shard_map/ppermute | solution.py:19
  5.1 42.6 %collective-permute-start.12 = (bf16[1024,512]{1,0:T(8,128)(2,1)}, bf16[1024,512]{1,0:T(8,128)(2,1)S(1)}, u32[]{:S(2)}, u32[]{:S(2)}) collective-permute-start(bf16[1024,512]{1,0:T(8,128)(2,1)} %refs_8_.2), channel_id=1, source_target_pairs={{0,8},{8,0},{16,24},{24,16},{1,9},{9,1},{17,25},{25,17},{2,10},{10... | collective-permute-start | bytes 3145736 | tf_op jit(solution)/shard_map/ppermute | solution.py:19
  5.1 22.5 %collective-permute-start.6 = (bf16[256,512]{1,0:T(8,128)(2,1)}, bf16[256,512]{1,0:T(8,128)(2,1)S(1)}, u32[]{:S(2)}, u32[]{:S(2)}) collective-permute-start(bf16[256,512]{1,0:T(8,128)(2,1)} %close_ref.1), channel_id=1, source_target_pairs={{0,4},{1,5},{2,6},{3,7},{4,0},{5,1},{6,2},{7,3},{8,12},{9,13},{10,... | collective-permute-start | bytes 786440 | tf_op jit(solution)/shard_map/ppermute | solution.py:19
  5.7 2.2 %collective-permute-start = (s32[2,8]{1,0:T(2,128)}, s32[2,8]{1,0:T(2,128)S(1)}, u32[]{:S(2)}, u32[]{:S(2)}) collective-permute-start(s32[2,8]{1,0:T(2,128)} %refs_0_.1), channel_id=1, source_target_pairs={{0,8},{8,0},{16,24},{24,16},{1,9},{9,1},{17,25},{25,17},{2,10},{10... | collective-permute-start | bytes 200 | tf_op jit(solution)/shard_map/ppermute | solution.py:19
  7.9 3.8 %collective-permute-start.1 = (s32[2,8]{1,0:T(2,128)}, s32[2,8]{1,0:T(2,128)S(1)}, u32[]{:S(2)}, u32[]{:S(2)}) collective-permute-start(s32[2,8]{1,0:T(2,128)} %refs_0_.1), channel_id=1, source_target_pairs={{0,16},{8,24},{16,0},{24,8},{1,17},{9,25},{17,1},{25,9},{2,18},{10... | collective-permute-start | bytes 200 | tf_op jit(solution)/shard_map/ppermute | solution.py:19
  11.7 3.2 %collective-permute-start.2 = (s32[2,8]{1,0:T(2,128)}, s32[2,8]{1,0:T(2,128)S(1)}, u32[]{:S(2)}, u32[]{:S(2)}) collective-permute-start(s32[2,8]{1,0:T(2,128)} %refs_0_.1), channel_id=1, source_target_pairs={{0,24},{8,16},{16,8},{24,0},{1,25},{9,17},{17,9},{25,1},{2,26},{10... | collective-permute-start | bytes 200 | tf_op jit(solution)/shard_map/ppermute | solution.py:19
  13.2 37.0 %copy-start.1 = (bf16[1024,512]{1,0:T(8,128)(2,1)S(1)}, bf16[1024,512]{1,0:T(8,128)(2,1)}, u32[]{:S(2)}) copy-start(bf16[1024,512]{1,0:T(8,128)(2,1)} %refs_8_.2) | copy-start | bytes 3145732
  14.9 20.6 %collective-permute-start.13 = (bf16[256,1024]{1,0:T(8,128)(2,1)S(1)}, bf16[256,1024]{1,0:T(8,128)(2,1)S(1)}, u32[]{:S(2)}, u32[]{:S(2)}) collective-permute-start(bf16[256,1024]{1,0:T(8,128)(2,1)S(1)} %slice.9), channel_id=1, source_target_pairs={{0,16},{8,24},{16,0},{24,8},{1,17},{9,25},{17,1},{25,9},{2,18},{10... | collective-permute-start | bytes 1572872 | tf_op jit(solution)/shard_map/ppermute | solution.py:19
  16.5 11.1 %collective-permute-start.4 = (bf16[256,512]{1,0:T(8,128)(2,1)S(1)}, bf16[256,512]{1,0:T(8,128)(2,1)S(1)}, u32[]{:S(2)}, u32[]{:S(2)}) collective-permute-start(bf16[256,512]{1,0:T(8,128)(2,1)S(1)} %get-tuple-element.42.refs_0_), channel_id=1, source_target_pairs={{0,1},{1,0},{2,3},{3,2},{4,5},{5,4},{6,7},{7,6},{8,9},{9,8},{10,11... | collective-permute-start | bytes 786440 | tf_op jit(solution)/shard_map/ppermute | solution.py:19
  18.5 16.1 %collective-permute-start.8 = (bf16[256,512]{1,0:T(8,128)(2,1)S(1)}, bf16[256,512]{1,0:T(8,128)(2,1)S(1)}, u32[]{:S(2)}, u32[]{:S(2)}) collective-permute-start(bf16[256,512]{1,0:T(8,128)(2,1)S(1)} %get-tuple-element.46), channel_id=1, source_target_pairs={{0,16},{8,24},{16,0},{24,8},{1,17},{9,25},{17,1},{25,9},{2,18},{10... | collective-permute-start | bytes 786440 | tf_op jit(solution)/shard_map/ppermute | solution.py:19
  27.6 29.1 %collective-permute-start.18 = (bf16[1024,512]{1,0:T(8,128)(2,1)}, bf16[1024,512]{1,0:T(8,128)(2,1)S(1)}, u32[]{:S(2)}, u32[]{:S(2)}) collective-permute-start(bf16[1024,512]{1,0:T(8,128)(2,1)} %refs_8_.3), channel_id=1, source_target_pairs={{0,8},{8,0},{16,24},{24,16},{1,9},{9,1},{17,25},{25,17},{2,10},{10... | collective-permute-start | bytes 3145736 | tf_op jit(solution)/shard_map/ppermute | solution.py:19
  27.6 9.0 %collective-permute-start.7 = (bf16[256,512]{1,0:T(8,128)(2,1)S(1)}, bf16[256,512]{1,0:T(8,128)(2,1)S(1)}, u32[]{:S(2)}, u32[]{:S(2)}) collective-permute-start(bf16[256,512]{1,0:T(8,128)(2,1)S(1)} %get-tuple-element.45.refs_2_), channel_id=1, source_target_pairs={{0,1},{1,0},{2,3},{3,2},{4,5},{5,4},{6,7},{7,6},{8,9},{9,8},{10,11... | collective-permute-start | bytes 786440 | tf_op jit(solution)/shard_map/ppermute | solution.py:19
  34.5 9.2 %collective-permute-start.10 = (bf16[256,512]{1,0:T(8,128)(2,1)S(1)}, bf16[256,512]{1,0:T(8,128)(2,1)S(1)}, u32[]{:S(2)}, u32[]{:S(2)}) collective-permute-start(bf16[256,512]{1,0:T(8,128)(2,1)S(1)} %get-tuple-element.47), channel_id=1, source_target_pairs={{0,16},{8,24},{16,0},{24,8},{1,17},{9,25},{17,1},{25,9},{2,18},{10... | collective-permute-start | bytes 786440 | tf_op jit(solution)/shard_map/ppermute | solution.py:19
  35.5 12.2 %collective-permute-start.14 = (bf16[128,1024]{1,0:T(8,128)(2,1)S(1)}, bf16[128,1024]{1,0:T(8,128)(2,1)S(1)}, u32[]{:S(2)}, u32[]{:S(2)}) collective-permute-start(bf16[128,1024]{1,0:T(8,128)(2,1)S(1)} %get-tuple-element.52), channel_id=1, source_target_pairs={{0,16},{8,24},{16,0},{24,8},{1,17},{9,25},{17,1},{25,9},{2,18},{10... | collective-permute-start | bytes 786440 | tf_op jit(solution)/shard_map/ppermute | solution.py:19
  36.7 11.4 %collective-permute-start.9 = (bf16[256,512]{1,0:T(8,128)(2,1)S(1)}, bf16[256,512]{1,0:T(8,128)(2,1)S(1)}, u32[]{:S(2)}, u32[]{:S(2)}) collective-permute-start(bf16[256,512]{1,0:T(8,128)(2,1)S(1)} %collective-permute-done.8.refs_4_), channel_id=1, source_target_pairs={{0,1},{1,0},{2,3},{3,2},{4,5},{5,4},{6,7},{7,6},{8,9},{9,8},{10,11... | collective-permute-start | bytes 786440 | tf_op jit(solution)/shard_map/ppermute | solution.py:19
  43.8 6.4 %collective-permute-start.11 = (bf16[256,512]{1,0:T(8,128)(2,1)S(1)}, bf16[256,512]{1,0:T(8,128)(2,1)S(1)}, u32[]{:S(2)}, u32[]{:S(2)}) collective-permute-start(bf16[256,512]{1,0:T(8,128)(2,1)S(1)} %collective-permute-done.10.refs_6_), channel_id=1, source_target_pairs={{0,1},{1,0},{2,3},{3,2},{4,5},{5,4},{6,7},{7,6},{8,9},{9,8},{10,11... | collective-permute-start | bytes 786440 | tf_op jit(solution)/shard_map/ppermute | solution.py:19
  47.7 28.2 %collective-permute-start.24 = (bf16[512,1024]{1,0:T(8,128)(2,1)S(1)}, bf16[512,1024]{1,0:T(8,128)(2,1)S(1)}, u32[]{:S(2)}, u32[]{:S(2)}) collective-permute-start(bf16[512,1024]{1,0:T(8,128)(2,1)S(1)} %copy-done), channel_id=1, source_target_pairs={{0,8},{8,0},{16,24},{24,16},{1,9},{9,1},{17,25},{25,17},{2,10},{10... | collective-permute-start | bytes 3145736 | tf_op jit(solution)/shard_map/ppermute | solution.py:19
  47.7 9.0 %copy-start.2 = (bf16[1024,512]{1,0:T(8,128)(2,1)S(1)}, bf16[1024,512]{1,0:T(8,128)(2,1)}, u32[]{:S(2)}) copy-start(bf16[1024,512]{1,0:T(8,128)(2,1)} %refs_8_.3) | copy-start | bytes 3145732
  47.7 8.7 %collective-permute-start.15 = (bf16[128,1024]{1,0:T(8,128)(2,1)S(1)}, bf16[128,1024]{1,0:T(8,128)(2,1)S(1)}, u32[]{:S(2)}, u32[]{:S(2)}) collective-permute-start(bf16[128,1024]{1,0:T(8,128)(2,1)S(1)} %get-tuple-element.53), channel_id=1, source_target_pairs={{0,16},{8,24},{16,0},{24,8},{1,17},{9,25},{17,1},{25,9},{2,18},{10... | collective-permute-start | bytes 786440 | tf_op jit(solution)/shard_map/ppermute | solution.py:19
  56.4 9.2 %collective-permute-start.16 = (bf16[512,256]{1,0:T(8,128)(2,1)S(1)}, bf16[512,256]{1,0:T(8,128)(2,1)S(1)}, u32[]{:S(2)}, u32[]{:S(2)}) collective-permute-start(bf16[512,256]{1,0:T(8,128)(2,1)S(1)} %get-tuple-element.54), channel_id=1, source_target_pairs={{0,16},{8,24},{16,0},{24,8},{1,17},{9,25},{17,1},{25,9},{2,18},{10... | collective-permute-start | bytes 786440 | tf_op jit(solution)/shard_map/ppermute | solution.py:19
  58.2 11.7 %collective-permute-start.19 = (bf16[512,256]{1,0:T(8,128)(2,1)S(1)}, bf16[512,256]{1,0:T(8,128)(2,1)S(1)}, u32[]{:S(2)}, u32[]{:S(2)}) collective-permute-start(bf16[512,256]{1,0:T(8,128)(2,1)S(1)} %get-tuple-element.59), channel_id=1, source_target_pairs={{0,16},{8,24},{16,0},{24,8},{1,17},{9,25},{17,1},{25,9},{2,18},{10... | collective-permute-start | bytes 786440 | tf_op jit(solution)/shard_map/ppermute | solution.py:19
  65.6 15.7 %collective-permute-start.25 = (bf16[256,1024]{1,0:T(8,128)(2,1)S(1)}, bf16[256,1024]{1,0:T(8,128)(2,1)S(1)}, u32[]{:S(2)}, u32[]{:S(2)}) collective-permute-start(bf16[256,1024]{1,0:T(8,128)(2,1)S(1)} %collective-permute-done.13.refs_6_), channel_id=1, source_target_pairs={{0,8},{8,0},{16,24},{24,16},{1,9},{9,1},{17,25},{25,17},{2,10},{10... | collective-permute-start | bytes 1572872 | tf_op jit(solution)/shard_map/ppermute | solution.py:19
  65.7 4.8 %collective-permute-start.17 = (bf16[512,128]{1,0:T(8,128)(2,1)S(1)}, bf16[512,128]{1,0:T(8,128)(2,1)S(1)}, u32[]{:S(2)}, u32[]{:S(2)}) collective-permute-start(bf16[512,128]{1,0:T(8,128)(2,1)S(1)} %get-tuple-element.56), channel_id=1, source_target_pairs={{0,8},{8,0},{16,24},{24,16},{1,9},{9,1},{17,25},{25,17},{2,10},{10... | collective-permute-start | bytes 393224 | tf_op jit(solution)/shard_map/ppermute | solution.py:19
  69.9 1.4 %copy-start.4 = (f32[237,4]{0,1:T(4,128)S(1)}, f32[237,4]{0,1:T(4,128)}, u32[]{:S(2)}) copy-start(f32[237,4]{0,1:T(4,128)} %param.11) | copy-start | bytes 11380
  70.0 1.4 %collective-permute-start.20 = (bf16[512,128]{1,0:T(8,128)(2,1)S(1)}, bf16[512,128]{1,0:T(8,128)(2,1)S(1)}, u32[]{:S(2)}, u32[]{:S(2)}) collective-permute-start(bf16[512,128]{1,0:T(8,128)(2,1)S(1)} %get-tuple-element.61), channel_id=1, source_target_pairs={{0,8},{8,0},{16,24},{24,16},{1,9},{9,1},{17,25},{25,17},{2,10},{10... | collective-permute-start | bytes 393224 | tf_op jit(solution)/shard_map/ppermute | solution.py:19
  70.0 11.3 %collective-permute-start.26 = (bf16[128,1024]{1,0:T(8,128)(2,1)S(1)}, bf16[128,1024]{1,0:T(8,128)(2,1)S(1)}, u32[]{:S(2)}, u32[]{:S(2)}) collective-permute-start(bf16[128,1024]{1,0:T(8,128)(2,1)S(1)} %collective-permute-done.14.refs_7_), channel_id=1, source_target_pairs={{0,8},{8,0},{16,24},{24,16},{1,9},{9,1},{17,25},{25,17},{2,10},{10... | collective-permute-start | bytes 786440 | tf_op jit(solution)/shard_map/ppermute | solution.py:19
  70.5 10.8 %collective-permute-start.27 = (bf16[128,1024]{1,0:T(8,128)(2,1)S(1)}, bf16[128,1024]{1,0:T(8,128)(2,1)S(1)}, u32[]{:S(2)}, u32[]{:S(2)}) collective-permute-start(bf16[128,1024]{1,0:T(8,128)(2,1)S(1)} %collective-permute-done.15.refs_8_), channel_id=1, source_target_pairs={{0,8},{8,0},{16,24},{24,16},{1,9},{9,1},{17,25},{25,17},{2,10},{10... | collective-permute-start | bytes 786440 | tf_op jit(solution)/shard_map/ppermute | solution.py:19
  71.4 0.7 copy-start.5
  75.6 1.3 %collective-permute-start.21 = (bf16[256,128]{1,0:T(8,128)(2,1)S(1)}, bf16[256,128]{1,0:T(8,128)(2,1)S(1)}, u32[]{:S(2)}, u32[]{:S(2)}) collective-permute-start(bf16[256,128]{1,0:T(8,128)(2,1)S(1)} %get-tuple-element.63), channel_id=1, source_target_pairs={{0,8},{8,0},{16,24},{24,16},{1,9},{9,1},{17,25},{25,17},{2,10},{10... | collective-permute-start | bytes 196616 | tf_op jit(solution)/shard_map/ppermute | solution.py:19
  75.9 4.7 %collective-permute-start.22 = (bf16[256,128]{1,0:T(8,128)(2,1)S(1)}, bf16[256,128]{1,0:T(8,128)(2,1)S(1)}, u32[]{:S(2)}, u32[]{:S(2)}) collective-permute-start(bf16[256,128]{1,0:T(8,128)(2,1)S(1)} %get-tuple-element.64), channel_id=1, source_target_pairs={{0,16},{8,24},{16,0},{24,8},{1,17},{9,25},{17,1},{25,9},{2,18},{10... | collective-permute-start | bytes 196616 | tf_op jit(solution)/shard_map/ppermute | solution.py:19
  77.0 4.3 %collective-permute-start.23 = (bf16[256,128]{1,0:T(8,128)(2,1)S(1)}, bf16[256,128]{1,0:T(8,128)(2,1)S(1)}, u32[]{:S(2)}, u32[]{:S(2)}) collective-permute-start(bf16[256,128]{1,0:T(8,128)(2,1)S(1)} %get-tuple-element.65), channel_id=1, source_target_pairs={{0,24},{8,16},{16,8},{24,0},{1,25},{9,17},{17,9},{25,1},{2,26},{10... | collective-permute-start | bytes 196616 | tf_op jit(solution)/shard_map/ppermute | solution.py:19
  83.0 9.2 %collective-permute-start.30 = (bf16[256,512]{1,0:T(8,128)(2,1)S(1)}, bf16[256,512]{1,0:T(8,128)(2,1)S(1)}, u32[]{:S(2)}, u32[]{:S(2)}) collective-permute-start(bf16[256,512]{1,0:T(8,128)(2,1)S(1)} %get-tuple-element.75), channel_id=1, source_target_pairs={{0,1},{1,0},{2,3},{3,2},{4,5},{5,4},{6,7},{7,6},{8,9},{9,8},{10,11... | collective-permute-start | bytes 786440 | tf_op jit(solution)/shard_map/ppermute | solution.py:19
  84.6 13.2 %collective-permute-start.28 = (bf16[256,512]{1,0:T(8,128)(2,1)S(1)}, bf16[256,512]{1,0:T(8,128)(2,1)S(1)}, u32[]{:S(2)}, u32[]{:S(2)}) collective-permute-start(bf16[256,512]{1,0:T(8,128)(2,1)S(1)} %get-tuple-element.72), channel_id=1, source_target_pairs={{0,1},{1,0},{2,3},{3,2},{4,5},{5,4},{6,7},{7,6},{8,9},{9,8},{10,11... | collective-permute-start | bytes 786440 | tf_op jit(solution)/shard_map/ppermute | solution.py:19
  92.3 11.2 %collective-permute-start.33 = (bf16[256,512]{1,0:T(8,128)(2,1)S(1)}, bf16[256,512]{1,0:T(8,128)(2,1)S(1)}, u32[]{:S(2)}, u32[]{:S(2)}) collective-permute-start(bf16[256,512]{1,0:T(8,128)(2,1)S(1)} %get-tuple-element.78), channel_id=1, source_target_pairs={{0,1},{1,0},{2,3},{3,2},{4,5},{5,4},{6,7},{7,6},{8,9},{9,8},{10,11... | collective-permute-start | bytes 786440 | tf_op jit(solution)/shard_map/ppermute | solution.py:19
  93.9 24.7 %collective-permute-start.31 = (bf16[256,512]{1,0:T(8,128)(2,1)S(1)}, bf16[256,512]{1,0:T(8,128)(2,1)S(1)}, u32[]{:S(2)}, u32[]{:S(2)}) collective-permute-start(bf16[256,512]{1,0:T(8,128)(2,1)S(1)} %add_convert_fusion.2), channel_id=1, source_target_pairs={{0,6},{1,7},{2,4},{3,5},{4,2},{5,3},{6,0},{7,1},{8,14},{9,15},{10,... | collective-permute-start | bytes 786440 | tf_op jit(solution)/shard_map/ppermute | solution.py:19
  97.9 20.7 %collective-permute-start.32 = (bf16[256,512]{1,0:T(8,128)(2,1)S(1)}, bf16[256,512]{1,0:T(8,128)(2,1)S(1)}, u32[]{:S(2)}, u32[]{:S(2)}) collective-permute-start(bf16[256,512]{1,0:T(8,128)(2,1)S(1)} %add_convert_fusion.3), channel_id=1, source_target_pairs={{0,4},{1,5},{2,6},{3,7},{4,0},{5,1},{6,2},{7,3},{8,12},{9,13},{10,... | collective-permute-start | bytes 786440 | tf_op jit(solution)/shard_map/ppermute | solution.py:19
  99.4 19.3 %collective-permute-start.29 = (bf16[256,512]{1,0:T(8,128)(2,1)S(1)}, bf16[256,512]{1,0:T(8,128)(2,1)S(1)}, u32[]{:S(2)}, u32[]{:S(2)}) collective-permute-start(bf16[256,512]{1,0:T(8,128)(2,1)S(1)} %get-tuple-element.73), channel_id=1, source_target_pairs={{0,1},{1,0},{2,3},{3,2},{4,5},{5,4},{6,7},{7,6},{8,9},{9,8},{10,11... | collective-permute-start | bytes 786440 | tf_op jit(solution)/shard_map/ppermute | solution.py:19
  103.5 15.1 %collective-permute-start.34 = (bf16[256,512]{1,0:T(8,128)(2,1)S(1)}, bf16[256,512]{1,0:T(8,128)(2,1)S(1)}, u32[]{:S(2)}, u32[]{:S(2)}) collective-permute-start(bf16[256,512]{1,0:T(8,128)(2,1)S(1)} %add_convert_fusion.1), channel_id=1, source_target_pairs={{0,2},{1,3},{2,0},{3,1},{4,6},{5,7},{6,4},{7,5},{8,10},{9,11},{10,... | collective-permute-start | bytes 786440 | tf_op jit(solution)/shard_map/ppermute | solution.py:19

commit v5 on v4

--- a/solution.py
+++ b/solution.py
@@ -35,27 +35,32 @@
     return node // 2 == head // 4
 
 
-def sort_kernel(close_ref, distant_ref, send_ref, keep_ref):
+def sort_kernel(close_ref, distant_ref, first_ref, second_ref, keep_ref):
     lined = in_line(lax.axis_index("node"), lax.axis_index("head"))
+    half = first_ref.shape[0]
+
+    def place(send_ref, held_ref):
+        first_ref[...] = send_ref[:half, :]
+        second_ref[...] = send_ref[half:, :]
+        keep_ref[...] = held_ref[...]
 
     @pl.when(lined)
     def _():
-        send_ref[...] = distant_ref[...]
-        keep_ref[...] = close_ref[...]
+        place(distant_ref, close_ref)
 
     @pl.when(jnp.logical_not(lined))
     def _():
-        send_ref[...] = close_ref[...]
-        keep_ref[...] = distant_ref[...]
+        place(close_ref, distant_ref)
 
 
 def sort(close, distant):
-    shape = jax.ShapeDtypeStruct(close.shape, close.dtype)
+    rows, cols = close.shape
+    half = jax.ShapeDtypeStruct((rows // 2, cols), close.dtype)
     return pl.pallas_call(
         sort_kernel,
-        out_shape=[shape, shape],
+        out_shape=[half, half, jax.ShapeDtypeStruct((rows, cols), close.dtype)],
         in_specs=[vmem_spec()] * 2,
-        out_specs=[vmem_spec()] * 2,
+        out_specs=[vmem_spec()] * 3,
         compiler_params=pltpu.CompilerParams(vmem_limit_bytes=8 * 2**20),
         cost_estimate=pl.CostEstimate(flops=0, bytes_accessed=8 * close.size, transcendentals=0),
         name="sort",
@@ -63,22 +68,28 @@
 
 
 def project_kernel(*refs):
-    pieces, weights, keep_ref, send_ref = refs[:8], refs[8:10], refs[10], refs[11]
-    feats, total, piece_sem = refs[12:]
+    pieces, weights, keep_ref, send_ref = refs[:12], refs[12:14], refs[14], refs[15]
+    feats, total, piece_sem = refs[16:]
     node, head = lax.axis_index("node"), lax.axis_index("head")
     side, core = node // 2, node % 2
     slot = (head // 2) % 2 ^ jnp.where(in_line(node, head), 0, 1)
     near = head % 2
+    _, rows, depth = feats.shape
     copies = []
-    for i in range(8):
-        block, plane, other = i // 4, (i // 2) % 2, i % 2
+    for i in range(12):
+        if i < 4:
+            block, plane, other, start, count = 0, i // 2, i % 2, 0, rows
+        else:
+            block, plane, other = 1, (i - 4) // 4, (i - 4) // 2 % 2
+            start, count = i % 2 * (rows // 2), rows // 2
         place = 4 * block + 2 * (slot ^ plane) + (near ^ other)
-        copy = pltpu.make_async_copy(pieces[i], feats.at[place], piece_sem.at[i])
+        copy = pltpu.make_async_copy(
+            pieces[i], feats.at[place, pl.ds(start, count)], piece_sem.at[i]
+        )
         copy.start()
         copies.append(copy)
     for copy in copies:
         copy.wait()
-    _, rows, depth = feats.shape
     width = keep_ref.shape[1]
     for block in range(2):
         for i in range(2):
@@ -109,12 +120,12 @@
             jax.ShapeDtypeStruct((2 * rows, cols // 2), jnp.float32),
             jax.ShapeDtypeStruct((2 * rows, cols // 2), jnp.bfloat16),
         ],
-        in_specs=[vmem_spec()] * 10,
+        in_specs=[vmem_spec()] * 14,
         out_specs=[vmem_spec()] * 2,
         scratch_shapes=[
             pltpu.VMEM((8, rows, depth), jnp.bfloat16),
             pltpu.VMEM((rows, cols), jnp.float32),
-            pltpu.SemaphoreType.DMA((8,)),
+            pltpu.SemaphoreType.DMA((12,)),
         ],
         compiler_params=pltpu.CompilerParams(vmem_limit_bytes=20 * 2**20),
         cost_estimate=pl.CostEstimate(flops=flops, bytes_accessed=moved, transcendentals=0),
@@ -147,29 +158,24 @@
     )(keep, moved)
 
 
-def attend_kernel(bias_ref, *refs):
-    edges, held, outs = refs[:4], refs[4:8], refs[8:12]
+def weigh_kernel(edge_ref, bias_ref, mine_ref, theirs_ref, weight_ref, total_ref):
     node = lax.axis_index("node")
     inv_root = 1.0 / DH**0.5
-    rows = outs[0].shape[0]
+    rows = mine_ref.shape[0] // 2
     tiles = rows // TILE
-
-    def block_of(pair, i):
-        return pair[i % 2], (i // 2) * rows
-
+    held = (mine_ref, theirs_ref)
     for i in range(4):
         for ti in range(tiles):
-            ref, base = block_of(held[:2], i)
-            mine = ref[base + ti * TILE : base + (ti + 1) * TILE, :]
+            base = i // 2 * rows + ti * TILE
+            queries = held[i % 2][base : base + TILE, :]
             scores = []
             for j in range(4):
-                ref, base = block_of(held[:2], j)
+                keys = held[j % 2][j // 2 * rows : (j // 2 + 1) * rows, :]
                 raw = lax.dot_general(
-                    mine, ref[base : base + rows, :], (((1,), (1,)), ((), ())),
-                    preferred_element_type=jnp.float32,
+                    queries, keys, (((1,), (1,)), ((), ())), preferred_element_type=jnp.float32
                 )
                 for tj in range(tiles):
-                    relation = edges[i][ti, tiles * (node ^ j) + tj]
+                    relation = edge_ref[i, ti, tiles * (node ^ j) + tj]
                     part = raw[:, tj * TILE : (tj + 1) * TILE] * inv_root + bias_ref[node, relation]
                     if i == j and ti == tj:
                         row_ids = lax.broadcasted_iota(jnp.int32, (TILE, TILE), 0)
@@ -179,32 +185,59 @@
             top = functools.reduce(jnp.maximum, scores)
             top = jnp.max(top, axis=1, keepdims=True)
             expd = [jnp.exp(part - top) for part in scores]
-            total = jnp.sum(functools.reduce(jnp.add, expd), axis=1, keepdims=True)
-            mixed = None
-            for j in range(4):
-                block = jnp.concatenate(
-                    [part.astype(jnp.bfloat16) for part in expd[tiles * j : tiles * (j + 1)]], axis=1
-                )
-                ref, base = block_of(held[2:], j)
-                term = jnp.dot(block, ref[base : base + rows, :], preferred_element_type=jnp.float32)
-                mixed = term if mixed is None else mixed + term
-            outs[i][ti * TILE : (ti + 1) * TILE, :] = (mixed / total).astype(jnp.bfloat16)
-
-
-def attend(bias, edges, queries, values):
-    rows = queries[0].shape[0] // 2
-    nodes = 4 * rows
+            here = slice(i * rows + ti * TILE, i * rows + (ti + 1) * TILE)
+            total_ref[here, :] = jnp.sum(functools.reduce(jnp.add, expd), axis=1, keepdims=True)
+            for k, part in enumerate(expd):
+                weight_ref[here, k * TILE : (k + 1) * TILE] = part.astype(jnp.bfloat16)
+
+
+def weigh(edges, bias, mine, theirs):
+    nodes = 2 * mine.shape[0]
     return pl.pallas_call(
-        attend_kernel,
-        out_shape=[jax.ShapeDtypeStruct((rows, DH), jnp.bfloat16)] * 4,
-        in_specs=[smem_spec()] * 5 + [vmem_spec()] * 4,
-        out_specs=[vmem_spec()] * 4,
+        weigh_kernel,
+        out_shape=[
+            jax.ShapeDtypeStruct((nodes, nodes), jnp.bfloat16),
+            jax.ShapeDtypeStruct((nodes, 1), jnp.float32),
+        ],
+        in_specs=[smem_spec()] * 2 + [vmem_spec()] * 2,
+        out_specs=[vmem_spec()] * 2,
         compiler_params=pltpu.CompilerParams(vmem_limit_bytes=16 * 2**20),
         cost_estimate=pl.CostEstimate(
-            flops=4 * nodes * nodes * DH, bytes_accessed=6 * nodes * DH, transcendentals=nodes * nodes
+            flops=2 * nodes * nodes * DH, bytes_accessed=2 * nodes * nodes, transcendentals=nodes * nodes
         ),
-        name="attend",
-    )(bias, *edges, *queries, *values)
+        name="weigh",
+    )(edges, bias, mine, theirs)
+
+
+def average_kernel(blocks, weight_ref, total_ref, mine_ref, theirs_ref, *outs):
+    rows = mine_ref.shape[0] // 2
+    held = (mine_ref, theirs_ref)
+    for out_ref, i in zip(outs, blocks):
+        here = slice(i * rows, (i + 1) * rows)
+        mixed = None
+        for j in range(4):
+            term = jnp.dot(
+                weight_ref[here, j * rows : (j + 1) * rows],
+                held[j % 2][j // 2 * rows : (j // 2 + 1) * rows, :],
+                preferred_element_type=jnp.float32,
+            )
+            mixed = term if mixed is None else mixed + term
+        out_ref[...] = (mixed / total_ref[here, :]).astype(jnp.bfloat16)
+
+
+def average(blocks, weights, total, mine, theirs):
+    rows = mine.shape[0] // 2
+    return pl.pallas_call(
+        functools.partial(average_kernel, blocks),
+        out_shape=[jax.ShapeDtypeStruct((rows, DH), jnp.bfloat16)] * len(blocks),
+        in_specs=[vmem_spec()] * 4,
+        out_specs=[vmem_spec()] * len(blocks),
+        compiler_params=pltpu.CompilerParams(vmem_limit_bytes=16 * 2**20),
+        cost_estimate=pl.CostEstimate(
+            flops=8 * len(blocks) * rows * rows * DH, bytes_accessed=weights.size, transcendentals=0
+        ),
+        name="average",
+    )(weights, total, mine, theirs)
 
 
 def emit_kernel(counts, *refs):
@@ -213,7 +246,7 @@
     for count in counts:
         weights.append(refs[:count])
         refs = refs[count:]
-    outs, heads, terms = refs[:8], refs[8], refs[9]
+    outs, heads, terms = refs[:9], refs[9], refs[10]
     node, head = lax.axis_index("node"), lax.axis_index("head")
     far, near = head // 2, head % 2
     for i in range(4):
@@ -233,21 +266,26 @@
                 )
                 total, first = term if total is None else total + term, last
             terms[4 * side + plane] = total.astype(jnp.bfloat16)
-    for i in range(8):
+    first = outs[7].shape[0]
+    for i in range(7):
         outs[i][...] = terms[i]
+    outs[7][...] = terms[7, :first, :]
+    outs[8][...] = terms[7, first:, :]
 
 
 def emit(parts, weights):
     rows = parts[0].shape[0]
     depth, cols = weights[0][0].shape
     counts = [len(pieces) for pieces in weights]
+    first = 3 * rows // 8
     flops = 2 * rows * depth * 4 * cols
     moved = 2 * (rows * depth + 4 * depth * cols + 4 * rows * cols)
     return pl.pallas_call(
         functools.partial(emit_kernel, counts),
-        out_shape=[jax.ShapeDtypeStruct((rows, cols // 2), jnp.bfloat16)] * 8,
+        out_shape=[jax.ShapeDtypeStruct((rows, cols // 2), jnp.bfloat16)] * 7
+        + [jax.ShapeDtypeStruct((part, cols // 2), jnp.bfloat16) for part in (first, rows - first)],
         in_specs=[vmem_spec()] * (4 + sum(counts)),
-        out_specs=[vmem_spec()] * 8,
+        out_specs=[vmem_spec()] * 9,
         scratch_shapes=[
             pltpu.VMEM((4, rows, DH), jnp.bfloat16),
             pltpu.VMEM((8, rows, cols // 2), jnp.bfloat16),
@@ -259,53 +297,60 @@
 
 
 def one_head_each(node_feats, w_qk, w_val, w_out, edge_types, rel_bias):
-    depth = w_out.shape[0]
+    depth, rows = w_out.shape[0], node_feats.shape[0]
     across = functools.partial(swap, axis="node", mask=2)
     beside = functools.partial(swap, axis="node", mask=1)
     along = functools.partial(swap, axis="head", mask=1)
 
-    edges = [edge_types] + [swap(edge_types, "node", i) for i in range(1, 4)]
     far = {i: swap(node_feats, "head", 2 * i) for i in (3, 2, 1)}
-    out_first = across(after(w_out[: depth // 2], *edges))
-    send_0, keep_0 = sort(node_feats, far[3])
-    moved_0, keep_0y = across(send_0), along(keep_0)
-    out_second = across(after(w_out[depth // 2 : 3 * depth // 4], moved_0, out_first))
-    moved_0y = along(moved_0)
-    send_1, keep_1 = sort(*lax.optimization_barrier((far[1], far[2], keep_0y))[:2])
-    moved_1, keep_1y = across(send_1), along(keep_1)
-    moved_1y = along(moved_1)
-    out_third = across(after(w_out[3 * depth // 4 :], moved_1, out_second))
-    qk_beside, val_beside, out_beside = beside(w_qk), beside(w_val), beside(w_out)
-    qk_beside = after(qk_beside, out_first)
-
-    pieces = [keep_0, keep_0y, keep_1, keep_1y, moved_0, moved_0y, moved_1, moved_1y]
+    out_first = across(w_out[: 5 * depth // 8])
+    tiles = jnp.stack([edge_types, beside(edge_types)])
+    *send_0, keep_0 = sort(node_feats, after(far[3], out_first))
+    keep_0y = along(keep_0)
+    moved_0 = [across(part) for part in send_0]
+    moved_0y = [along(part) for part in moved_0]
+    gate = (keep_0y, moved_0[1], moved_0y[0], tiles)
+    close, distant = lax.optimization_barrier((far[1], far[2], *gate))[:2]
+    *send_1, keep_1 = sort(close, distant)
+    moved_1 = [across(part) for part in send_1]
+    keep_1y = along(keep_1)
+    moved_1y = [along(part) for part in moved_1]
+    out_second = across(after(w_out[5 * depth // 8 :], moved_1[1]))
+    qk_beside, val_beside = beside(w_qk), beside(w_val)
+    edges = jnp.concatenate([tiles, across(after(tiles, moved_1[0]))])
+
+    keep_1y = after(keep_1y, edges)
+    pieces = [keep_0, keep_0y, keep_1, keep_1y, *moved_0, *moved_0y, *moved_1, *moved_1y]
     qk_keep, qk_send = project(pieces, [w_qk, qk_beside])
-    qk_moved = across(after(qk_send, out_third))
+    qk_moved = across(qk_send)
     val_keep, val_send = project(pieces, [w_val, val_beside])
-    val_moved = across(after(val_send, out_third))
-    qk_mine, qk_give = combine(qk_keep, qk_moved)
-    qk_theirs = beside(qk_give)
-    val_mine, val_give = combine(val_keep, val_moved)
-    val_theirs = beside(val_give)
-    attn = attend(rel_bias.T, edges, [qk_mine, qk_theirs], [val_mine, val_theirs])
+    val_moved = across(val_send)
+    qk_mine, qk_give = combine(qk_keep, after(qk_moved, val_send, out_second))
+    weights, total = weigh(edges, rel_bias.T, qk_mine, beside(qk_give))
+    val_mine, val_give = combine(val_keep, after(val_moved, total))
+    attn = average((0, 1, 2, 3), weights, total, val_mine, beside(val_give))
     attn = [attn[0]] + [swap(attn[i], "node", i) for i in range(1, 4)]
 
-    out_across = [out_first, out_second, out_third]
-    out_diagonal = [beside(after(piece, qk_moved)) for piece in out_across]
+    out_across = [out_first, out_second]
+    out_beside = beside(after(w_out, moved_1[0]))
+    out_diagonal = [beside(after(out_first, moved_1[0])), beside(out_second)]
     terms = emit(attn, [[w_out], [out_beside], out_across, out_diagonal])
-    total, other, pairs = None, {}, {}
-    for i in (3, 2, 1, 0):
-        send = terms[4 + i]
-        if i < 2:
-            send = after(send, pairs[i + 2])
-        other[i] = along(send)
-        pair = terms[i].astype(jnp.float32) + other[i].astype(jnp.float32)
-        if i > 0:
-            pairs[i] = pair.astype(jnp.bfloat16)
-        else:
-            total = pair
-    for i in (3, 2, 1):
-        total = total + swap(pairs[i], "head", 2 * i).astype(jnp.float32)
+
+    def pair(mine, send):
+        return mine.astype(jnp.float32) + along(send).astype(jnp.float32)
+
+    first = terms[7].shape[0]
+    pair_3 = [
+        pair(terms[3][:first], terms[7]).astype(jnp.bfloat16),
+        pair(terms[3][first:], terms[8]).astype(jnp.bfloat16),
+    ]
+    home_3 = [swap(part, "head", 6) for part in pair_3]
+    pair_2 = pair(terms[2], after(terms[6], pair_3[0])).astype(jnp.bfloat16)
+    pair_1 = pair(terms[1], after(terms[5], pair_3[1])).astype(jnp.bfloat16)
+    total = pair(terms[0], after(terms[4], home_3[0]))
+    total = total + swap(pair_2, "head", 4).astype(jnp.float32)
+    total = total + swap(after(pair_1, home_3[1]), "head", 2).astype(jnp.float32)
+    total = total + jnp.concatenate(home_3).astype(jnp.float32)
     return total.astype(jnp.bfloat16)
 
 

time: 120 us -> 121 us (level)
  waiting for transfers between devices: 72.5 us -> 61 us
  starting transfers between devices: 35.4 us -> 44.2 us
  Pallas kernels: 8.53 us -> 10.6 us
  other arithmetic: 1.07 us -> 2.43 us
    ppermute x35 -> x38, waiting for transfers between devices: 72.5 us -> 61 us  [swap(): return lax.ppermute(value, axis, [(i, i ^ mask) for i in range(peers)])]
    ppermute x35 -> x38, starting transfers between devices: 35.4 us -> 44.2 us  [swap(): return lax.ppermute(value, axis, [(i, i ^ mask) for i in range(peers)])]
    pallas_call x2, Pallas kernels: 3.05 us -> 5.83 us  [project(): pl.pallas_call(project_kernel, out_shape=[jax.ShapeDtypeStruct((2 * rows,...]
    pallas_call x3 -> x4, Pallas kernels: 3.67 us -> 2.96 us  [the longest x1 2.19 us: weigh(): pl.pallas_call(weigh_kernel, out_shape=[jax.ShapeDtypeStruct((nodes, node...]
  transfers between devices with their start and end apart: 35 -> 38, of which waited for: 20 -> 23; matrix products, arithmetic and copies ran while one was open for 1% -> 1% of each run, Pallas kernels for 6% -> 7%
where the time goes in v5:
time: 121 us
  waiting for transfers between devices  61 us (50%)
  starting transfers between devices  44.2 us (37%)
  Pallas kernels  10.6 us (9%)
  other arithmetic  2.43 us (2%)
  local copies, waits for them, and re-layouts  2.3 us (2%)
    ppermute x38, waiting for transfers between devices, swap(): return lax.ppermute(value, axis, [(i, i ^ mask) for i in range(peers)])  61 us
    ppermute x38, starting transfers between devices, swap(): return lax.ppermute(value, axis, [(i, i ^ mask) for i in range(peers)])  44.2 us
    pallas_call x2, Pallas kernels, project(): pl.pallas_call(project_kernel, out_shape=[jax.ShapeDtypeStruct((2 * rows,...  5.83 us
  transfers between devices with their start and end apart: 38, of which 23 were waited for; matrix products, arithmetic and copies ran while one was open for 1% of the time, Pallas kernels for 7%

profile of v5, /device:TPU:0, one launch (start us, length us, event | category | flops | bytes accessed | tf_op | source)
XLA Modules:
  0.0 120.7 jit_solution(1908706090079539397)
XLA Ops:
  0.0 1.3 %slice.12 = bf16[320,1024]{1,0:T(8,128)(2,1)S(1)} slice(bf16[512,1024]{1,0:T(8,128)(2,1)} %refs_4_.1), slice={[0:320], [0:1024]} | slice | bytes 1310720 | tf_op jit(solution)/shard_map/slice | solution.py:306
  1.3 3.0 %collective-permute-start.4 = (bf16[320,1024]{1,0:T(8,128)(2,1)S(1)}, bf16[320,1024]{1,0:T(8,128)(2,1)S(1)}, u32[]{:S(2)}, u32[]{:S(2)}) collective-permute-start(bf16[320,1024]{1,0:T(8,128)(2,1)S(1)} %slice.12), channel_id=1, source_target_pairs={{0,16},{8,24},{16,0},{24,8},{1,17},{9,25},{17,1},{25,9},{2,18},{10... | collective-permute-start | bytes 1966088 | tf_op jit(solution)/shard_map/ppermute | solution.py:19
  4.3 3.6 %collective-permute-start.3 = (bf16[256,512]{1,0:T(8,128)(2,1)}, bf16[256,512]{1,0:T(8,128)(2,1)S(1)}, u32[]{:S(2)}, u32[]{:S(2)}) collective-permute-start(bf16[256,512]{1,0:T(8,128)(2,1)} %close_ref.1), channel_id=1, source_target_pairs={{0,6},{1,7},{2,4},{3,5},{4,2},{5,3},{6,0},{7,1},{8,14},{9,15},{10,... | collective-permute-start | bytes 786440 | tf_op jit(solution)/shard_map/ppermute | solution.py:19
  7.9 0.2 collective-permute-start.18
  8.1 7.4 %collective-permute-done.3.distant_ref = bf16[256,512]{1,0:T(8,128)(2,1)S(1)} collective-permute-done((bf16[256,512]{1,0:T(8,128)(2,1)}, bf16[256,512]{1,0:T(8,128)(2,1)S(1)}, u32[]{:S(2)}, u32[]{:S(2)}) %collective-permute-start.3) | collective-permute-done | bytes 262176 | tf_op jit(solution)/shard_map/ppermute | solution.py:19
  15.5 5.9 %collective-permute-start.2 = (bf16[256,512]{1,0:T(8,128)(2,1)}, bf16[256,512]{1,0:T(8,128)(2,1)S(1)}, u32[]{:S(2)}, u32[]{:S(2)}) collective-permute-start(bf16[256,512]{1,0:T(8,128)(2,1)} %close_ref.1), channel_id=1, source_target_pairs={{0,4},{1,5},{2,6},{3,7},{4,0},{5,1},{6,2},{7,3},{8,12},{9,13},{10,... | collective-permute-start | bytes 786440 | tf_op jit(solution)/shard_map/ppermute | solution.py:19
  21.4 1.0 copy-done.3
  22.5 0.3 collective-permute-done
  22.8 0.5 collective-permute-start.7
  23.3 1.5 %collective-permute-start.5 = (bf16[256,512]{1,0:T(8,128)(2,1)S(1)}, bf16[256,512]{1,0:T(8,128)(2,1)S(1)}, u32[]{:S(2)}, u32[]{:S(2)}) collective-permute-start(bf16[256,512]{1,0:T(8,128)(2,1)S(1)} %get-tuple-element.49.refs_0_), channel_id=1, source_target_pairs={{0,1},{1,0},{2,3},{3,2},{4,5},{5,4},{6,7},{7,6},{8,9},{9,8},{10,11... | collective-permute-start | bytes 786440 | tf_op jit(solution)/shard_map/ppermute | solution.py:19
  24.8 8.6 %collective-permute-done.2.distant_ref = bf16[256,512]{1,0:T(8,128)(2,1)S(1)} collective-permute-done((bf16[256,512]{1,0:T(8,128)(2,1)}, bf16[256,512]{1,0:T(8,128)(2,1)S(1)}, u32[]{:S(2)}, u32[]{:S(2)}) %collective-permute-start.2) | collective-permute-done | bytes 262176 | tf_op jit(solution)/shard_map/ppermute | solution.py:19
  33.5 0.5 collective-permute-start.6
  34.0 1.5 %collective-permute-start.8 = (bf16[128,512]{1,0:T(8,128)(2,1)S(1)}, bf16[128,512]{1,0:T(8,128)(2,1)S(1)}, u32[]{:S(2)}, u32[]{:S(2)}) collective-permute-start(bf16[128,512]{1,0:T(8,128)(2,1)S(1)} %collective-permute-done.7.refs_4_), channel_id=1, source_target_pairs={{0,1},{1,0},{2,3},{3,2},{4,5},{5,4},{6,7},{7,6},{8,9},{9,8},{10,11... | collective-permute-start | bytes 393224 | tf_op jit(solution)/shard_map/ppermute | solution.py:19
  35.5 0.7 pad_add_fusion.1
  36.2 2.2 %collective-permute-done.6.refs_5_ = bf16[128,512]{1,0:T(8,128)(2,1)S(1)} collective-permute-done((bf16[128,512]{1,0:T(8,128)(2,1)S(1)}, bf16[128,512]{1,0:T(8,128)(2,1)S(1)}, u32[]{:S(2)}, u32[]{:S(2)}) %collective-permute-start.6) | collective-permute-done | bytes 131104 | tf_op jit(solution)/shard_map/ppermute | solution.py:19
  38.4 0.5 collective-permute-done.8.refs_6_
  39.0 1.6 %collective-permute-start.9 = (bf16[128,512]{1,0:T(8,128)(2,1)S(1)}, bf16[128,512]{1,0:T(8,128)(2,1)S(1)}, u32[]{:S(2)}, u32[]{:S(2)}) collective-permute-start(bf16[128,512]{1,0:T(8,128)(2,1)S(1)} %get-tuple-element.54), channel_id=1, source_target_pairs={{0,16},{8,24},{16,0},{24,8},{1,17},{9,25},{17,1},{25,9},{2,18},{10... | collective-permute-start | bytes 393224 | tf_op jit(solution)/shard_map/ppermute | solution.py:19
  40.6 1.5 %collective-permute-start.12 = (bf16[128,512]{1,0:T(8,128)(2,1)S(1)}, bf16[128,512]{1,0:T(8,128)(2,1)S(1)}, u32[]{:S(2)}, u32[]{:S(2)}) collective-permute-start(bf16[128,512]{1,0:T(8,128)(2,1)S(1)} %collective-permute-done.6.refs_5_), channel_id=1, source_target_pairs={{0,1},{1,0},{2,3},{3,2},{4,5},{5,4},{6,7},{7,6},{8,9},{9,8},{10,11... | collective-permute-start | bytes 393224 | tf_op jit(solution)/shard_map/ppermute | solution.py:19
  42.1 0.5 collective-permute-start.11
  42.6 1.5 %collective-permute-done.9.refs_8_ = bf16[128,512]{1,0:T(8,128)(2,1)S(1)} collective-permute-done((bf16[128,512]{1,0:T(8,128)(2,1)S(1)}, bf16[128,512]{1,0:T(8,128)(2,1)S(1)}, u32[]{:S(2)}, u32[]{:S(2)}) %collective-permute-start.9) | collective-permute-done | bytes 131104 | tf_op jit(solution)/shard_map/ppermute | solution.py:19
  44.0 2.5 %collective-permute-done.12.refs_7_ = bf16[128,512]{1,0:T(8,128)(2,1)S(1)} collective-permute-done((bf16[128,512]{1,0:T(8,128)(2,1)S(1)}, bf16[128,512]{1,0:T(8,128)(2,1)S(1)}, u32[]{:S(2)}, u32[]{:S(2)}) %collective-permute-start.12) | collective-permute-done | bytes 131104 | tf_op jit(solution)/shard_map/ppermute | solution.py:19
  46.5 0.4 collective-permute-start.13
  46.9 4.6 %collective-permute-done.13.refs_9_ = bf16[128,512]{1,0:T(8,128)(2,1)S(1)} collective-permute-done((bf16[128,512]{1,0:T(8,128)(2,1)S(1)}, bf16[128,512]{1,0:T(8,128)(2,1)S(1)}, u32[]{:S(2)}, u32[]{:S(2)}) %collective-permute-start.13) | collective-permute-done | bytes 131104 | tf_op jit(solution)/shard_map/ppermute | solution.py:19
  51.5 0.3 collective-permute-start.10
  51.8 1.5 %collective-permute-start.14 = (bf16[128,512]{1,0:T(8,128)(2,1)S(1)}, bf16[128,512]{1,0:T(8,128)(2,1)S(1)}, u32[]{:S(2)}, u32[]{:S(2)}) collective-permute-start(bf16[128,512]{1,0:T(8,128)(2,1)S(1)} %collective-permute-done.9.refs_8_), channel_id=1, source_target_pairs={{0,1},{1,0},{2,3},{3,2},{4,5},{5,4},{6,7},{7,6},{8,9},{9,8},{10,11... | collective-permute-start | bytes 393224 | tf_op jit(solution)/shard_map/ppermute | solution.py:19
  53.4 1.7 %collective-permute-done.10 = s32[2,2,8]{2,1,0:T(2,128)S(1)} collective-permute-done((s32[2,2,8]{2,1,0:T(2,128)S(1)}, s32[2,2,8]{2,1,0:T(2,128)S(1)}, u32[]{:S(2)}, u32[]{:S(2)}) %collective-permute-start.10) | collective-permute-done | bytes 160 | tf_op jit(solution)/shard_map/ppermute | solution.py:19
  55.1 1.5 %collective-permute-start.15 = (bf16[128,512]{1,0:T(8,128)(2,1)S(1)}, bf16[128,512]{1,0:T(8,128)(2,1)S(1)}, u32[]{:S(2)}, u32[]{:S(2)}) collective-permute-start(bf16[128,512]{1,0:T(8,128)(2,1)S(1)} %collective-permute-done.13.refs_9_), channel_id=1, source_target_pairs={{0,1},{1,0},{2,3},{3,2},{4,5},{5,4},{6,7},{7,6},{8,9},{9,8},{10,11... | collective-permute-start | bytes 393224 | tf_op jit(solution)/shard_map/ppermute | solution.py:19
  56.7 0.4 collective-permute-start.19
  57.1 0.7 pad_add_fusion.edge_ref
  57.8 0.1 collective-permute-start.27
  57.8 2.2 %collective-permute-done.15.refs_11_ = bf16[128,512]{1,0:T(8,128)(2,1)S(1)} collective-permute-done((bf16[128,512]{1,0:T(8,128)(2,1)S(1)}, bf16[128,512]{1,0:T(8,128)(2,1)S(1)}, u32[]{:S(2)}, u32[]{:S(2)}) %collective-permute-start.15) | collective-permute-done | bytes 131104 | tf_op jit(solution)/shard_map/ppermute | solution.py:19
  60.1 2.9 %project.2 = (f32[512,256]{1,0:T(8,128)S(1)}, bf16[512,256]{1,0:T(8,128)(2,1)S(1)}) custom-call(bf16[256,512]{1,0:T(8,128)(2,1)S(1)} %get-tuple-element.49.refs_0_, bf16[256,512]{1,0:T(8,128)(2,1)S(1)} %collective-permute-done.5.refs_1_, bf16[256,512]{1,0:T(8,128)(2,1)S(1)} %get-tuple-element.56.refs_2_, ...), custom_call_target="tpu_custom_call" | custom-call | flops 1073741824 | bytes 4980736 | tf_op jit(solution)/shard_map/project/pallas_call | solution.py:117
  63.0 0.4 collective-permute-start.17
  63.4 2.9 %project.3 = (f32[512,256]{1,0:T(8,128)S(1)}, bf16[512,256]{1,0:T(8,128)(2,1)S(1)}) custom-call(bf16[256,512]{1,0:T(8,128)(2,1)S(1)} %get-tuple-element.49.refs_0_, bf16[256,512]{1,0:T(8,128)(2,1)S(1)} %collective-permute-done.5.refs_1_, bf16[256,512]{1,0:T(8,128)(2,1)S(1)} %get-tuple-element.56.refs_2_, ...), custom_call_target="tpu_custom_call" | custom-call | flops 1073741824 | bytes 4980736 | tf_op jit(solution)/shard_map/project/pallas_call | solution.py:117
  66.3 1.8 %collective-permute-start.21 = (bf16[512,256]{1,0:T(8,128)(2,1)S(1)}, bf16[512,256]{1,0:T(8,128)(2,1)S(1)}, u32[]{:S(2)}, u32[]{:S(2)}) collective-permute-start(bf16[512,256]{1,0:T(8,128)(2,1)S(1)} %get-tuple-element.61), channel_id=1, source_target_pairs={{0,16},{8,24},{16,0},{24,8},{1,17},{9,25},{17,1},{25,9},{2,18},{10... | collective-permute-start | bytes 786440 | tf_op jit(solution)/shard_map/ppermute | solution.py:19
  68.1 3.7 %collective-permute-done.17.moved_ref = bf16[512,256]{1,0:T(8,128)(2,1)S(1)} collective-permute-done((bf16[512,256]{1,0:T(8,128)(2,1)S(1)}, bf16[512,256]{1,0:T(8,128)(2,1)S(1)}, u32[]{:S(2)}, u32[]{:S(2)}) %collective-permute-start.17) | collective-permute-done | bytes 262176 | tf_op jit(solution)/shard_map/ppermute | solution.py:19
  72.0 1.3 %collective-permute-done.20.theirs_ref = bf16[512,128]{1,0:T(8,128)(2,1)S(1)} collective-permute-done((bf16[512,128]{1,0:T(8,128)(2,1)S(1)}, bf16[512,128]{1,0:T(8,128)(2,1)S(1)}, u32[]{:S(2)}, u32[]{:S(2)}) %collective-permute-start.20) | collective-permute-done | bytes 131104 | tf_op jit(solution)/shard_map/ppermute | solution.py:19
  73.3 2.2 %weigh.1 = (bf16[1024,1024]{1,0:T(8,128)(2,1)S(1)}, f32[1024,1]{1,0:T(8,128)S(1)}) custom-call(s32[4,2,8]{2,1,0:T(2,128)S(1)} %pad_add_fusion.edge_ref, f32[4,237]{1,0:T(4,128)S(1)} %bitcast.3, bf16[512,128]{1,0:T(8,128)(2,1)S(1)} %get-tuple-element.64.mine_ref, bf16[512,128]{1,0:T(8,128)(2,1)S(1)} %collective-permute-done.20.theirs_ref), custom_call_target="tpu_custom_call" | custom-call | flops 268435456 | bytes 2097152 | tf_op jit(solution)/shard_map/weigh/pallas_call | solution.py:196
  75.5 0.2 collective-permute-done.21.moved_ref
  75.9 1.3 %collective-permute-done.22.theirs_ref = bf16[512,128]{1,0:T(8,128)(2,1)S(1)} collective-permute-done((bf16[512,128]{1,0:T(8,128)(2,1)S(1)}, bf16[512,128]{1,0:T(8,128)(2,1)S(1)}, u32[]{:S(2)}, u32[]{:S(2)}) %collective-permute-start.22) | collective-permute-done | bytes 131104 | tf_op jit(solution)/shard_map/ppermute | solution.py:19
  77.2 0.7 average.1
  77.9 0.2 collective-permute-start.23
  78.1 1.1 collective-permute-start.24
  79.3 0.6 collective-permute-start.25
  79.8 2.9 %collective-permute-done.24.refs_2_ = bf16[256,128]{1,0:T(8,128)(2,1)S(1)} collective-permute-done((bf16[256,128]{1,0:T(8,128)(2,1)S(1)}, bf16[256,128]{1,0:T(8,128)(2,1)S(1)}, u32[]{:S(2)}, u32[]{:S(2)}) %collective-permute-start.24) | collective-permute-done | bytes 65568 | tf_op jit(solution)/shard_map/ppermute | solution.py:19
  82.8 0.8 collective-permute-done.25.refs_3_
  83.6 1.7 %emit.1 = (bf16[256,512]{1,0:T(8,128)(2,1)S(1)}, bf16[256,512]{1,0:T(8,128)(2,1)S(1)}, bf16[256,512]{1,0:T(8,128)(2,1)S(1)}, bf16[256,512]{1,0:T(8,128)(2,1)S(1)...) custom-call(bf16[256,128]{1,0:T(8,128)(2,1)S(1)} %get-tuple-element., ...), custom_call_target="tpu_custom_call" | custom-call | flops 1073741824 | bytes 6553600 | tf_op jit(solution)/shard_map/emit/pallas_call | solution.py:283
  85.3 1.1 collective-permute-start.29
  86.4 1.0 collective-permute-start.34
  87.4 3.6 %collective-permute-done.29 = bf16[96,512]{1,0:T(8,128)(2,1)S(1)} collective-permute-done((bf16[96,512]{1,0:T(8,128)(2,1)S(1)}, bf16[96,512]{1,0:T(8,128)(2,1)S(1)}, u32[]{:S(2)}, u32[]{:S(2)}) %collective-permute-start.29) | collective-permute-done | bytes 98336 | tf_op jit(solution)/shard_map/ppermute | solution.py:19
  91.0 1.1 collective-permute-start.32
  92.1 1.4 %collective-permute-start.30 = (bf16[96,512]{1,0:T(8,128)(2,1)S(1)}, bf16[96,512]{1,0:T(8,128)(2,1)S(1)}, u32[]{:S(2)}, u32[]{:S(2)}) collective-permute-start(bf16[96,512]{1,0:T(8,128)(2,1)S(1)} %add_convert_fusion.4), channel_id=1, source_target_pairs={{0,6},{1,7},{2,4},{3,5},{4,2},{5,3},{6,0},{7,1},{8,14},{9,15},{10,... | collective-permute-start | bytes 294920 | tf_op jit(solution)/shard_map/ppermute | solution.py:19
  93.4 1.1 collective-permute-done.34
  94.5 1.1 collective-permute-start.35
  95.6 1.4 %collective-permute-start.36 = (bf16[160,512]{1,0:T(8,128)(2,1)S(1)}, bf16[160,512]{1,0:T(8,128)(2,1)S(1)}, u32[]{:S(2)}, u32[]{:S(2)}) collective-permute-start(bf16[160,512]{1,0:T(8,128)(2,1)S(1)} %add_convert_fusion.3), channel_id=1, source_target_pairs={{0,6},{1,7},{2,4},{3,5},{4,2},{5,3},{6,0},{7,1},{8,14},{9,15},{10,... | collective-permute-start | bytes 491528 | tf_op jit(solution)/shard_map/ppermute | solution.py:19
  97.0 1.8 %collective-permute-done.30 = bf16[96,512]{1,0:T(8,128)(2,1)S(1)} collective-permute-done((bf16[96,512]{1,0:T(8,128)(2,1)S(1)}, bf16[96,512]{1,0:T(8,128)(2,1)S(1)}, u32[]{:S(2)}, u32[]{:S(2)}) %collective-permute-start.30) | collective-permute-done | bytes 98336 | tf_op jit(solution)/shard_map/ppermute | solution.py:19
  98.8 1.1 collective-permute-start.31
  99.9 0.4 collective-permute-done.32
  100.4 1.8 %collective-permute-start.33 = (bf16[256,512]{1,0:T(8,128)(2,1)S(1)}, bf16[256,512]{1,0:T(8,128)(2,1)S(1)}, u32[]{:S(2)}, u32[]{:S(2)}) collective-permute-start(bf16[256,512]{1,0:T(8,128)(2,1)S(1)} %add_convert_fusion.2), channel_id=1, source_target_pairs={{0,4},{1,5},{2,6},{3,7},{4,0},{5,1},{6,2},{7,3},{8,12},{9,13},{10,... | collective-permute-start | bytes 786440 | tf_op jit(solution)/shard_map/ppermute | solution.py:19
  102.2 3.8 %collective-permute-done.35 = bf16[256,512]{1,0:T(8,128)(2,1)S(1)} collective-permute-done((bf16[256,512]{1,0:T(8,128)(2,1)S(1)}, bf16[256,512]{1,0:T(8,128)(2,1)S(1)}, u32[]{:S(2)}, u32[]{:S(2)}) %collective-permute-start.35) | collective-permute-done | bytes 262176 | tf_op jit(solution)/shard_map/ppermute | solution.py:19
  106.0 5.4 %collective-permute-start.37 = (bf16[256,512]{1,0:T(8,128)(2,1)S(1)}, bf16[256,512]{1,0:T(8,128)(2,1)S(1)}, u32[]{:S(2)}, u32[]{:S(2)}) collective-permute-start(bf16[256,512]{1,0:T(8,128)(2,1)S(1)} %add_convert_fusion.1), channel_id=1, source_target_pairs={{0,2},{1,3},{2,0},{3,1},{4,6},{5,7},{6,4},{7,5},{8,10},{9,11},{10,... | collective-permute-start | bytes 786440 | tf_op jit(solution)/shard_map/ppermute | solution.py:19
  111.4 3.8 %collective-permute-done.33 = bf16[256,512]{1,0:T(8,128)(2,1)S(1)} collective-permute-done((bf16[256,512]{1,0:T(8,128)(2,1)S(1)}, bf16[256,512]{1,0:T(8,128)(2,1)S(1)}, u32[]{:S(2)}, u32[]{:S(2)}) %collective-permute-start.33) | collective-permute-done | bytes 262176 | tf_op jit(solution)/shard_map/ppermute | solution.py:19
  115.2 4.6 %collective-permute-done.37 = bf16[256,512]{1,0:T(8,128)(2,1)S(1)} collective-permute-done((bf16[256,512]{1,0:T(8,128)(2,1)S(1)}, bf16[256,512]{1,0:T(8,128)(2,1)S(1)}, u32[]{:S(2)}, u32[]{:S(2)}) %collective-permute-start.37) | collective-permute-done | bytes 262176 | tf_op jit(solution)/shard_map/ppermute | solution.py:19
  119.8 0.9 add_convert_fusion
  (40 shorter events, 0.6 us)
Async XLA Ops:
  0.0 44.0 %copy-start = (bf16[512,1024]{1,0:T(8,128)(2,1)S(1)}, bf16[512,1024]{1,0:T(8,128)(2,1)}, u32[]{:S(2)}) copy-start(bf16[512,1024]{1,0:T(8,128)(2,1)} %refs_4_.1) | copy-start | bytes 3145732
  0.0 60.1 %copy-start.1 = (bf16[1024,512]{1,0:T(8,128)(2,1)S(1)}, bf16[1024,512]{1,0:T(8,128)(2,1)}, u32[]{:S(2)}) copy-start(bf16[1024,512]{1,0:T(8,128)(2,1)} %refs_12_.2) | copy-start | bytes 3145732
  1.3 20.1 %collective-permute-start.4 = (bf16[320,1024]{1,0:T(8,128)(2,1)S(1)}, bf16[320,1024]{1,0:T(8,128)(2,1)S(1)}, u32[]{:S(2)}, u32[]{:S(2)}) collective-permute-start(bf16[320,1024]{1,0:T(8,128)(2,1)S(1)} %slice.12), channel_id=1, source_target_pairs={{0,16},{8,24},{16,0},{24,8},{1,17},{9,25},{17,1},{25,9},{2,18},{10... | collective-permute-start | bytes 1966088 | tf_op jit(solution)/shard_map/ppermute | solution.py:19
  4.3 47.6 %collective-permute-start.16 = (bf16[1024,512]{1,0:T(8,128)(2,1)}, bf16[1024,512]{1,0:T(8,128)(2,1)S(1)}, u32[]{:S(2)}, u32[]{:S(2)}) collective-permute-start(bf16[1024,512]{1,0:T(8,128)(2,1)} %refs_12_.2), channel_id=1, source_target_pairs={{0,8},{8,0},{16,24},{24,16},{1,9},{9,1},{17,25},{25,17},{2,10},{10... | collective-permute-start | bytes 3145736 | tf_op jit(solution)/shard_map/ppermute | solution.py:19
  4.3 11.2 %collective-permute-start.3 = (bf16[256,512]{1,0:T(8,128)(2,1)}, bf16[256,512]{1,0:T(8,128)(2,1)S(1)}, u32[]{:S(2)}, u32[]{:S(2)}) collective-permute-start(bf16[256,512]{1,0:T(8,128)(2,1)} %close_ref.1), channel_id=1, source_target_pairs={{0,6},{1,7},{2,4},{3,5},{4,2},{5,3},{6,0},{7,1},{8,14},{9,15},{10,... | collective-permute-start | bytes 786440 | tf_op jit(solution)/shard_map/ppermute | solution.py:19
  7.9 15.4 %collective-permute-start.1 = (bf16[256,512]{1,0:T(8,128)(2,1)}, bf16[256,512]{1,0:T(8,128)(2,1)S(1)}, u32[]{:S(2)}, u32[]{:S(2)}) collective-permute-start(bf16[256,512]{1,0:T(8,128)(2,1)} %close_ref.1), channel_id=1, source_target_pairs={{0,2},{1,3},{2,0},{3,1},{4,6},{5,7},{6,4},{7,5},{8,10},{9,11},{10,... | collective-permute-start | bytes 786440 | tf_op jit(solution)/shard_map/ppermute | solution.py:19
  7.9 55.5 %collective-permute-start.18 = (bf16[1024,512]{1,0:T(8,128)(2,1)}, bf16[1024,512]{1,0:T(8,128)(2,1)S(1)}, u32[]{:S(2)}, u32[]{:S(2)}) collective-permute-start(bf16[1024,512]{1,0:T(8,128)(2,1)} %refs_12_.3), channel_id=1, source_target_pairs={{0,8},{8,0},{16,24},{24,16},{1,9},{9,1},{17,25},{25,17},{2,10},{10... | collective-permute-start | bytes 3145736 | tf_op jit(solution)/shard_map/ppermute | solution.py:19
  15.5 18.0 %collective-permute-start.2 = (bf16[256,512]{1,0:T(8,128)(2,1)}, bf16[256,512]{1,0:T(8,128)(2,1)S(1)}, u32[]{:S(2)}, u32[]{:S(2)}) collective-permute-start(bf16[256,512]{1,0:T(8,128)(2,1)} %close_ref.1), channel_id=1, source_target_pairs={{0,4},{1,5},{2,6},{3,7},{4,0},{5,1},{6,2},{7,3},{8,12},{9,13},{10,... | collective-permute-start | bytes 786440 | tf_op jit(solution)/shard_map/ppermute | solution.py:19
  21.4 1.4 %collective-permute-start = (s32[2,8]{1,0:T(2,128)}, s32[2,8]{1,0:T(2,128)S(1)}, u32[]{:S(2)}, u32[]{:S(2)}) collective-permute-start(s32[2,8]{1,0:T(2,128)} %param.10), channel_id=1, source_target_pairs={{0,8},{8,0},{16,24},{24,16},{1,9},{9,1},{17,25},{25,17},{2,10},{10... | collective-permute-start | bytes 200 | tf_op jit(solution)/shard_map/ppermute | solution.py:19
  21.4 1.0 copy-start.3
  22.8 11.2 %collective-permute-start.7 = (bf16[128,512]{1,0:T(8,128)(2,1)S(1)}, bf16[128,512]{1,0:T(8,128)(2,1)S(1)}, u32[]{:S(2)}, u32[]{:S(2)}) collective-permute-start(bf16[128,512]{1,0:T(8,128)(2,1)S(1)} %get-tuple-element.51), channel_id=1, source_target_pairs={{0,16},{8,24},{16,0},{24,8},{1,17},{9,25},{17,1},{25,9},{2,18},{10... | collective-permute-start | bytes 393224 | tf_op jit(solution)/shard_map/ppermute | solution.py:19
  23.3 15.6 %collective-permute-start.5 = (bf16[256,512]{1,0:T(8,128)(2,1)S(1)}, bf16[256,512]{1,0:T(8,128)(2,1)S(1)}, u32[]{:S(2)}, u32[]{:S(2)}) collective-permute-start(bf16[256,512]{1,0:T(8,128)(2,1)S(1)} %get-tuple-element.49.refs_0_), channel_id=1, source_target_pairs={{0,1},{1,0},{2,3},{3,2},{4,5},{5,4},{6,7},{7,6},{8,9},{9,8},{10,11... | collective-permute-start | bytes 786440 | tf_op jit(solution)/shard_map/ppermute | solution.py:19
  33.5 5.0 %collective-permute-start.6 = (bf16[128,512]{1,0:T(8,128)(2,1)S(1)}, bf16[128,512]{1,0:T(8,128)(2,1)S(1)}, u32[]{:S(2)}, u32[]{:S(2)}) collective-permute-start(bf16[128,512]{1,0:T(8,128)(2,1)S(1)} %get-tuple-element.50), channel_id=1, source_target_pairs={{0,16},{8,24},{16,0},{24,8},{1,17},{9,25},{17,1},{25,9},{2,18},{10... | collective-permute-start | bytes 393224 | tf_op jit(solution)/shard_map/ppermute | solution.py:19
  34.0 5.0 %collective-permute-start.8 = (bf16[128,512]{1,0:T(8,128)(2,1)S(1)}, bf16[128,512]{1,0:T(8,128)(2,1)S(1)}, u32[]{:S(2)}, u32[]{:S(2)}) collective-permute-start(bf16[128,512]{1,0:T(8,128)(2,1)S(1)} %collective-permute-done.7.refs_4_), channel_id=1, source_target_pairs={{0,1},{1,0},{2,3},{3,2},{4,5},{5,4},{6,7},{7,6},{8,9},{9,8},{10,11... | collective-permute-start | bytes 393224 | tf_op jit(solution)/shard_map/ppermute | solution.py:19
  39.0 5.0 %collective-permute-start.9 = (bf16[128,512]{1,0:T(8,128)(2,1)S(1)}, bf16[128,512]{1,0:T(8,128)(2,1)S(1)}, u32[]{:S(2)}, u32[]{:S(2)}) collective-permute-start(bf16[128,512]{1,0:T(8,128)(2,1)S(1)} %get-tuple-element.54), channel_id=1, source_target_pairs={{0,16},{8,24},{16,0},{24,8},{1,17},{9,25},{17,1},{25,9},{2,18},{10... | collective-permute-start | bytes 393224 | tf_op jit(solution)/shard_map/ppermute | solution.py:19
  40.6 6.0 %collective-permute-start.12 = (bf16[128,512]{1,0:T(8,128)(2,1)S(1)}, bf16[128,512]{1,0:T(8,128)(2,1)S(1)}, u32[]{:S(2)}, u32[]{:S(2)}) collective-permute-start(bf16[128,512]{1,0:T(8,128)(2,1)S(1)} %collective-permute-done.6.refs_5_), channel_id=1, source_target_pairs={{0,1},{1,0},{2,3},{3,2},{4,5},{5,4},{6,7},{7,6},{8,9},{9,8},{10,11... | collective-permute-start | bytes 393224 | tf_op jit(solution)/shard_map/ppermute | solution.py:19
  42.1 14.6 %collective-permute-start.11 = (bf16[256,512]{1,0:T(8,128)(2,1)S(1)}, bf16[256,512]{1,0:T(8,128)(2,1)S(1)}, u32[]{:S(2)}, u32[]{:S(2)}) collective-permute-start(bf16[256,512]{1,0:T(8,128)(2,1)S(1)} %get-tuple-element.56.refs_2_), channel_id=1, source_target_pairs={{0,1},{1,0},{2,3},{3,2},{4,5},{5,4},{6,7},{7,6},{8,9},{9,8},{10,11... | collective-permute-start | bytes 786440 | tf_op jit(solution)/shard_map/ppermute | solution.py:19
  44.0 39.5 %collective-permute-start.26 = (bf16[512,1024]{1,0:T(8,128)(2,1)S(1)}, bf16[512,1024]{1,0:T(8,128)(2,1)S(1)}, u32[]{:S(2)}, u32[]{:S(2)}) collective-permute-start(bf16[512,1024]{1,0:T(8,128)(2,1)S(1)} %copy-done), channel_id=1, source_target_pairs={{0,8},{8,0},{16,24},{24,16},{1,9},{9,1},{17,25},{25,17},{2,10},{10... | collective-permute-start | bytes 3145736 | tf_op jit(solution)/shard_map/ppermute | solution.py:19
  46.5 5.0 %collective-permute-start.13 = (bf16[128,512]{1,0:T(8,128)(2,1)S(1)}, bf16[128,512]{1,0:T(8,128)(2,1)S(1)}, u32[]{:S(2)}, u32[]{:S(2)}) collective-permute-start(bf16[128,512]{1,0:T(8,128)(2,1)S(1)} %get-tuple-element.58), channel_id=1, source_target_pairs={{0,16},{8,24},{16,0},{24,8},{1,17},{9,25},{17,1},{25,9},{2,18},{10... | collective-permute-start | bytes 393224 | tf_op jit(solution)/shard_map/ppermute | solution.py:19
  51.5 3.6 %collective-permute-start.10 = (s32[2,2,8]{2,1,0:T(2,128)S(1)}, s32[2,2,8]{2,1,0:T(2,128)S(1)}, u32[]{:S(2)}, u32[]{:S(2)}) collective-permute-start(s32[2,2,8]{2,1,0:T(2,128)S(1)} %pad_add_fusion.1), channel_id=1, source_target_pairs={{0,16},{8,24},{16,0},{24,8},{1,17},{9,25},{17,1},{25,9},{2,18},{10... | collective-permute-start | bytes 392 | tf_op jit(solution)/shard_map/ppermute | solution.py:19
  51.8 5.9 %collective-permute-start.14 = (bf16[128,512]{1,0:T(8,128)(2,1)S(1)}, bf16[128,512]{1,0:T(8,128)(2,1)S(1)}, u32[]{:S(2)}, u32[]{:S(2)}) collective-permute-start(bf16[128,512]{1,0:T(8,128)(2,1)S(1)} %collective-permute-done.9.refs_8_), channel_id=1, source_target_pairs={{0,1},{1,0},{2,3},{3,2},{4,5},{5,4},{6,7},{7,6},{8,9},{9,8},{10,11... | collective-permute-start | bytes 393224 | tf_op jit(solution)/shard_map/ppermute | solution.py:19
  55.1 5.0 %collective-permute-start.15 = (bf16[128,512]{1,0:T(8,128)(2,1)S(1)}, bf16[128,512]{1,0:T(8,128)(2,1)S(1)}, u32[]{:S(2)}, u32[]{:S(2)}) collective-permute-start(bf16[128,512]{1,0:T(8,128)(2,1)S(1)} %collective-permute-done.13.refs_9_), channel_id=1, source_target_pairs={{0,1},{1,0},{2,3},{3,2},{4,5},{5,4},{6,7},{7,6},{8,9},{9,8},{10,11... | collective-permute-start | bytes 393224 | tf_op jit(solution)/shard_map/ppermute | solution.py:19
  56.7 11.4 %collective-permute-start.19 = (bf16[192,1024]{1,0:T(8,128)(2,1)S(1)}, bf16[192,1024]{1,0:T(8,128)(2,1)S(1)}, u32[]{:S(2)}, u32[]{:S(2)}) collective-permute-start(bf16[192,1024]{1,0:T(8,128)(2,1)S(1)} %slice.13), channel_id=1, source_target_pairs={{0,16},{8,24},{16,0},{24,8},{1,17},{9,25},{17,1},{25,9},{2,18},{10... | collective-permute-start | bytes 1179656 | tf_op jit(solution)/shard_map/ppermute | solution.py:19
  57.8 5.6 %copy-start.2 = (bf16[1024,512]{1,0:T(8,128)(2,1)S(1)}, bf16[1024,512]{1,0:T(8,128)(2,1)}, u32[]{:S(2)}) copy-start(bf16[1024,512]{1,0:T(8,128)(2,1)} %refs_12_.3) | copy-start | bytes 3145732
  57.8 21.5 %collective-permute-start.27 = (bf16[320,1024]{1,0:T(8,128)(2,1)S(1)}, bf16[320,1024]{1,0:T(8,128)(2,1)S(1)}, u32[]{:S(2)}, u32[]{:S(2)}) collective-permute-start(bf16[320,1024]{1,0:T(8,128)(2,1)S(1)} %collective-permute-done.4.refs_6_), channel_id=1, source_target_pairs={{0,8},{8,0},{16,24},{24,16},{1,9},{9,1},{17,25},{25,17},{2,10},{10... | collective-permute-start | bytes 1966088 | tf_op jit(solution)/shard_map/ppermute | solution.py:19
  63.0 10.3 %copy-start.4 = (f32[237,4]{0,1:T(4,128)S(1)}, f32[237,4]{0,1:T(4,128)}, u32[]{:S(2)}) copy-start(f32[237,4]{0,1:T(4,128)} %param.11) | copy-start | bytes 11380
  63.0 8.8 %collective-permute-start.17 = (bf16[512,256]{1,0:T(8,128)(2,1)S(1)}, bf16[512,256]{1,0:T(8,128)(2,1)S(1)}, u32[]{:S(2)}, u32[]{:S(2)}) collective-permute-start(bf16[512,256]{1,0:T(8,128)(2,1)S(1)} %get-tuple-element.60), channel_id=1, source_target_pairs={{0,16},{8,24},{16,0},{24,8},{1,17},{9,25},{17,1},{25,9},{2,18},{10... | collective-permute-start | bytes 786440 | tf_op jit(solution)/shard_map/ppermute | solution.py:19
  66.3 9.4 %collective-permute-start.21 = (bf16[512,256]{1,0:T(8,128)(2,1)S(1)}, bf16[512,256]{1,0:T(8,128)(2,1)S(1)}, u32[]{:S(2)}, u32[]{:S(2)}) collective-permute-start(bf16[512,256]{1,0:T(8,128)(2,1)S(1)} %get-tuple-element.61), channel_id=1, source_target_pairs={{0,16},{8,24},{16,0},{24,8},{1,17},{9,25},{17,1},{25,9},{2,18},{10... | collective-permute-start | bytes 786440 | tf_op jit(solution)/shard_map/ppermute | solution.py:19
  68.1 15.5 %collective-permute-start.28 = (bf16[192,1024]{1,0:T(8,128)(2,1)S(1)}, bf16[192,1024]{1,0:T(8,128)(2,1)S(1)}, u32[]{:S(2)}, u32[]{:S(2)}) collective-permute-start(bf16[192,1024]{1,0:T(8,128)(2,1)S(1)} %collective-permute-done.19.refs_7_), channel_id=1, source_target_pairs={{0,8},{8,0},{16,24},{24,16},{1,9},{9,1},{17,25},{25,17},{2,10},{10... | collective-permute-start | bytes 1179656 | tf_op jit(solution)/shard_map/ppermute | solution.py:19
  71.9 1.4 %collective-permute-start.20 = (bf16[512,128]{1,0:T(8,128)(2,1)S(1)}, bf16[512,128]{1,0:T(8,128)(2,1)S(1)}, u32[]{:S(2)}, u32[]{:S(2)}) collective-permute-start(bf16[512,128]{1,0:T(8,128)(2,1)S(1)} %get-tuple-element.65), channel_id=1, source_target_pairs={{0,8},{8,0},{16,24},{24,16},{1,9},{9,1},{17,25},{25,17},{2,10},{10... | collective-permute-start | bytes 393224 | tf_op jit(solution)/shard_map/ppermute | solution.py:19
  75.8 1.4 %collective-permute-start.22 = (bf16[512,128]{1,0:T(8,128)(2,1)S(1)}, bf16[512,128]{1,0:T(8,128)(2,1)S(1)}, u32[]{:S(2)}, u32[]{:S(2)}) collective-permute-start(bf16[512,128]{1,0:T(8,128)(2,1)S(1)} %get-tuple-element.71), channel_id=1, source_target_pairs={{0,8},{8,0},{16,24},{24,16},{1,9},{9,1},{17,25},{25,17},{2,10},{10... | collective-permute-start | bytes 393224 | tf_op jit(solution)/shard_map/ppermute | solution.py:19
  77.9 1.9 %collective-permute-start.23 = (bf16[256,128]{1,0:T(8,128)(2,1)S(1)}, bf16[256,128]{1,0:T(8,128)(2,1)S(1)}, u32[]{:S(2)}, u32[]{:S(2)}) collective-permute-start(bf16[256,128]{1,0:T(8,128)(2,1)S(1)} %get-tuple-element.73), channel_id=1, source_target_pairs={{0,8},{8,0},{16,24},{24,16},{1,9},{9,1},{17,25},{25,17},{2,10},{10... | collective-permute-start | bytes 196616 | tf_op jit(solution)/shard_map/ppermute | solution.py:19
  78.1 4.7 %collective-permute-start.24 = (bf16[256,128]{1,0:T(8,128)(2,1)S(1)}, bf16[256,128]{1,0:T(8,128)(2,1)S(1)}, u32[]{:S(2)}, u32[]{:S(2)}) collective-permute-start(bf16[256,128]{1,0:T(8,128)(2,1)S(1)} %get-tuple-element.74), channel_id=1, source_target_pairs={{0,16},{8,24},{16,0},{24,8},{1,17},{9,25},{17,1},{25,9},{2,18},{10... | collective-permute-start | bytes 196616 | tf_op jit(solution)/shard_map/ppermute | solution.py:19
  79.3 4.3 %collective-permute-start.25 = (bf16[256,128]{1,0:T(8,128)(2,1)S(1)}, bf16[256,128]{1,0:T(8,128)(2,1)S(1)}, u32[]{:S(2)}, u32[]{:S(2)}) collective-permute-start(bf16[256,128]{1,0:T(8,128)(2,1)S(1)} %get-tuple-element.75), channel_id=1, source_target_pairs={{0,24},{8,16},{16,8},{24,0},{1,25},{9,17},{17,9},{25,1},{2,26},{10... | collective-permute-start | bytes 196616 | tf_op jit(solution)/shard_map/ppermute | solution.py:19
  85.3 5.7 %collective-permute-start.29 = (bf16[96,512]{1,0:T(8,128)(2,1)S(1)}, bf16[96,512]{1,0:T(8,128)(2,1)S(1)}, u32[]{:S(2)}, u32[]{:S(2)}) collective-permute-start(bf16[96,512]{1,0:T(8,128)(2,1)S(1)} %get-tuple-element.81), channel_id=1, source_target_pairs={{0,1},{1,0},{2,3},{3,2},{4,5},{5,4},{6,7},{7,6},{8,9},{9,8},{10,11... | collective-permute-start | bytes 294920 | tf_op jit(solution)/shard_map/ppermute | solution.py:19
  86.4 8.1 %collective-permute-start.34 = (bf16[160,512]{1,0:T(8,128)(2,1)S(1)}, bf16[160,512]{1,0:T(8,128)(2,1)S(1)}, u32[]{:S(2)}, u32[]{:S(2)}) collective-permute-start(bf16[160,512]{1,0:T(8,128)(2,1)S(1)} %get-tuple-element.88), channel_id=1, source_target_pairs={{0,1},{1,0},{2,3},{3,2},{4,5},{5,4},{6,7},{7,6},{8,9},{9,8},{10,11... | collective-permute-start | bytes 491528 | tf_op jit(solution)/shard_map/ppermute | solution.py:19
  91.0 9.3 %collective-permute-start.32 = (bf16[256,512]{1,0:T(8,128)(2,1)S(1)}, bf16[256,512]{1,0:T(8,128)(2,1)S(1)}, u32[]{:S(2)}, u32[]{:S(2)}) collective-permute-start(bf16[256,512]{1,0:T(8,128)(2,1)S(1)} %get-tuple-element.85), channel_id=1, source_target_pairs={{0,1},{1,0},{2,3},{3,2},{4,5},{5,4},{6,7},{7,6},{8,9},{9,8},{10,11... | collective-permute-start | bytes 786440 | tf_op jit(solution)/shard_map/ppermute | solution.py:19
  92.1 6.7 %collective-permute-start.30 = (bf16[96,512]{1,0:T(8,128)(2,1)S(1)}, bf16[96,512]{1,0:T(8,128)(2,1)S(1)}, u32[]{:S(2)}, u32[]{:S(2)}) collective-permute-start(bf16[96,512]{1,0:T(8,128)(2,1)S(1)} %add_convert_fusion.4), channel_id=1, source_target_pairs={{0,6},{1,7},{2,4},{3,5},{4,2},{5,3},{6,0},{7,1},{8,14},{9,15},{10,... | collective-permute-start | bytes 294920 | tf_op jit(solution)/shard_map/ppermute | solution.py:19
  94.5 11.4 %collective-permute-start.35 = (bf16[256,512]{1,0:T(8,128)(2,1)S(1)}, bf16[256,512]{1,0:T(8,128)(2,1)S(1)}, u32[]{:S(2)}, u32[]{:S(2)}) collective-permute-start(bf16[256,512]{1,0:T(8,128)(2,1)S(1)} %get-tuple-element.89), channel_id=1, source_target_pairs={{0,1},{1,0},{2,3},{3,2},{4,5},{5,4},{6,7},{7,6},{8,9},{9,8},{10,11... | collective-permute-start | bytes 786440 | tf_op jit(solution)/shard_map/ppermute | solution.py:19
  95.6 10.4 %collective-permute-start.36 = (bf16[160,512]{1,0:T(8,128)(2,1)S(1)}, bf16[160,512]{1,0:T(8,128)(2,1)S(1)}, u32[]{:S(2)}, u32[]{:S(2)}) collective-permute-start(bf16[160,512]{1,0:T(8,128)(2,1)S(1)} %add_convert_fusion.3), channel_id=1, source_target_pairs={{0,6},{1,7},{2,4},{3,5},{4,2},{5,3},{6,0},{7,1},{8,14},{9,15},{10,... | collective-permute-start | bytes 491528 | tf_op jit(solution)/shard_map/ppermute | solution.py:19
  98.8 12.6 %collective-permute-start.31 = (bf16[256,512]{1,0:T(8,128)(2,1)S(1)}, bf16[256,512]{1,0:T(8,128)(2,1)S(1)}, u32[]{:S(2)}, u32[]{:S(2)}) collective-permute-start(bf16[256,512]{1,0:T(8,128)(2,1)S(1)} %get-tuple-element.82), channel_id=1, source_target_pairs={{0,1},{1,0},{2,3},{3,2},{4,5},{5,4},{6,7},{7,6},{8,9},{9,8},{10,11... | collective-permute-start | bytes 786440 | tf_op jit(solution)/shard_map/ppermute | solution.py:19
  100.4 14.9 %collective-permute-start.33 = (bf16[256,512]{1,0:T(8,128)(2,1)S(1)}, bf16[256,512]{1,0:T(8,128)(2,1)S(1)}, u32[]{:S(2)}, u32[]{:S(2)}) collective-permute-start(bf16[256,512]{1,0:T(8,128)(2,1)S(1)} %add_convert_fusion.2), channel_id=1, source_target_pairs={{0,4},{1,5},{2,6},{3,7},{4,0},{5,1},{6,2},{7,3},{8,12},{9,13},{10,... | collective-permute-start | bytes 786440 | tf_op jit(solution)/shard_map/ppermute | solution.py:19
  106.0 13.8 %collective-permute-start.37 = (bf16[256,512]{1,0:T(8,128)(2,1)S(1)}, bf16[256,512]{1,0:T(8,128)(2,1)S(1)}, u32[]{:S(2)}, u32[]{:S(2)}) collective-permute-start(bf16[256,512]{1,0:T(8,128)(2,1)S(1)} %add_convert_fusion.1), channel_id=1, source_target_pairs={{0,2},{1,3},{2,0},{3,1},{4,6},{5,7},{6,4},{7,5},{8,10},{9,11},{10,... | collective-permute-start | bytes 786440 | tf_op jit(solution)/shard_map/ppermute | solution.py:19

commit v6 on v5

--- a/solution.py
+++ b/solution.py
@@ -35,14 +35,15 @@
     return node // 2 == head // 4
 
 
-def sort_kernel(close_ref, distant_ref, first_ref, second_ref, keep_ref):
+def sort_kernel(keeps, close_ref, distant_ref, *outs):
     lined = in_line(lax.axis_index("node"), lax.axis_index("head"))
-    half = first_ref.shape[0]
-
-    def place(send_ref, held_ref):
-        first_ref[...] = send_ref[:half, :]
-        second_ref[...] = send_ref[half:, :]
-        keep_ref[...] = held_ref[...]
+
+    def place(send_ref, keep_ref):
+        for ref, parts in ((keep_ref, outs[:keeps]), (send_ref, outs[keeps:])):
+            start = 0
+            for part in parts:
+                part[...] = ref[start : start + part.shape[0], :]
+                start += part.shape[0]
 
     @pl.when(lined)
     def _():
@@ -53,84 +54,84 @@
         place(close_ref, distant_ref)
 
 
-def sort(close, distant):
+def sort(close, distant, keeps, sends):
     rows, cols = close.shape
-    half = jax.ShapeDtypeStruct((rows // 2, cols), close.dtype)
-    return pl.pallas_call(
-        sort_kernel,
-        out_shape=[half, half, jax.ShapeDtypeStruct((rows, cols), close.dtype)],
+    shapes = [
+        jax.ShapeDtypeStruct((rows // parts, cols), close.dtype)
+        for parts in (keeps, sends)
+        for _ in range(parts)
+    ]
+    outs = pl.pallas_call(
+        functools.partial(sort_kernel, keeps),
+        out_shape=shapes,
         in_specs=[vmem_spec()] * 2,
-        out_specs=[vmem_spec()] * 3,
+        out_specs=[vmem_spec()] * len(shapes),
         compiler_params=pltpu.CompilerParams(vmem_limit_bytes=8 * 2**20),
         cost_estimate=pl.CostEstimate(flops=0, bytes_accessed=8 * close.size, transcendentals=0),
         name="sort",
     )(close, distant)
-
-
-def project_kernel(*refs):
-    pieces, weights, keep_ref, send_ref = refs[:12], refs[12:14], refs[14], refs[15]
-    feats, total, piece_sem = refs[16:]
+    return outs[:keeps], outs[keeps:]
+
+
+def project_kernel(counts, *refs):
+    pieces = []
+    for count in counts:
+        pieces.append(refs[:count])
+        refs = refs[count:]
+    weights, (keep_ref, send_ref, total) = refs[:2], refs[2:]
     node, head = lax.axis_index("node"), lax.axis_index("head")
     side, core = node // 2, node % 2
     slot = (head // 2) % 2 ^ jnp.where(in_line(node, head), 0, 1)
     near = head % 2
-    _, rows, depth = feats.shape
-    copies = []
-    for i in range(12):
-        if i < 4:
-            block, plane, other, start, count = 0, i // 2, i % 2, 0, rows
-        else:
-            block, plane, other = 1, (i - 4) // 4, (i - 4) // 2 % 2
-            start, count = i % 2 * (rows // 2), rows // 2
-        place = 4 * block + 2 * (slot ^ plane) + (near ^ other)
-        copy = pltpu.make_async_copy(
-            pieces[i], feats.at[place, pl.ds(start, count)], piece_sem.at[i]
-        )
-        copy.start()
-        copies.append(copy)
-    for copy in copies:
-        copy.wait()
+    rows, depth = sum(ref.shape[0] for ref in pieces[0]), pieces[0][0].shape[1]
     width = keep_ref.shape[1]
-    for block in range(2):
-        for i in range(2):
-            for part in range(2):
-                term = jnp.dot(
-                    feats[4 * block + 2 * (core ^ i) + part],
-                    weights[i][part * depth : (part + 1) * depth, :],
-                    preferred_element_type=jnp.float32,
-                )
-                if i == 0 and part == 0:
-                    total[...] = term
-                else:
-                    total[...] += term
-        mine = pl.ds(pl.multiple_of(side * width, width), width)
-        theirs = pl.ds(pl.multiple_of((1 - side) * width, width), width)
-        keep_ref[block * rows : (block + 1) * rows, :] = total[:, mine]
-        send_ref[block * rows : (block + 1) * rows, :] = total[:, theirs].astype(jnp.bfloat16)
+    mine = pl.ds(pl.multiple_of(side * width, width), width)
+    theirs = pl.ds(pl.multiple_of((1 - side) * width, width), width)
+
+    def piece(block, plane, other):
+        held = pieces[4 * block + 2 * plane + other]
+        return jnp.concatenate([ref[...] for ref in held], axis=0)
+
+    def work(flip):
+        for block in range(2):
+            out = slice(block * rows, (block + 1) * rows)
+            sum_so_far = None
+            for plane in range(2):
+                for other in range(2):
+                    start = pl.multiple_of((near ^ other) * depth, depth)
+                    term = jnp.dot(
+                        piece(block, plane, other),
+                        weights[plane ^ flip][pl.ds(start, depth), :],
+                        preferred_element_type=jnp.float32,
+                    )
+                    sum_so_far = term if sum_so_far is None else sum_so_far + term
+            total[...] = sum_so_far
+            keep_ref[out, :] = total[:, mine]
+            send_ref[out, :] = total[:, theirs].astype(jnp.bfloat16)
+
+    for flip in range(2):
+        pl.when(slot ^ core == flip)(functools.partial(work, flip))
 
 
 def project(pieces, weights):
-    rows, depth = pieces[0].shape
+    rows, depth = sum(ref.shape[0] for ref in pieces[0]), pieces[0][0].shape[1]
     cols = weights[0].shape[1]
+    counts = [len(held) for held in pieces]
     flops = 2 * 2 * rows * 4 * depth * cols
     moved = 2 * (8 * rows * depth + 4 * depth * cols + 3 * rows * cols)
     return pl.pallas_call(
-        project_kernel,
+        functools.partial(project_kernel, counts),
         out_shape=[
             jax.ShapeDtypeStruct((2 * rows, cols // 2), jnp.float32),
             jax.ShapeDtypeStruct((2 * rows, cols // 2), jnp.bfloat16),
         ],
-        in_specs=[vmem_spec()] * 14,
+        in_specs=[vmem_spec()] * (sum(counts) + 2),
         out_specs=[vmem_spec()] * 2,
-        scratch_shapes=[
-            pltpu.VMEM((8, rows, depth), jnp.bfloat16),
-            pltpu.VMEM((rows, cols), jnp.float32),
-            pltpu.SemaphoreType.DMA((12,)),
-        ],
+        scratch_shapes=[pltpu.VMEM((rows, cols), jnp.float32)],
         compiler_params=pltpu.CompilerParams(vmem_limit_bytes=20 * 2**20),
         cost_estimate=pl.CostEstimate(flops=flops, bytes_accessed=moved, transcendentals=0),
         name="project",
-    )(*pieces, *weights)
+    )(*[piece for held in pieces for piece in held], *weights)
 
 
 def combine_kernel(keep_ref, moved_ref, mine_ref, give_ref):
@@ -302,38 +303,37 @@
     beside = functools.partial(swap, axis="node", mask=1)
     along = functools.partial(swap, axis="head", mask=1)
 
+    edges = [edge_types] + [swap(edge_types, "node", i) for i in range(1, 4)]
     far = {i: swap(node_feats, "head", 2 * i) for i in (3, 2, 1)}
-    out_first = across(w_out[: 5 * depth // 8])
-    tiles = jnp.stack([edge_types, beside(edge_types)])
-    *send_0, keep_0 = sort(node_feats, after(far[3], out_first))
-    keep_0y = along(keep_0)
-    moved_0 = [across(part) for part in send_0]
-    moved_0y = [along(part) for part in moved_0]
-    gate = (keep_0y, moved_0[1], moved_0y[0], tiles)
-    close, distant = lax.optimization_barrier((far[1], far[2], *gate))[:2]
-    *send_1, keep_1 = sort(close, distant)
+    out_first = across(after(w_out[: depth // 2], *edges))
+    edges = jnp.stack(edges)
+    keep_0, send_0 = sort(node_feats, far[3], 1, 1)
+    moved_0, keep_0y = [across(send_0[0])], [along(keep_0[0])]
+    out_second = across(after(w_out[depth // 2 : 3 * depth // 4], moved_0[0], out_first))
+    moved_0y = [along(moved_0[0])]
+    close, distant = lax.optimization_barrier((far[1], far[2], keep_0y[0]))[:2]
+    keep_1, send_1 = sort(close, distant, 1, 1)
     moved_1 = [across(part) for part in send_1]
-    keep_1y = along(keep_1)
+    keep_1y = [along(keep_1[0])]
     moved_1y = [along(part) for part in moved_1]
-    out_second = across(after(w_out[5 * depth // 8 :], moved_1[1]))
+    out_third = across(after(w_out[3 * depth // 4 :], moved_1[-1], out_second))
     qk_beside, val_beside = beside(w_qk), beside(w_val)
-    edges = jnp.concatenate([tiles, across(after(tiles, moved_1[0]))])
-
-    keep_1y = after(keep_1y, edges)
-    pieces = [keep_0, keep_0y, keep_1, keep_1y, *moved_0, *moved_0y, *moved_1, *moved_1y]
+    qk_beside = after(qk_beside, out_first)
+    pieces = [keep_0, keep_0y, keep_1, keep_1y, moved_0, moved_0y, moved_1, moved_1y]
+
     qk_keep, qk_send = project(pieces, [w_qk, qk_beside])
     qk_moved = across(qk_send)
     val_keep, val_send = project(pieces, [w_val, val_beside])
     val_moved = across(val_send)
-    qk_mine, qk_give = combine(qk_keep, after(qk_moved, val_send, out_second))
+    qk_mine, qk_give = combine(qk_keep, after(qk_moved, val_send, out_third))
     weights, total = weigh(edges, rel_bias.T, qk_mine, beside(qk_give))
     val_mine, val_give = combine(val_keep, after(val_moved, total))
     attn = average((0, 1, 2, 3), weights, total, val_mine, beside(val_give))
     attn = [attn[0]] + [swap(attn[i], "node", i) for i in range(1, 4)]
 
-    out_across = [out_first, out_second]
+    out_across = [out_first, out_second, out_third]
     out_beside = beside(after(w_out, moved_1[0]))
-    out_diagonal = [beside(after(out_first, moved_1[0])), beside(out_second)]
+    out_diagonal = [beside(after(piece, moved_1[0])) for piece in out_across[:2]] + [beside(out_third)]
     terms = emit(attn, [[w_out], [out_beside], out_across, out_diagonal])
 
     def pair(mine, send):

time: 121 us -> 117 us (0.967)
  Pallas kernels: 10.6 us -> 7.39 us
  starting transfers between devices: 44.2 us -> 47.3 us
  waiting for transfers between devices: 61 us -> 58 us
  other arithmetic: 2.43 us -> 1.07 us
    pallas_call x4, Pallas kernels: 5.91 us -> 2.72 us  [the longest x2 2.63 us: project(): pl.pallas_call(functools.partial(project_kernel, counts), out_shape=[jax....]
    ppermute x38 -> x37, starting transfers between devices: 44.2 us -> 47.3 us  [swap(): return lax.ppermute(value, axis, [(i, i ^ mask) for i in range(peers)])]
    ppermute x38 -> x37, waiting for transfers between devices: 61 us -> 58 us  [swap(): return lax.ppermute(value, axis, [(i, i ^ mask) for i in range(peers)])]
  transfers between devices with their start and end apart: 38 -> 37, of which waited for: 23 -> 18; matrix products, arithmetic and copies ran while one was open for 1% -> 2% of each run, Pallas kernels for 7% -> 5%
where the time goes in v6:
time: 117 us
  waiting for transfers between devices  58 us (50%)
  starting transfers between devices  47.3 us (40%)
  Pallas kernels  7.39 us (6%)
  local copies, waits for them, and re-layouts  3.12 us (3%)
    ppermute x37, waiting for transfers between devices, swap(): return lax.ppermute(value, axis, [(i, i ^ mask) for i in range(peers)])  58 us
    ppermute x37, starting transfers between devices, swap(): return lax.ppermute(value, axis, [(i, i ^ mask) for i in range(peers)])  47.3 us
    pallas_call x2, Pallas kernels, project(): pl.pallas_call(functools.partial(project_kernel, counts), out_shape=[jax....  2.63 us
  transfers between devices with their start and end apart: 37, of which 18 were waited for; matrix products, arithmetic and copies ran while one was open for 2% of the time, Pallas kernels for 5%

profile of v6, /device:TPU:0, one launch (start us, length us, event | category | flops | bytes accessed | tf_op | source)
XLA Modules:
  0.0 117.1 jit_solution(5201160646883141311)
XLA Ops:
  0.0 0.5 collective-permute-start.12
  0.5 4.7 %collective-permute-start.3 = (bf16[256,512]{1,0:T(8,128)(2,1)}, bf16[256,512]{1,0:T(8,128)(2,1)S(1)}, u32[]{:S(2)}, u32[]{:S(2)}) collective-permute-start(bf16[256,512]{1,0:T(8,128)(2,1)} %close_ref.1), channel_id=1, source_target_pairs={{0,6},{1,7},{2,4},{3,5},{4,2},{5,3},{6,0},{7,1},{8,14},{9,15},{10,... | collective-permute-start | bytes 786440 | tf_op jit(solution)/shard_map/ppermute | solution.py:19
  5.1 0.2 collective-permute-start
  5.3 1.5 %collective-permute-start.1 = (s32[2,8]{1,0:T(2,128)}, s32[2,8]{1,0:T(2,128)S(1)}, u32[]{:S(2)}, u32[]{:S(2)}) collective-permute-start(s32[2,8]{1,0:T(2,128)} %param.10), channel_id=1, source_target_pairs={{0,16},{8,24},{16,0},{24,8},{1,17},{9,25},{17,1},{25,9},{2,18},{10... | collective-permute-start | bytes 200 | tf_op jit(solution)/shard_map/ppermute | solution.py:19
  6.8 1.1 slice.15
  7.9 0.3 collective-permute-start.2
  8.1 0.9 collective-permute-done.1
  9.1 2.1 %collective-permute-done.2 = s32[2,8]{1,0:T(2,128)S(1)} collective-permute-done((s32[2,8]{1,0:T(2,128)}, s32[2,8]{1,0:T(2,128)S(1)}, u32[]{:S(2)}, u32[]{:S(2)}) %collective-permute-start.2) | collective-permute-done | bytes 96 | tf_op jit(solution)/shard_map/ppermute | solution.py:19
  11.1 0.5 collective-permute-start.13
  11.7 0.5 collective-permute-start.6
  12.2 0.4 collective-permute-done.3.distant_ref
  12.6 0.9 copy-done.3
  13.6 1.7 %collective-permute-start.4 = (bf16[256,512]{1,0:T(8,128)(2,1)S(1)}, bf16[256,512]{1,0:T(8,128)(2,1)S(1)}, u32[]{:S(2)}, u32[]{:S(2)}) collective-permute-start(bf16[256,512]{1,0:T(8,128)(2,1)S(1)} %get-tuple-element.47.refs_0_), channel_id=1, source_target_pairs={{0,1},{1,0},{2,3},{3,2},{4,5},{5,4},{6,7},{7,6},{8,9},{9,8},{10,11... | collective-permute-start | bytes 786440 | tf_op jit(solution)/shard_map/ppermute | solution.py:19
  15.3 3.7 %collective-permute-done.5.close_ref = bf16[256,512]{1,0:T(8,128)(2,1)S(1)} collective-permute-done((bf16[256,512]{1,0:T(8,128)(2,1)}, bf16[256,512]{1,0:T(8,128)(2,1)S(1)}, u32[]{:S(2)}, u32[]{:S(2)}) %collective-permute-start.5) | collective-permute-done | bytes 262176 | tf_op jit(solution)/shard_map/ppermute | solution.py:19
  19.0 1.5 %collective-permute-start.8 = (bf16[256,512]{1,0:T(8,128)(2,1)S(1)}, bf16[256,512]{1,0:T(8,128)(2,1)S(1)}, u32[]{:S(2)}, u32[]{:S(2)}) collective-permute-start(bf16[256,512]{1,0:T(8,128)(2,1)S(1)} %get-tuple-element.51), channel_id=1, source_target_pairs={{0,16},{8,24},{16,0},{24,8},{1,17},{9,25},{17,1},{25,9},{2,18},{10... | collective-permute-start | bytes 786440 | tf_op jit(solution)/shard_map/ppermute | solution.py:19
  20.5 7.8 %collective-permute-done.6.distant_ref = bf16[256,512]{1,0:T(8,128)(2,1)S(1)} collective-permute-done((bf16[256,512]{1,0:T(8,128)(2,1)}, bf16[256,512]{1,0:T(8,128)(2,1)S(1)}, u32[]{:S(2)}, u32[]{:S(2)}) %collective-permute-start.6) | collective-permute-done | bytes 262176 | tf_op jit(solution)/shard_map/ppermute | solution.py:19
  28.3 1.1 fusion
  29.3 0.1 sort.3
  29.4 1.6 %collective-permute-start.10 = (bf16[256,512]{1,0:T(8,128)(2,1)S(1)}, bf16[256,512]{1,0:T(8,128)(2,1)S(1)}, u32[]{:S(2)}, u32[]{:S(2)}) collective-permute-start(bf16[256,512]{1,0:T(8,128)(2,1)S(1)} %get-tuple-element.52), channel_id=1, source_target_pairs={{0,16},{8,24},{16,0},{24,8},{1,17},{9,25},{17,1},{25,9},{2,18},{10... | collective-permute-start | bytes 786440 | tf_op jit(solution)/shard_map/ppermute | solution.py:19
  31.0 0.5 collective-permute-start.16
  31.5 1.5 %collective-permute-start.7 = (bf16[256,512]{1,0:T(8,128)(2,1)S(1)}, bf16[256,512]{1,0:T(8,128)(2,1)S(1)}, u32[]{:S(2)}, u32[]{:S(2)}) collective-permute-start(bf16[256,512]{1,0:T(8,128)(2,1)S(1)} %get-tuple-element.50.refs_2_), channel_id=1, source_target_pairs={{0,1},{1,0},{2,3},{3,2},{4,5},{5,4},{6,7},{7,6},{8,9},{9,8},{10,11... | collective-permute-start | bytes 786440 | tf_op jit(solution)/shard_map/ppermute | solution.py:19
  33.0 5.5 %collective-permute-done.10.refs_6_ = bf16[256,512]{1,0:T(8,128)(2,1)S(1)} collective-permute-done((bf16[256,512]{1,0:T(8,128)(2,1)S(1)}, bf16[256,512]{1,0:T(8,128)(2,1)S(1)}, u32[]{:S(2)}, u32[]{:S(2)}) %collective-permute-start.10) | collective-permute-done | bytes 262176 | tf_op jit(solution)/shard_map/ppermute | solution.py:19
  38.6 1.5 %collective-permute-start.9 = (bf16[256,512]{1,0:T(8,128)(2,1)S(1)}, bf16[256,512]{1,0:T(8,128)(2,1)S(1)}, u32[]{:S(2)}, u32[]{:S(2)}) collective-permute-start(bf16[256,512]{1,0:T(8,128)(2,1)S(1)} %collective-permute-done.8.refs_4_), channel_id=1, source_target_pairs={{0,1},{1,0},{2,3},{3,2},{4,5},{5,4},{6,7},{7,6},{8,9},{9,8},{10,11... | collective-permute-start | bytes 786440 | tf_op jit(solution)/shard_map/ppermute | solution.py:19
  40.1 3.7 %collective-permute-done.16.refs_7_ = bf16[128,1024]{1,0:T(8,128)(2,1)S(1)} collective-permute-done((bf16[128,1024]{1,0:T(8,128)(2,1)S(1)}, bf16[128,1024]{1,0:T(8,128)(2,1)S(1)}, u32[]{:S(2)}, u32[]{:S(2)}) %collective-permute-start.16) | collective-permute-done | bytes 262176 | tf_op jit(solution)/shard_map/ppermute | solution.py:19
  43.8 1.5 %collective-permute-start.11 = (bf16[256,512]{1,0:T(8,128)(2,1)S(1)}, bf16[256,512]{1,0:T(8,128)(2,1)S(1)}, u32[]{:S(2)}, u32[]{:S(2)}) collective-permute-start(bf16[256,512]{1,0:T(8,128)(2,1)S(1)} %collective-permute-done.10.refs_6_), channel_id=1, source_target_pairs={{0,1},{1,0},{2,3},{3,2},{4,5},{5,4},{6,7},{7,6},{8,9},{9,8},{10,11... | collective-permute-start | bytes 786440 | tf_op jit(solution)/shard_map/ppermute | solution.py:19
  45.4 1.6 %collective-permute-start.17 = (bf16[128,1024]{1,0:T(8,128)(2,1)S(1)}, bf16[128,1024]{1,0:T(8,128)(2,1)S(1)}, u32[]{:S(2)}, u32[]{:S(2)}) collective-permute-start(bf16[128,1024]{1,0:T(8,128)(2,1)S(1)} %get-tuple-element.59), channel_id=1, source_target_pairs={{0,16},{8,24},{16,0},{24,8},{1,17},{9,25},{17,1},{25,9},{2,18},{10... | collective-permute-start | bytes 786440 | tf_op jit(solution)/shard_map/ppermute | solution.py:19
  46.9 4.8 %collective-permute-done.11.refs_7_ = bf16[256,512]{1,0:T(8,128)(2,1)S(1)} collective-permute-done((bf16[256,512]{1,0:T(8,128)(2,1)S(1)}, bf16[256,512]{1,0:T(8,128)(2,1)S(1)}, u32[]{:S(2)}, u32[]{:S(2)}) %collective-permute-start.11) | collective-permute-done | bytes 262176 | tf_op jit(solution)/shard_map/ppermute | solution.py:19
  51.7 1.3 %project.2 = (f32[512,256]{1,0:T(8,128)S(1)}, bf16[512,256]{1,0:T(8,128)(2,1)S(1)}) custom-call(bf16[256,512]{1,0:T(8,128)(2,1)S(1)} %get-tuple-element.47.refs_0_, bf16[256,512]{1,0:T(8,128)(2,1)S(1)} %collective-permute-done.4.refs_1_, bf16[256,512]{1,0:T(8,128)(2,1)S(1)} %get-tuple-element.50.refs_2_, ...), custom_call_target="tpu_custom_call" | custom-call | flops 1073741824 | bytes 4980736 | tf_op jit(solution)/shard_map/project/pallas_call | solution.py:122
  53.1 1.6 %collective-permute-start.14 = (bf16[512,256]{1,0:T(8,128)(2,1)S(1)}, bf16[512,256]{1,0:T(8,128)(2,1)S(1)}, u32[]{:S(2)}, u32[]{:S(2)}) collective-permute-start(bf16[512,256]{1,0:T(8,128)(2,1)S(1)} %get-tuple-element.56), channel_id=1, source_target_pairs={{0,16},{8,24},{16,0},{24,8},{1,17},{9,25},{17,1},{25,9},{2,18},{10... | collective-permute-start | bytes 786440 | tf_op jit(solution)/shard_map/ppermute | solution.py:19
  54.6 1.3 %project.3 = (f32[512,256]{1,0:T(8,128)S(1)}, bf16[512,256]{1,0:T(8,128)(2,1)S(1)}) custom-call(bf16[256,512]{1,0:T(8,128)(2,1)S(1)} %get-tuple-element.47.refs_0_, bf16[256,512]{1,0:T(8,128)(2,1)S(1)} %collective-permute-done.4.refs_1_, bf16[256,512]{1,0:T(8,128)(2,1)S(1)} %get-tuple-element.50.refs_2_, ...), custom_call_target="tpu_custom_call" | custom-call | flops 1073741824 | bytes 4980736 | tf_op jit(solution)/shard_map/project/pallas_call | solution.py:122
  56.0 4.2 %collective-permute-done.14.moved_ref = bf16[512,256]{1,0:T(8,128)(2,1)S(1)} collective-permute-done((bf16[512,256]{1,0:T(8,128)(2,1)S(1)}, bf16[512,256]{1,0:T(8,128)(2,1)S(1)}, u32[]{:S(2)}, u32[]{:S(2)}) %collective-permute-start.14) | collective-permute-done | bytes 262176 | tf_op jit(solution)/shard_map/ppermute | solution.py:19
  60.2 0.1 combine.2
  60.2 0.1 collective-permute-start.18
  60.3 1.6 %collective-permute-start.19 = (bf16[512,256]{1,0:T(8,128)(2,1)S(1)}, bf16[512,256]{1,0:T(8,128)(2,1)S(1)}, u32[]{:S(2)}, u32[]{:S(2)}) collective-permute-start(bf16[512,256]{1,0:T(8,128)(2,1)S(1)} %get-tuple-element.57), channel_id=1, source_target_pairs={{0,16},{8,24},{16,0},{24,8},{1,17},{9,25},{17,1},{25,9},{2,18},{10... | collective-permute-start | bytes 786440 | tf_op jit(solution)/shard_map/ppermute | solution.py:19
  61.9 0.2 collective-permute-start.26
  62.0 0.3 collective-permute-start.27
  62.4 2.2 %weigh.1 = (bf16[1024,1024]{1,0:T(8,128)(2,1)S(1)}, f32[1024,1]{1,0:T(8,128)S(1)}) custom-call(s32[4,2,8]{2,1,0:T(2,128)S(1)} %pad_add_fusion.edge_ref, f32[4,237]{1,0:T(4,128)S(1)} %bitcast.5, bf16[512,128]{1,0:T(8,128)(2,1)S(1)} %get-tuple-element.61.mine_ref, bf16[512,128]{1,0:T(8,128)(2,1)S(1)} %collective-permute-done.18.theirs_ref), custom_call_target="tpu_custom_call" | custom-call | flops 268435456 | bytes 2097152 | tf_op jit(solution)/shard_map/weigh/pallas_call | solution.py:197
  64.6 4.4 %collective-permute-done.19.moved_ref = bf16[512,256]{1,0:T(8,128)(2,1)S(1)} collective-permute-done((bf16[512,256]{1,0:T(8,128)(2,1)S(1)}, bf16[512,256]{1,0:T(8,128)(2,1)S(1)}, u32[]{:S(2)}, u32[]{:S(2)}) %collective-permute-start.19) | collective-permute-done | bytes 262176 | tf_op jit(solution)/shard_map/ppermute | solution.py:19
  69.1 0.1 collective-permute-start.20
  69.2 1.3 %collective-permute-done.20.theirs_ref = bf16[512,128]{1,0:T(8,128)(2,1)S(1)} collective-permute-done((bf16[512,128]{1,0:T(8,128)(2,1)S(1)}, bf16[512,128]{1,0:T(8,128)(2,1)S(1)}, u32[]{:S(2)}, u32[]{:S(2)}) %collective-permute-start.20) | collective-permute-done | bytes 131104 | tf_op jit(solution)/shard_map/ppermute | solution.py:19
  70.5 0.7 average.1
  71.2 0.2 collective-permute-start.21
  71.4 1.5 %collective-permute-start.22 = (bf16[256,128]{1,0:T(8,128)(2,1)S(1)}, bf16[256,128]{1,0:T(8,128)(2,1)S(1)}, u32[]{:S(2)}, u32[]{:S(2)}) collective-permute-start(bf16[256,128]{1,0:T(8,128)(2,1)S(1)} %get-tuple-element.71), channel_id=1, source_target_pairs={{0,16},{8,24},{16,0},{24,8},{1,17},{9,25},{17,1},{25,9},{2,18},{10... | collective-permute-start | bytes 196616 | tf_op jit(solution)/shard_map/ppermute | solution.py:19
  72.9 0.2 collective-permute-start.23
  73.2 2.6 %collective-permute-done.22.refs_2_ = bf16[256,128]{1,0:T(8,128)(2,1)S(1)} collective-permute-done((bf16[256,128]{1,0:T(8,128)(2,1)S(1)}, bf16[256,128]{1,0:T(8,128)(2,1)S(1)}, u32[]{:S(2)}, u32[]{:S(2)}) %collective-permute-start.22) | collective-permute-done | bytes 65568 | tf_op jit(solution)/shard_map/ppermute | solution.py:19
  75.8 1.3 %collective-permute-done.23.refs_3_ = bf16[256,128]{1,0:T(8,128)(2,1)S(1)} collective-permute-done((bf16[256,128]{1,0:T(8,128)(2,1)S(1)}, bf16[256,128]{1,0:T(8,128)(2,1)S(1)}, u32[]{:S(2)}, u32[]{:S(2)}) %collective-permute-start.23) | collective-permute-done | bytes 65568 | tf_op jit(solution)/shard_map/ppermute | solution.py:19
  77.1 1.7 %emit.1 = (bf16[256,512]{1,0:T(8,128)(2,1)S(1)}, bf16[256,512]{1,0:T(8,128)(2,1)S(1)}, bf16[256,512]{1,0:T(8,128)(2,1)S(1)}, bf16[256,512]{1,0:T(8,128)(2,1)S(1)...) custom-call(bf16[256,128]{1,0:T(8,128)(2,1)S(1)} %get-tuple-element., ...), custom_call_target="tpu_custom_call" | custom-call | flops 1073741824 | bytes 6553600 | tf_op jit(solution)/shard_map/emit/pallas_call | solution.py:284
  78.8 1.6 %collective-permute-start.28 = (bf16[96,512]{1,0:T(8,128)(2,1)S(1)}, bf16[96,512]{1,0:T(8,128)(2,1)S(1)}, u32[]{:S(2)}, u32[]{:S(2)}) collective-permute-start(bf16[96,512]{1,0:T(8,128)(2,1)S(1)} %get-tuple-element.79), channel_id=1, source_target_pairs={{0,1},{1,0},{2,3},{3,2},{4,5},{5,4},{6,7},{7,6},{8,9},{9,8},{10,11... | collective-permute-start | bytes 294920 | tf_op jit(solution)/shard_map/ppermute | solution.py:19
  80.4 0.5 collective-permute-start.33
  80.9 3.6 %collective-permute-done.28 = bf16[96,512]{1,0:T(8,128)(2,1)S(1)} collective-permute-done((bf16[96,512]{1,0:T(8,128)(2,1)S(1)}, bf16[96,512]{1,0:T(8,128)(2,1)S(1)}, u32[]{:S(2)}, u32[]{:S(2)}) %collective-permute-start.28) | collective-permute-done | bytes 98336 | tf_op jit(solution)/shard_map/ppermute | solution.py:19
  84.5 1.6 %collective-permute-start.31 = (bf16[256,512]{1,0:T(8,128)(2,1)S(1)}, bf16[256,512]{1,0:T(8,128)(2,1)S(1)}, u32[]{:S(2)}, u32[]{:S(2)}) collective-permute-start(bf16[256,512]{1,0:T(8,128)(2,1)S(1)} %get-tuple-element.83), channel_id=1, source_target_pairs={{0,1},{1,0},{2,3},{3,2},{4,5},{5,4},{6,7},{7,6},{8,9},{9,8},{10,11... | collective-permute-start | bytes 786440 | tf_op jit(solution)/shard_map/ppermute | solution.py:19
  86.1 2.5 %collective-permute-start.29 = (bf16[96,512]{1,0:T(8,128)(2,1)S(1)}, bf16[96,512]{1,0:T(8,128)(2,1)S(1)}, u32[]{:S(2)}, u32[]{:S(2)}) collective-permute-start(bf16[96,512]{1,0:T(8,128)(2,1)S(1)} %add_convert_fusion.4), channel_id=1, source_target_pairs={{0,6},{1,7},{2,4},{3,5},{4,2},{5,3},{6,0},{7,1},{8,14},{9,15},{10,... | collective-permute-start | bytes 294920 | tf_op jit(solution)/shard_map/ppermute | solution.py:19
  88.7 1.0 collective-permute-start.34
  89.6 2.5 %collective-permute-start.35 = (bf16[160,512]{1,0:T(8,128)(2,1)S(1)}, bf16[160,512]{1,0:T(8,128)(2,1)S(1)}, u32[]{:S(2)}, u32[]{:S(2)}) collective-permute-start(bf16[160,512]{1,0:T(8,128)(2,1)S(1)} %add_convert_fusion.3), channel_id=1, source_target_pairs={{0,6},{1,7},{2,4},{3,5},{4,2},{5,3},{6,0},{7,1},{8,14},{9,15},{10,... | collective-permute-start | bytes 491528 | tf_op jit(solution)/shard_map/ppermute | solution.py:19
  92.1 0.8 collective-permute-done.29
  93.0 0.4 collective-permute-start.30
  93.4 0.4 collective-permute-done.31
  93.8 0.1 add_convert_fusion.2
  93.9 6.9 %collective-permute-start.32 = (bf16[256,512]{1,0:T(8,128)(2,1)S(1)}, bf16[256,512]{1,0:T(8,128)(2,1)S(1)}, u32[]{:S(2)}, u32[]{:S(2)}) collective-permute-start(bf16[256,512]{1,0:T(8,128)(2,1)S(1)} %add_convert_fusion.2), channel_id=1, source_target_pairs={{0,4},{1,5},{2,6},{3,7},{4,0},{5,1},{6,2},{7,3},{8,12},{9,13},{10,... | collective-permute-start | bytes 786440 | tf_op jit(solution)/shard_map/ppermute | solution.py:19
  100.8 0.1 add_convert_fusion.1
  100.9 5.0 %collective-permute-start.36 = (bf16[256,512]{1,0:T(8,128)(2,1)S(1)}, bf16[256,512]{1,0:T(8,128)(2,1)S(1)}, u32[]{:S(2)}, u32[]{:S(2)}) collective-permute-start(bf16[256,512]{1,0:T(8,128)(2,1)S(1)} %add_convert_fusion.1), channel_id=1, source_target_pairs={{0,2},{1,3},{2,0},{3,1},{4,6},{5,7},{6,4},{7,5},{8,10},{9,11},{10,... | collective-permute-start | bytes 786440 | tf_op jit(solution)/shard_map/ppermute | solution.py:19
  105.9 4.8 %collective-permute-done.32 = bf16[256,512]{1,0:T(8,128)(2,1)S(1)} collective-permute-done((bf16[256,512]{1,0:T(8,128)(2,1)S(1)}, bf16[256,512]{1,0:T(8,128)(2,1)S(1)}, u32[]{:S(2)}, u32[]{:S(2)}) %collective-permute-start.32) | collective-permute-done | bytes 262176 | tf_op jit(solution)/shard_map/ppermute | solution.py:19
  110.7 5.5 %collective-permute-done.36 = bf16[256,512]{1,0:T(8,128)(2,1)S(1)} collective-permute-done((bf16[256,512]{1,0:T(8,128)(2,1)S(1)}, bf16[256,512]{1,0:T(8,128)(2,1)S(1)}, u32[]{:S(2)}, u32[]{:S(2)}) %collective-permute-start.36) | collective-permute-done | bytes 262176 | tf_op jit(solution)/shard_map/ppermute | solution.py:19
  116.2 0.9 add_convert_fusion
  (39 shorter events, 0.3 us)
Async XLA Ops:
  0.0 51.7 %copy-start.1 = (bf16[1024,512]{1,0:T(8,128)(2,1)S(1)}, bf16[1024,512]{1,0:T(8,128)(2,1)}, u32[]{:S(2)}) copy-start(bf16[1024,512]{1,0:T(8,128)(2,1)} %refs_8_.2) | copy-start | bytes 3145732
  0.0 45.3 %copy-start = (bf16[512,1024]{1,0:T(8,128)(2,1)S(1)}, bf16[512,1024]{1,0:T(8,128)(2,1)}, u32[]{:S(2)}) copy-start(bf16[512,1024]{1,0:T(8,128)(2,1)} %refs_4_.1) | copy-start | bytes 3145732
  0.0 45.3 %collective-permute-start.12 = (bf16[1024,512]{1,0:T(8,128)(2,1)}, bf16[1024,512]{1,0:T(8,128)(2,1)S(1)}, u32[]{:S(2)}, u32[]{:S(2)}) collective-permute-start(bf16[1024,512]{1,0:T(8,128)(2,1)} %refs_8_.2), channel_id=1, source_target_pairs={{0,8},{8,0},{16,24},{24,16},{1,9},{9,1},{17,25},{25,17},{2,10},{10... | collective-permute-start | bytes 3145736 | tf_op jit(solution)/shard_map/ppermute | solution.py:19
  0.5 12.1 %collective-permute-start.3 = (bf16[256,512]{1,0:T(8,128)(2,1)}, bf16[256,512]{1,0:T(8,128)(2,1)S(1)}, u32[]{:S(2)}, u32[]{:S(2)}) collective-permute-start(bf16[256,512]{1,0:T(8,128)(2,1)} %close_ref.1), channel_id=1, source_target_pairs={{0,6},{1,7},{2,4},{3,5},{4,2},{5,3},{6,0},{7,1},{8,14},{9,15},{10,... | collective-permute-start | bytes 786440 | tf_op jit(solution)/shard_map/ppermute | solution.py:19
  5.1 13.9 %collective-permute-start.5 = (bf16[256,512]{1,0:T(8,128)(2,1)}, bf16[256,512]{1,0:T(8,128)(2,1)S(1)}, u32[]{:S(2)}, u32[]{:S(2)}) collective-permute-start(bf16[256,512]{1,0:T(8,128)(2,1)} %close_ref.1), channel_id=1, source_target_pairs={{0,2},{1,3},{2,0},{3,1},{4,6},{5,7},{6,4},{7,5},{8,10},{9,11},{10,... | collective-permute-start | bytes 786440 | tf_op jit(solution)/shard_map/ppermute | solution.py:19
  5.1 2.7 %collective-permute-start = (s32[2,8]{1,0:T(2,128)}, s32[2,8]{1,0:T(2,128)S(1)}, u32[]{:S(2)}, u32[]{:S(2)}) collective-permute-start(s32[2,8]{1,0:T(2,128)} %param.10), channel_id=1, source_target_pairs={{0,8},{8,0},{16,24},{24,16},{1,9},{9,1},{17,25},{25,17},{2,10},{10... | collective-permute-start | bytes 200 | tf_op jit(solution)/shard_map/ppermute | solution.py:19
  5.3 3.8 %collective-permute-start.1 = (s32[2,8]{1,0:T(2,128)}, s32[2,8]{1,0:T(2,128)S(1)}, u32[]{:S(2)}, u32[]{:S(2)}) collective-permute-start(s32[2,8]{1,0:T(2,128)} %param.10), channel_id=1, source_target_pairs={{0,16},{8,24},{16,0},{24,8},{1,17},{9,25},{17,1},{25,9},{2,18},{10... | collective-permute-start | bytes 200 | tf_op jit(solution)/shard_map/ppermute | solution.py:19
  7.9 3.3 %collective-permute-start.2 = (s32[2,8]{1,0:T(2,128)}, s32[2,8]{1,0:T(2,128)S(1)}, u32[]{:S(2)}, u32[]{:S(2)}) collective-permute-start(s32[2,8]{1,0:T(2,128)} %param.10), channel_id=1, source_target_pairs={{0,24},{8,16},{16,8},{24,0},{1,25},{9,17},{17,9},{25,1},{2,26},{10... | collective-permute-start | bytes 200 | tf_op jit(solution)/shard_map/ppermute | solution.py:19
  11.1 19.8 %collective-permute-start.13 = (bf16[256,1024]{1,0:T(8,128)(2,1)S(1)}, bf16[256,1024]{1,0:T(8,128)(2,1)S(1)}, u32[]{:S(2)}, u32[]{:S(2)}) collective-permute-start(bf16[256,1024]{1,0:T(8,128)(2,1)S(1)} %slice.15), channel_id=1, source_target_pairs={{0,16},{8,24},{16,0},{24,8},{1,17},{9,25},{17,1},{25,9},{2,18},{10... | collective-permute-start | bytes 1572872 | tf_op jit(solution)/shard_map/ppermute | solution.py:19
  11.7 16.6 %collective-permute-start.6 = (bf16[256,512]{1,0:T(8,128)(2,1)}, bf16[256,512]{1,0:T(8,128)(2,1)S(1)}, u32[]{:S(2)}, u32[]{:S(2)}) collective-permute-start(bf16[256,512]{1,0:T(8,128)(2,1)} %close_ref.1), channel_id=1, source_target_pairs={{0,4},{1,5},{2,6},{3,7},{4,0},{5,1},{6,2},{7,3},{8,12},{9,13},{10,... | collective-permute-start | bytes 786440 | tf_op jit(solution)/shard_map/ppermute | solution.py:19
  12.6 1.0 copy-start.3
  13.6 15.7 %collective-permute-start.4 = (bf16[256,512]{1,0:T(8,128)(2,1)S(1)}, bf16[256,512]{1,0:T(8,128)(2,1)S(1)}, u32[]{:S(2)}, u32[]{:S(2)}) collective-permute-start(bf16[256,512]{1,0:T(8,128)(2,1)S(1)} %get-tuple-element.47.refs_0_), channel_id=1, source_target_pairs={{0,1},{1,0},{2,3},{3,2},{4,5},{5,4},{6,7},{7,6},{8,9},{9,8},{10,11... | collective-permute-start | bytes 786440 | tf_op jit(solution)/shard_map/ppermute | solution.py:19
  19.0 12.0 %collective-permute-start.8 = (bf16[256,512]{1,0:T(8,128)(2,1)S(1)}, bf16[256,512]{1,0:T(8,128)(2,1)S(1)}, u32[]{:S(2)}, u32[]{:S(2)}) collective-permute-start(bf16[256,512]{1,0:T(8,128)(2,1)S(1)} %get-tuple-element.51), channel_id=1, source_target_pairs={{0,16},{8,24},{16,0},{24,8},{1,17},{9,25},{17,1},{25,9},{2,18},{10... | collective-permute-start | bytes 786440 | tf_op jit(solution)/shard_map/ppermute | solution.py:19
  28.3 26.4 %collective-permute-start.15 = (bf16[1024,512]{1,0:T(8,128)(2,1)}, bf16[1024,512]{1,0:T(8,128)(2,1)S(1)}, u32[]{:S(2)}, u32[]{:S(2)}) collective-permute-start(bf16[1024,512]{1,0:T(8,128)(2,1)} %refs_8_.3), channel_id=1, source_target_pairs={{0,8},{8,0},{16,24},{24,16},{1,9},{9,1},{17,25},{25,17},{2,10},{10... | collective-permute-start | bytes 3145736 | tf_op jit(solution)/shard_map/ppermute | solution.py:19
  29.4 9.2 %collective-permute-start.10 = (bf16[256,512]{1,0:T(8,128)(2,1)S(1)}, bf16[256,512]{1,0:T(8,128)(2,1)S(1)}, u32[]{:S(2)}, u32[]{:S(2)}) collective-permute-start(bf16[256,512]{1,0:T(8,128)(2,1)S(1)} %get-tuple-element.52), channel_id=1, source_target_pairs={{0,16},{8,24},{16,0},{24,8},{1,17},{9,25},{17,1},{25,9},{2,18},{10... | collective-permute-start | bytes 786440 | tf_op jit(solution)/shard_map/ppermute | solution.py:19
  31.0 12.8 %collective-permute-start.16 = (bf16[128,1024]{1,0:T(8,128)(2,1)S(1)}, bf16[128,1024]{1,0:T(8,128)(2,1)S(1)}, u32[]{:S(2)}, u32[]{:S(2)}) collective-permute-start(bf16[128,1024]{1,0:T(8,128)(2,1)S(1)} %get-tuple-element.58), channel_id=1, source_target_pairs={{0,16},{8,24},{16,0},{24,8},{1,17},{9,25},{17,1},{25,9},{2,18},{10... | collective-permute-start | bytes 786440 | tf_op jit(solution)/shard_map/ppermute | solution.py:19
  31.5 13.8 %collective-permute-start.7 = (bf16[256,512]{1,0:T(8,128)(2,1)S(1)}, bf16[256,512]{1,0:T(8,128)(2,1)S(1)}, u32[]{:S(2)}, u32[]{:S(2)}) collective-permute-start(bf16[256,512]{1,0:T(8,128)(2,1)S(1)} %get-tuple-element.50.refs_2_), channel_id=1, source_target_pairs={{0,1},{1,0},{2,3},{3,2},{4,5},{5,4},{6,7},{7,6},{8,9},{9,8},{10,11... | collective-permute-start | bytes 786440 | tf_op jit(solution)/shard_map/ppermute | solution.py:19
  38.6 8.3 %collective-permute-start.9 = (bf16[256,512]{1,0:T(8,128)(2,1)S(1)}, bf16[256,512]{1,0:T(8,128)(2,1)S(1)}, u32[]{:S(2)}, u32[]{:S(2)}) collective-permute-start(bf16[256,512]{1,0:T(8,128)(2,1)S(1)} %collective-permute-done.8.refs_4_), channel_id=1, source_target_pairs={{0,1},{1,0},{2,3},{3,2},{4,5},{5,4},{6,7},{7,6},{8,9},{9,8},{10,11... | collective-permute-start | bytes 786440 | tf_op jit(solution)/shard_map/ppermute | solution.py:19
  43.8 7.9 %collective-permute-start.11 = (bf16[256,512]{1,0:T(8,128)(2,1)S(1)}, bf16[256,512]{1,0:T(8,128)(2,1)S(1)}, u32[]{:S(2)}, u32[]{:S(2)}) collective-permute-start(bf16[256,512]{1,0:T(8,128)(2,1)S(1)} %collective-permute-done.10.refs_6_), channel_id=1, source_target_pairs={{0,1},{1,0},{2,3},{3,2},{4,5},{5,4},{6,7},{7,6},{8,9},{9,8},{10,11... | collective-permute-start | bytes 786440 | tf_op jit(solution)/shard_map/ppermute | solution.py:19
  45.3 31.8 %collective-permute-start.24 = (bf16[512,1024]{1,0:T(8,128)(2,1)S(1)}, bf16[512,1024]{1,0:T(8,128)(2,1)S(1)}, u32[]{:S(2)}, u32[]{:S(2)}) collective-permute-start(bf16[512,1024]{1,0:T(8,128)(2,1)S(1)} %copy-done), channel_id=1, source_target_pairs={{0,8},{8,0},{16,24},{24,16},{1,9},{9,1},{17,25},{25,17},{2,10},{10... | collective-permute-start | bytes 3145736 | tf_op jit(solution)/shard_map/ppermute | solution.py:19
  45.3 9.3 %copy-start.2 = (bf16[1024,512]{1,0:T(8,128)(2,1)S(1)}, bf16[1024,512]{1,0:T(8,128)(2,1)}, u32[]{:S(2)}) copy-start(bf16[1024,512]{1,0:T(8,128)(2,1)} %refs_8_.3) | copy-start | bytes 3145732
  45.4 10.6 %collective-permute-start.17 = (bf16[128,1024]{1,0:T(8,128)(2,1)S(1)}, bf16[128,1024]{1,0:T(8,128)(2,1)S(1)}, u32[]{:S(2)}, u32[]{:S(2)}) collective-permute-start(bf16[128,1024]{1,0:T(8,128)(2,1)S(1)} %get-tuple-element.59), channel_id=1, source_target_pairs={{0,16},{8,24},{16,0},{24,8},{1,17},{9,25},{17,1},{25,9},{2,18},{10... | collective-permute-start | bytes 786440 | tf_op jit(solution)/shard_map/ppermute | solution.py:19
  53.0 9.3 %copy-start.5 = (s32[2,8]{1,0:T(2,128)S(1)}, s32[2,8]{1,0:T(2,128)}, u32[]{:S(2)}) copy-start(s32[2,8]{1,0:T(2,128)} %param.10) | copy-start | bytes 196
  53.1 9.3 %copy-start.4 = (f32[237,4]{0,1:T(4,128)S(1)}, f32[237,4]{0,1:T(4,128)}, u32[]{:S(2)}) copy-start(f32[237,4]{0,1:T(4,128)} %param.11) | copy-start | bytes 11380
  53.1 7.1 %collective-permute-start.14 = (bf16[512,256]{1,0:T(8,128)(2,1)S(1)}, bf16[512,256]{1,0:T(8,128)(2,1)S(1)}, u32[]{:S(2)}, u32[]{:S(2)}) collective-permute-start(bf16[512,256]{1,0:T(8,128)(2,1)S(1)} %get-tuple-element.56), channel_id=1, source_target_pairs={{0,16},{8,24},{16,0},{24,8},{1,17},{9,25},{17,1},{25,9},{2,18},{10... | collective-permute-start | bytes 786440 | tf_op jit(solution)/shard_map/ppermute | solution.py:19
  54.6 18.3 %collective-permute-start.25 = (bf16[256,1024]{1,0:T(8,128)(2,1)S(1)}, bf16[256,1024]{1,0:T(8,128)(2,1)S(1)}, u32[]{:S(2)}, u32[]{:S(2)}) collective-permute-start(bf16[256,1024]{1,0:T(8,128)(2,1)S(1)} %collective-permute-done.13.refs_6_), channel_id=1, source_target_pairs={{0,8},{8,0},{16,24},{24,16},{1,9},{9,1},{17,25},{25,17},{2,10},{10... | collective-permute-start | bytes 1572872 | tf_op jit(solution)/shard_map/ppermute | solution.py:19
  60.2 1.8 %collective-permute-start.18 = (bf16[512,128]{1,0:T(8,128)(2,1)S(1)}, bf16[512,128]{1,0:T(8,128)(2,1)S(1)}, u32[]{:S(2)}, u32[]{:S(2)}) collective-permute-start(bf16[512,128]{1,0:T(8,128)(2,1)S(1)} %get-tuple-element.62), channel_id=1, source_target_pairs={{0,8},{8,0},{16,24},{24,16},{1,9},{9,1},{17,25},{25,17},{2,10},{10... | collective-permute-start | bytes 393224 | tf_op jit(solution)/shard_map/ppermute | solution.py:19
  60.3 8.7 %collective-permute-start.19 = (bf16[512,256]{1,0:T(8,128)(2,1)S(1)}, bf16[512,256]{1,0:T(8,128)(2,1)S(1)}, u32[]{:S(2)}, u32[]{:S(2)}) collective-permute-start(bf16[512,256]{1,0:T(8,128)(2,1)S(1)} %get-tuple-element.57), channel_id=1, source_target_pairs={{0,16},{8,24},{16,0},{24,8},{1,17},{9,25},{17,1},{25,9},{2,18},{10... | collective-permute-start | bytes 786440 | tf_op jit(solution)/shard_map/ppermute | solution.py:19
  61.9 9.6 %collective-permute-start.26 = (bf16[128,1024]{1,0:T(8,128)(2,1)S(1)}, bf16[128,1024]{1,0:T(8,128)(2,1)S(1)}, u32[]{:S(2)}, u32[]{:S(2)}) collective-permute-start(bf16[128,1024]{1,0:T(8,128)(2,1)S(1)} %collective-permute-done.16.refs_7_), channel_id=1, source_target_pairs={{0,8},{8,0},{16,24},{24,16},{1,9},{9,1},{17,25},{25,17},{2,10},{10... | collective-permute-start | bytes 786440 | tf_op jit(solution)/shard_map/ppermute | solution.py:19
  62.0 11.1 %collective-permute-start.27 = (bf16[128,1024]{1,0:T(8,128)(2,1)S(1)}, bf16[128,1024]{1,0:T(8,128)(2,1)S(1)}, u32[]{:S(2)}, u32[]{:S(2)}) collective-permute-start(bf16[128,1024]{1,0:T(8,128)(2,1)S(1)} %collective-permute-done.17.refs_8_), channel_id=1, source_target_pairs={{0,8},{8,0},{16,24},{24,16},{1,9},{9,1},{17,25},{25,17},{2,10},{10... | collective-permute-start | bytes 786440 | tf_op jit(solution)/shard_map/ppermute | solution.py:19
  69.1 1.4 %collective-permute-start.20 = (bf16[512,128]{1,0:T(8,128)(2,1)S(1)}, bf16[512,128]{1,0:T(8,128)(2,1)S(1)}, u32[]{:S(2)}, u32[]{:S(2)}) collective-permute-start(bf16[512,128]{1,0:T(8,128)(2,1)S(1)} %get-tuple-element.68), channel_id=1, source_target_pairs={{0,8},{8,0},{16,24},{24,16},{1,9},{9,1},{17,25},{25,17},{2,10},{10... | collective-permute-start | bytes 393224 | tf_op jit(solution)/shard_map/ppermute | solution.py:19
  71.2 1.9 %collective-permute-start.21 = (bf16[256,128]{1,0:T(8,128)(2,1)S(1)}, bf16[256,128]{1,0:T(8,128)(2,1)S(1)}, u32[]{:S(2)}, u32[]{:S(2)}) collective-permute-start(bf16[256,128]{1,0:T(8,128)(2,1)S(1)} %get-tuple-element.70), channel_id=1, source_target_pairs={{0,8},{8,0},{16,24},{24,16},{1,9},{9,1},{17,25},{25,17},{2,10},{10... | collective-permute-start | bytes 196616 | tf_op jit(solution)/shard_map/ppermute | solution.py:19
  71.4 4.4 %collective-permute-start.22 = (bf16[256,128]{1,0:T(8,128)(2,1)S(1)}, bf16[256,128]{1,0:T(8,128)(2,1)S(1)}, u32[]{:S(2)}, u32[]{:S(2)}) collective-permute-start(bf16[256,128]{1,0:T(8,128)(2,1)S(1)} %get-tuple-element.71), channel_id=1, source_target_pairs={{0,16},{8,24},{16,0},{24,8},{1,17},{9,25},{17,1},{25,9},{2,18},{10... | collective-permute-start | bytes 196616 | tf_op jit(solution)/shard_map/ppermute | solution.py:19
  72.9 4.1 %collective-permute-start.23 = (bf16[256,128]{1,0:T(8,128)(2,1)S(1)}, bf16[256,128]{1,0:T(8,128)(2,1)S(1)}, u32[]{:S(2)}, u32[]{:S(2)}) collective-permute-start(bf16[256,128]{1,0:T(8,128)(2,1)S(1)} %get-tuple-element.72), channel_id=1, source_target_pairs={{0,24},{8,16},{16,8},{24,0},{1,25},{9,17},{17,9},{25,1},{2,26},{10... | collective-permute-start | bytes 196616 | tf_op jit(solution)/shard_map/ppermute | solution.py:19
  78.8 5.7 %collective-permute-start.28 = (bf16[96,512]{1,0:T(8,128)(2,1)S(1)}, bf16[96,512]{1,0:T(8,128)(2,1)S(1)}, u32[]{:S(2)}, u32[]{:S(2)}) collective-permute-start(bf16[96,512]{1,0:T(8,128)(2,1)S(1)} %get-tuple-element.79), channel_id=1, source_target_pairs={{0,1},{1,0},{2,3},{3,2},{4,5},{5,4},{6,7},{7,6},{8,9},{9,8},{10,11... | collective-permute-start | bytes 294920 | tf_op jit(solution)/shard_map/ppermute | solution.py:19
  80.4 8.3 %collective-permute-start.33 = (bf16[160,512]{1,0:T(8,128)(2,1)S(1)}, bf16[160,512]{1,0:T(8,128)(2,1)S(1)}, u32[]{:S(2)}, u32[]{:S(2)}) collective-permute-start(bf16[160,512]{1,0:T(8,128)(2,1)S(1)} %get-tuple-element.86), channel_id=1, source_target_pairs={{0,1},{1,0},{2,3},{3,2},{4,5},{5,4},{6,7},{7,6},{8,9},{9,8},{10,11... | collective-permute-start | bytes 491528 | tf_op jit(solution)/shard_map/ppermute | solution.py:19
  84.5 9.3 %collective-permute-start.31 = (bf16[256,512]{1,0:T(8,128)(2,1)S(1)}, bf16[256,512]{1,0:T(8,128)(2,1)S(1)}, u32[]{:S(2)}, u32[]{:S(2)}) collective-permute-start(bf16[256,512]{1,0:T(8,128)(2,1)S(1)} %get-tuple-element.83), channel_id=1, source_target_pairs={{0,1},{1,0},{2,3},{3,2},{4,5},{5,4},{6,7},{7,6},{8,9},{9,8},{10,11... | collective-permute-start | bytes 786440 | tf_op jit(solution)/shard_map/ppermute | solution.py:19
  86.1 6.9 %collective-permute-start.29 = (bf16[96,512]{1,0:T(8,128)(2,1)S(1)}, bf16[96,512]{1,0:T(8,128)(2,1)S(1)}, u32[]{:S(2)}, u32[]{:S(2)}) collective-permute-start(bf16[96,512]{1,0:T(8,128)(2,1)S(1)} %add_convert_fusion.4), channel_id=1, source_target_pairs={{0,6},{1,7},{2,4},{3,5},{4,2},{5,3},{6,0},{7,1},{8,14},{9,15},{10,... | collective-permute-start | bytes 294920 | tf_op jit(solution)/shard_map/ppermute | solution.py:19
  88.7 12.1 %collective-permute-start.34 = (bf16[256,512]{1,0:T(8,128)(2,1)S(1)}, bf16[256,512]{1,0:T(8,128)(2,1)S(1)}, u32[]{:S(2)}, u32[]{:S(2)}) collective-permute-start(bf16[256,512]{1,0:T(8,128)(2,1)S(1)} %get-tuple-element.87), channel_id=1, source_target_pairs={{0,1},{1,0},{2,3},{3,2},{4,5},{5,4},{6,7},{7,6},{8,9},{9,8},{10,11... | collective-permute-start | bytes 786440 | tf_op jit(solution)/shard_map/ppermute | solution.py:19
  89.6 11.2 %collective-permute-start.35 = (bf16[160,512]{1,0:T(8,128)(2,1)S(1)}, bf16[160,512]{1,0:T(8,128)(2,1)S(1)}, u32[]{:S(2)}, u32[]{:S(2)}) collective-permute-start(bf16[160,512]{1,0:T(8,128)(2,1)S(1)} %add_convert_fusion.3), channel_id=1, source_target_pairs={{0,6},{1,7},{2,4},{3,5},{4,2},{5,3},{6,0},{7,1},{8,14},{9,15},{10,... | collective-permute-start | bytes 491528 | tf_op jit(solution)/shard_map/ppermute | solution.py:19
  93.0 12.9 %collective-permute-start.30 = (bf16[256,512]{1,0:T(8,128)(2,1)S(1)}, bf16[256,512]{1,0:T(8,128)(2,1)S(1)}, u32[]{:S(2)}, u32[]{:S(2)}) collective-permute-start(bf16[256,512]{1,0:T(8,128)(2,1)S(1)} %get-tuple-element.80), channel_id=1, source_target_pairs={{0,1},{1,0},{2,3},{3,2},{4,5},{5,4},{6,7},{7,6},{8,9},{9,8},{10,11... | collective-permute-start | bytes 786440 | tf_op jit(solution)/shard_map/ppermute | solution.py:19
  93.9 16.8 %collective-permute-start.32 = (bf16[256,512]{1,0:T(8,128)(2,1)S(1)}, bf16[256,512]{1,0:T(8,128)(2,1)S(1)}, u32[]{:S(2)}, u32[]{:S(2)}) collective-permute-start(bf16[256,512]{1,0:T(8,128)(2,1)S(1)} %add_convert_fusion.2), channel_id=1, source_target_pairs={{0,4},{1,5},{2,6},{3,7},{4,0},{5,1},{6,2},{7,3},{8,12},{9,13},{10,... | collective-permute-start | bytes 786440 | tf_op jit(solution)/shard_map/ppermute | solution.py:19
  100.9 15.4 %collective-permute-start.36 = (bf16[256,512]{1,0:T(8,128)(2,1)S(1)}, bf16[256,512]{1,0:T(8,128)(2,1)S(1)}, u32[]{:S(2)}, u32[]{:S(2)}) collective-permute-start(bf16[256,512]{1,0:T(8,128)(2,1)S(1)} %add_convert_fusion.1), channel_id=1, source_target_pairs={{0,2},{1,3},{2,0},{3,1},{4,6},{5,7},{6,4},{7,5},{8,10},{9,11},{10,... | collective-permute-start | bytes 786440 | tf_op jit(solution)/shard_map/ppermute | solution.py:19

commit v7 on v6

--- a/solution.py
+++ b/solution.py
@@ -247,7 +247,7 @@
     for count in counts:
         weights.append(refs[:count])
         refs = refs[count:]
-    outs, heads, terms = refs[:9], refs[9], refs[10]
+    outs, heads, terms = refs[:8], refs[8], refs[9]
     node, head = lax.axis_index("node"), lax.axis_index("head")
     far, near = head // 2, head % 2
     for i in range(4):
@@ -267,26 +267,21 @@
                 )
                 total, first = term if total is None else total + term, last
             terms[4 * side + plane] = total.astype(jnp.bfloat16)
-    first = outs[7].shape[0]
-    for i in range(7):
+    for i in range(8):
         outs[i][...] = terms[i]
-    outs[7][...] = terms[7, :first, :]
-    outs[8][...] = terms[7, first:, :]
 
 
 def emit(parts, weights):
     rows = parts[0].shape[0]
     depth, cols = weights[0][0].shape
     counts = [len(pieces) for pieces in weights]
-    first = 3 * rows // 8
     flops = 2 * rows * depth * 4 * cols
     moved = 2 * (rows * depth + 4 * depth * cols + 4 * rows * cols)
     return pl.pallas_call(
         functools.partial(emit_kernel, counts),
-        out_shape=[jax.ShapeDtypeStruct((rows, cols // 2), jnp.bfloat16)] * 7
-        + [jax.ShapeDtypeStruct((part, cols // 2), jnp.bfloat16) for part in (first, rows - first)],
+        out_shape=[jax.ShapeDtypeStruct((rows, cols // 2), jnp.bfloat16)] * 8,
         in_specs=[vmem_spec()] * (4 + sum(counts)),
-        out_specs=[vmem_spec()] * 9,
+        out_specs=[vmem_spec()] * 8,
         scratch_shapes=[
             pltpu.VMEM((4, rows, DH), jnp.bfloat16),
             pltpu.VMEM((8, rows, cols // 2), jnp.bfloat16),
@@ -339,18 +334,12 @@
     def pair(mine, send):
         return mine.astype(jnp.float32) + along(send).astype(jnp.float32)
 
-    first = terms[7].shape[0]
-    pair_3 = [
-        pair(terms[3][:first], terms[7]).astype(jnp.bfloat16),
-        pair(terms[3][first:], terms[8]).astype(jnp.bfloat16),
-    ]
-    home_3 = [swap(part, "head", 6) for part in pair_3]
-    pair_2 = pair(terms[2], after(terms[6], pair_3[0])).astype(jnp.bfloat16)
-    pair_1 = pair(terms[1], after(terms[5], pair_3[1])).astype(jnp.bfloat16)
-    total = pair(terms[0], after(terms[4], home_3[0]))
-    total = total + swap(pair_2, "head", 4).astype(jnp.float32)
-    total = total + swap(after(pair_1, home_3[1]), "head", 2).astype(jnp.float32)
-    total = total + jnp.concatenate(home_3).astype(jnp.float32)
+    pair_3 = pair(terms[3], terms[7]).astype(jnp.bfloat16)
+    pair_2 = pair(terms[2], terms[6]).astype(jnp.bfloat16)
+    pair_1 = pair(terms[1], after(terms[5], pair_3)).astype(jnp.bfloat16)
+    total = pair(terms[0], after(terms[4], pair_2))
+    for i, part in ((3, pair_3), (2, pair_2), (1, pair_1)):
+        total = total + swap(part, "head", 2 * i).astype(jnp.float32)
     return total.astype(jnp.bfloat16)
 
 

time: 117 us -> 115 us (0.983)
  starting transfers between devices: 47.3 us -> 34.3 us
  waiting for transfers between devices: 58 us -> 68.2 us
    ppermute x37 -> x35, starting transfers between devices: 47.3 us -> 34.3 us  [swap(): return lax.ppermute(value, axis, [(i, i ^ mask) for i in range(peers)])]
    ppermute x37 -> x35, waiting for transfers between devices: 58 us -> 68.2 us  [swap(): return lax.ppermute(value, axis, [(i, i ^ mask) for i in range(peers)])]
  transfers between devices with their start and end apart: 37 -> 35, of which waited for: 18 -> 18; matrix products, arithmetic and copies ran while one was open for 2% -> 2% of each run, Pallas kernels for 5% -> 5%
where the time goes in v7:
time: 115 us; the launch traced here: 114 us
  waiting for transfers between devices  68.2 us (59%)
  starting transfers between devices  34.3 us (30%)
  Pallas kernels  7.39 us (6%)
  local copies, waits for them, and re-layouts  3.12 us (3%)
    ppermute x35, waiting for transfers between devices, swap(): return lax.ppermute(value, axis, [(i, i ^ mask) for i in range(peers)])  68.2 us
    ppermute x35, starting transfers between devices, swap(): return lax.ppermute(value, axis, [(i, i ^ mask) for i in range(peers)])  34.3 us
    pallas_call x2, Pallas kernels, project(): pl.pallas_call(functools.partial(project_kernel, counts), out_shape=[jax....  2.63 us
  transfers between devices with their start and end apart: 35, of which 18 were waited for; matrix products, arithmetic and copies ran while one was open for 2% of the time, Pallas kernels for 5%

profile of v7, /device:TPU:0, one launch (start us, length us, event | category | flops | bytes accessed | tf_op | source)
XLA Modules:
  0.0 114.4 jit_solution(11132787643274774163)
XLA Ops:
  0.0 0.5 collective-permute-start.12
  0.5 4.7 %collective-permute-start.3 = (bf16[256,512]{1,0:T(8,128)(2,1)}, bf16[256,512]{1,0:T(8,128)(2,1)S(1)}, u32[]{:S(2)}, u32[]{:S(2)}) collective-permute-start(bf16[256,512]{1,0:T(8,128)(2,1)} %close_ref.1), channel_id=1, source_target_pairs={{0,6},{1,7},{2,4},{3,5},{4,2},{5,3},{6,0},{7,1},{8,14},{9,15},{10,... | collective-permute-start | bytes 786440 | tf_op jit(solution)/shard_map/ppermute | solution.py:19
  5.1 0.2 collective-permute-start
  5.3 1.5 %collective-permute-start.1 = (s32[2,8]{1,0:T(2,128)}, s32[2,8]{1,0:T(2,128)S(1)}, u32[]{:S(2)}, u32[]{:S(2)}) collective-permute-start(s32[2,8]{1,0:T(2,128)} %param.10), channel_id=1, source_target_pairs={{0,16},{8,24},{16,0},{24,8},{1,17},{9,25},{17,1},{25,9},{2,18},{10... | collective-permute-start | bytes 200 | tf_op jit(solution)/shard_map/ppermute | solution.py:19
  6.8 1.1 slice.9
  7.9 0.3 collective-permute-start.2
  8.1 0.9 collective-permute-done.1
  9.1 2.1 %collective-permute-done.2 = s32[2,8]{1,0:T(2,128)S(1)} collective-permute-done((s32[2,8]{1,0:T(2,128)}, s32[2,8]{1,0:T(2,128)S(1)}, u32[]{:S(2)}, u32[]{:S(2)}) %collective-permute-start.2) | collective-permute-done | bytes 96 | tf_op jit(solution)/shard_map/ppermute | solution.py:19
  11.1 0.5 collective-permute-start.13
  11.7 0.5 collective-permute-start.6
  12.2 0.4 collective-permute-done.3.distant_ref
  12.6 0.9 copy-done.3
  13.6 1.7 %collective-permute-start.4 = (bf16[256,512]{1,0:T(8,128)(2,1)S(1)}, bf16[256,512]{1,0:T(8,128)(2,1)S(1)}, u32[]{:S(2)}, u32[]{:S(2)}) collective-permute-start(bf16[256,512]{1,0:T(8,128)(2,1)S(1)} %get-tuple-element.44.refs_0_), channel_id=1, source_target_pairs={{0,1},{1,0},{2,3},{3,2},{4,5},{5,4},{6,7},{7,6},{8,9},{9,8},{10,11... | collective-permute-start | bytes 786440 | tf_op jit(solution)/shard_map/ppermute | solution.py:19
  15.3 3.7 %collective-permute-done.5.close_ref = bf16[256,512]{1,0:T(8,128)(2,1)S(1)} collective-permute-done((bf16[256,512]{1,0:T(8,128)(2,1)}, bf16[256,512]{1,0:T(8,128)(2,1)S(1)}, u32[]{:S(2)}, u32[]{:S(2)}) %collective-permute-start.5) | collective-permute-done | bytes 262176 | tf_op jit(solution)/shard_map/ppermute | solution.py:19
  19.0 1.5 %collective-permute-start.8 = (bf16[256,512]{1,0:T(8,128)(2,1)S(1)}, bf16[256,512]{1,0:T(8,128)(2,1)S(1)}, u32[]{:S(2)}, u32[]{:S(2)}) collective-permute-start(bf16[256,512]{1,0:T(8,128)(2,1)S(1)} %get-tuple-element.48), channel_id=1, source_target_pairs={{0,16},{8,24},{16,0},{24,8},{1,17},{9,25},{17,1},{25,9},{2,18},{10... | collective-permute-start | bytes 786440 | tf_op jit(solution)/shard_map/ppermute | solution.py:19
  20.5 7.8 %collective-permute-done.6.distant_ref = bf16[256,512]{1,0:T(8,128)(2,1)S(1)} collective-permute-done((bf16[256,512]{1,0:T(8,128)(2,1)}, bf16[256,512]{1,0:T(8,128)(2,1)S(1)}, u32[]{:S(2)}, u32[]{:S(2)}) %collective-permute-start.6) | collective-permute-done | bytes 262176 | tf_op jit(solution)/shard_map/ppermute | solution.py:19
  28.3 1.1 fusion
  29.3 0.1 sort.3
  29.4 1.6 %collective-permute-start.10 = (bf16[256,512]{1,0:T(8,128)(2,1)S(1)}, bf16[256,512]{1,0:T(8,128)(2,1)S(1)}, u32[]{:S(2)}, u32[]{:S(2)}) collective-permute-start(bf16[256,512]{1,0:T(8,128)(2,1)S(1)} %get-tuple-element.49), channel_id=1, source_target_pairs={{0,16},{8,24},{16,0},{24,8},{1,17},{9,25},{17,1},{25,9},{2,18},{10... | collective-permute-start | bytes 786440 | tf_op jit(solution)/shard_map/ppermute | solution.py:19
  31.0 0.5 collective-permute-start.16
  31.5 1.5 %collective-permute-start.7 = (bf16[256,512]{1,0:T(8,128)(2,1)S(1)}, bf16[256,512]{1,0:T(8,128)(2,1)S(1)}, u32[]{:S(2)}, u32[]{:S(2)}) collective-permute-start(bf16[256,512]{1,0:T(8,128)(2,1)S(1)} %get-tuple-element.47.refs_2_), channel_id=1, source_target_pairs={{0,1},{1,0},{2,3},{3,2},{4,5},{5,4},{6,7},{7,6},{8,9},{9,8},{10,11... | collective-permute-start | bytes 786440 | tf_op jit(solution)/shard_map/ppermute | solution.py:19
  33.0 5.5 %collective-permute-done.10.refs_6_ = bf16[256,512]{1,0:T(8,128)(2,1)S(1)} collective-permute-done((bf16[256,512]{1,0:T(8,128)(2,1)S(1)}, bf16[256,512]{1,0:T(8,128)(2,1)S(1)}, u32[]{:S(2)}, u32[]{:S(2)}) %collective-permute-start.10) | collective-permute-done | bytes 262176 | tf_op jit(solution)/shard_map/ppermute | solution.py:19
  38.6 1.5 %collective-permute-start.9 = (bf16[256,512]{1,0:T(8,128)(2,1)S(1)}, bf16[256,512]{1,0:T(8,128)(2,1)S(1)}, u32[]{:S(2)}, u32[]{:S(2)}) collective-permute-start(bf16[256,512]{1,0:T(8,128)(2,1)S(1)} %collective-permute-done.8.refs_4_), channel_id=1, source_target_pairs={{0,1},{1,0},{2,3},{3,2},{4,5},{5,4},{6,7},{7,6},{8,9},{9,8},{10,11... | collective-permute-start | bytes 786440 | tf_op jit(solution)/shard_map/ppermute | solution.py:19
  40.1 3.7 %collective-permute-done.16.refs_7_ = bf16[128,1024]{1,0:T(8,128)(2,1)S(1)} collective-permute-done((bf16[128,1024]{1,0:T(8,128)(2,1)S(1)}, bf16[128,1024]{1,0:T(8,128)(2,1)S(1)}, u32[]{:S(2)}, u32[]{:S(2)}) %collective-permute-start.16) | collective-permute-done | bytes 262176 | tf_op jit(solution)/shard_map/ppermute | solution.py:19
  43.8 1.5 %collective-permute-start.11 = (bf16[256,512]{1,0:T(8,128)(2,1)S(1)}, bf16[256,512]{1,0:T(8,128)(2,1)S(1)}, u32[]{:S(2)}, u32[]{:S(2)}) collective-permute-start(bf16[256,512]{1,0:T(8,128)(2,1)S(1)} %collective-permute-done.10.refs_6_), channel_id=1, source_target_pairs={{0,1},{1,0},{2,3},{3,2},{4,5},{5,4},{6,7},{7,6},{8,9},{9,8},{10,11... | collective-permute-start | bytes 786440 | tf_op jit(solution)/shard_map/ppermute | solution.py:19
  45.4 1.6 %collective-permute-start.17 = (bf16[128,1024]{1,0:T(8,128)(2,1)S(1)}, bf16[128,1024]{1,0:T(8,128)(2,1)S(1)}, u32[]{:S(2)}, u32[]{:S(2)}) collective-permute-start(bf16[128,1024]{1,0:T(8,128)(2,1)S(1)} %get-tuple-element.56), channel_id=1, source_target_pairs={{0,16},{8,24},{16,0},{24,8},{1,17},{9,25},{17,1},{25,9},{2,18},{10... | collective-permute-start | bytes 786440 | tf_op jit(solution)/shard_map/ppermute | solution.py:19
  46.9 4.8 %collective-permute-done.11.refs_7_ = bf16[256,512]{1,0:T(8,128)(2,1)S(1)} collective-permute-done((bf16[256,512]{1,0:T(8,128)(2,1)S(1)}, bf16[256,512]{1,0:T(8,128)(2,1)S(1)}, u32[]{:S(2)}, u32[]{:S(2)}) %collective-permute-start.11) | collective-permute-done | bytes 262176 | tf_op jit(solution)/shard_map/ppermute | solution.py:19
  51.7 1.3 %project.2 = (f32[512,256]{1,0:T(8,128)S(1)}, bf16[512,256]{1,0:T(8,128)(2,1)S(1)}) custom-call(bf16[256,512]{1,0:T(8,128)(2,1)S(1)} %get-tuple-element.44.refs_0_, bf16[256,512]{1,0:T(8,128)(2,1)S(1)} %collective-permute-done.4.refs_1_, bf16[256,512]{1,0:T(8,128)(2,1)S(1)} %get-tuple-element.47.refs_2_, ...), custom_call_target="tpu_custom_call" | custom-call | flops 1073741824 | bytes 4980736 | tf_op jit(solution)/shard_map/project/pallas_call | solution.py:122
  53.1 1.6 %collective-permute-start.14 = (bf16[512,256]{1,0:T(8,128)(2,1)S(1)}, bf16[512,256]{1,0:T(8,128)(2,1)S(1)}, u32[]{:S(2)}, u32[]{:S(2)}) collective-permute-start(bf16[512,256]{1,0:T(8,128)(2,1)S(1)} %get-tuple-element.53), channel_id=1, source_target_pairs={{0,16},{8,24},{16,0},{24,8},{1,17},{9,25},{17,1},{25,9},{2,18},{10... | collective-permute-start | bytes 786440 | tf_op jit(solution)/shard_map/ppermute | solution.py:19
  54.6 1.3 %project.3 = (f32[512,256]{1,0:T(8,128)S(1)}, bf16[512,256]{1,0:T(8,128)(2,1)S(1)}) custom-call(bf16[256,512]{1,0:T(8,128)(2,1)S(1)} %get-tuple-element.44.refs_0_, bf16[256,512]{1,0:T(8,128)(2,1)S(1)} %collective-permute-done.4.refs_1_, bf16[256,512]{1,0:T(8,128)(2,1)S(1)} %get-tuple-element.47.refs_2_, ...), custom_call_target="tpu_custom_call" | custom-call | flops 1073741824 | bytes 4980736 | tf_op jit(solution)/shard_map/project/pallas_call | solution.py:122
  56.0 4.2 %collective-permute-done.14.moved_ref = bf16[512,256]{1,0:T(8,128)(2,1)S(1)} collective-permute-done((bf16[512,256]{1,0:T(8,128)(2,1)S(1)}, bf16[512,256]{1,0:T(8,128)(2,1)S(1)}, u32[]{:S(2)}, u32[]{:S(2)}) %collective-permute-start.14) | collective-permute-done | bytes 262176 | tf_op jit(solution)/shard_map/ppermute | solution.py:19
  60.2 0.1 combine.2
  60.2 0.1 collective-permute-start.18
  60.3 1.6 %collective-permute-start.19 = (bf16[512,256]{1,0:T(8,128)(2,1)S(1)}, bf16[512,256]{1,0:T(8,128)(2,1)S(1)}, u32[]{:S(2)}, u32[]{:S(2)}) collective-permute-start(bf16[512,256]{1,0:T(8,128)(2,1)S(1)} %get-tuple-element.54), channel_id=1, source_target_pairs={{0,16},{8,24},{16,0},{24,8},{1,17},{9,25},{17,1},{25,9},{2,18},{10... | collective-permute-start | bytes 786440 | tf_op jit(solution)/shard_map/ppermute | solution.py:19
  61.9 0.2 collective-permute-start.26
  62.0 0.3 collective-permute-start.27
  62.4 2.2 %weigh.1 = (bf16[1024,1024]{1,0:T(8,128)(2,1)S(1)}, f32[1024,1]{1,0:T(8,128)S(1)}) custom-call(s32[4,2,8]{2,1,0:T(2,128)S(1)} %pad_add_fusion.edge_ref, f32[4,237]{1,0:T(4,128)S(1)} %bitcast.5, bf16[512,128]{1,0:T(8,128)(2,1)S(1)} %get-tuple-element.58.mine_ref, bf16[512,128]{1,0:T(8,128)(2,1)S(1)} %collective-permute-done.18.theirs_ref), custom_call_target="tpu_custom_call" | custom-call | flops 268435456 | bytes 2097152 | tf_op jit(solution)/shard_map/weigh/pallas_call | solution.py:197
  64.6 4.4 %collective-permute-done.19.moved_ref = bf16[512,256]{1,0:T(8,128)(2,1)S(1)} collective-permute-done((bf16[512,256]{1,0:T(8,128)(2,1)S(1)}, bf16[512,256]{1,0:T(8,128)(2,1)S(1)}, u32[]{:S(2)}, u32[]{:S(2)}) %collective-permute-start.19) | collective-permute-done | bytes 262176 | tf_op jit(solution)/shard_map/ppermute | solution.py:19
  69.0 0.1 combine.3
  69.1 0.1 collective-permute-start.20
  69.2 1.3 %collective-permute-done.20.theirs_ref = bf16[512,128]{1,0:T(8,128)(2,1)S(1)} collective-permute-done((bf16[512,128]{1,0:T(8,128)(2,1)S(1)}, bf16[512,128]{1,0:T(8,128)(2,1)S(1)}, u32[]{:S(2)}, u32[]{:S(2)}) %collective-permute-start.20) | collective-permute-done | bytes 131104 | tf_op jit(solution)/shard_map/ppermute | solution.py:19
  70.5 0.7 average.1
  71.2 0.2 collective-permute-start.21
  71.4 1.5 %collective-permute-start.22 = (bf16[256,128]{1,0:T(8,128)(2,1)S(1)}, bf16[256,128]{1,0:T(8,128)(2,1)S(1)}, u32[]{:S(2)}, u32[]{:S(2)}) collective-permute-start(bf16[256,128]{1,0:T(8,128)(2,1)S(1)} %get-tuple-element.68), channel_id=1, source_target_pairs={{0,16},{8,24},{16,0},{24,8},{1,17},{9,25},{17,1},{25,9},{2,18},{10... | collective-permute-start | bytes 196616 | tf_op jit(solution)/shard_map/ppermute | solution.py:19
  72.9 0.2 collective-permute-start.23
  73.2 2.6 %collective-permute-done.22.refs_2_ = bf16[256,128]{1,0:T(8,128)(2,1)S(1)} collective-permute-done((bf16[256,128]{1,0:T(8,128)(2,1)S(1)}, bf16[256,128]{1,0:T(8,128)(2,1)S(1)}, u32[]{:S(2)}, u32[]{:S(2)}) %collective-permute-start.22) | collective-permute-done | bytes 65568 | tf_op jit(solution)/shard_map/ppermute | solution.py:19
  75.8 1.3 %collective-permute-done.23.refs_3_ = bf16[256,128]{1,0:T(8,128)(2,1)S(1)} collective-permute-done((bf16[256,128]{1,0:T(8,128)(2,1)S(1)}, bf16[256,128]{1,0:T(8,128)(2,1)S(1)}, u32[]{:S(2)}, u32[]{:S(2)}) %collective-permute-start.23) | collective-permute-done | bytes 65568 | tf_op jit(solution)/shard_map/ppermute | solution.py:19
  77.1 1.7 %emit.1 = (bf16[256,512]{1,0:T(8,128)(2,1)S(1)}, bf16[256,512]{1,0:T(8,128)(2,1)S(1)}, bf16[256,512]{1,0:T(8,128)(2,1)S(1)}, bf16[256,512]{1,0:T(8,128)(2,1)S(1)...) custom-call(bf16[256,128]{1,0:T(8,128)(2,1)S(1)} %get-tuple-element., ...), custom_call_target="tpu_custom_call" | custom-call | flops 1073741824 | bytes 6553600 | tf_op jit(solution)/shard_map/emit/pallas_call | solution.py:280
  78.8 1.6 %collective-permute-start.30 = (bf16[256,512]{1,0:T(8,128)(2,1)S(1)}, bf16[256,512]{1,0:T(8,128)(2,1)S(1)}, u32[]{:S(2)}, u32[]{:S(2)}) collective-permute-start(bf16[256,512]{1,0:T(8,128)(2,1)S(1)} %get-tuple-element.79), channel_id=1, source_target_pairs={{0,1},{1,0},{2,3},{3,2},{4,5},{5,4},{6,7},{7,6},{8,9},{9,8},{10,11... | collective-permute-start | bytes 786440 | tf_op jit(solution)/shard_map/ppermute | solution.py:19
  80.4 0.5 collective-permute-start.28
  80.9 7.1 %collective-permute-done.30 = bf16[256,512]{1,0:T(8,128)(2,1)S(1)} collective-permute-done((bf16[256,512]{1,0:T(8,128)(2,1)S(1)}, bf16[256,512]{1,0:T(8,128)(2,1)S(1)}, u32[]{:S(2)}, u32[]{:S(2)}) %collective-permute-start.30) | collective-permute-done | bytes 262176 | tf_op jit(solution)/shard_map/ppermute | solution.py:19
  88.0 0.1 add_convert_fusion.2
  88.1 1.6 %collective-permute-start.33 = (bf16[256,512]{1,0:T(8,128)(2,1)S(1)}, bf16[256,512]{1,0:T(8,128)(2,1)S(1)}, u32[]{:S(2)}, u32[]{:S(2)}) collective-permute-start(bf16[256,512]{1,0:T(8,128)(2,1)S(1)} %get-tuple-element.82), channel_id=1, source_target_pairs={{0,1},{1,0},{2,3},{3,2},{4,5},{5,4},{6,7},{7,6},{8,9},{9,8},{10,11... | collective-permute-start | bytes 786440 | tf_op jit(solution)/shard_map/ppermute | solution.py:19
  89.7 2.5 %collective-permute-start.31 = (bf16[256,512]{1,0:T(8,128)(2,1)S(1)}, bf16[256,512]{1,0:T(8,128)(2,1)S(1)}, u32[]{:S(2)}, u32[]{:S(2)}) collective-permute-start(bf16[256,512]{1,0:T(8,128)(2,1)S(1)} %add_convert_fusion.2), channel_id=1, source_target_pairs={{0,6},{1,7},{2,4},{3,5},{4,2},{5,3},{6,0},{7,1},{8,14},{9,15},{10,... | collective-permute-start | bytes 786440 | tf_op jit(solution)/shard_map/ppermute | solution.py:19
  92.2 1.4 %collective-permute-done.28 = bf16[256,512]{1,0:T(8,128)(2,1)S(1)} collective-permute-done((bf16[256,512]{1,0:T(8,128)(2,1)S(1)}, bf16[256,512]{1,0:T(8,128)(2,1)S(1)}, u32[]{:S(2)}, u32[]{:S(2)}) %collective-permute-start.28) | collective-permute-done | bytes 262176 | tf_op jit(solution)/shard_map/ppermute | solution.py:19
  93.6 0.1 add_convert_fusion.3
  93.7 0.1 collective-permute-start.32
  93.8 1.6 %collective-permute-start.29 = (bf16[256,512]{1,0:T(8,128)(2,1)S(1)}, bf16[256,512]{1,0:T(8,128)(2,1)S(1)}, u32[]{:S(2)}, u32[]{:S(2)}) collective-permute-start(bf16[256,512]{1,0:T(8,128)(2,1)S(1)} %get-tuple-element.77), channel_id=1, source_target_pairs={{0,1},{1,0},{2,3},{3,2},{4,5},{5,4},{6,7},{7,6},{8,9},{9,8},{10,11... | collective-permute-start | bytes 786440 | tf_op jit(solution)/shard_map/ppermute | solution.py:19
  95.3 3.9 %collective-permute-done.33 = bf16[256,512]{1,0:T(8,128)(2,1)S(1)} collective-permute-done((bf16[256,512]{1,0:T(8,128)(2,1)S(1)}, bf16[256,512]{1,0:T(8,128)(2,1)S(1)}, u32[]{:S(2)}, u32[]{:S(2)}) %collective-permute-start.33) | collective-permute-done | bytes 262176 | tf_op jit(solution)/shard_map/ppermute | solution.py:19
  99.2 0.1 add_convert_fusion.1
  99.3 1.2 %collective-permute-start.34 = (bf16[256,512]{1,0:T(8,128)(2,1)S(1)}, bf16[256,512]{1,0:T(8,128)(2,1)S(1)}, u32[]{:S(2)}, u32[]{:S(2)}) collective-permute-start(bf16[256,512]{1,0:T(8,128)(2,1)S(1)} %add_convert_fusion.1), channel_id=1, source_target_pairs={{0,2},{1,3},{2,0},{3,1},{4,6},{5,7},{6,4},{7,5},{8,10},{9,11},{10,... | collective-permute-start | bytes 786440 | tf_op jit(solution)/shard_map/ppermute | solution.py:19
  100.5 3.5 %collective-permute-done.29 = bf16[256,512]{1,0:T(8,128)(2,1)S(1)} collective-permute-done((bf16[256,512]{1,0:T(8,128)(2,1)S(1)}, bf16[256,512]{1,0:T(8,128)(2,1)S(1)}, u32[]{:S(2)}, u32[]{:S(2)}) %collective-permute-start.29) | collective-permute-done | bytes 262176 | tf_op jit(solution)/shard_map/ppermute | solution.py:19
  104.0 9.5 %collective-permute-done.32 = bf16[256,512]{1,0:T(8,128)(2,1)S(1)} collective-permute-done((bf16[256,512]{1,0:T(8,128)(2,1)S(1)}, bf16[256,512]{1,0:T(8,128)(2,1)S(1)}, u32[]{:S(2)}, u32[]{:S(2)}) %collective-permute-start.32) | collective-permute-done | bytes 262176 | tf_op jit(solution)/shard_map/ppermute | solution.py:19
  113.5 0.9 add_convert_fusion
  (34 shorter events, 0.1 us)
Async XLA Ops:
  0.0 51.7 %copy-start.1 = (bf16[1024,512]{1,0:T(8,128)(2,1)S(1)}, bf16[1024,512]{1,0:T(8,128)(2,1)}, u32[]{:S(2)}) copy-start(bf16[1024,512]{1,0:T(8,128)(2,1)} %refs_8_.2) | copy-start | bytes 3145732
  0.0 45.3 %copy-start = (bf16[512,1024]{1,0:T(8,128)(2,1)S(1)}, bf16[512,1024]{1,0:T(8,128)(2,1)}, u32[]{:S(2)}) copy-start(bf16[512,1024]{1,0:T(8,128)(2,1)} %refs_4_.1) | copy-start | bytes 3145732
  0.0 45.3 %collective-permute-start.12 = (bf16[1024,512]{1,0:T(8,128)(2,1)}, bf16[1024,512]{1,0:T(8,128)(2,1)S(1)}, u32[]{:S(2)}, u32[]{:S(2)}) collective-permute-start(bf16[1024,512]{1,0:T(8,128)(2,1)} %refs_8_.2), channel_id=1, source_target_pairs={{0,8},{8,0},{16,24},{24,16},{1,9},{9,1},{17,25},{25,17},{2,10},{10... | collective-permute-start | bytes 3145736 | tf_op jit(solution)/shard_map/ppermute | solution.py:19
  0.5 12.1 %collective-permute-start.3 = (bf16[256,512]{1,0:T(8,128)(2,1)}, bf16[256,512]{1,0:T(8,128)(2,1)S(1)}, u32[]{:S(2)}, u32[]{:S(2)}) collective-permute-start(bf16[256,512]{1,0:T(8,128)(2,1)} %close_ref.1), channel_id=1, source_target_pairs={{0,6},{1,7},{2,4},{3,5},{4,2},{5,3},{6,0},{7,1},{8,14},{9,15},{10,... | collective-permute-start | bytes 786440 | tf_op jit(solution)/shard_map/ppermute | solution.py:19
  5.1 13.9 %collective-permute-start.5 = (bf16[256,512]{1,0:T(8,128)(2,1)}, bf16[256,512]{1,0:T(8,128)(2,1)S(1)}, u32[]{:S(2)}, u32[]{:S(2)}) collective-permute-start(bf16[256,512]{1,0:T(8,128)(2,1)} %close_ref.1), channel_id=1, source_target_pairs={{0,2},{1,3},{2,0},{3,1},{4,6},{5,7},{6,4},{7,5},{8,10},{9,11},{10,... | collective-permute-start | bytes 786440 | tf_op jit(solution)/shard_map/ppermute | solution.py:19
  5.1 2.7 %collective-permute-start = (s32[2,8]{1,0:T(2,128)}, s32[2,8]{1,0:T(2,128)S(1)}, u32[]{:S(2)}, u32[]{:S(2)}) collective-permute-start(s32[2,8]{1,0:T(2,128)} %param.10), channel_id=1, source_target_pairs={{0,8},{8,0},{16,24},{24,16},{1,9},{9,1},{17,25},{25,17},{2,10},{10... | collective-permute-start | bytes 200 | tf_op jit(solution)/shard_map/ppermute | solution.py:19
  5.3 3.8 %collective-permute-start.1 = (s32[2,8]{1,0:T(2,128)}, s32[2,8]{1,0:T(2,128)S(1)}, u32[]{:S(2)}, u32[]{:S(2)}) collective-permute-start(s32[2,8]{1,0:T(2,128)} %param.10), channel_id=1, source_target_pairs={{0,16},{8,24},{16,0},{24,8},{1,17},{9,25},{17,1},{25,9},{2,18},{10... | collective-permute-start | bytes 200 | tf_op jit(solution)/shard_map/ppermute | solution.py:19
  7.9 3.3 %collective-permute-start.2 = (s32[2,8]{1,0:T(2,128)}, s32[2,8]{1,0:T(2,128)S(1)}, u32[]{:S(2)}, u32[]{:S(2)}) collective-permute-start(s32[2,8]{1,0:T(2,128)} %param.10), channel_id=1, source_target_pairs={{0,24},{8,16},{16,8},{24,0},{1,25},{9,17},{17,9},{25,1},{2,26},{10... | collective-permute-start | bytes 200 | tf_op jit(solution)/shard_map/ppermute | solution.py:19
  11.1 19.8 %collective-permute-start.13 = (bf16[256,1024]{1,0:T(8,128)(2,1)S(1)}, bf16[256,1024]{1,0:T(8,128)(2,1)S(1)}, u32[]{:S(2)}, u32[]{:S(2)}) collective-permute-start(bf16[256,1024]{1,0:T(8,128)(2,1)S(1)} %slice.9), channel_id=1, source_target_pairs={{0,16},{8,24},{16,0},{24,8},{1,17},{9,25},{17,1},{25,9},{2,18},{10... | collective-permute-start | bytes 1572872 | tf_op jit(solution)/shard_map/ppermute | solution.py:19
  11.7 16.6 %collective-permute-start.6 = (bf16[256,512]{1,0:T(8,128)(2,1)}, bf16[256,512]{1,0:T(8,128)(2,1)S(1)}, u32[]{:S(2)}, u32[]{:S(2)}) collective-permute-start(bf16[256,512]{1,0:T(8,128)(2,1)} %close_ref.1), channel_id=1, source_target_pairs={{0,4},{1,5},{2,6},{3,7},{4,0},{5,1},{6,2},{7,3},{8,12},{9,13},{10,... | collective-permute-start | bytes 786440 | tf_op jit(solution)/shard_map/ppermute | solution.py:19
  12.6 1.0 copy-start.3
  13.6 15.7 %collective-permute-start.4 = (bf16[256,512]{1,0:T(8,128)(2,1)S(1)}, bf16[256,512]{1,0:T(8,128)(2,1)S(1)}, u32[]{:S(2)}, u32[]{:S(2)}) collective-permute-start(bf16[256,512]{1,0:T(8,128)(2,1)S(1)} %get-tuple-element.44.refs_0_), channel_id=1, source_target_pairs={{0,1},{1,0},{2,3},{3,2},{4,5},{5,4},{6,7},{7,6},{8,9},{9,8},{10,11... | collective-permute-start | bytes 786440 | tf_op jit(solution)/shard_map/ppermute | solution.py:19
  19.0 12.0 %collective-permute-start.8 = (bf16[256,512]{1,0:T(8,128)(2,1)S(1)}, bf16[256,512]{1,0:T(8,128)(2,1)S(1)}, u32[]{:S(2)}, u32[]{:S(2)}) collective-permute-start(bf16[256,512]{1,0:T(8,128)(2,1)S(1)} %get-tuple-element.48), channel_id=1, source_target_pairs={{0,16},{8,24},{16,0},{24,8},{1,17},{9,25},{17,1},{25,9},{2,18},{10... | collective-permute-start | bytes 786440 | tf_op jit(solution)/shard_map/ppermute | solution.py:19
  28.3 26.4 %collective-permute-start.15 = (bf16[1024,512]{1,0:T(8,128)(2,1)}, bf16[1024,512]{1,0:T(8,128)(2,1)S(1)}, u32[]{:S(2)}, u32[]{:S(2)}) collective-permute-start(bf16[1024,512]{1,0:T(8,128)(2,1)} %refs_8_.3), channel_id=1, source_target_pairs={{0,8},{8,0},{16,24},{24,16},{1,9},{9,1},{17,25},{25,17},{2,10},{10... | collective-permute-start | bytes 3145736 | tf_op jit(solution)/shard_map/ppermute | solution.py:19
  29.4 9.2 %collective-permute-start.10 = (bf16[256,512]{1,0:T(8,128)(2,1)S(1)}, bf16[256,512]{1,0:T(8,128)(2,1)S(1)}, u32[]{:S(2)}, u32[]{:S(2)}) collective-permute-start(bf16[256,512]{1,0:T(8,128)(2,1)S(1)} %get-tuple-element.49), channel_id=1, source_target_pairs={{0,16},{8,24},{16,0},{24,8},{1,17},{9,25},{17,1},{25,9},{2,18},{10... | collective-permute-start | bytes 786440 | tf_op jit(solution)/shard_map/ppermute | solution.py:19
  31.0 12.8 %collective-permute-start.16 = (bf16[128,1024]{1,0:T(8,128)(2,1)S(1)}, bf16[128,1024]{1,0:T(8,128)(2,1)S(1)}, u32[]{:S(2)}, u32[]{:S(2)}) collective-permute-start(bf16[128,1024]{1,0:T(8,128)(2,1)S(1)} %get-tuple-element.55), channel_id=1, source_target_pairs={{0,16},{8,24},{16,0},{24,8},{1,17},{9,25},{17,1},{25,9},{2,18},{10... | collective-permute-start | bytes 786440 | tf_op jit(solution)/shard_map/ppermute | solution.py:19
  31.5 13.8 %collective-permute-start.7 = (bf16[256,512]{1,0:T(8,128)(2,1)S(1)}, bf16[256,512]{1,0:T(8,128)(2,1)S(1)}, u32[]{:S(2)}, u32[]{:S(2)}) collective-permute-start(bf16[256,512]{1,0:T(8,128)(2,1)S(1)} %get-tuple-element.47.refs_2_), channel_id=1, source_target_pairs={{0,1},{1,0},{2,3},{3,2},{4,5},{5,4},{6,7},{7,6},{8,9},{9,8},{10,11... | collective-permute-start | bytes 786440 | tf_op jit(solution)/shard_map/ppermute | solution.py:19
  38.6 8.3 %collective-permute-start.9 = (bf16[256,512]{1,0:T(8,128)(2,1)S(1)}, bf16[256,512]{1,0:T(8,128)(2,1)S(1)}, u32[]{:S(2)}, u32[]{:S(2)}) collective-permute-start(bf16[256,512]{1,0:T(8,128)(2,1)S(1)} %collective-permute-done.8.refs_4_), channel_id=1, source_target_pairs={{0,1},{1,0},{2,3},{3,2},{4,5},{5,4},{6,7},{7,6},{8,9},{9,8},{10,11... | collective-permute-start | bytes 786440 | tf_op jit(solution)/shard_map/ppermute | solution.py:19
  43.8 7.9 %collective-permute-start.11 = (bf16[256,512]{1,0:T(8,128)(2,1)S(1)}, bf16[256,512]{1,0:T(8,128)(2,1)S(1)}, u32[]{:S(2)}, u32[]{:S(2)}) collective-permute-start(bf16[256,512]{1,0:T(8,128)(2,1)S(1)} %collective-permute-done.10.refs_6_), channel_id=1, source_target_pairs={{0,1},{1,0},{2,3},{3,2},{4,5},{5,4},{6,7},{7,6},{8,9},{9,8},{10,11... | collective-permute-start | bytes 786440 | tf_op jit(solution)/shard_map/ppermute | solution.py:19
  45.3 31.8 %collective-permute-start.24 = (bf16[512,1024]{1,0:T(8,128)(2,1)S(1)}, bf16[512,1024]{1,0:T(8,128)(2,1)S(1)}, u32[]{:S(2)}, u32[]{:S(2)}) collective-permute-start(bf16[512,1024]{1,0:T(8,128)(2,1)S(1)} %copy-done), channel_id=1, source_target_pairs={{0,8},{8,0},{16,24},{24,16},{1,9},{9,1},{17,25},{25,17},{2,10},{10... | collective-permute-start | bytes 3145736 | tf_op jit(solution)/shard_map/ppermute | solution.py:19
  45.3 9.3 %copy-start.2 = (bf16[1024,512]{1,0:T(8,128)(2,1)S(1)}, bf16[1024,512]{1,0:T(8,128)(2,1)}, u32[]{:S(2)}) copy-start(bf16[1024,512]{1,0:T(8,128)(2,1)} %refs_8_.3) | copy-start | bytes 3145732
  45.4 10.6 %collective-permute-start.17 = (bf16[128,1024]{1,0:T(8,128)(2,1)S(1)}, bf16[128,1024]{1,0:T(8,128)(2,1)S(1)}, u32[]{:S(2)}, u32[]{:S(2)}) collective-permute-start(bf16[128,1024]{1,0:T(8,128)(2,1)S(1)} %get-tuple-element.56), channel_id=1, source_target_pairs={{0,16},{8,24},{16,0},{24,8},{1,17},{9,25},{17,1},{25,9},{2,18},{10... | collective-permute-start | bytes 786440 | tf_op jit(solution)/shard_map/ppermute | solution.py:19
  53.0 9.3 %copy-start.5 = (s32[2,8]{1,0:T(2,128)S(1)}, s32[2,8]{1,0:T(2,128)}, u32[]{:S(2)}) copy-start(s32[2,8]{1,0:T(2,128)} %param.10) | copy-start | bytes 196
  53.1 9.3 %copy-start.4 = (f32[237,4]{0,1:T(4,128)S(1)}, f32[237,4]{0,1:T(4,128)}, u32[]{:S(2)}) copy-start(f32[237,4]{0,1:T(4,128)} %param.11) | copy-start | bytes 11380
  53.1 7.1 %collective-permute-start.14 = (bf16[512,256]{1,0:T(8,128)(2,1)S(1)}, bf16[512,256]{1,0:T(8,128)(2,1)S(1)}, u32[]{:S(2)}, u32[]{:S(2)}) collective-permute-start(bf16[512,256]{1,0:T(8,128)(2,1)S(1)} %get-tuple-element.53), channel_id=1, source_target_pairs={{0,16},{8,24},{16,0},{24,8},{1,17},{9,25},{17,1},{25,9},{2,18},{10... | collective-permute-start | bytes 786440 | tf_op jit(solution)/shard_map/ppermute | solution.py:19
  54.6 18.3 %collective-permute-start.25 = (bf16[256,1024]{1,0:T(8,128)(2,1)S(1)}, bf16[256,1024]{1,0:T(8,128)(2,1)S(1)}, u32[]{:S(2)}, u32[]{:S(2)}) collective-permute-start(bf16[256,1024]{1,0:T(8,128)(2,1)S(1)} %collective-permute-done.13.refs_6_), channel_id=1, source_target_pairs={{0,8},{8,0},{16,24},{24,16},{1,9},{9,1},{17,25},{25,17},{2,10},{10... | collective-permute-start | bytes 1572872 | tf_op jit(solution)/shard_map/ppermute | solution.py:19
  60.2 1.8 %collective-permute-start.18 = (bf16[512,128]{1,0:T(8,128)(2,1)S(1)}, bf16[512,128]{1,0:T(8,128)(2,1)S(1)}, u32[]{:S(2)}, u32[]{:S(2)}) collective-permute-start(bf16[512,128]{1,0:T(8,128)(2,1)S(1)} %get-tuple-element.59), channel_id=1, source_target_pairs={{0,8},{8,0},{16,24},{24,16},{1,9},{9,1},{17,25},{25,17},{2,10},{10... | collective-permute-start | bytes 393224 | tf_op jit(solution)/shard_map/ppermute | solution.py:19
  60.3 8.7 %collective-permute-start.19 = (bf16[512,256]{1,0:T(8,128)(2,1)S(1)}, bf16[512,256]{1,0:T(8,128)(2,1)S(1)}, u32[]{:S(2)}, u32[]{:S(2)}) collective-permute-start(bf16[512,256]{1,0:T(8,128)(2,1)S(1)} %get-tuple-element.54), channel_id=1, source_target_pairs={{0,16},{8,24},{16,0},{24,8},{1,17},{9,25},{17,1},{25,9},{2,18},{10... | collective-permute-start | bytes 786440 | tf_op jit(solution)/shard_map/ppermute | solution.py:19
  61.9 9.6 %collective-permute-start.26 = (bf16[128,1024]{1,0:T(8,128)(2,1)S(1)}, bf16[128,1024]{1,0:T(8,128)(2,1)S(1)}, u32[]{:S(2)}, u32[]{:S(2)}) collective-permute-start(bf16[128,1024]{1,0:T(8,128)(2,1)S(1)} %collective-permute-done.16.refs_7_), channel_id=1, source_target_pairs={{0,8},{8,0},{16,24},{24,16},{1,9},{9,1},{17,25},{25,17},{2,10},{10... | collective-permute-start | bytes 786440 | tf_op jit(solution)/shard_map/ppermute | solution.py:19
  62.0 11.1 %collective-permute-start.27 = (bf16[128,1024]{1,0:T(8,128)(2,1)S(1)}, bf16[128,1024]{1,0:T(8,128)(2,1)S(1)}, u32[]{:S(2)}, u32[]{:S(2)}) collective-permute-start(bf16[128,1024]{1,0:T(8,128)(2,1)S(1)} %collective-permute-done.17.refs_8_), channel_id=1, source_target_pairs={{0,8},{8,0},{16,24},{24,16},{1,9},{9,1},{17,25},{25,17},{2,10},{10... | collective-permute-start | bytes 786440 | tf_op jit(solution)/shard_map/ppermute | solution.py:19
  69.1 1.4 %collective-permute-start.20 = (bf16[512,128]{1,0:T(8,128)(2,1)S(1)}, bf16[512,128]{1,0:T(8,128)(2,1)S(1)}, u32[]{:S(2)}, u32[]{:S(2)}) collective-permute-start(bf16[512,128]{1,0:T(8,128)(2,1)S(1)} %get-tuple-element.65), channel_id=1, source_target_pairs={{0,8},{8,0},{16,24},{24,16},{1,9},{9,1},{17,25},{25,17},{2,10},{10... | collective-permute-start | bytes 393224 | tf_op jit(solution)/shard_map/ppermute | solution.py:19
  71.2 1.9 %collective-permute-start.21 = (bf16[256,128]{1,0:T(8,128)(2,1)S(1)}, bf16[256,128]{1,0:T(8,128)(2,1)S(1)}, u32[]{:S(2)}, u32[]{:S(2)}) collective-permute-start(bf16[256,128]{1,0:T(8,128)(2,1)S(1)} %get-tuple-element.67), channel_id=1, source_target_pairs={{0,8},{8,0},{16,24},{24,16},{1,9},{9,1},{17,25},{25,17},{2,10},{10... | collective-permute-start | bytes 196616 | tf_op jit(solution)/shard_map/ppermute | solution.py:19
  71.4 4.4 %collective-permute-start.22 = (bf16[256,128]{1,0:T(8,128)(2,1)S(1)}, bf16[256,128]{1,0:T(8,128)(2,1)S(1)}, u32[]{:S(2)}, u32[]{:S(2)}) collective-permute-start(bf16[256,128]{1,0:T(8,128)(2,1)S(1)} %get-tuple-element.68), channel_id=1, source_target_pairs={{0,16},{8,24},{16,0},{24,8},{1,17},{9,25},{17,1},{25,9},{2,18},{10... | collective-permute-start | bytes 196616 | tf_op jit(solution)/shard_map/ppermute | solution.py:19
  72.9 4.1 %collective-permute-start.23 = (bf16[256,128]{1,0:T(8,128)(2,1)S(1)}, bf16[256,128]{1,0:T(8,128)(2,1)S(1)}, u32[]{:S(2)}, u32[]{:S(2)}) collective-permute-start(bf16[256,128]{1,0:T(8,128)(2,1)S(1)} %get-tuple-element.69), channel_id=1, source_target_pairs={{0,24},{8,16},{16,8},{24,0},{1,25},{9,17},{17,9},{25,1},{2,26},{10... | collective-permute-start | bytes 196616 | tf_op jit(solution)/shard_map/ppermute | solution.py:19
  78.8 9.2 %collective-permute-start.30 = (bf16[256,512]{1,0:T(8,128)(2,1)S(1)}, bf16[256,512]{1,0:T(8,128)(2,1)S(1)}, u32[]{:S(2)}, u32[]{:S(2)}) collective-permute-start(bf16[256,512]{1,0:T(8,128)(2,1)S(1)} %get-tuple-element.79), channel_id=1, source_target_pairs={{0,1},{1,0},{2,3},{3,2},{4,5},{5,4},{6,7},{7,6},{8,9},{9,8},{10,11... | collective-permute-start | bytes 786440 | tf_op jit(solution)/shard_map/ppermute | solution.py:19
  80.4 13.2 %collective-permute-start.28 = (bf16[256,512]{1,0:T(8,128)(2,1)S(1)}, bf16[256,512]{1,0:T(8,128)(2,1)S(1)}, u32[]{:S(2)}, u32[]{:S(2)}) collective-permute-start(bf16[256,512]{1,0:T(8,128)(2,1)S(1)} %get-tuple-element.76), channel_id=1, source_target_pairs={{0,1},{1,0},{2,3},{3,2},{4,5},{5,4},{6,7},{7,6},{8,9},{9,8},{10,11... | collective-permute-start | bytes 786440 | tf_op jit(solution)/shard_map/ppermute | solution.py:19
  88.1 11.2 %collective-permute-start.33 = (bf16[256,512]{1,0:T(8,128)(2,1)S(1)}, bf16[256,512]{1,0:T(8,128)(2,1)S(1)}, u32[]{:S(2)}, u32[]{:S(2)}) collective-permute-start(bf16[256,512]{1,0:T(8,128)(2,1)S(1)} %get-tuple-element.82), channel_id=1, source_target_pairs={{0,1},{1,0},{2,3},{3,2},{4,5},{5,4},{6,7},{7,6},{8,9},{9,8},{10,11... | collective-permute-start | bytes 786440 | tf_op jit(solution)/shard_map/ppermute | solution.py:19
  89.7 23.8 %collective-permute-start.31 = (bf16[256,512]{1,0:T(8,128)(2,1)S(1)}, bf16[256,512]{1,0:T(8,128)(2,1)S(1)}, u32[]{:S(2)}, u32[]{:S(2)}) collective-permute-start(bf16[256,512]{1,0:T(8,128)(2,1)S(1)} %add_convert_fusion.2), channel_id=1, source_target_pairs={{0,6},{1,7},{2,4},{3,5},{4,2},{5,3},{6,0},{7,1},{8,14},{9,15},{10,... | collective-permute-start | bytes 786440 | tf_op jit(solution)/shard_map/ppermute | solution.py:19
  93.7 19.8 %collective-permute-start.32 = (bf16[256,512]{1,0:T(8,128)(2,1)S(1)}, bf16[256,512]{1,0:T(8,128)(2,1)S(1)}, u32[]{:S(2)}, u32[]{:S(2)}) collective-permute-start(bf16[256,512]{1,0:T(8,128)(2,1)S(1)} %add_convert_fusion.3), channel_id=1, source_target_pairs={{0,4},{1,5},{2,6},{3,7},{4,0},{5,1},{6,2},{7,3},{8,12},{9,13},{10,... | collective-permute-start | bytes 786440 | tf_op jit(solution)/shard_map/ppermute | solution.py:19
  93.8 10.3 %collective-permute-start.29 = (bf16[256,512]{1,0:T(8,128)(2,1)S(1)}, bf16[256,512]{1,0:T(8,128)(2,1)S(1)}, u32[]{:S(2)}, u32[]{:S(2)}) collective-permute-start(bf16[256,512]{1,0:T(8,128)(2,1)S(1)} %get-tuple-element.77), channel_id=1, source_target_pairs={{0,1},{1,0},{2,3},{3,2},{4,5},{5,4},{6,7},{7,6},{8,9},{9,8},{10,11... | collective-permute-start | bytes 786440 | tf_op jit(solution)/shard_map/ppermute | solution.py:19
  99.3 14.2 %collective-permute-start.34 = (bf16[256,512]{1,0:T(8,128)(2,1)S(1)}, bf16[256,512]{1,0:T(8,128)(2,1)S(1)}, u32[]{:S(2)}, u32[]{:S(2)}) collective-permute-start(bf16[256,512]{1,0:T(8,128)(2,1)S(1)} %add_convert_fusion.1), channel_id=1, source_target_pairs={{0,2},{1,3},{2,0},{3,1},{4,6},{5,7},{6,4},{7,5},{8,10},{9,11},{10,... | collective-permute-start | bytes 786440 | tf_op jit(solution)/shard_map/ppermute | solution.py:19

commit v8 on v7

--- a/solution.py
+++ b/solution.py
@@ -241,34 +241,78 @@
     )(weights, total, mine, theirs)
 
 
-def emit_kernel(counts, *refs):
+def unpack(counts, refs):
     parts, refs = refs[:4], refs[4:]
     weights = []
     for count in counts:
         weights.append(refs[:count])
         refs = refs[count:]
-    outs, heads, terms = refs[:8], refs[8], refs[9]
+    return parts, weights, refs
+
+
+def gather_heads(parts, heads):
+    node = lax.axis_index("node")
+    for i in range(4):
+        heads[node ^ i] = parts[i][...]
+    return jnp.concatenate([heads[i] for i in range(4)], axis=1)
+
+
+def product(attn, held, start, width):
+    total, first = None, 0
+    for ref in held:
+        last = first + ref.shape[0]
+        term = jnp.dot(
+            attn[:, first:last], ref[:, pl.ds(start, width)], preferred_element_type=jnp.float32
+        )
+        total, first = term if total is None else total + term, last
+    return total.astype(jnp.bfloat16)
+
+
+def lead_kernel(counts, *refs):
+    parts, weights, (out_ref, heads) = unpack(counts, refs)
+    node, head = lax.axis_index("node"), lax.axis_index("head")
+    attn = gather_heads(parts, heads)
+    width = out_ref.shape[1]
+    start = pl.multiple_of((head % 2 ^ 1) * width, width)
+
+    def work(i):
+        out_ref[...] = product(attn, weights[i], start, width)
+
+    for i in range(4):
+        pl.when(node ^ i ^ (head // 2) == 3)(functools.partial(work, i))
+
+
+def emit_kernel(counts, *refs):
+    parts, weights, refs = unpack(counts, refs)
+    outs, heads, terms = refs[:7], refs[7], refs[8]
     node, head = lax.axis_index("node"), lax.axis_index("head")
     far, near = head // 2, head % 2
-    for i in range(4):
-        heads[node ^ i] = parts[i][...]
-    attn = jnp.concatenate([heads[i] for i in range(4)], axis=1)
+    attn = gather_heads(parts, heads)
     width = outs[0].shape[1]
     for i in range(4):
-        plane = node ^ i ^ far
         for side in range(2):
             start = pl.multiple_of((near ^ side) * width, width)
-            total, first = None, 0
-            for ref in weights[i]:
-                last = first + ref.shape[0]
-                term = jnp.dot(
-                    attn[:, first:last], ref[:, pl.ds(start, width)],
-                    preferred_element_type=jnp.float32,
-                )
-                total, first = term if total is None else total + term, last
-            terms[4 * side + plane] = total.astype(jnp.bfloat16)
-    for i in range(8):
+            terms[4 * side + (node ^ i ^ far)] = product(attn, weights[i], start, width)
+    for i in range(7):
         outs[i][...] = terms[i]
+
+
+def lead(parts, weights):
+    rows = parts[0].shape[0]
+    depth, cols = weights[0][0].shape
+    counts = [len(pieces) for pieces in weights]
+    return pl.pallas_call(
+        functools.partial(lead_kernel, counts),
+        out_shape=jax.ShapeDtypeStruct((rows, cols // 2), jnp.bfloat16),
+        in_specs=[vmem_spec()] * (4 + sum(counts)),
+        out_specs=vmem_spec(),
+        scratch_shapes=[pltpu.VMEM((4, rows, DH), jnp.bfloat16)],
+        compiler_params=pltpu.CompilerParams(vmem_limit_bytes=16 * 2**20),
+        cost_estimate=pl.CostEstimate(
+            flops=rows * depth * cols, bytes_accessed=depth * cols, transcendentals=0
+        ),
+        name="lead",
+    )(*parts, *[piece for pieces in weights for piece in pieces])
 
 
 def emit(parts, weights):
@@ -279,9 +323,9 @@
     moved = 2 * (rows * depth + 4 * depth * cols + 4 * rows * cols)
     return pl.pallas_call(
         functools.partial(emit_kernel, counts),
-        out_shape=[jax.ShapeDtypeStruct((rows, cols // 2), jnp.bfloat16)] * 8,
+        out_shape=[jax.ShapeDtypeStruct((rows, cols // 2), jnp.bfloat16)] * 7,
         in_specs=[vmem_spec()] * (4 + sum(counts)),
-        out_specs=[vmem_spec()] * 8,
+        out_specs=[vmem_spec()] * 7,
         scratch_shapes=[
             pltpu.VMEM((4, rows, DH), jnp.bfloat16),
             pltpu.VMEM((8, rows, cols // 2), jnp.bfloat16),
@@ -313,7 +357,7 @@
     moved_1y = [along(part) for part in moved_1]
     out_third = across(after(w_out[3 * depth // 4 :], moved_1[-1], out_second))
     qk_beside, val_beside = beside(w_qk), beside(w_val)
-    qk_beside = after(qk_beside, out_first)
+
     pieces = [keep_0, keep_0y, keep_1, keep_1y, moved_0, moved_0y, moved_1, moved_1y]
 
     qk_keep, qk_send = project(pieces, [w_qk, qk_beside])
@@ -329,12 +373,13 @@
     out_across = [out_first, out_second, out_third]
     out_beside = beside(after(w_out, moved_1[0]))
     out_diagonal = [beside(after(piece, moved_1[0])) for piece in out_across[:2]] + [beside(out_third)]
+    first_send = lead(attn, [[w_out], [out_beside], out_across, out_diagonal])
     terms = emit(attn, [[w_out], [out_beside], out_across, out_diagonal])
 
     def pair(mine, send):
         return mine.astype(jnp.float32) + along(send).astype(jnp.float32)
 
-    pair_3 = pair(terms[3], terms[7]).astype(jnp.bfloat16)
+    pair_3 = pair(terms[3], first_send).astype(jnp.bfloat16)
     pair_2 = pair(terms[2], terms[6]).astype(jnp.bfloat16)
     pair_1 = pair(terms[1], after(terms[5], pair_3)).astype(jnp.bfloat16)
     total = pair(terms[0], after(terms[4], pair_2))

time: 115 us -> 115 us (level)
  starting transfers between devices: 34.3 us -> 40.1 us
  waiting for transfers between devices: 68.2 us -> 63.4 us
    ppermute x35, starting transfers between devices: 34.3 us -> 40.1 us  [swap(): return lax.ppermute(value, axis, [(i, i ^ mask) for i in range(peers)])]
    ppermute x35, waiting for transfers between devices: 68.2 us -> 63.4 us  [swap(): return lax.ppermute(value, axis, [(i, i ^ mask) for i in range(peers)])]
  transfers between devices with their start and end apart: 35 -> 35, of which waited for: 18 -> 20; matrix products, arithmetic and copies ran while one was open for 2% -> 1% of each run, Pallas kernels for 5% -> 6%
where the time goes in v8:
time: 115 us
  waiting for transfers between devices  63.4 us (55%)
  starting transfers between devices  40.1 us (35%)
  Pallas kernels  7.81 us (7%)
  local copies, waits for them, and re-layouts  2.09 us (2%)
    ppermute x35, waiting for transfers between devices, swap(): return lax.ppermute(value, axis, [(i, i ^ mask) for i in range(peers)])  63.4 us
    ppermute x35, starting transfers between devices, swap(): return lax.ppermute(value, axis, [(i, i ^ mask) for i in range(peers)])  40.1 us
    pallas_call x2, Pallas kernels, project(): pl.pallas_call(functools.partial(project_kernel, counts), out_shape=[jax....  2.63 us
  transfers between devices with their start and end apart: 35, of which 20 were waited for; matrix products, arithmetic and copies ran while one was open for 1% of the time, Pallas kernels for 6%

profile of v8, /device:TPU:0, one launch (start us, length us, event | category | flops | bytes accessed | tf_op | source)
XLA Modules:
  0.0 114.6 jit_solution(15348172950557310352)
XLA Ops:
  0.0 5.0 %collective-permute-start.3 = (bf16[256,512]{1,0:T(8,128)(2,1)}, bf16[256,512]{1,0:T(8,128)(2,1)S(1)}, u32[]{:S(2)}, u32[]{:S(2)}) collective-permute-start(bf16[256,512]{1,0:T(8,128)(2,1)} %close_ref.1), channel_id=1, source_target_pairs={{0,6},{1,7},{2,4},{3,5},{4,2},{5,3},{6,0},{7,1},{8,14},{9,15},{10,... | collective-permute-start | bytes 786440 | tf_op jit(solution)/shard_map/ppermute | solution.py:19
  5.1 0.6 collective-permute-start.6
  5.7 1.7 %collective-permute-start.2 = (s32[2,8]{1,0:T(2,128)}, s32[2,8]{1,0:T(2,128)S(1)}, u32[]{:S(2)}, u32[]{:S(2)}) collective-permute-start(s32[2,8]{1,0:T(2,128)} %param.10), channel_id=1, source_target_pairs={{0,24},{8,16},{16,8},{24,0},{1,25},{9,17},{17,9},{25,1},{2,26},{10... | collective-permute-start | bytes 200 | tf_op jit(solution)/shard_map/ppermute | solution.py:19
  7.4 1.5 %collective-permute-done.2 = s32[2,8]{1,0:T(2,128)S(1)} collective-permute-done((s32[2,8]{1,0:T(2,128)}, s32[2,8]{1,0:T(2,128)S(1)}, u32[]{:S(2)}, u32[]{:S(2)}) %collective-permute-start.2) | collective-permute-done | bytes 96 | tf_op jit(solution)/shard_map/ppermute | solution.py:19
  9.0 1.6 %collective-permute-start.1 = (s32[2,8]{1,0:T(2,128)}, s32[2,8]{1,0:T(2,128)S(1)}, u32[]{:S(2)}, u32[]{:S(2)}) collective-permute-start(s32[2,8]{1,0:T(2,128)} %param.10), channel_id=1, source_target_pairs={{0,16},{8,24},{16,0},{24,8},{1,17},{9,25},{17,1},{25,9},{2,18},{10... | collective-permute-start | bytes 200 | tf_op jit(solution)/shard_map/ppermute | solution.py:19
  10.5 2.2 %collective-permute-done.1 = s32[2,8]{1,0:T(2,128)S(1)} collective-permute-done((s32[2,8]{1,0:T(2,128)}, s32[2,8]{1,0:T(2,128)S(1)}, u32[]{:S(2)}, u32[]{:S(2)}) %collective-permute-start.1) | collective-permute-done | bytes 96 | tf_op jit(solution)/shard_map/ppermute | solution.py:19
  12.7 1.1 slice.11
  13.8 0.3 collective-permute-done
  14.1 1.6 %collective-permute-start.15 = (bf16[256,1024]{1,0:T(8,128)(2,1)S(1)}, bf16[256,1024]{1,0:T(8,128)(2,1)S(1)}, u32[]{:S(2)}, u32[]{:S(2)}) collective-permute-start(bf16[256,1024]{1,0:T(8,128)(2,1)S(1)} %slice.11), channel_id=1, source_target_pairs={{0,16},{8,24},{16,0},{24,8},{1,17},{9,25},{17,1},{25,9},{2,18},{10... | collective-permute-start | bytes 1572872 | tf_op jit(solution)/shard_map/ppermute | solution.py:19
  15.7 0.9 copy-done.3
  16.7 1.6 %collective-permute-start.4 = (bf16[256,512]{1,0:T(8,128)(2,1)S(1)}, bf16[256,512]{1,0:T(8,128)(2,1)S(1)}, u32[]{:S(2)}, u32[]{:S(2)}) collective-permute-start(bf16[256,512]{1,0:T(8,128)(2,1)S(1)} %get-tuple-element.42.refs_0_), channel_id=1, source_target_pairs={{0,1},{1,0},{2,3},{3,2},{4,5},{5,4},{6,7},{7,6},{8,9},{9,8},{10,11... | collective-permute-start | bytes 786440 | tf_op jit(solution)/shard_map/ppermute | solution.py:19
  18.3 0.1 collective-permute-done.5.close_ref
  18.3 1.4 %collective-permute-start.8 = (bf16[256,512]{1,0:T(8,128)(2,1)S(1)}, bf16[256,512]{1,0:T(8,128)(2,1)S(1)}, u32[]{:S(2)}, u32[]{:S(2)}) collective-permute-start(bf16[256,512]{1,0:T(8,128)(2,1)S(1)} %get-tuple-element.46), channel_id=1, source_target_pairs={{0,16},{8,24},{16,0},{24,8},{1,17},{9,25},{17,1},{25,9},{2,18},{10... | collective-permute-start | bytes 786440 | tf_op jit(solution)/shard_map/ppermute | solution.py:19
  19.7 7.9 %collective-permute-done.6.distant_ref = bf16[256,512]{1,0:T(8,128)(2,1)S(1)} collective-permute-done((bf16[256,512]{1,0:T(8,128)(2,1)}, bf16[256,512]{1,0:T(8,128)(2,1)S(1)}, u32[]{:S(2)}, u32[]{:S(2)}) %collective-permute-start.6) | collective-permute-done | bytes 262176 | tf_op jit(solution)/shard_map/ppermute | solution.py:19
  27.6 1.6 %collective-permute-start.7 = (bf16[256,512]{1,0:T(8,128)(2,1)S(1)}, bf16[256,512]{1,0:T(8,128)(2,1)S(1)}, u32[]{:S(2)}, u32[]{:S(2)}) collective-permute-start(bf16[256,512]{1,0:T(8,128)(2,1)S(1)} %get-tuple-element.45.refs_2_), channel_id=1, source_target_pairs={{0,1},{1,0},{2,3},{3,2},{4,5},{5,4},{6,7},{7,6},{8,9},{9,8},{10,11... | collective-permute-start | bytes 786440 | tf_op jit(solution)/shard_map/ppermute | solution.py:19
  29.2 4.6 %collective-permute-done.8.refs_4_ = bf16[256,512]{1,0:T(8,128)(2,1)S(1)} collective-permute-done((bf16[256,512]{1,0:T(8,128)(2,1)S(1)}, bf16[256,512]{1,0:T(8,128)(2,1)S(1)}, u32[]{:S(2)}, u32[]{:S(2)}) %collective-permute-start.8) | collective-permute-done | bytes 262176 | tf_op jit(solution)/shard_map/ppermute | solution.py:19
  33.9 1.6 %collective-permute-start.10 = (bf16[256,512]{1,0:T(8,128)(2,1)S(1)}, bf16[256,512]{1,0:T(8,128)(2,1)S(1)}, u32[]{:S(2)}, u32[]{:S(2)}) collective-permute-start(bf16[256,512]{1,0:T(8,128)(2,1)S(1)} %get-tuple-element.47), channel_id=1, source_target_pairs={{0,16},{8,24},{16,0},{24,8},{1,17},{9,25},{17,1},{25,9},{2,18},{10... | collective-permute-start | bytes 786440 | tf_op jit(solution)/shard_map/ppermute | solution.py:19
  35.5 0.5 collective-permute-start.16
  36.0 0.4 collective-permute-done.7.refs_3_
  36.4 1.5 %collective-permute-start.9 = (bf16[256,512]{1,0:T(8,128)(2,1)S(1)}, bf16[256,512]{1,0:T(8,128)(2,1)S(1)}, u32[]{:S(2)}, u32[]{:S(2)}) collective-permute-start(bf16[256,512]{1,0:T(8,128)(2,1)S(1)} %collective-permute-done.8.refs_4_), channel_id=1, source_target_pairs={{0,1},{1,0},{2,3},{3,2},{4,5},{5,4},{6,7},{7,6},{8,9},{9,8},{10,11... | collective-permute-start | bytes 786440 | tf_op jit(solution)/shard_map/ppermute | solution.py:19
  37.9 5.2 %collective-permute-done.10.refs_6_ = bf16[256,512]{1,0:T(8,128)(2,1)S(1)} collective-permute-done((bf16[256,512]{1,0:T(8,128)(2,1)S(1)}, bf16[256,512]{1,0:T(8,128)(2,1)S(1)}, u32[]{:S(2)}, u32[]{:S(2)}) %collective-permute-start.10) | collective-permute-done | bytes 262176 | tf_op jit(solution)/shard_map/ppermute | solution.py:19
  43.1 1.6 %collective-permute-start.11 = (bf16[256,512]{1,0:T(8,128)(2,1)S(1)}, bf16[256,512]{1,0:T(8,128)(2,1)S(1)}, u32[]{:S(2)}, u32[]{:S(2)}) collective-permute-start(bf16[256,512]{1,0:T(8,128)(2,1)S(1)} %collective-permute-done.10.refs_6_), channel_id=1, source_target_pairs={{0,1},{1,0},{2,3},{3,2},{4,5},{5,4},{6,7},{7,6},{8,9},{9,8},{10,11... | collective-permute-start | bytes 786440 | tf_op jit(solution)/shard_map/ppermute | solution.py:19
  44.7 2.5 %collective-permute-done.16.refs_7_ = bf16[128,1024]{1,0:T(8,128)(2,1)S(1)} collective-permute-done((bf16[128,1024]{1,0:T(8,128)(2,1)S(1)}, bf16[128,1024]{1,0:T(8,128)(2,1)S(1)}, u32[]{:S(2)}, u32[]{:S(2)}) %collective-permute-start.16) | collective-permute-done | bytes 262176 | tf_op jit(solution)/shard_map/ppermute | solution.py:19
  47.2 1.6 %collective-permute-start.17 = (bf16[128,1024]{1,0:T(8,128)(2,1)S(1)}, bf16[128,1024]{1,0:T(8,128)(2,1)S(1)}, u32[]{:S(2)}, u32[]{:S(2)}) collective-permute-start(bf16[128,1024]{1,0:T(8,128)(2,1)S(1)} %get-tuple-element.53), channel_id=1, source_target_pairs={{0,16},{8,24},{16,0},{24,8},{1,17},{9,25},{17,1},{25,9},{2,18},{10... | collective-permute-start | bytes 786440 | tf_op jit(solution)/shard_map/ppermute | solution.py:19
  48.8 1.1 collective-permute-done.11.refs_7_
  50.0 1.3 %project.2 = (f32[512,256]{1,0:T(8,128)S(1)}, bf16[512,256]{1,0:T(8,128)(2,1)S(1)}) custom-call(bf16[256,512]{1,0:T(8,128)(2,1)S(1)} %get-tuple-element.42.refs_0_, bf16[256,512]{1,0:T(8,128)(2,1)S(1)} %collective-permute-done.4.refs_1_, bf16[256,512]{1,0:T(8,128)(2,1)S(1)} %get-tuple-element.45.refs_2_, ...), custom_call_target="tpu_custom_call" | custom-call | flops 1073741824 | bytes 4980736 | tf_op jit(solution)/shard_map/project/pallas_call | solution.py:122
  51.3 0.0 copy-start.5
  51.3 1.5 %collective-permute-start.13 = (bf16[512,256]{1,0:T(8,128)(2,1)S(1)}, bf16[512,256]{1,0:T(8,128)(2,1)S(1)}, u32[]{:S(2)}, u32[]{:S(2)}) collective-permute-start(bf16[512,256]{1,0:T(8,128)(2,1)S(1)} %get-tuple-element.49), channel_id=1, source_target_pairs={{0,16},{8,24},{16,0},{24,8},{1,17},{9,25},{17,1},{25,9},{2,18},{10... | collective-permute-start | bytes 786440 | tf_op jit(solution)/shard_map/ppermute | solution.py:19
  52.9 1.3 %project.3 = (f32[512,256]{1,0:T(8,128)S(1)}, bf16[512,256]{1,0:T(8,128)(2,1)S(1)}) custom-call(bf16[256,512]{1,0:T(8,128)(2,1)S(1)} %get-tuple-element.42.refs_0_, bf16[256,512]{1,0:T(8,128)(2,1)S(1)} %collective-permute-done.4.refs_1_, bf16[256,512]{1,0:T(8,128)(2,1)S(1)} %get-tuple-element.45.refs_2_, ...), custom_call_target="tpu_custom_call" | custom-call | flops 1073741824 | bytes 4980736 | tf_op jit(solution)/shard_map/project/pallas_call | solution.py:122
  54.2 2.2 %collective-permute-done.17.refs_8_ = bf16[128,1024]{1,0:T(8,128)(2,1)S(1)} collective-permute-done((bf16[128,1024]{1,0:T(8,128)(2,1)S(1)}, bf16[128,1024]{1,0:T(8,128)(2,1)S(1)}, u32[]{:S(2)}, u32[]{:S(2)}) %collective-permute-start.17) | collective-permute-done | bytes 262176 | tf_op jit(solution)/shard_map/ppermute | solution.py:19
  56.4 5.2 %collective-permute-done.13.moved_ref = bf16[512,256]{1,0:T(8,128)(2,1)S(1)} collective-permute-done((bf16[512,256]{1,0:T(8,128)(2,1)S(1)}, bf16[512,256]{1,0:T(8,128)(2,1)S(1)}, u32[]{:S(2)}, u32[]{:S(2)}) %collective-permute-start.13) | collective-permute-done | bytes 262176 | tf_op jit(solution)/shard_map/ppermute | solution.py:19
  61.5 0.1 combine.2
  61.6 0.1 collective-permute-start.18
  61.7 1.6 %collective-permute-start.19 = (bf16[512,256]{1,0:T(8,128)(2,1)S(1)}, bf16[512,256]{1,0:T(8,128)(2,1)S(1)}, u32[]{:S(2)}, u32[]{:S(2)}) collective-permute-start(bf16[512,256]{1,0:T(8,128)(2,1)S(1)} %get-tuple-element.50), channel_id=1, source_target_pairs={{0,16},{8,24},{16,0},{24,8},{1,17},{9,25},{17,1},{25,9},{2,18},{10... | collective-permute-start | bytes 786440 | tf_op jit(solution)/shard_map/ppermute | solution.py:19
  63.3 0.2 collective-permute-start.26
  63.5 0.3 collective-permute-start.27
  63.8 2.2 %weigh.1 = (bf16[1024,1024]{1,0:T(8,128)(2,1)S(1)}, f32[1024,1]{1,0:T(8,128)S(1)}) custom-call(s32[4,2,8]{2,1,0:T(2,128)S(1)} %pad_add_fusion.edge_ref, f32[4,237]{1,0:T(4,128)S(1)} %bitcast.5, bf16[512,128]{1,0:T(8,128)(2,1)S(1)} %get-tuple-element.55.mine_ref, bf16[512,128]{1,0:T(8,128)(2,1)S(1)} %collective-permute-done.18.theirs_ref), custom_call_target="tpu_custom_call" | custom-call | flops 268435456 | bytes 2097152 | tf_op jit(solution)/shard_map/weigh/pallas_call | solution.py:197
  66.1 4.3 %collective-permute-done.19.moved_ref = bf16[512,256]{1,0:T(8,128)(2,1)S(1)} collective-permute-done((bf16[512,256]{1,0:T(8,128)(2,1)S(1)}, bf16[512,256]{1,0:T(8,128)(2,1)S(1)}, u32[]{:S(2)}, u32[]{:S(2)}) %collective-permute-start.19) | collective-permute-done | bytes 262176 | tf_op jit(solution)/shard_map/ppermute | solution.py:19
  70.4 0.1 combine.3
  70.5 0.1 collective-permute-start.20
  70.6 1.3 %collective-permute-done.20.theirs_ref = bf16[512,128]{1,0:T(8,128)(2,1)S(1)} collective-permute-done((bf16[512,128]{1,0:T(8,128)(2,1)S(1)}, bf16[512,128]{1,0:T(8,128)(2,1)S(1)}, u32[]{:S(2)}, u32[]{:S(2)}) %collective-permute-start.20) | collective-permute-done | bytes 131104 | tf_op jit(solution)/shard_map/ppermute | solution.py:19
  71.9 0.7 average.1
  72.6 0.2 collective-permute-start.21
  72.8 1.6 %collective-permute-start.22 = (bf16[256,128]{1,0:T(8,128)(2,1)S(1)}, bf16[256,128]{1,0:T(8,128)(2,1)S(1)}, u32[]{:S(2)}, u32[]{:S(2)}) collective-permute-start(bf16[256,128]{1,0:T(8,128)(2,1)S(1)} %get-tuple-element.65), channel_id=1, source_target_pairs={{0,16},{8,24},{16,0},{24,8},{1,17},{9,25},{17,1},{25,9},{2,18},{10... | collective-permute-start | bytes 196616 | tf_op jit(solution)/shard_map/ppermute | solution.py:19
  74.4 0.1 collective-permute-start.23
  74.5 2.6 %collective-permute-done.22.refs_2_ = bf16[256,128]{1,0:T(8,128)(2,1)S(1)} collective-permute-done((bf16[256,128]{1,0:T(8,128)(2,1)S(1)}, bf16[256,128]{1,0:T(8,128)(2,1)S(1)}, u32[]{:S(2)}, u32[]{:S(2)}) %collective-permute-start.22) | collective-permute-done | bytes 65568 | tf_op jit(solution)/shard_map/ppermute | solution.py:19
  77.2 1.4 %collective-permute-done.23.refs_3_ = bf16[256,128]{1,0:T(8,128)(2,1)S(1)} collective-permute-done((bf16[256,128]{1,0:T(8,128)(2,1)S(1)}, bf16[256,128]{1,0:T(8,128)(2,1)S(1)}, u32[]{:S(2)}, u32[]{:S(2)}) %collective-permute-start.23) | collective-permute-done | bytes 65568 | tf_op jit(solution)/shard_map/ppermute | solution.py:19
  78.6 0.4 lead.1
  79.0 1.6 %collective-permute-start.30 = (bf16[256,512]{1,0:T(8,128)(2,1)S(1)}, bf16[256,512]{1,0:T(8,128)(2,1)S(1)}, u32[]{:S(2)}, u32[]{:S(2)}) collective-permute-start(bf16[256,512]{1,0:T(8,128)(2,1)S(1)} %lead.1), channel_id=1, source_target_pairs={{0,1},{1,0},{2,3},{3,2},{4,5},{5,4},{6,7},{7,6},{8,9},{9,8},{10,11... | collective-permute-start | bytes 786440 | tf_op jit(solution)/shard_map/ppermute | solution.py:19
  80.5 1.7 %emit.1 = (bf16[256,512]{1,0:T(8,128)(2,1)S(1)}, bf16[256,512]{1,0:T(8,128)(2,1)S(1)}, bf16[256,512]{1,0:T(8,128)(2,1)S(1)}, bf16[256,512]{1,0:T(8,128)(2,1)S(1)...) custom-call(bf16[256,128]{1,0:T(8,128)(2,1)S(1)} %get-tuple-element.63.refs_0_, ...), custom_call_target="tpu_custom_call" | custom-call | flops 1073741824 | bytes 6553600 | tf_op jit(solution)/shard_map/emit/pallas_call | solution.py:324
  82.2 0.6 collective-permute-start.28
  82.8 5.4 %collective-permute-done.30 = bf16[256,512]{1,0:T(8,128)(2,1)S(1)} collective-permute-done((bf16[256,512]{1,0:T(8,128)(2,1)S(1)}, bf16[256,512]{1,0:T(8,128)(2,1)S(1)}, u32[]{:S(2)}, u32[]{:S(2)}) %collective-permute-start.30) | collective-permute-done | bytes 262176 | tf_op jit(solution)/shard_map/ppermute | solution.py:19
  88.2 0.1 add_convert_fusion.2
  88.3 1.6 %collective-permute-start.33 = (bf16[256,512]{1,0:T(8,128)(2,1)S(1)}, bf16[256,512]{1,0:T(8,128)(2,1)S(1)}, u32[]{:S(2)}, u32[]{:S(2)}) collective-permute-start(bf16[256,512]{1,0:T(8,128)(2,1)S(1)} %get-tuple-element.78), channel_id=1, source_target_pairs={{0,1},{1,0},{2,3},{3,2},{4,5},{5,4},{6,7},{7,6},{8,9},{9,8},{10,11... | collective-permute-start | bytes 786440 | tf_op jit(solution)/shard_map/ppermute | solution.py:19
  89.8 3.6 %collective-permute-start.31 = (bf16[256,512]{1,0:T(8,128)(2,1)S(1)}, bf16[256,512]{1,0:T(8,128)(2,1)S(1)}, u32[]{:S(2)}, u32[]{:S(2)}) collective-permute-start(bf16[256,512]{1,0:T(8,128)(2,1)S(1)} %add_convert_fusion.2), channel_id=1, source_target_pairs={{0,6},{1,7},{2,4},{3,5},{4,2},{5,3},{6,0},{7,1},{8,14},{9,15},{10,... | collective-permute-start | bytes 786440 | tf_op jit(solution)/shard_map/ppermute | solution.py:19
  93.4 0.4 collective-permute-done.28
  93.8 0.1 add_convert_fusion.3
  93.9 2.2 %collective-permute-start.32 = (bf16[256,512]{1,0:T(8,128)(2,1)S(1)}, bf16[256,512]{1,0:T(8,128)(2,1)S(1)}, u32[]{:S(2)}, u32[]{:S(2)}) collective-permute-start(bf16[256,512]{1,0:T(8,128)(2,1)S(1)} %add_convert_fusion.3), channel_id=1, source_target_pairs={{0,4},{1,5},{2,6},{3,7},{4,0},{5,1},{6,2},{7,3},{8,12},{9,13},{10,... | collective-permute-start | bytes 786440 | tf_op jit(solution)/shard_map/ppermute | solution.py:19
  96.0 1.5 %collective-permute-start.29 = (bf16[256,512]{1,0:T(8,128)(2,1)S(1)}, bf16[256,512]{1,0:T(8,128)(2,1)S(1)}, u32[]{:S(2)}, u32[]{:S(2)}) collective-permute-start(bf16[256,512]{1,0:T(8,128)(2,1)S(1)} %get-tuple-element.74), channel_id=1, source_target_pairs={{0,1},{1,0},{2,3},{3,2},{4,5},{5,4},{6,7},{7,6},{8,9},{9,8},{10,11... | collective-permute-start | bytes 786440 | tf_op jit(solution)/shard_map/ppermute | solution.py:19
  97.6 1.9 %collective-permute-done.33 = bf16[256,512]{1,0:T(8,128)(2,1)S(1)} collective-permute-done((bf16[256,512]{1,0:T(8,128)(2,1)S(1)}, bf16[256,512]{1,0:T(8,128)(2,1)S(1)}, u32[]{:S(2)}, u32[]{:S(2)}) %collective-permute-start.33) | collective-permute-done | bytes 262176 | tf_op jit(solution)/shard_map/ppermute | solution.py:19
  99.4 0.1 add_convert_fusion.1
  99.5 1.3 %collective-permute-start.34 = (bf16[256,512]{1,0:T(8,128)(2,1)S(1)}, bf16[256,512]{1,0:T(8,128)(2,1)S(1)}, u32[]{:S(2)}, u32[]{:S(2)}) collective-permute-start(bf16[256,512]{1,0:T(8,128)(2,1)S(1)} %add_convert_fusion.1), channel_id=1, source_target_pairs={{0,2},{1,3},{2,0},{3,1},{4,6},{5,7},{6,4},{7,5},{8,10},{9,11},{10,... | collective-permute-start | bytes 786440 | tf_op jit(solution)/shard_map/ppermute | solution.py:19
  100.8 13.0 %collective-permute-done.32 = bf16[256,512]{1,0:T(8,128)(2,1)S(1)} collective-permute-done((bf16[256,512]{1,0:T(8,128)(2,1)S(1)}, bf16[256,512]{1,0:T(8,128)(2,1)S(1)}, u32[]{:S(2)}, u32[]{:S(2)}) %collective-permute-start.32) | collective-permute-done | bytes 262176 | tf_op jit(solution)/shard_map/ppermute | solution.py:19
  113.8 0.9 add_convert_fusion
  (35 shorter events, 0.2 us)
Async XLA Ops:
  0.0 50.0 %copy-start.1 = (bf16[1024,512]{1,0:T(8,128)(2,1)S(1)}, bf16[1024,512]{1,0:T(8,128)(2,1)}, u32[]{:S(2)}) copy-start(bf16[1024,512]{1,0:T(8,128)(2,1)} %refs_8_.2) | copy-start | bytes 3145732
  0.0 35.4 %copy-start = (bf16[512,1024]{1,0:T(8,128)(2,1)S(1)}, bf16[512,1024]{1,0:T(8,128)(2,1)}, u32[]{:S(2)}) copy-start(bf16[512,1024]{1,0:T(8,128)(2,1)} %refs_4_.3) | copy-start | bytes 3145732
  0.0 15.7 %collective-permute-start.3 = (bf16[256,512]{1,0:T(8,128)(2,1)}, bf16[256,512]{1,0:T(8,128)(2,1)S(1)}, u32[]{:S(2)}, u32[]{:S(2)}) collective-permute-start(bf16[256,512]{1,0:T(8,128)(2,1)} %close_ref.1), channel_id=1, source_target_pairs={{0,6},{1,7},{2,4},{3,5},{4,2},{5,3},{6,0},{7,1},{8,14},{9,15},{10,... | collective-permute-start | bytes 786440 | tf_op jit(solution)/shard_map/ppermute | solution.py:19
  5.1 13.3 %collective-permute-start.5 = (bf16[256,512]{1,0:T(8,128)(2,1)}, bf16[256,512]{1,0:T(8,128)(2,1)S(1)}, u32[]{:S(2)}, u32[]{:S(2)}) collective-permute-start(bf16[256,512]{1,0:T(8,128)(2,1)} %close_ref.1), channel_id=1, source_target_pairs={{0,2},{1,3},{2,0},{3,1},{4,6},{5,7},{6,4},{7,5},{8,10},{9,11},{10,... | collective-permute-start | bytes 786440 | tf_op jit(solution)/shard_map/ppermute | solution.py:19
  5.1 22.5 %collective-permute-start.6 = (bf16[256,512]{1,0:T(8,128)(2,1)}, bf16[256,512]{1,0:T(8,128)(2,1)S(1)}, u32[]{:S(2)}, u32[]{:S(2)}) collective-permute-start(bf16[256,512]{1,0:T(8,128)(2,1)} %close_ref.1), channel_id=1, source_target_pairs={{0,4},{1,5},{2,6},{3,7},{4,0},{5,1},{6,2},{7,3},{8,12},{9,13},{10,... | collective-permute-start | bytes 786440 | tf_op jit(solution)/shard_map/ppermute | solution.py:19
  5.7 44.3 %collective-permute-start.12 = (bf16[1024,512]{1,0:T(8,128)(2,1)}, bf16[1024,512]{1,0:T(8,128)(2,1)S(1)}, u32[]{:S(2)}, u32[]{:S(2)}) collective-permute-start(bf16[1024,512]{1,0:T(8,128)(2,1)} %refs_8_.2), channel_id=1, source_target_pairs={{0,8},{8,0},{16,24},{24,16},{1,9},{9,1},{17,25},{25,17},{2,10},{10... | collective-permute-start | bytes 3145736 | tf_op jit(solution)/shard_map/ppermute | solution.py:19
  5.7 3.3 %collective-permute-start.2 = (s32[2,8]{1,0:T(2,128)}, s32[2,8]{1,0:T(2,128)S(1)}, u32[]{:S(2)}, u32[]{:S(2)}) collective-permute-start(s32[2,8]{1,0:T(2,128)} %param.10), channel_id=1, source_target_pairs={{0,24},{8,16},{16,8},{24,0},{1,25},{9,17},{17,9},{25,1},{2,26},{10... | collective-permute-start | bytes 200 | tf_op jit(solution)/shard_map/ppermute | solution.py:19
  9.0 3.8 %collective-permute-start.1 = (s32[2,8]{1,0:T(2,128)}, s32[2,8]{1,0:T(2,128)S(1)}, u32[]{:S(2)}, u32[]{:S(2)}) collective-permute-start(s32[2,8]{1,0:T(2,128)} %param.10), channel_id=1, source_target_pairs={{0,16},{8,24},{16,0},{24,8},{1,17},{9,25},{17,1},{25,9},{2,18},{10... | collective-permute-start | bytes 200 | tf_op jit(solution)/shard_map/ppermute | solution.py:19
  12.7 1.4 %collective-permute-start = (s32[2,8]{1,0:T(2,128)}, s32[2,8]{1,0:T(2,128)S(1)}, u32[]{:S(2)}, u32[]{:S(2)}) collective-permute-start(s32[2,8]{1,0:T(2,128)} %param.10), channel_id=1, source_target_pairs={{0,8},{8,0},{16,24},{24,16},{1,9},{9,1},{17,25},{25,17},{2,10},{10... | collective-permute-start | bytes 200 | tf_op jit(solution)/shard_map/ppermute | solution.py:19
  14.1 21.4 %collective-permute-start.15 = (bf16[256,1024]{1,0:T(8,128)(2,1)S(1)}, bf16[256,1024]{1,0:T(8,128)(2,1)S(1)}, u32[]{:S(2)}, u32[]{:S(2)}) collective-permute-start(bf16[256,1024]{1,0:T(8,128)(2,1)S(1)} %slice.11), channel_id=1, source_target_pairs={{0,16},{8,24},{16,0},{24,8},{1,17},{9,25},{17,1},{25,9},{2,18},{10... | collective-permute-start | bytes 1572872 | tf_op jit(solution)/shard_map/ppermute | solution.py:19
  15.7 1.0 copy-start.3
  16.7 10.9 %collective-permute-start.4 = (bf16[256,512]{1,0:T(8,128)(2,1)S(1)}, bf16[256,512]{1,0:T(8,128)(2,1)S(1)}, u32[]{:S(2)}, u32[]{:S(2)}) collective-permute-start(bf16[256,512]{1,0:T(8,128)(2,1)S(1)} %get-tuple-element.42.refs_0_), channel_id=1, source_target_pairs={{0,1},{1,0},{2,3},{3,2},{4,5},{5,4},{6,7},{7,6},{8,9},{9,8},{10,11... | collective-permute-start | bytes 786440 | tf_op jit(solution)/shard_map/ppermute | solution.py:19
  18.3 15.5 %collective-permute-start.8 = (bf16[256,512]{1,0:T(8,128)(2,1)S(1)}, bf16[256,512]{1,0:T(8,128)(2,1)S(1)}, u32[]{:S(2)}, u32[]{:S(2)}) collective-permute-start(bf16[256,512]{1,0:T(8,128)(2,1)S(1)} %get-tuple-element.46), channel_id=1, source_target_pairs={{0,16},{8,24},{16,0},{24,8},{1,17},{9,25},{17,1},{25,9},{2,18},{10... | collective-permute-start | bytes 786440 | tf_op jit(solution)/shard_map/ppermute | solution.py:19
  27.6 25.3 %collective-permute-start.14 = (bf16[1024,512]{1,0:T(8,128)(2,1)}, bf16[1024,512]{1,0:T(8,128)(2,1)S(1)}, u32[]{:S(2)}, u32[]{:S(2)}) collective-permute-start(bf16[1024,512]{1,0:T(8,128)(2,1)} %refs_8_.3), channel_id=1, source_target_pairs={{0,8},{8,0},{16,24},{24,16},{1,9},{9,1},{17,25},{25,17},{2,10},{10... | collective-permute-start | bytes 3145736 | tf_op jit(solution)/shard_map/ppermute | solution.py:19
  27.6 8.8 %collective-permute-start.7 = (bf16[256,512]{1,0:T(8,128)(2,1)S(1)}, bf16[256,512]{1,0:T(8,128)(2,1)S(1)}, u32[]{:S(2)}, u32[]{:S(2)}) collective-permute-start(bf16[256,512]{1,0:T(8,128)(2,1)S(1)} %get-tuple-element.45.refs_2_), channel_id=1, source_target_pairs={{0,1},{1,0},{2,3},{3,2},{4,5},{5,4},{6,7},{7,6},{8,9},{9,8},{10,11... | collective-permute-start | bytes 786440 | tf_op jit(solution)/shard_map/ppermute | solution.py:19
  33.9 9.2 %collective-permute-start.10 = (bf16[256,512]{1,0:T(8,128)(2,1)S(1)}, bf16[256,512]{1,0:T(8,128)(2,1)S(1)}, u32[]{:S(2)}, u32[]{:S(2)}) collective-permute-start(bf16[256,512]{1,0:T(8,128)(2,1)S(1)} %get-tuple-element.47), channel_id=1, source_target_pairs={{0,16},{8,24},{16,0},{24,8},{1,17},{9,25},{17,1},{25,9},{2,18},{10... | collective-permute-start | bytes 786440 | tf_op jit(solution)/shard_map/ppermute | solution.py:19
  35.5 11.7 %collective-permute-start.16 = (bf16[128,1024]{1,0:T(8,128)(2,1)S(1)}, bf16[128,1024]{1,0:T(8,128)(2,1)S(1)}, u32[]{:S(2)}, u32[]{:S(2)}) collective-permute-start(bf16[128,1024]{1,0:T(8,128)(2,1)S(1)} %get-tuple-element.52), channel_id=1, source_target_pairs={{0,16},{8,24},{16,0},{24,8},{1,17},{9,25},{17,1},{25,9},{2,18},{10... | collective-permute-start | bytes 786440 | tf_op jit(solution)/shard_map/ppermute | solution.py:19
  36.4 10.8 %collective-permute-start.9 = (bf16[256,512]{1,0:T(8,128)(2,1)S(1)}, bf16[256,512]{1,0:T(8,128)(2,1)S(1)}, u32[]{:S(2)}, u32[]{:S(2)}) collective-permute-start(bf16[256,512]{1,0:T(8,128)(2,1)S(1)} %collective-permute-done.8.refs_4_), channel_id=1, source_target_pairs={{0,1},{1,0},{2,3},{3,2},{4,5},{5,4},{6,7},{7,6},{8,9},{9,8},{10,11... | collective-permute-start | bytes 786440 | tf_op jit(solution)/shard_map/ppermute | solution.py:19
  43.1 6.9 %collective-permute-start.11 = (bf16[256,512]{1,0:T(8,128)(2,1)S(1)}, bf16[256,512]{1,0:T(8,128)(2,1)S(1)}, u32[]{:S(2)}, u32[]{:S(2)}) collective-permute-start(bf16[256,512]{1,0:T(8,128)(2,1)S(1)} %collective-permute-done.10.refs_6_), channel_id=1, source_target_pairs={{0,1},{1,0},{2,3},{3,2},{4,5},{5,4},{6,7},{7,6},{8,9},{9,8},{10,11... | collective-permute-start | bytes 786440 | tf_op jit(solution)/shard_map/ppermute | solution.py:19
  47.2 31.4 %collective-permute-start.24 = (bf16[512,1024]{1,0:T(8,128)(2,1)S(1)}, bf16[512,1024]{1,0:T(8,128)(2,1)S(1)}, u32[]{:S(2)}, u32[]{:S(2)}) collective-permute-start(bf16[512,1024]{1,0:T(8,128)(2,1)S(1)} %copy-done), channel_id=1, source_target_pairs={{0,8},{8,0},{16,24},{24,16},{1,9},{9,1},{17,25},{25,17},{2,10},{10... | collective-permute-start | bytes 3145736 | tf_op jit(solution)/shard_map/ppermute | solution.py:19
  47.2 5.7 %copy-start.2 = (bf16[1024,512]{1,0:T(8,128)(2,1)S(1)}, bf16[1024,512]{1,0:T(8,128)(2,1)}, u32[]{:S(2)}) copy-start(bf16[1024,512]{1,0:T(8,128)(2,1)} %refs_8_.3) | copy-start | bytes 3145732
  47.2 9.2 %collective-permute-start.17 = (bf16[128,1024]{1,0:T(8,128)(2,1)S(1)}, bf16[128,1024]{1,0:T(8,128)(2,1)S(1)}, u32[]{:S(2)}, u32[]{:S(2)}) collective-permute-start(bf16[128,1024]{1,0:T(8,128)(2,1)S(1)} %get-tuple-element.53), channel_id=1, source_target_pairs={{0,16},{8,24},{16,0},{24,8},{1,17},{9,25},{17,1},{25,9},{2,18},{10... | collective-permute-start | bytes 786440 | tf_op jit(solution)/shard_map/ppermute | solution.py:19
  51.3 12.6 %copy-start.5 = (s32[2,8]{1,0:T(2,128)S(1)}, s32[2,8]{1,0:T(2,128)}, u32[]{:S(2)}) copy-start(s32[2,8]{1,0:T(2,128)} %param.10) | copy-start | bytes 196
  51.3 12.6 %copy-start.4 = (f32[237,4]{0,1:T(4,128)S(1)}, f32[237,4]{0,1:T(4,128)}, u32[]{:S(2)}) copy-start(f32[237,4]{0,1:T(4,128)} %param.11) | copy-start | bytes 11380
  51.3 10.2 %collective-permute-start.13 = (bf16[512,256]{1,0:T(8,128)(2,1)S(1)}, bf16[512,256]{1,0:T(8,128)(2,1)S(1)}, u32[]{:S(2)}, u32[]{:S(2)}) collective-permute-start(bf16[512,256]{1,0:T(8,128)(2,1)S(1)} %get-tuple-element.49), channel_id=1, source_target_pairs={{0,16},{8,24},{16,0},{24,8},{1,17},{9,25},{17,1},{25,9},{2,18},{10... | collective-permute-start | bytes 786440 | tf_op jit(solution)/shard_map/ppermute | solution.py:19
  52.8 21.6 %collective-permute-start.25 = (bf16[256,1024]{1,0:T(8,128)(2,1)S(1)}, bf16[256,1024]{1,0:T(8,128)(2,1)S(1)}, u32[]{:S(2)}, u32[]{:S(2)}) collective-permute-start(bf16[256,1024]{1,0:T(8,128)(2,1)S(1)} %collective-permute-done.15.refs_6_), channel_id=1, source_target_pairs={{0,8},{8,0},{16,24},{24,16},{1,9},{9,1},{17,25},{25,17},{2,10},{10... | collective-permute-start | bytes 1572872 | tf_op jit(solution)/shard_map/ppermute | solution.py:19
  61.6 1.9 %collective-permute-start.18 = (bf16[512,128]{1,0:T(8,128)(2,1)S(1)}, bf16[512,128]{1,0:T(8,128)(2,1)S(1)}, u32[]{:S(2)}, u32[]{:S(2)}) collective-permute-start(bf16[512,128]{1,0:T(8,128)(2,1)S(1)} %get-tuple-element.56), channel_id=1, source_target_pairs={{0,8},{8,0},{16,24},{24,16},{1,9},{9,1},{17,25},{25,17},{2,10},{10... | collective-permute-start | bytes 393224 | tf_op jit(solution)/shard_map/ppermute | solution.py:19
  61.7 8.7 %collective-permute-start.19 = (bf16[512,256]{1,0:T(8,128)(2,1)S(1)}, bf16[512,256]{1,0:T(8,128)(2,1)S(1)}, u32[]{:S(2)}, u32[]{:S(2)}) collective-permute-start(bf16[512,256]{1,0:T(8,128)(2,1)S(1)} %get-tuple-element.50), channel_id=1, source_target_pairs={{0,16},{8,24},{16,0},{24,8},{1,17},{9,25},{17,1},{25,9},{2,18},{10... | collective-permute-start | bytes 786440 | tf_op jit(solution)/shard_map/ppermute | solution.py:19
  63.3 9.5 %collective-permute-start.26 = (bf16[128,1024]{1,0:T(8,128)(2,1)S(1)}, bf16[128,1024]{1,0:T(8,128)(2,1)S(1)}, u32[]{:S(2)}, u32[]{:S(2)}) collective-permute-start(bf16[128,1024]{1,0:T(8,128)(2,1)S(1)} %collective-permute-done.16.refs_7_), channel_id=1, source_target_pairs={{0,8},{8,0},{16,24},{24,16},{1,9},{9,1},{17,25},{25,17},{2,10},{10... | collective-permute-start | bytes 786440 | tf_op jit(solution)/shard_map/ppermute | solution.py:19
  63.5 11.0 %collective-permute-start.27 = (bf16[128,1024]{1,0:T(8,128)(2,1)S(1)}, bf16[128,1024]{1,0:T(8,128)(2,1)S(1)}, u32[]{:S(2)}, u32[]{:S(2)}) collective-permute-start(bf16[128,1024]{1,0:T(8,128)(2,1)S(1)} %collective-permute-done.17.refs_8_), channel_id=1, source_target_pairs={{0,8},{8,0},{16,24},{24,16},{1,9},{9,1},{17,25},{25,17},{2,10},{10... | collective-permute-start | bytes 786440 | tf_op jit(solution)/shard_map/ppermute | solution.py:19
  70.5 1.4 %collective-permute-start.20 = (bf16[512,128]{1,0:T(8,128)(2,1)S(1)}, bf16[512,128]{1,0:T(8,128)(2,1)S(1)}, u32[]{:S(2)}, u32[]{:S(2)}) collective-permute-start(bf16[512,128]{1,0:T(8,128)(2,1)S(1)} %get-tuple-element.62), channel_id=1, source_target_pairs={{0,8},{8,0},{16,24},{24,16},{1,9},{9,1},{17,25},{25,17},{2,10},{10... | collective-permute-start | bytes 393224 | tf_op jit(solution)/shard_map/ppermute | solution.py:19
  72.6 1.9 %collective-permute-start.21 = (bf16[256,128]{1,0:T(8,128)(2,1)S(1)}, bf16[256,128]{1,0:T(8,128)(2,1)S(1)}, u32[]{:S(2)}, u32[]{:S(2)}) collective-permute-start(bf16[256,128]{1,0:T(8,128)(2,1)S(1)} %get-tuple-element.64), channel_id=1, source_target_pairs={{0,8},{8,0},{16,24},{24,16},{1,9},{9,1},{17,25},{25,17},{2,10},{10... | collective-permute-start | bytes 196616 | tf_op jit(solution)/shard_map/ppermute | solution.py:19
  72.8 4.4 %collective-permute-start.22 = (bf16[256,128]{1,0:T(8,128)(2,1)S(1)}, bf16[256,128]{1,0:T(8,128)(2,1)S(1)}, u32[]{:S(2)}, u32[]{:S(2)}) collective-permute-start(bf16[256,128]{1,0:T(8,128)(2,1)S(1)} %get-tuple-element.65), channel_id=1, source_target_pairs={{0,16},{8,24},{16,0},{24,8},{1,17},{9,25},{17,1},{25,9},{2,18},{10... | collective-permute-start | bytes 196616 | tf_op jit(solution)/shard_map/ppermute | solution.py:19
  74.4 4.1 %collective-permute-start.23 = (bf16[256,128]{1,0:T(8,128)(2,1)S(1)}, bf16[256,128]{1,0:T(8,128)(2,1)S(1)}, u32[]{:S(2)}, u32[]{:S(2)}) collective-permute-start(bf16[256,128]{1,0:T(8,128)(2,1)S(1)} %get-tuple-element.66), channel_id=1, source_target_pairs={{0,24},{8,16},{16,8},{24,0},{1,25},{9,17},{17,9},{25,1},{2,26},{10... | collective-permute-start | bytes 196616 | tf_op jit(solution)/shard_map/ppermute | solution.py:19
  79.0 9.2 %collective-permute-start.30 = (bf16[256,512]{1,0:T(8,128)(2,1)S(1)}, bf16[256,512]{1,0:T(8,128)(2,1)S(1)}, u32[]{:S(2)}, u32[]{:S(2)}) collective-permute-start(bf16[256,512]{1,0:T(8,128)(2,1)S(1)} %lead.1), channel_id=1, source_target_pairs={{0,1},{1,0},{2,3},{3,2},{4,5},{5,4},{6,7},{7,6},{8,9},{9,8},{10,11... | collective-permute-start | bytes 786440 | tf_op jit(solution)/shard_map/ppermute | solution.py:19
  82.2 11.6 %collective-permute-start.28 = (bf16[256,512]{1,0:T(8,128)(2,1)S(1)}, bf16[256,512]{1,0:T(8,128)(2,1)S(1)}, u32[]{:S(2)}, u32[]{:S(2)}) collective-permute-start(bf16[256,512]{1,0:T(8,128)(2,1)S(1)} %get-tuple-element.73), channel_id=1, source_target_pairs={{0,1},{1,0},{2,3},{3,2},{4,5},{5,4},{6,7},{7,6},{8,9},{9,8},{10,11... | collective-permute-start | bytes 786440 | tf_op jit(solution)/shard_map/ppermute | solution.py:19
  88.3 11.2 %collective-permute-start.33 = (bf16[256,512]{1,0:T(8,128)(2,1)S(1)}, bf16[256,512]{1,0:T(8,128)(2,1)S(1)}, u32[]{:S(2)}, u32[]{:S(2)}) collective-permute-start(bf16[256,512]{1,0:T(8,128)(2,1)S(1)} %get-tuple-element.78), channel_id=1, source_target_pairs={{0,1},{1,0},{2,3},{3,2},{4,5},{5,4},{6,7},{7,6},{8,9},{9,8},{10,11... | collective-permute-start | bytes 786440 | tf_op jit(solution)/shard_map/ppermute | solution.py:19
  89.8 23.9 %collective-permute-start.31 = (bf16[256,512]{1,0:T(8,128)(2,1)S(1)}, bf16[256,512]{1,0:T(8,128)(2,1)S(1)}, u32[]{:S(2)}, u32[]{:S(2)}) collective-permute-start(bf16[256,512]{1,0:T(8,128)(2,1)S(1)} %add_convert_fusion.2), channel_id=1, source_target_pairs={{0,6},{1,7},{2,4},{3,5},{4,2},{5,3},{6,0},{7,1},{8,14},{9,15},{10,... | collective-permute-start | bytes 786440 | tf_op jit(solution)/shard_map/ppermute | solution.py:19
  93.9 19.9 %collective-permute-start.32 = (bf16[256,512]{1,0:T(8,128)(2,1)S(1)}, bf16[256,512]{1,0:T(8,128)(2,1)S(1)}, u32[]{:S(2)}, u32[]{:S(2)}) collective-permute-start(bf16[256,512]{1,0:T(8,128)(2,1)S(1)} %add_convert_fusion.3), channel_id=1, source_target_pairs={{0,4},{1,5},{2,6},{3,7},{4,0},{5,1},{6,2},{7,3},{8,12},{9,13},{10,... | collective-permute-start | bytes 786440 | tf_op jit(solution)/shard_map/ppermute | solution.py:19
  96.0 17.7 %collective-permute-start.29 = (bf16[256,512]{1,0:T(8,128)(2,1)S(1)}, bf16[256,512]{1,0:T(8,128)(2,1)S(1)}, u32[]{:S(2)}, u32[]{:S(2)}) collective-permute-start(bf16[256,512]{1,0:T(8,128)(2,1)S(1)} %get-tuple-element.74), channel_id=1, source_target_pairs={{0,1},{1,0},{2,3},{3,2},{4,5},{5,4},{6,7},{7,6},{8,9},{9,8},{10,11... | collective-permute-start | bytes 786440 | tf_op jit(solution)/shard_map/ppermute | solution.py:19
  99.5 14.3 %collective-permute-start.34 = (bf16[256,512]{1,0:T(8,128)(2,1)S(1)}, bf16[256,512]{1,0:T(8,128)(2,1)S(1)}, u32[]{:S(2)}, u32[]{:S(2)}) collective-permute-start(bf16[256,512]{1,0:T(8,128)(2,1)S(1)} %add_convert_fusion.1), channel_id=1, source_target_pairs={{0,2},{1,3},{2,0},{3,1},{4,6},{5,7},{6,4},{7,5},{8,10},{9,11},{10,... | collective-permute-start | bytes 786440 | tf_op jit(solution)/shard_map/ppermute | solution.py:19

commit v9 on v8

--- a/solution.py
+++ b/solution.py
@@ -357,7 +357,7 @@
     moved_1y = [along(part) for part in moved_1]
     out_third = across(after(w_out[3 * depth // 4 :], moved_1[-1], out_second))
     qk_beside, val_beside = beside(w_qk), beside(w_val)
-
+    qk_beside = after(qk_beside, out_first)
     pieces = [keep_0, keep_0y, keep_1, keep_1y, moved_0, moved_0y, moved_1, moved_1y]
 
     qk_keep, qk_send = project(pieces, [w_qk, qk_beside])
@@ -372,7 +372,7 @@
 
     out_across = [out_first, out_second, out_third]
     out_beside = beside(after(w_out, moved_1[0]))
-    out_diagonal = [beside(after(piece, moved_1[0])) for piece in out_across[:2]] + [beside(out_third)]
+    out_diagonal = [beside(after(piece, total)) for piece in out_across[:2]] + [beside(out_third)]
     first_send = lead(attn, [[w_out], [out_beside], out_across, out_diagonal])
     terms = emit(attn, [[w_out], [out_beside], out_across, out_diagonal])
 

time: 115 us -> 112 us (0.974)
  starting transfers between devices: 40.1 us -> 33.8 us
  waiting for transfers between devices: 63.4 us -> 65.8 us
    ppermute x35, starting transfers between devices: 40.1 us -> 33.8 us  [swap(): return lax.ppermute(value, axis, [(i, i ^ mask) for i in range(peers)])]
    ppermute x35, waiting for transfers between devices: 63.4 us -> 65.8 us  [swap(): return lax.ppermute(value, axis, [(i, i ^ mask) for i in range(peers)])]
  transfers between devices with their start and end apart: 35 -> 35, of which waited for: 20 -> 17; matrix products, arithmetic and copies ran while one was open for 1% -> 2% of each run, Pallas kernels for 6% -> 7%
where the time goes in v9:
time: 112 us
  waiting for transfers between devices  65.8 us (59%)
  starting transfers between devices  33.8 us (30%)
  Pallas kernels  7.75 us (7%)
  local copies, waits for them, and re-layouts  3.12 us (3%)
    ppermute x35, waiting for transfers between devices, swap(): return lax.ppermute(value, axis, [(i, i ^ mask) for i in range(peers)])  65.8 us
    ppermute x35, starting transfers between devices, swap(): return lax.ppermute(value, axis, [(i, i ^ mask) for i in range(peers)])  33.8 us
    pallas_call x2, Pallas kernels, project(): pl.pallas_call(functools.partial(project_kernel, counts), out_shape=[jax....  2.6 us
  transfers between devices with their start and end apart: 35, of which 17 were waited for; matrix products, arithmetic and copies ran while one was open for 2% of the time, Pallas kernels for 7%

profile of v9, /device:TPU:0, one launch (start us, length us, event | category | flops | bytes accessed | tf_op | source)
XLA Modules:
  0.0 111.8 jit_solution(9745689034173780638)
XLA Ops:
  0.0 0.5 collective-permute-start.12
  0.5 4.7 %collective-permute-start.3 = (bf16[256,512]{1,0:T(8,128)(2,1)}, bf16[256,512]{1,0:T(8,128)(2,1)S(1)}, u32[]{:S(2)}, u32[]{:S(2)}) collective-permute-start(bf16[256,512]{1,0:T(8,128)(2,1)} %close_ref.1), channel_id=1, source_target_pairs={{0,6},{1,7},{2,4},{3,5},{4,2},{5,3},{6,0},{7,1},{8,14},{9,15},{10,... | collective-permute-start | bytes 786440 | tf_op jit(solution)/shard_map/ppermute | solution.py:19
  5.1 1.3 %collective-permute-start.2 = (s32[2,8]{1,0:T(2,128)}, s32[2,8]{1,0:T(2,128)S(1)}, u32[]{:S(2)}, u32[]{:S(2)}) collective-permute-start(s32[2,8]{1,0:T(2,128)} %param.10), channel_id=1, source_target_pairs={{0,24},{8,16},{16,8},{24,0},{1,25},{9,17},{17,9},{25,1},{2,26},{10... | collective-permute-start | bytes 200 | tf_op jit(solution)/shard_map/ppermute | solution.py:19
  6.4 0.5 collective-permute-start.1
  6.9 0.1 collective-permute-start
  7.0 1.1 slice.9
  8.1 0.3 collective-permute-done.2
  8.3 1.8 %collective-permute-done.1 = s32[2,8]{1,0:T(2,128)S(1)} collective-permute-done((s32[2,8]{1,0:T(2,128)}, s32[2,8]{1,0:T(2,128)S(1)}, u32[]{:S(2)}, u32[]{:S(2)}) %collective-permute-start.1) | collective-permute-done | bytes 96 | tf_op jit(solution)/shard_map/ppermute | solution.py:19
  10.2 0.5 collective-permute-start.13
  10.7 1.8 %collective-permute-done.3.distant_ref = bf16[256,512]{1,0:T(8,128)(2,1)S(1)} collective-permute-done((bf16[256,512]{1,0:T(8,128)(2,1)}, bf16[256,512]{1,0:T(8,128)(2,1)S(1)}, u32[]{:S(2)}, u32[]{:S(2)}) %collective-permute-start.3) | collective-permute-done | bytes 262176 | tf_op jit(solution)/shard_map/ppermute | solution.py:19
  12.6 0.9 copy-done.3
  13.5 1.7 %collective-permute-start.4 = (bf16[256,512]{1,0:T(8,128)(2,1)S(1)}, bf16[256,512]{1,0:T(8,128)(2,1)S(1)}, u32[]{:S(2)}, u32[]{:S(2)}) collective-permute-start(bf16[256,512]{1,0:T(8,128)(2,1)S(1)} %get-tuple-element.43.refs_0_), channel_id=1, source_target_pairs={{0,1},{1,0},{2,3},{3,2},{4,5},{5,4},{6,7},{7,6},{8,9},{9,8},{10,11... | collective-permute-start | bytes 786440 | tf_op jit(solution)/shard_map/ppermute | solution.py:19
  15.3 3.7 %collective-permute-done.5.close_ref = bf16[256,512]{1,0:T(8,128)(2,1)S(1)} collective-permute-done((bf16[256,512]{1,0:T(8,128)(2,1)}, bf16[256,512]{1,0:T(8,128)(2,1)S(1)}, u32[]{:S(2)}, u32[]{:S(2)}) %collective-permute-start.5) | collective-permute-done | bytes 262176 | tf_op jit(solution)/shard_map/ppermute | solution.py:19
  19.0 1.5 %collective-permute-start.8 = (bf16[256,512]{1,0:T(8,128)(2,1)S(1)}, bf16[256,512]{1,0:T(8,128)(2,1)S(1)}, u32[]{:S(2)}, u32[]{:S(2)}) collective-permute-start(bf16[256,512]{1,0:T(8,128)(2,1)S(1)} %get-tuple-element.47), channel_id=1, source_target_pairs={{0,16},{8,24},{16,0},{24,8},{1,17},{9,25},{17,1},{25,9},{2,18},{10... | collective-permute-start | bytes 786440 | tf_op jit(solution)/shard_map/ppermute | solution.py:19
  20.4 7.8 %collective-permute-done.6.distant_ref = bf16[256,512]{1,0:T(8,128)(2,1)S(1)} collective-permute-done((bf16[256,512]{1,0:T(8,128)(2,1)}, bf16[256,512]{1,0:T(8,128)(2,1)S(1)}, u32[]{:S(2)}, u32[]{:S(2)}) %collective-permute-start.6) | collective-permute-done | bytes 262176 | tf_op jit(solution)/shard_map/ppermute | solution.py:19
  28.3 1.1 fusion
  29.3 0.1 sort.3
  29.4 1.6 %collective-permute-start.10 = (bf16[256,512]{1,0:T(8,128)(2,1)S(1)}, bf16[256,512]{1,0:T(8,128)(2,1)S(1)}, u32[]{:S(2)}, u32[]{:S(2)}) collective-permute-start(bf16[256,512]{1,0:T(8,128)(2,1)S(1)} %get-tuple-element.48), channel_id=1, source_target_pairs={{0,16},{8,24},{16,0},{24,8},{1,17},{9,25},{17,1},{25,9},{2,18},{10... | collective-permute-start | bytes 786440 | tf_op jit(solution)/shard_map/ppermute | solution.py:19
  31.0 0.5 collective-permute-start.16
  31.5 1.5 %collective-permute-start.7 = (bf16[256,512]{1,0:T(8,128)(2,1)S(1)}, bf16[256,512]{1,0:T(8,128)(2,1)S(1)}, u32[]{:S(2)}, u32[]{:S(2)}) collective-permute-start(bf16[256,512]{1,0:T(8,128)(2,1)S(1)} %get-tuple-element.46.refs_2_), channel_id=1, source_target_pairs={{0,1},{1,0},{2,3},{3,2},{4,5},{5,4},{6,7},{7,6},{8,9},{9,8},{10,11... | collective-permute-start | bytes 786440 | tf_op jit(solution)/shard_map/ppermute | solution.py:19
  33.0 5.5 %collective-permute-done.10.refs_6_ = bf16[256,512]{1,0:T(8,128)(2,1)S(1)} collective-permute-done((bf16[256,512]{1,0:T(8,128)(2,1)S(1)}, bf16[256,512]{1,0:T(8,128)(2,1)S(1)}, u32[]{:S(2)}, u32[]{:S(2)}) %collective-permute-start.10) | collective-permute-done | bytes 262176 | tf_op jit(solution)/shard_map/ppermute | solution.py:19
  38.6 1.5 %collective-permute-start.9 = (bf16[256,512]{1,0:T(8,128)(2,1)S(1)}, bf16[256,512]{1,0:T(8,128)(2,1)S(1)}, u32[]{:S(2)}, u32[]{:S(2)}) collective-permute-start(bf16[256,512]{1,0:T(8,128)(2,1)S(1)} %collective-permute-done.8.refs_4_), channel_id=1, source_target_pairs={{0,1},{1,0},{2,3},{3,2},{4,5},{5,4},{6,7},{7,6},{8,9},{9,8},{10,11... | collective-permute-start | bytes 786440 | tf_op jit(solution)/shard_map/ppermute | solution.py:19
  40.1 3.7 %collective-permute-done.16.refs_7_ = bf16[128,1024]{1,0:T(8,128)(2,1)S(1)} collective-permute-done((bf16[128,1024]{1,0:T(8,128)(2,1)S(1)}, bf16[128,1024]{1,0:T(8,128)(2,1)S(1)}, u32[]{:S(2)}, u32[]{:S(2)}) %collective-permute-start.16) | collective-permute-done | bytes 262176 | tf_op jit(solution)/shard_map/ppermute | solution.py:19
  43.8 1.5 %collective-permute-start.11 = (bf16[256,512]{1,0:T(8,128)(2,1)S(1)}, bf16[256,512]{1,0:T(8,128)(2,1)S(1)}, u32[]{:S(2)}, u32[]{:S(2)}) collective-permute-start(bf16[256,512]{1,0:T(8,128)(2,1)S(1)} %collective-permute-done.10.refs_6_), channel_id=1, source_target_pairs={{0,1},{1,0},{2,3},{3,2},{4,5},{5,4},{6,7},{7,6},{8,9},{9,8},{10,11... | collective-permute-start | bytes 786440 | tf_op jit(solution)/shard_map/ppermute | solution.py:19
  45.4 1.6 %collective-permute-start.17 = (bf16[128,1024]{1,0:T(8,128)(2,1)S(1)}, bf16[128,1024]{1,0:T(8,128)(2,1)S(1)}, u32[]{:S(2)}, u32[]{:S(2)}) collective-permute-start(bf16[128,1024]{1,0:T(8,128)(2,1)S(1)} %get-tuple-element.55), channel_id=1, source_target_pairs={{0,16},{8,24},{16,0},{24,8},{1,17},{9,25},{17,1},{25,9},{2,18},{10... | collective-permute-start | bytes 786440 | tf_op jit(solution)/shard_map/ppermute | solution.py:19
  46.9 4.8 %collective-permute-done.11.refs_7_ = bf16[256,512]{1,0:T(8,128)(2,1)S(1)} collective-permute-done((bf16[256,512]{1,0:T(8,128)(2,1)S(1)}, bf16[256,512]{1,0:T(8,128)(2,1)S(1)}, u32[]{:S(2)}, u32[]{:S(2)}) %collective-permute-start.11) | collective-permute-done | bytes 262176 | tf_op jit(solution)/shard_map/ppermute | solution.py:19
  51.7 1.3 %project.2 = (f32[512,256]{1,0:T(8,128)S(1)}, bf16[512,256]{1,0:T(8,128)(2,1)S(1)}) custom-call(bf16[256,512]{1,0:T(8,128)(2,1)S(1)} %get-tuple-element.43.refs_0_, bf16[256,512]{1,0:T(8,128)(2,1)S(1)} %collective-permute-done.4.refs_1_, bf16[256,512]{1,0:T(8,128)(2,1)S(1)} %get-tuple-element.46.refs_2_, ...), custom_call_target="tpu_custom_call" | custom-call | flops 1073741824 | bytes 4980736 | tf_op jit(solution)/shard_map/project/pallas_call | solution.py:122
  53.1 1.6 %collective-permute-start.14 = (bf16[512,256]{1,0:T(8,128)(2,1)S(1)}, bf16[512,256]{1,0:T(8,128)(2,1)S(1)}, u32[]{:S(2)}, u32[]{:S(2)}) collective-permute-start(bf16[512,256]{1,0:T(8,128)(2,1)S(1)} %get-tuple-element.52), channel_id=1, source_target_pairs={{0,16},{8,24},{16,0},{24,8},{1,17},{9,25},{17,1},{25,9},{2,18},{10... | collective-permute-start | bytes 786440 | tf_op jit(solution)/shard_map/ppermute | solution.py:19
  54.6 1.3 %project.3 = (f32[512,256]{1,0:T(8,128)S(1)}, bf16[512,256]{1,0:T(8,128)(2,1)S(1)}) custom-call(bf16[256,512]{1,0:T(8,128)(2,1)S(1)} %get-tuple-element.43.refs_0_, bf16[256,512]{1,0:T(8,128)(2,1)S(1)} %collective-permute-done.4.refs_1_, bf16[256,512]{1,0:T(8,128)(2,1)S(1)} %get-tuple-element.46.refs_2_, ...), custom_call_target="tpu_custom_call" | custom-call | flops 1073741824 | bytes 4980736 | tf_op jit(solution)/shard_map/project/pallas_call | solution.py:122
  55.9 4.2 %collective-permute-done.14.moved_ref = bf16[512,256]{1,0:T(8,128)(2,1)S(1)} collective-permute-done((bf16[512,256]{1,0:T(8,128)(2,1)S(1)}, bf16[512,256]{1,0:T(8,128)(2,1)S(1)}, u32[]{:S(2)}, u32[]{:S(2)}) %collective-permute-start.14) | collective-permute-done | bytes 262176 | tf_op jit(solution)/shard_map/ppermute | solution.py:19
  60.2 0.1 combine.2
  60.2 0.1 collective-permute-start.18
  60.3 1.6 %collective-permute-start.19 = (bf16[512,256]{1,0:T(8,128)(2,1)S(1)}, bf16[512,256]{1,0:T(8,128)(2,1)S(1)}, u32[]{:S(2)}, u32[]{:S(2)}) collective-permute-start(bf16[512,256]{1,0:T(8,128)(2,1)S(1)} %get-tuple-element.53), channel_id=1, source_target_pairs={{0,16},{8,24},{16,0},{24,8},{1,17},{9,25},{17,1},{25,9},{2,18},{10... | collective-permute-start | bytes 786440 | tf_op jit(solution)/shard_map/ppermute | solution.py:19
  61.9 2.2 %weigh.1 = (bf16[1024,1024]{1,0:T(8,128)(2,1)S(1)}, f32[1024,1]{1,0:T(8,128)S(1)}) custom-call(s32[4,2,8]{2,1,0:T(2,128)S(1)} %pad_add_fusion.edge_ref, f32[4,237]{1,0:T(4,128)S(1)} %bitcast.5, bf16[512,128]{1,0:T(8,128)(2,1)S(1)} %get-tuple-element.57.mine_ref, bf16[512,128]{1,0:T(8,128)(2,1)S(1)} %collective-permute-done.18.theirs_ref), custom_call_target="tpu_custom_call" | custom-call | flops 268435456 | bytes 2097152 | tf_op jit(solution)/shard_map/weigh/pallas_call | solution.py:197
  64.1 0.2 collective-permute-start.25
  64.3 0.3 collective-permute-start.27
  64.7 4.4 %collective-permute-done.19.moved_ref = bf16[512,256]{1,0:T(8,128)(2,1)S(1)} collective-permute-done((bf16[512,256]{1,0:T(8,128)(2,1)S(1)}, bf16[512,256]{1,0:T(8,128)(2,1)S(1)}, u32[]{:S(2)}, u32[]{:S(2)}) %collective-permute-start.19) | collective-permute-done | bytes 262176 | tf_op jit(solution)/shard_map/ppermute | solution.py:19
  69.0 0.1 combine.3
  69.1 0.1 collective-permute-start.20
  69.2 0.5 collective-permute-start.26
  69.7 0.8 collective-permute-done.20.theirs_ref
  70.5 0.7 average.1
  71.2 0.2 collective-permute-start.21
  71.4 1.5 %collective-permute-start.22 = (bf16[256,128]{1,0:T(8,128)(2,1)S(1)}, bf16[256,128]{1,0:T(8,128)(2,1)S(1)}, u32[]{:S(2)}, u32[]{:S(2)}) collective-permute-start(bf16[256,128]{1,0:T(8,128)(2,1)S(1)} %get-tuple-element.67), channel_id=1, source_target_pairs={{0,16},{8,24},{16,0},{24,8},{1,17},{9,25},{17,1},{25,9},{2,18},{10... | collective-permute-start | bytes 196616 | tf_op jit(solution)/shard_map/ppermute | solution.py:19
  72.9 0.8 collective-permute-start.23
  73.8 2.0 %collective-permute-done.22.refs_2_ = bf16[256,128]{1,0:T(8,128)(2,1)S(1)} collective-permute-done((bf16[256,128]{1,0:T(8,128)(2,1)S(1)}, bf16[256,128]{1,0:T(8,128)(2,1)S(1)}, u32[]{:S(2)}, u32[]{:S(2)}) %collective-permute-start.22) | collective-permute-done | bytes 65568 | tf_op jit(solution)/shard_map/ppermute | solution.py:19
  75.8 1.3 %collective-permute-done.23.refs_3_ = bf16[256,128]{1,0:T(8,128)(2,1)S(1)} collective-permute-done((bf16[256,128]{1,0:T(8,128)(2,1)S(1)}, bf16[256,128]{1,0:T(8,128)(2,1)S(1)}, u32[]{:S(2)}, u32[]{:S(2)}) %collective-permute-start.23) | collective-permute-done | bytes 65568 | tf_op jit(solution)/shard_map/ppermute | solution.py:19
  77.1 0.4 lead.1
  77.5 1.6 %collective-permute-start.30 = (bf16[256,512]{1,0:T(8,128)(2,1)S(1)}, bf16[256,512]{1,0:T(8,128)(2,1)S(1)}, u32[]{:S(2)}, u32[]{:S(2)}) collective-permute-start(bf16[256,512]{1,0:T(8,128)(2,1)S(1)} %lead.1), channel_id=1, source_target_pairs={{0,1},{1,0},{2,3},{3,2},{4,5},{5,4},{6,7},{7,6},{8,9},{9,8},{10,11... | collective-permute-start | bytes 786440 | tf_op jit(solution)/shard_map/ppermute | solution.py:19
  79.1 1.7 %emit.1 = (bf16[256,512]{1,0:T(8,128)(2,1)S(1)}, bf16[256,512]{1,0:T(8,128)(2,1)S(1)}, bf16[256,512]{1,0:T(8,128)(2,1)S(1)}, bf16[256,512]{1,0:T(8,128)(2,1)S(1)...) custom-call(bf16[256,128]{1,0:T(8,128)(2,1)S(1)} %get-tuple-element.65.refs_0_, ...), custom_call_target="tpu_custom_call" | custom-call | flops 1073741824 | bytes 6553600 | tf_op jit(solution)/shard_map/emit/pallas_call | solution.py:324
  80.8 0.6 collective-permute-start.28
  81.3 5.4 %collective-permute-done.30 = bf16[256,512]{1,0:T(8,128)(2,1)S(1)} collective-permute-done((bf16[256,512]{1,0:T(8,128)(2,1)S(1)}, bf16[256,512]{1,0:T(8,128)(2,1)S(1)}, u32[]{:S(2)}, u32[]{:S(2)}) %collective-permute-start.30) | collective-permute-done | bytes 262176 | tf_op jit(solution)/shard_map/ppermute | solution.py:19
  86.7 0.1 add_convert_fusion.2
  86.8 1.6 %collective-permute-start.33 = (bf16[256,512]{1,0:T(8,128)(2,1)S(1)}, bf16[256,512]{1,0:T(8,128)(2,1)S(1)}, u32[]{:S(2)}, u32[]{:S(2)}) collective-permute-start(bf16[256,512]{1,0:T(8,128)(2,1)S(1)} %get-tuple-element.80), channel_id=1, source_target_pairs={{0,1},{1,0},{2,3},{3,2},{4,5},{5,4},{6,7},{7,6},{8,9},{9,8},{10,11... | collective-permute-start | bytes 786440 | tf_op jit(solution)/shard_map/ppermute | solution.py:19
  88.4 2.5 %collective-permute-start.31 = (bf16[256,512]{1,0:T(8,128)(2,1)S(1)}, bf16[256,512]{1,0:T(8,128)(2,1)S(1)}, u32[]{:S(2)}, u32[]{:S(2)}) collective-permute-start(bf16[256,512]{1,0:T(8,128)(2,1)S(1)} %add_convert_fusion.2), channel_id=1, source_target_pairs={{0,6},{1,7},{2,4},{3,5},{4,2},{5,3},{6,0},{7,1},{8,14},{9,15},{10,... | collective-permute-start | bytes 786440 | tf_op jit(solution)/shard_map/ppermute | solution.py:19
  90.9 1.5 %collective-permute-done.28 = bf16[256,512]{1,0:T(8,128)(2,1)S(1)} collective-permute-done((bf16[256,512]{1,0:T(8,128)(2,1)S(1)}, bf16[256,512]{1,0:T(8,128)(2,1)S(1)}, u32[]{:S(2)}, u32[]{:S(2)}) %collective-permute-start.28) | collective-permute-done | bytes 262176 | tf_op jit(solution)/shard_map/ppermute | solution.py:19
  92.4 0.1 add_convert_fusion.3
  92.4 0.1 collective-permute-start.32
  92.5 1.6 %collective-permute-start.29 = (bf16[256,512]{1,0:T(8,128)(2,1)S(1)}, bf16[256,512]{1,0:T(8,128)(2,1)S(1)}, u32[]{:S(2)}, u32[]{:S(2)}) collective-permute-start(bf16[256,512]{1,0:T(8,128)(2,1)S(1)} %get-tuple-element.76), channel_id=1, source_target_pairs={{0,1},{1,0},{2,3},{3,2},{4,5},{5,4},{6,7},{7,6},{8,9},{9,8},{10,11... | collective-permute-start | bytes 786440 | tf_op jit(solution)/shard_map/ppermute | solution.py:19
  94.1 3.9 %collective-permute-done.33 = bf16[256,512]{1,0:T(8,128)(2,1)S(1)} collective-permute-done((bf16[256,512]{1,0:T(8,128)(2,1)S(1)}, bf16[256,512]{1,0:T(8,128)(2,1)S(1)}, u32[]{:S(2)}, u32[]{:S(2)}) %collective-permute-start.33) | collective-permute-done | bytes 262176 | tf_op jit(solution)/shard_map/ppermute | solution.py:19
  98.0 0.1 add_convert_fusion.1
  98.0 0.1 collective-permute-start.34
  98.1 12.7 %collective-permute-done.32 = bf16[256,512]{1,0:T(8,128)(2,1)S(1)} collective-permute-done((bf16[256,512]{1,0:T(8,128)(2,1)S(1)}, bf16[256,512]{1,0:T(8,128)(2,1)S(1)}, u32[]{:S(2)}, u32[]{:S(2)}) %collective-permute-start.32) | collective-permute-done | bytes 262176 | tf_op jit(solution)/shard_map/ppermute | solution.py:19
  110.9 0.9 add_convert_fusion
  (35 shorter events, 0.1 us)
Async XLA Ops:
  0.0 51.7 %copy-start.1 = (bf16[1024,512]{1,0:T(8,128)(2,1)S(1)}, bf16[1024,512]{1,0:T(8,128)(2,1)}, u32[]{:S(2)}) copy-start(bf16[1024,512]{1,0:T(8,128)(2,1)} %refs_8_.2) | copy-start | bytes 3145732
  0.0 45.3 %copy-start = (bf16[512,1024]{1,0:T(8,128)(2,1)S(1)}, bf16[512,1024]{1,0:T(8,128)(2,1)}, u32[]{:S(2)}) copy-start(bf16[512,1024]{1,0:T(8,128)(2,1)} %refs_4_.3) | copy-start | bytes 3145732
  0.0 45.3 %collective-permute-start.12 = (bf16[1024,512]{1,0:T(8,128)(2,1)}, bf16[1024,512]{1,0:T(8,128)(2,1)S(1)}, u32[]{:S(2)}, u32[]{:S(2)}) collective-permute-start(bf16[1024,512]{1,0:T(8,128)(2,1)} %refs_8_.2), channel_id=1, source_target_pairs={{0,8},{8,0},{16,24},{24,16},{1,9},{9,1},{17,25},{25,17},{2,10},{10... | collective-permute-start | bytes 3145736 | tf_op jit(solution)/shard_map/ppermute | solution.py:19
  0.5 12.1 %collective-permute-start.3 = (bf16[256,512]{1,0:T(8,128)(2,1)}, bf16[256,512]{1,0:T(8,128)(2,1)S(1)}, u32[]{:S(2)}, u32[]{:S(2)}) collective-permute-start(bf16[256,512]{1,0:T(8,128)(2,1)} %close_ref.1), channel_id=1, source_target_pairs={{0,6},{1,7},{2,4},{3,5},{4,2},{5,3},{6,0},{7,1},{8,14},{9,15},{10,... | collective-permute-start | bytes 786440 | tf_op jit(solution)/shard_map/ppermute | solution.py:19
  5.1 3.2 %collective-permute-start.2 = (s32[2,8]{1,0:T(2,128)}, s32[2,8]{1,0:T(2,128)S(1)}, u32[]{:S(2)}, u32[]{:S(2)}) collective-permute-start(s32[2,8]{1,0:T(2,128)} %param.10), channel_id=1, source_target_pairs={{0,24},{8,16},{16,8},{24,0},{1,25},{9,17},{17,9},{25,1},{2,26},{10... | collective-permute-start | bytes 200 | tf_op jit(solution)/shard_map/ppermute | solution.py:19
  6.4 3.8 %collective-permute-start.1 = (s32[2,8]{1,0:T(2,128)}, s32[2,8]{1,0:T(2,128)S(1)}, u32[]{:S(2)}, u32[]{:S(2)}) collective-permute-start(s32[2,8]{1,0:T(2,128)} %param.10), channel_id=1, source_target_pairs={{0,16},{8,24},{16,0},{24,8},{1,17},{9,25},{17,1},{25,9},{2,18},{10... | collective-permute-start | bytes 200 | tf_op jit(solution)/shard_map/ppermute | solution.py:19
  6.9 3.2 %collective-permute-start = (s32[2,8]{1,0:T(2,128)}, s32[2,8]{1,0:T(2,128)S(1)}, u32[]{:S(2)}, u32[]{:S(2)}) collective-permute-start(s32[2,8]{1,0:T(2,128)} %param.10), channel_id=1, source_target_pairs={{0,8},{8,0},{16,24},{24,16},{1,9},{9,1},{17,25},{25,17},{2,10},{10... | collective-permute-start | bytes 200 | tf_op jit(solution)/shard_map/ppermute | solution.py:19
  8.3 10.6 %collective-permute-start.5 = (bf16[256,512]{1,0:T(8,128)(2,1)}, bf16[256,512]{1,0:T(8,128)(2,1)S(1)}, u32[]{:S(2)}, u32[]{:S(2)}) collective-permute-start(bf16[256,512]{1,0:T(8,128)(2,1)} %close_ref.1), channel_id=1, source_target_pairs={{0,2},{1,3},{2,0},{3,1},{4,6},{5,7},{6,4},{7,5},{8,10},{9,11},{10,... | collective-permute-start | bytes 786440 | tf_op jit(solution)/shard_map/ppermute | solution.py:19
  10.2 20.8 %collective-permute-start.13 = (bf16[256,1024]{1,0:T(8,128)(2,1)S(1)}, bf16[256,1024]{1,0:T(8,128)(2,1)S(1)}, u32[]{:S(2)}, u32[]{:S(2)}) collective-permute-start(bf16[256,1024]{1,0:T(8,128)(2,1)S(1)} %slice.9), channel_id=1, source_target_pairs={{0,16},{8,24},{16,0},{24,8},{1,17},{9,25},{17,1},{25,9},{2,18},{10... | collective-permute-start | bytes 1572872 | tf_op jit(solution)/shard_map/ppermute | solution.py:19
  10.7 17.5 %collective-permute-start.6 = (bf16[256,512]{1,0:T(8,128)(2,1)}, bf16[256,512]{1,0:T(8,128)(2,1)S(1)}, u32[]{:S(2)}, u32[]{:S(2)}) collective-permute-start(bf16[256,512]{1,0:T(8,128)(2,1)} %close_ref.1), channel_id=1, source_target_pairs={{0,4},{1,5},{2,6},{3,7},{4,0},{5,1},{6,2},{7,3},{8,12},{9,13},{10,... | collective-permute-start | bytes 786440 | tf_op jit(solution)/shard_map/ppermute | solution.py:19
  12.5 1.0 copy-start.3
  13.5 15.8 %collective-permute-start.4 = (bf16[256,512]{1,0:T(8,128)(2,1)S(1)}, bf16[256,512]{1,0:T(8,128)(2,1)S(1)}, u32[]{:S(2)}, u32[]{:S(2)}) collective-permute-start(bf16[256,512]{1,0:T(8,128)(2,1)S(1)} %get-tuple-element.43.refs_0_), channel_id=1, source_target_pairs={{0,1},{1,0},{2,3},{3,2},{4,5},{5,4},{6,7},{7,6},{8,9},{9,8},{10,11... | collective-permute-start | bytes 786440 | tf_op jit(solution)/shard_map/ppermute | solution.py:19
  19.0 12.0 %collective-permute-start.8 = (bf16[256,512]{1,0:T(8,128)(2,1)S(1)}, bf16[256,512]{1,0:T(8,128)(2,1)S(1)}, u32[]{:S(2)}, u32[]{:S(2)}) collective-permute-start(bf16[256,512]{1,0:T(8,128)(2,1)S(1)} %get-tuple-element.47), channel_id=1, source_target_pairs={{0,16},{8,24},{16,0},{24,8},{1,17},{9,25},{17,1},{25,9},{2,18},{10... | collective-permute-start | bytes 786440 | tf_op jit(solution)/shard_map/ppermute | solution.py:19
  28.3 26.4 %collective-permute-start.15 = (bf16[1024,512]{1,0:T(8,128)(2,1)}, bf16[1024,512]{1,0:T(8,128)(2,1)S(1)}, u32[]{:S(2)}, u32[]{:S(2)}) collective-permute-start(bf16[1024,512]{1,0:T(8,128)(2,1)} %refs_8_.3), channel_id=1, source_target_pairs={{0,8},{8,0},{16,24},{24,16},{1,9},{9,1},{17,25},{25,17},{2,10},{10... | collective-permute-start | bytes 3145736 | tf_op jit(solution)/shard_map/ppermute | solution.py:19
  29.4 9.2 %collective-permute-start.10 = (bf16[256,512]{1,0:T(8,128)(2,1)S(1)}, bf16[256,512]{1,0:T(8,128)(2,1)S(1)}, u32[]{:S(2)}, u32[]{:S(2)}) collective-permute-start(bf16[256,512]{1,0:T(8,128)(2,1)S(1)} %get-tuple-element.48), channel_id=1, source_target_pairs={{0,16},{8,24},{16,0},{24,8},{1,17},{9,25},{17,1},{25,9},{2,18},{10... | collective-permute-start | bytes 786440 | tf_op jit(solution)/shard_map/ppermute | solution.py:19
  31.0 12.8 %collective-permute-start.16 = (bf16[128,1024]{1,0:T(8,128)(2,1)S(1)}, bf16[128,1024]{1,0:T(8,128)(2,1)S(1)}, u32[]{:S(2)}, u32[]{:S(2)}) collective-permute-start(bf16[128,1024]{1,0:T(8,128)(2,1)S(1)} %get-tuple-element.54), channel_id=1, source_target_pairs={{0,16},{8,24},{16,0},{24,8},{1,17},{9,25},{17,1},{25,9},{2,18},{10... | collective-permute-start | bytes 786440 | tf_op jit(solution)/shard_map/ppermute | solution.py:19
  31.5 13.8 %collective-permute-start.7 = (bf16[256,512]{1,0:T(8,128)(2,1)S(1)}, bf16[256,512]{1,0:T(8,128)(2,1)S(1)}, u32[]{:S(2)}, u32[]{:S(2)}) collective-permute-start(bf16[256,512]{1,0:T(8,128)(2,1)S(1)} %get-tuple-element.46.refs_2_), channel_id=1, source_target_pairs={{0,1},{1,0},{2,3},{3,2},{4,5},{5,4},{6,7},{7,6},{8,9},{9,8},{10,11... | collective-permute-start | bytes 786440 | tf_op jit(solution)/shard_map/ppermute | solution.py:19
  38.6 8.3 %collective-permute-start.9 = (bf16[256,512]{1,0:T(8,128)(2,1)S(1)}, bf16[256,512]{1,0:T(8,128)(2,1)S(1)}, u32[]{:S(2)}, u32[]{:S(2)}) collective-permute-start(bf16[256,512]{1,0:T(8,128)(2,1)S(1)} %collective-permute-done.8.refs_4_), channel_id=1, source_target_pairs={{0,1},{1,0},{2,3},{3,2},{4,5},{5,4},{6,7},{7,6},{8,9},{9,8},{10,11... | collective-permute-start | bytes 786440 | tf_op jit(solution)/shard_map/ppermute | solution.py:19
  43.8 7.9 %collective-permute-start.11 = (bf16[256,512]{1,0:T(8,128)(2,1)S(1)}, bf16[256,512]{1,0:T(8,128)(2,1)S(1)}, u32[]{:S(2)}, u32[]{:S(2)}) collective-permute-start(bf16[256,512]{1,0:T(8,128)(2,1)S(1)} %collective-permute-done.10.refs_6_), channel_id=1, source_target_pairs={{0,1},{1,0},{2,3},{3,2},{4,5},{5,4},{6,7},{7,6},{8,9},{9,8},{10,11... | collective-permute-start | bytes 786440 | tf_op jit(solution)/shard_map/ppermute | solution.py:19
  45.3 31.8 %collective-permute-start.24 = (bf16[512,1024]{1,0:T(8,128)(2,1)S(1)}, bf16[512,1024]{1,0:T(8,128)(2,1)S(1)}, u32[]{:S(2)}, u32[]{:S(2)}) collective-permute-start(bf16[512,1024]{1,0:T(8,128)(2,1)S(1)} %copy-done), channel_id=1, source_target_pairs={{0,8},{8,0},{16,24},{24,16},{1,9},{9,1},{17,25},{25,17},{2,10},{10... | collective-permute-start | bytes 3145736 | tf_op jit(solution)/shard_map/ppermute | solution.py:19
  45.3 9.3 %copy-start.2 = (bf16[1024,512]{1,0:T(8,128)(2,1)S(1)}, bf16[1024,512]{1,0:T(8,128)(2,1)}, u32[]{:S(2)}) copy-start(bf16[1024,512]{1,0:T(8,128)(2,1)} %refs_8_.3) | copy-start | bytes 3145732
  45.4 10.6 %collective-permute-start.17 = (bf16[128,1024]{1,0:T(8,128)(2,1)S(1)}, bf16[128,1024]{1,0:T(8,128)(2,1)S(1)}, u32[]{:S(2)}, u32[]{:S(2)}) collective-permute-start(bf16[128,1024]{1,0:T(8,128)(2,1)S(1)} %get-tuple-element.55), channel_id=1, source_target_pairs={{0,16},{8,24},{16,0},{24,8},{1,17},{9,25},{17,1},{25,9},{2,18},{10... | collective-permute-start | bytes 786440 | tf_op jit(solution)/shard_map/ppermute | solution.py:19
  53.0 8.8 %copy-start.5 = (s32[2,8]{1,0:T(2,128)S(1)}, s32[2,8]{1,0:T(2,128)}, u32[]{:S(2)}) copy-start(s32[2,8]{1,0:T(2,128)} %param.10) | copy-start | bytes 196
  53.1 8.8 %copy-start.4 = (f32[237,4]{0,1:T(4,128)S(1)}, f32[237,4]{0,1:T(4,128)}, u32[]{:S(2)}) copy-start(f32[237,4]{0,1:T(4,128)} %param.11) | copy-start | bytes 11380
  53.1 7.1 %collective-permute-start.14 = (bf16[512,256]{1,0:T(8,128)(2,1)S(1)}, bf16[512,256]{1,0:T(8,128)(2,1)S(1)}, u32[]{:S(2)}, u32[]{:S(2)}) collective-permute-start(bf16[512,256]{1,0:T(8,128)(2,1)S(1)} %get-tuple-element.52), channel_id=1, source_target_pairs={{0,16},{8,24},{16,0},{24,8},{1,17},{9,25},{17,1},{25,9},{2,18},{10... | collective-permute-start | bytes 786440 | tf_op jit(solution)/shard_map/ppermute | solution.py:19
  60.2 1.7 %collective-permute-start.18 = (bf16[512,128]{1,0:T(8,128)(2,1)S(1)}, bf16[512,128]{1,0:T(8,128)(2,1)S(1)}, u32[]{:S(2)}, u32[]{:S(2)}) collective-permute-start(bf16[512,128]{1,0:T(8,128)(2,1)S(1)} %get-tuple-element.58), channel_id=1, source_target_pairs={{0,8},{8,0},{16,24},{24,16},{1,9},{9,1},{17,25},{25,17},{2,10},{10... | collective-permute-start | bytes 393224 | tf_op jit(solution)/shard_map/ppermute | solution.py:19
  60.3 8.7 %collective-permute-start.19 = (bf16[512,256]{1,0:T(8,128)(2,1)S(1)}, bf16[512,256]{1,0:T(8,128)(2,1)S(1)}, u32[]{:S(2)}, u32[]{:S(2)}) collective-permute-start(bf16[512,256]{1,0:T(8,128)(2,1)S(1)} %get-tuple-element.53), channel_id=1, source_target_pairs={{0,16},{8,24},{16,0},{24,8},{1,17},{9,25},{17,1},{25,9},{2,18},{10... | collective-permute-start | bytes 786440 | tf_op jit(solution)/shard_map/ppermute | solution.py:19
  64.1 13.0 %collective-permute-start.25 = (bf16[256,1024]{1,0:T(8,128)(2,1)S(1)}, bf16[256,1024]{1,0:T(8,128)(2,1)S(1)}, u32[]{:S(2)}, u32[]{:S(2)}) collective-permute-start(bf16[256,1024]{1,0:T(8,128)(2,1)S(1)} %collective-permute-done.13.refs_6_), channel_id=1, source_target_pairs={{0,8},{8,0},{16,24},{24,16},{1,9},{9,1},{17,25},{25,17},{2,10},{10... | collective-permute-start | bytes 1572872 | tf_op jit(solution)/shard_map/ppermute | solution.py:19
  64.3 7.1 %collective-permute-start.27 = (bf16[128,1024]{1,0:T(8,128)(2,1)S(1)}, bf16[128,1024]{1,0:T(8,128)(2,1)S(1)}, u32[]{:S(2)}, u32[]{:S(2)}) collective-permute-start(bf16[128,1024]{1,0:T(8,128)(2,1)S(1)} %collective-permute-done.17.refs_8_), channel_id=1, source_target_pairs={{0,8},{8,0},{16,24},{24,16},{1,9},{9,1},{17,25},{25,17},{2,10},{10... | collective-permute-start | bytes 786440 | tf_op jit(solution)/shard_map/ppermute | solution.py:19
  69.1 1.4 %collective-permute-start.20 = (bf16[512,128]{1,0:T(8,128)(2,1)S(1)}, bf16[512,128]{1,0:T(8,128)(2,1)S(1)}, u32[]{:S(2)}, u32[]{:S(2)}) collective-permute-start(bf16[512,128]{1,0:T(8,128)(2,1)S(1)} %get-tuple-element.64), channel_id=1, source_target_pairs={{0,8},{8,0},{16,24},{24,16},{1,9},{9,1},{17,25},{25,17},{2,10},{10... | collective-permute-start | bytes 393224 | tf_op jit(solution)/shard_map/ppermute | solution.py:19
  69.2 7.9 %collective-permute-start.26 = (bf16[128,1024]{1,0:T(8,128)(2,1)S(1)}, bf16[128,1024]{1,0:T(8,128)(2,1)S(1)}, u32[]{:S(2)}, u32[]{:S(2)}) collective-permute-start(bf16[128,1024]{1,0:T(8,128)(2,1)S(1)} %collective-permute-done.16.refs_7_), channel_id=1, source_target_pairs={{0,8},{8,0},{16,24},{24,16},{1,9},{9,1},{17,25},{25,17},{2,10},{10... | collective-permute-start | bytes 786440 | tf_op jit(solution)/shard_map/ppermute | solution.py:19
  71.2 1.7 %collective-permute-start.21 = (bf16[256,128]{1,0:T(8,128)(2,1)S(1)}, bf16[256,128]{1,0:T(8,128)(2,1)S(1)}, u32[]{:S(2)}, u32[]{:S(2)}) collective-permute-start(bf16[256,128]{1,0:T(8,128)(2,1)S(1)} %get-tuple-element.66), channel_id=1, source_target_pairs={{0,8},{8,0},{16,24},{24,16},{1,9},{9,1},{17,25},{25,17},{2,10},{10... | collective-permute-start | bytes 196616 | tf_op jit(solution)/shard_map/ppermute | solution.py:19
  71.4 4.4 %collective-permute-start.22 = (bf16[256,128]{1,0:T(8,128)(2,1)S(1)}, bf16[256,128]{1,0:T(8,128)(2,1)S(1)}, u32[]{:S(2)}, u32[]{:S(2)}) collective-permute-start(bf16[256,128]{1,0:T(8,128)(2,1)S(1)} %get-tuple-element.67), channel_id=1, source_target_pairs={{0,16},{8,24},{16,0},{24,8},{1,17},{9,25},{17,1},{25,9},{2,18},{10... | collective-permute-start | bytes 196616 | tf_op jit(solution)/shard_map/ppermute | solution.py:19
  72.9 4.1 %collective-permute-start.23 = (bf16[256,128]{1,0:T(8,128)(2,1)S(1)}, bf16[256,128]{1,0:T(8,128)(2,1)S(1)}, u32[]{:S(2)}, u32[]{:S(2)}) collective-permute-start(bf16[256,128]{1,0:T(8,128)(2,1)S(1)} %get-tuple-element.68), channel_id=1, source_target_pairs={{0,24},{8,16},{16,8},{24,0},{1,25},{9,17},{17,9},{25,1},{2,26},{10... | collective-permute-start | bytes 196616 | tf_op jit(solution)/shard_map/ppermute | solution.py:19
  77.5 9.2 %collective-permute-start.30 = (bf16[256,512]{1,0:T(8,128)(2,1)S(1)}, bf16[256,512]{1,0:T(8,128)(2,1)S(1)}, u32[]{:S(2)}, u32[]{:S(2)}) collective-permute-start(bf16[256,512]{1,0:T(8,128)(2,1)S(1)} %lead.1), channel_id=1, source_target_pairs={{0,1},{1,0},{2,3},{3,2},{4,5},{5,4},{6,7},{7,6},{8,9},{9,8},{10,11... | collective-permute-start | bytes 786440 | tf_op jit(solution)/shard_map/ppermute | solution.py:19
  80.8 11.6 %collective-permute-start.28 = (bf16[256,512]{1,0:T(8,128)(2,1)S(1)}, bf16[256,512]{1,0:T(8,128)(2,1)S(1)}, u32[]{:S(2)}, u32[]{:S(2)}) collective-permute-start(bf16[256,512]{1,0:T(8,128)(2,1)S(1)} %get-tuple-element.75), channel_id=1, source_target_pairs={{0,1},{1,0},{2,3},{3,2},{4,5},{5,4},{6,7},{7,6},{8,9},{9,8},{10,11... | collective-permute-start | bytes 786440 | tf_op jit(solution)/shard_map/ppermute | solution.py:19
  86.8 11.2 %collective-permute-start.33 = (bf16[256,512]{1,0:T(8,128)(2,1)S(1)}, bf16[256,512]{1,0:T(8,128)(2,1)S(1)}, u32[]{:S(2)}, u32[]{:S(2)}) collective-permute-start(bf16[256,512]{1,0:T(8,128)(2,1)S(1)} %get-tuple-element.80), channel_id=1, source_target_pairs={{0,1},{1,0},{2,3},{3,2},{4,5},{5,4},{6,7},{7,6},{8,9},{9,8},{10,11... | collective-permute-start | bytes 786440 | tf_op jit(solution)/shard_map/ppermute | solution.py:19
  88.4 22.5 %collective-permute-start.31 = (bf16[256,512]{1,0:T(8,128)(2,1)S(1)}, bf16[256,512]{1,0:T(8,128)(2,1)S(1)}, u32[]{:S(2)}, u32[]{:S(2)}) collective-permute-start(bf16[256,512]{1,0:T(8,128)(2,1)S(1)} %add_convert_fusion.2), channel_id=1, source_target_pairs={{0,6},{1,7},{2,4},{3,5},{4,2},{5,3},{6,0},{7,1},{8,14},{9,15},{10,... | collective-permute-start | bytes 786440 | tf_op jit(solution)/shard_map/ppermute | solution.py:19
  92.4 18.4 %collective-permute-start.32 = (bf16[256,512]{1,0:T(8,128)(2,1)S(1)}, bf16[256,512]{1,0:T(8,128)(2,1)S(1)}, u32[]{:S(2)}, u32[]{:S(2)}) collective-permute-start(bf16[256,512]{1,0:T(8,128)(2,1)S(1)} %add_convert_fusion.3), channel_id=1, source_target_pairs={{0,4},{1,5},{2,6},{3,7},{4,0},{5,1},{6,2},{7,3},{8,12},{9,13},{10,... | collective-permute-start | bytes 786440 | tf_op jit(solution)/shard_map/ppermute | solution.py:19
  92.5 18.4 %collective-permute-start.29 = (bf16[256,512]{1,0:T(8,128)(2,1)S(1)}, bf16[256,512]{1,0:T(8,128)(2,1)S(1)}, u32[]{:S(2)}, u32[]{:S(2)}) collective-permute-start(bf16[256,512]{1,0:T(8,128)(2,1)S(1)} %get-tuple-element.76), channel_id=1, source_target_pairs={{0,1},{1,0},{2,3},{3,2},{4,5},{5,4},{6,7},{7,6},{8,9},{9,8},{10,11... | collective-permute-start | bytes 786440 | tf_op jit(solution)/shard_map/ppermute | solution.py:19
  98.0 12.8 %collective-permute-start.34 = (bf16[256,512]{1,0:T(8,128)(2,1)S(1)}, bf16[256,512]{1,0:T(8,128)(2,1)S(1)}, u32[]{:S(2)}, u32[]{:S(2)}) collective-permute-start(bf16[256,512]{1,0:T(8,128)(2,1)S(1)} %add_convert_fusion.1), channel_id=1, source_target_pairs={{0,2},{1,3},{2,0},{3,1},{4,6},{5,7},{6,4},{7,5},{8,10},{9,11},{10,... | collective-permute-start | bytes 786440 | tf_op jit(solution)/shard_map/ppermute | solution.py:19
